TPU v7x, 128 devices: a whole 4x4x4 slice. The times are simulated.
128 devices in a mesh: patch: 32 (over z, x, core), feat: 4 (over y).
Axes of the slice: x: 4, y: 4, z: 4, core: 2. Of those that a mesh axis runs over, the one named last changes fastest.
Arguments:
- node_lat: bfloat16 [32768, 512], P(('patch', 'feat')), may hold values from -6 to 6
- edge_lat: bfloat16 [262144, 512], P(('patch', 'feat')), may hold values from -6 to 6
- edge_src: int32 [262144], P(('patch', 'feat')), may hold values from 0 to 831, as said below
- edge_dst: int32 [262144], P(('patch', 'feat')), may hold values from 0 to 255
- edge_count: int32 [128], P(('patch', 'feat')), may hold values from 512 to 2048, as said below
- halo_send: int32 [128, 2, 32], P(('patch', 'feat')), may hold values from 0 to 255
- coarse_of: int32 [128, 4], P(('patch', 'feat')), may hold values from 0 to 255
- edge_w1: bfloat16 [3, 512, 512], P(None, None, 'feat'), may hold values from -0.15625 to 0.15625
- edge_w2: bfloat16 [512, 512], P('feat'), may hold values from -0.25 to 0.25
- node_w1: bfloat16 [2, 512, 512], P(None, None, 'feat'), may hold values from -0.1875 to 0.1875
- node_w2: bfloat16 [512, 512], P('feat'), may hold values from -0.25 to 0.25
- grad_node: bfloat16 [32768, 512], P(('patch', 'feat')), may hold values from -6 to 6
- grad_edge: bfloat16 [262144, 512], P(('patch', 'feat')), may hold values from -6 to 6
Outputs:
- edge_out: bfloat16 [262144, 512], P(('patch', 'feat'))
- node_out: bfloat16 [32768, 512], P(('patch', 'feat'))
- node_grad: float32 [32768, 512], P(('patch', 'feat'))
- edge_grad: bfloat16 [262144, 512], P(('patch', 'feat'))
- edge_w1_grad: float32 [3, 512, 512], P(None, None, 'feat')
- edge_w2_grad: float32 [512, 512], P('feat')
- node_w1_grad: float32 [2, 512, 512], P(None, None, 'feat')
- node_w2_grad: float32 [512, 512], P('feat')
Inputs may be any that keep to these rules, and one draw needn't show every extreme that they name: `edge_src`: below 256: a node of the device; then 32 rows from the previous device, 32 rows from the next device, then the 512 coarse rows, all in the order of the lookup. `edge_count`: A multiple of 128; the first that many edge slots of the device are live, the others are padding; some device is full. `halo_send`: node rows of the device; list 0 goes to the previous device, list 1 to the next. `coarse_of`: node rows of the device. `edge_dst`: A node row of the device.
All inputs are finite; a program needn't handle non-finite values.
Results may differ from a plain program's by a relative error of at most 0.013.
Values may be sent and summed in bfloat16 or wider, within the bound.
No kernel may reach another device: no remote copies, remote signals or barrier semaphores. Data moves between devices by JAX's collectives and lax.ppermute only.
A program may use at most 128 MiB of HBM per device.

v0:
```python
import jax
import jax.numpy as jnp
from jax import lax
from jax.sharding import PartitionSpec as P

EPSILON = 1e-05


def shifted(value, axis, steps):
    count = lax.axis_size(axis)
    pairs = [(source, (source + steps) % count) for source in range(count)]
    return lax.ppermute(value, axis, pairs)


def product(left, right):
    return jnp.dot(left, right, preferred_element_type=jnp.float32)


def contract_rows(left, right):
    return lax.dot_general(
        left, right, (((0,), (0,)), ((), ())), preferred_element_type=jnp.float32
    )


def times_transposed(left, right):
    return lax.dot_general(
        left, right, (((1,), (1,)), ((), ())), preferred_element_type=jnp.float32
    )


def exact_transposed(left, right):
    return lax.dot_general(
        left,
        right.astype(jnp.float32),
        (((1,), (1,)), ((), ())),
        precision=lax.Precision.HIGHEST,
        preferred_element_type=jnp.float32,
    )


def normalize(values):
    centre = values - jnp.mean(values, axis=-1, keepdims=True)
    factor = lax.rsqrt(jnp.mean(centre * centre, axis=-1, keepdims=True) + EPSILON)
    return (centre * factor, factor)


def normalize_back(upstream, normed, factor):
    first_mean = jnp.mean(upstream, axis=-1, keepdims=True)
    second_mean = jnp.mean(upstream * normed, axis=-1, keepdims=True)
    return factor * (upstream - first_mean - normed * second_mean)


def swish_slope(values):
    sigmoid = jax.nn.sigmoid(values)
    return sigmoid * (1.0 + values * (1.0 - sigmoid))


def one_hot_rows(indices, count):
    return (indices[:, None] == jnp.arange(count, dtype=jnp.int32)[None, :]).astype(jnp.bfloat16)


def local_step(
    node_rows,
    lookup_table,
    edge_rows,
    senders,
    receivers,
    live_count,
    upstream_node,
    upstream_edge,
    edge_first,
    edge_second,
    node_first,
    node_second,
):
    node_number = node_rows.shape[0]
    recv_hot = one_hot_rows(receivers, node_number)
    send_hot = one_hot_rows(senders, lookup_table.shape[0])
    sender_rows = product(send_hot, lookup_table).astype(jnp.bfloat16)
    receiver_rows = product(recv_hot, node_rows).astype(jnp.bfloat16)
    edge_pre = (
        product(edge_rows, edge_first[0])
        + product(sender_rows, edge_first[1])
        + product(receiver_rows, edge_first[2])
    )
    edge_act = jax.nn.silu(edge_pre).astype(jnp.bfloat16)
    edge_normed, edge_factor = normalize(product(edge_act, edge_second))
    live_flag = jnp.arange(edge_rows.shape[0]) < live_count
    active = live_flag.astype(jnp.float32)[:, None]
    edge_new = (edge_rows.astype(jnp.float32) + active * edge_normed).astype(jnp.bfloat16)
    live_hot = recv_hot * live_flag.astype(jnp.bfloat16)[:, None]
    incoming = contract_rows(live_hot, edge_new).astype(jnp.bfloat16)
    node_pre = product(node_rows, node_first[0]) + product(incoming, node_first[1])
    node_act = jax.nn.silu(node_pre).astype(jnp.bfloat16)
    node_normed, node_factor = normalize(product(node_act, node_second))
    node_new = (node_rows.astype(jnp.float32) + node_normed).astype(jnp.bfloat16)
    upstream = upstream_node.astype(jnp.float32)
    node_delta = normalize_back(upstream, node_normed, node_factor).astype(jnp.bfloat16)
    grad_node_second = contract_rows(node_act, node_delta)
    node_pre_grad = (times_transposed(node_delta, node_second) * swish_slope(node_pre)).astype(
        jnp.bfloat16
    )
    grad_node_first = jnp.stack(
        [contract_rows(node_rows, node_pre_grad), contract_rows(incoming, node_pre_grad)]
    )
    node_total = upstream + times_transposed(node_pre_grad, node_first[0])
    edge_node_grad = product(recv_hot, node_pre_grad).astype(jnp.bfloat16)
    edge_total = upstream_edge.astype(jnp.float32) + active * times_transposed(
        edge_node_grad, node_first[1]
    )
    edge_delta = normalize_back(active * edge_total, edge_normed, edge_factor).astype(jnp.bfloat16)
    grad_edge_second = contract_rows(edge_act, edge_delta)
    edge_pre_grad = (times_transposed(edge_delta, edge_second) * swish_slope(edge_pre)).astype(
        jnp.bfloat16
    )
    grad_edge_first = jnp.stack(
        [
            contract_rows(edge_rows, edge_pre_grad),
            contract_rows(sender_rows, edge_pre_grad),
            contract_rows(receiver_rows, edge_pre_grad),
        ]
    )
    edge_out_grad = (edge_total + times_transposed(edge_pre_grad, edge_first[0])).astype(
        jnp.bfloat16
    )
    node_total = node_total + exact_transposed(
        contract_rows(recv_hot, edge_pre_grad), edge_first[2]
    )
    lookup_grad = exact_transposed(contract_rows(send_hot, edge_pre_grad), edge_first[1])
    node_total = node_total + lookup_grad[:node_number]
    return (
        edge_new,
        node_new,
        edge_out_grad,
        node_total,
        lookup_grad[node_number:],
        (grad_edge_first, grad_edge_second, grad_node_first, grad_node_second),
    )


def shards(
    node_lat,
    edge_lat,
    edge_src,
    edge_dst,
    edge_count,
    halo_send,
    coarse_of,
    edge_w1,
    edge_w2,
    node_w1,
    node_w2,
    grad_node,
    grad_edge,
):
    edge_first, node_first = (
        lax.all_gather(edge_w1, "feat", axis=2, tiled=True),
        lax.all_gather(node_w1, "feat", axis=2, tiled=True),
    )
    edge_second, node_second = (
        lax.all_gather(edge_w2, "feat", axis=0, tiled=True),
        lax.all_gather(node_w2, "feat", axis=0, tiled=True),
    )
    send_lists = halo_send[0]
    owned_index = coarse_of[0]
    halo_width = send_lists.shape[1]
    from_prev = shifted(node_lat[send_lists[1]], ("patch", "feat"), 1)
    from_next = shifted(node_lat[send_lists[0]], ("patch", "feat"), -1)
    owned_rows = node_lat[owned_index]
    coarse_rows = lax.all_gather(owned_rows, ("patch", "feat"), axis=0, tiled=True)
    lookup_table = jnp.concatenate([node_lat, from_prev, from_next, coarse_rows], axis=0)
    edge_new, node_new, edge_out_grad, node_total, remote_grad, weight_grads = local_step(
        node_lat,
        lookup_table,
        edge_lat,
        edge_src,
        edge_dst,
        edge_count[0],
        grad_node,
        grad_edge,
        edge_first,
        edge_second,
        node_first,
        node_second,
    )
    back_ahead = shifted(
        remote_grad[:halo_width].astype(jnp.bfloat16), ("patch", "feat"), -1
    ).astype(jnp.float32)
    back_behind = shifted(
        remote_grad[halo_width : 2 * halo_width].astype(jnp.bfloat16), ("patch", "feat"), 1
    ).astype(jnp.float32)
    node_total = node_total.at[send_lists[1]].add(back_ahead).at[send_lists[0]].add(back_behind)
    coarse_grad = remote_grad[2 * halo_width :]
    owned_grad = lax.psum_scatter(coarse_grad, ("patch", "feat"), scatter_dimension=0, tiled=True)
    node_total = node_total.at[owned_index].add(owned_grad)
    first_edge_grad, second_edge_grad, first_node_grad, second_node_grad = weight_grads
    local_width = edge_w1.shape[2]
    summed = lax.psum(
        (first_edge_grad, second_edge_grad, first_node_grad, second_node_grad), ("patch", "feat")
    )
    offset = lax.axis_index("feat") * local_width
    edge_first_grad = lax.dynamic_slice_in_dim(summed[0], offset, local_width, 2)
    edge_second_grad = lax.dynamic_slice_in_dim(summed[1], offset, local_width, 0)
    node_first_grad = lax.dynamic_slice_in_dim(summed[2], offset, local_width, 2)
    node_second_grad = lax.dynamic_slice_in_dim(summed[3], offset, local_width, 0)
    return (
        edge_new,
        node_new,
        node_total,
        edge_out_grad,
        edge_first_grad,
        edge_second_grad,
        node_first_grad,
        node_second_grad,
    )


def solution(mesh):
    placed = (
        P(("patch", "feat"), None),
        P(("patch", "feat"), None),
        P(("patch", "feat")),
        P(("patch", "feat")),
        P(("patch", "feat")),
        P(("patch", "feat"), None, None),
        P(("patch", "feat"), None),
        P(None, None, "feat"),
        P("feat", None),
        P(None, None, "feat"),
        P("feat", None),
        P(("patch", "feat"), None),
        P(("patch", "feat"), None),
    )
    return jax.shard_map(
        shards,
        mesh=mesh,
        in_specs=placed,
        out_specs=(
            P(("patch", "feat"), None),
            P(("patch", "feat"), None),
            P(("patch", "feat"), None),
            P(("patch", "feat"), None),
            P(None, None, "feat"),
            P("feat", None),
            P(None, None, "feat"),
            P("feat", None),
        ),
        check_vma=False,
    )
```

profile of v0, /device:TPU:1, one launch (start us, length us, event | category | flops | bytes accessed | tf_op | source)
XLA Modules:
  0.0 349.1 jit_solution(8136843327356264502)
XLA Ops:
  9.5 1.6 gather_fusion.1
  11.1 4.2 %collective-permute-start.1 = (bf16[32,512]{1,0:T(8,128)(2,1)S(1)}, bf16[32,512]{1,0:T(8,128)(2,1)S(1)}, u32[]{:S(2)}, u32[]{:S(2)}) collective-permute-start(bf16[32,512]{1,0:T(8,128)(2,1)S(1)} %gather_fusion.1), channel_id=1, source_target_pairs={{0,127},{1,0},{2,1},{3,2},{4,3},{5,4},{6,5},{7,6},{8,7},{9,8},{10,... | collective-permute-start | bytes 98312 | tf_op jit(solution)/shard_map/ppermute | solution.py:12
  15.3 1.6 gather_fusion
  17.7 1.6 gather_fusion.2
  19.9 12.9 %all_gather.17 = bf16[512,512]{1,0:T(8,128)(2,1)S(1)} all-gather(bf16[128,512]{1,0:T(8,128)(2,1)} %param.21), channel_id=1, replica_groups=mesh['patch'=32,'feat'=4] {'feat'}, dimensions={0}, use_global_device_ids=true | all-gather | bytes 655360 | tf_op jit(solution)/shard_map/all_gather | solution.py:161
  32.8 13.5 %all_gather.19 = bf16[512,512]{1,0:T(8,128)(2,1)} all-gather(bf16[128,512]{1,0:T(8,128)(2,1)} %param.23), channel_id=1, replica_groups=mesh['patch'=32,'feat'=4] {'feat'}, dimensions={0}, use_global_device_ids=true | all-gather | bytes 655360 | tf_op jit(solution)/shard_map/all_gather | solution.py:162
  46.3 56.8 %all-gather.1 = bf16[128,4,512]{2,1,0:T(4,128)(2,1)S(1)} all-gather(bf16[1,4,512]{2,1,0:T(4,128)(2,1)S(1)} %bitcast.88), channel_id=2, replica_groups=mesh['patch'=32,'feat'=4] {'patch','feat'}, dimensions={0}, use_global_device_ids=true | all-gather | bytes 528384 | tf_op jit(solution)/shard_map/all_gather | solution.py:170
  103.1 2.0 convolution_convert_fusion.1
  105.1 2.4 copy.31
  108.4 4.0 %copy.32 = bf16[2048,512]{0,1:T(8,128)(2,1)} copy(bf16[2048,512]{1,0:T(8,128)(2,1)} %param.25) | data formatting | bytes 4194304 | tf_op args[12]
  112.4 4.4 %fusion.4 = bf16[2048,512]{1,0:T(8,128)(2,1)} fusion(s32[2048]{0:T(1024)S(1)} %copy-done.34, bf16[512,512]{1,0:T(8,128)(2,1)S(1)} %copy-done.32, bf16[32,512]{1,0:T(8,128)(2,1)S(1)} %collective-permute-done.1, bf16[32,512]{1,0:T(8,128)(2,1)} %collective-permute-done, bf16[256,512]{1,0:T(8,128)(2,1)S(1)} %copy-done.3), kind=kOutput, calls=%fused_computation.24 | convolution fusion | flops 1750990848 | bytes 2957312 | tf_op jit(solution)/shard_map/dot_general | solution.py:16
  116.8 2.1 fusion.31
  119.0 2.4 fusion.28
  121.4 1.3 fusion.30
  123.0 3.9 %multiply_convert_fusion.2 = (bf16[2048,512]{1,0:T(8,128)(2,1)S(1)}, f32[2048,512]{1,0:T(8,128)}) fusion(bf16[2048,512]{1,0:T(8,128)(2,1)S(1)} %copy-done.7, bf16[3,512,512]{2,1,0:T(8,128)(2,1)S(1)} %copy-done.12, f32[2048,512]{1,0:T(8,128)S(1)} %fusion.28, f32[2048,512]{1,0:T(8,128)S(1)} %fusion.30), kind=kOutput, calls=%fused_computation.16 | convolution fusion | flops 1081081856 | bytes 17301504 | tf_op jit(solution)/shard_map/dot_general | solution.py:16
  126.9 1.3 fusion.50
  128.8 1.6 copy-done
  132.3 1.4 convolution_convert_fusion.2
  136.8 1.2 fusion.8
  138.0 5.9 %multiply_reduce_fusion.2 = (f32[2048]{0:T(1024)S(1)}, f32[2048]{0:T(1024)S(1)}, f32[2048,512]{0,1:T(8,128)}) fusion(f32[2048]{0:T(1024)S(1)} %fusion.39, f32[2048]{0:T(1024)S(1)} %add_rsqrt_fusion, f32[2048,512]{0,1:T(8,128)} %copy-done, f32[2048]{0:T(1024)S(1)} %broadcast_multiply_fusion.2, bf16[2,512,512]{2,1,0:T(8,128)(2,1)S(1)} %copy-done.16, ...), kind=kOutput, calls=%fused_computation.20 | convolution fusion | flops 1621618688 | bytes 11321344 | tf_op jit(solution)/shard_map/dot_general | solution.py:26
  143.9 4.7 %multiply_convert_fusion.1 = bf16[2048,512]{0,1:T(8,128)(2,1)S(1)} fusion(f32[2048,512]{0,1:T(8,128)} %get-tuple-element.44, f32[2048,512]{0,1:T(8,128)} %copy-done, f32[2048]{0:T(1024)S(1)} %broadcast_multiply_fusion, f32[2048]{0:T(1024)S(1)} %broadcast_multiply_fusion.1, f32[2048]{0:T(1024)S(1)} %add_rsqrt_fusion, f32[2048]{0:T(1024)S(1)} %broadcast_multiply_fusion.2, ...), kind=kLoop, calls=%fused_computation.11 | loop fusion | flops 8388608 | bytes 10526720 | tf_op jit(solution)/shard_map/convert_element_type | solution.py:111
  148.7 2.5 multiply_convert_fusion
  151.2 2.5 fusion
  153.7 1.3 convolution_bitcast_fusion.2
  155.3 1.3 convolution_bitcast_fusion.3
  156.6 1.3 convolution_bitcast_fusion.4
  158.2 2.3 fusion.53
  161.8 1.5 fusion.45
  163.4 2.8 fusion.52
  166.1 1.2 copy-done.11
  167.3 1.0 slice.73
  168.3 1.5 pad_maximum_fusion.1
  169.8 2.1 pad_maximum_fusion
  172.7 3.3 collective-permute-start.2
  176.4 2.9 fusion.5
  179.2 4.3 %add_convert_fusion = bf16[2048,512]{0,1:T(8,128)(2,1)} fusion(f32[2048,512]{0,1:T(8,128)S(1)} %copy-done.1, bf16[2048,512]{1,0:T(8,128)(2,1)} %copy-done.18, bf16[3,512,512]{2,1,0:T(8,128)(2,1)S(1)} %copy-done.13), kind=kOutput, calls=%fused_computation.9 | convolution fusion | flops 1075838976 | bytes 8912896 | tf_op jit(solution)/shard_map/dot_general | solution.py:26
  183.5 2.0 fusion.7
  185.6 2.5 copy.37
  188.1 4.0 %copy.38 = bf16[2048,512]{1,0:T(8,128)(2,1)} copy(bf16[2048,512]{0,1:T(8,128)(2,1)} %add_convert_fusion) | data formatting | bytes 4194304
  192.1 1.0 scatter_custom_fusion
  193.1 1.0 scatter_custom_fusion.1
  194.1 138.9 %all-reduce.4.cloned.1.call-done = (f32[512,512]{1,0:T(8,128)}, f32[3,512,512]{1,2,0:T(8,128)}, f32[512,512]{1,0:T(8,128)}, f32[2,512,512]{1,2,0:T(8,128)}, f32[512,512]{1,0:T(8,128)}) async-done(((f32[512,512]{1,0:T(8,128)}, f32[3,512,512]{1,2,0:T(8,128)}, f32[512,512]{1,0:T(8,128)}, f32[2,512,512]{1,2,0:T(8,128)}, f32[512,512]{1,0:T(8,128)}), (f32[512,512]{1,0:T(8,128)}, f32[3,512,512]{1,2,0:T(8,128)}, ...) | async-done | bytes 8388624
  333.0 1.2 constant_dynamic-slice_fusion.3
  334.2 1.1 copy.39
  335.3 1.7 constant_dynamic-slice_fusion.2
  337.0 1.1 constant_dynamic-slice_fusion.1
  339.1 1.7 constant_dynamic-slice_fusion
  340.7 1.0 scatter_custom_fusion.2
  (110 shorter events, 14.6 us)
Async XLA Ops:
  7.2 95.9 %copy-start.3 = (bf16[256,512]{1,0:T(8,128)(2,1)S(1)}, bf16[256,512]{1,0:T(8,128)(2,1)}, u32[]{:S(2)}) copy-start(bf16[256,512]{1,0:T(8,128)(2,1)} %param.13) | copy-start | bytes 786436
  7.2 95.9 %copy-start.33 = (s32[2048]{0:T(1024)S(1)}, s32[2048]{0:T(1024)}, u32[]{:S(2)}) copy-start(s32[2048]{0:T(1024)} %param.16) | copy-start | bytes 24580
  7.2 109.6 %all-gather.7.cloned.1.call-start = ((), (), s32[]{:S(2)}) async-start(), calls=%async_computation.1 | async-start | bytes 1310720 | tf_op jit(solution)/shard_map/all_gather | solution.py:158
  7.9 111.0 %all-gather.5.cloned.1.call-start = ((), (), s32[]{:S(2)}) async-start(), calls=%async_computation | async-start | bytes 1966080 | tf_op jit(solution)/shard_map/all_gather | solution.py:157
  8.7 324.3 %all-reduce.4.cloned.1.call-start = ((), (), s32[]{:S(2)}) async-start(), calls=%async_computation.2 | async-start | bytes 16777216
  11.1 101.3 %collective-permute-start.1 = (bf16[32,512]{1,0:T(8,128)(2,1)S(1)}, bf16[32,512]{1,0:T(8,128)(2,1)S(1)}, u32[]{:S(2)}, u32[]{:S(2)}) collective-permute-start(bf16[32,512]{1,0:T(8,128)(2,1)S(1)} %gather_fusion.1), channel_id=1, source_target_pairs={{0,127},{1,0},{2,1},{3,2},{4,3},{5,4},{6,5},{7,6},{8,7},{9,8},{10,... | collective-permute-start | bytes 98312 | tf_op jit(solution)/shard_map/ppermute | solution.py:12
  16.9 95.5 %collective-permute-start = (bf16[32,512]{1,0:T(8,128)(2,1)S(1)}, bf16[32,512]{1,0:T(8,128)(2,1)}, u32[]{:S(2)}, u32[]{:S(2)}) collective-permute-start(bf16[32,512]{1,0:T(8,128)(2,1)S(1)} %gather_fusion), channel_id=1, source_target_pairs={{0,1},{1,2},{2,3},{3,4},{4,5},{5,6},{6,7},{7,8},{8,9},{9,10},{10,1... | collective-permute-start | bytes 98312 | tf_op jit(solution)/shard_map/ppermute | solution.py:12
  32.8 94.1 %copy-start.19 = (bf16[512,512]{1,0:T(8,128)(2,1)}, bf16[512,512]{1,0:T(8,128)(2,1)S(1)}, u32[]{:S(2)}) copy-start(bf16[512,512]{1,0:T(8,128)(2,1)S(1)} %all_gather.17) | copy-start | bytes 1572868
  103.1 2.0 copy-start.2
  108.4 4.1 %copy-start.32 = (bf16[512,512]{1,0:T(8,128)(2,1)S(1)}, bf16[512,512]{1,0:T(8,128)(2,1)}, u32[]{:S(2)}) copy-start(bf16[512,512]{1,0:T(8,128)(2,1)} %reshape.204) | copy-start | bytes 1572868
  108.4 4.1 %copy-start.34 = (s32[2048]{0:T(1024)S(1)}, s32[2048]{0:T(1024)}, u32[]{:S(2)}) copy-start(s32[2048]{0:T(1024)} %param.15) | copy-start | bytes 24580
  119.0 2.4 copy-start.12
  119.0 2.5 copy-start.14
  121.4 1.6 copy-start.7
  126.9 1.3 copy-start.9
  128.3 2.1 copy-start
  128.3 3.1 copy-start.6
  132.3 1.4 copy-start.4
  132.3 2.0 copy-start.16
  132.3 2.1 copy-start.21
  132.3 2.4 copy-start.31
  134.4 0.7 copy-start.26
  134.7 2.1 copy-start.28
  134.7 1.1 copy-start.24
  135.2 1.7 copy-start.22
  143.9 4.8 %copy-start.20 = (bf16[512,512]{1,0:T(8,128)(2,1)S(1)}, bf16[512,512]{1,0:T(8,128)(2,1)}, u32[]{:S(2)}) copy-start(bf16[512,512]{1,0:T(8,128)(2,1)} %copy-done.19) | copy-start | bytes 1572868
  143.9 4.8 %copy-start.35 = (f32[2048,512]{1,0:T(8,128)S(1)}, f32[2048,512]{1,0:T(8,128)}, u32[]{:S(2)}) copy-start(f32[2048,512]{1,0:T(8,128)} %get-tuple-element.39) | copy-start | bytes 12582916
  151.2 5.4 %copy-start.18 = (bf16[2048,512]{1,0:T(8,128)(2,1)}, bf16[2048,512]{1,0:T(8,128)(2,1)S(1)}, u32[]{:S(2)}) copy-start(bf16[2048,512]{1,0:T(8,128)(2,1)S(1)} %multiply_convert_fusion) | copy-start | bytes 6291460
  151.2 2.5 copy-start.8
  153.7 1.6 copy-start.15
  156.6 1.6 copy-start.10
  158.2 2.3 copy-start.17
  158.2 2.3 copy-start.27
  160.6 1.0 copy-start.23
  160.6 1.1 copy-start.25
  160.6 1.3 copy-start.29
  161.8 1.5 copy-start.13
  166.1 1.2 copy-start.11
  172.7 19.3 %collective-permute-start.2 = (bf16[32,512]{1,0:T(8,128)(2,1)S(1)}, bf16[32,512]{1,0:T(8,128)(2,1)S(1)}, u32[]{:S(2)}, u32[]{:S(2)}) collective-permute-start(bf16[32,512]{1,0:T(8,128)(2,1)S(1)} %get-tuple-element.34), channel_id=1, source_target_pairs={{0,127},{1,0},{2,1},{3,2},{4,3},{5,4},{6,5},{7,6},{8,7},{9,8},{10,... | collective-permute-start | bytes 98312 | tf_op jit(solution)/shard_map/ppermute | solution.py:12
  176.0 17.0 %collective-permute-start.3 = (bf16[32,512]{1,0:T(8,128)(2,1)S(1)}, bf16[32,512]{1,0:T(8,128)(2,1)S(1)}, u32[]{:S(2)}, u32[]{:S(2)}) collective-permute-start(bf16[32,512]{1,0:T(8,128)(2,1)S(1)} %get-tuple-element.33), channel_id=1, source_target_pairs={{0,1},{1,2},{2,3},{3,4},{4,5},{5,6},{6,7},{7,8},{8,9},{9,10},{10,1... | collective-permute-start | bytes 98312 | tf_op jit(solution)/shard_map/ppermute | solution.py:12
  176.0 3.2 copy-start.1
  183.5 2.1 copy-start.5
  341.8 0.8 copy-start.30
Sparse Core Ops, SparseCore 0:
  9.7 31.0 all-gather.6
  42.4 33.1 all-gather.4
  172.0 160.8 all-reduce.3
where the time goes:
time: 350 us; the launch traced here: 349 us
  waiting for transfers between devices  140 us (40%)
  blocking collectives  83.2 us (24%)
  matrix products  52.2 us (15%)
  local copies, waits for them, and re-layouts  35.5 us (10%)
  other arithmetic  15.3 us (4%)
  between operations  14.9 us (4%)
  starting transfers between devices  7.71 us (2%)
    unnamed x4, waiting for transfers between devices  140 us
    all_gather x1, blocking collectives, shards(): lax.all_gather(owned_rows, ('patch', 'feat'), axis=0, tiled=True)  56.8 us
    unnamed x79, local copies, waits for them, and re-layouts  23.3 us
    dot_general x9, matrix products, product(): return jnp.dot(left, right, preferred_element_type=jnp.float32)  18.1 us
    dot_general x10, matrix products, contract_rows(): lax.dot_general(left, right, (((0,), (0,)), ((), ())), preferred_element_...  15.1 us
    dot_general x5, matrix products, times_transposed(): lax.dot_general(left, right, (((1,), (1,)), ((), ())), preferred_element_...  14.1 us
    all_gather x1, blocking collectives, shards(): lax.all_gather(node_w2, 'feat', axis=0, tiled=True)  13.5 us
    all_gather x1, blocking collectives, shards(): lax.all_gather(edge_w2, 'feat', axis=0, tiled=True)  12.9 us
  transfers between devices with their start and end apart: 7, of which 1 were waited for; matrix products, arithmetic and copies ran while one was open for 12% of the time, Pallas kernels for 0%

commit v1 on v0

v1 whole, which is shorter than its diff:
```python
import jax
import jax.numpy as jnp
from jax import lax
from jax.experimental import pallas as pl
from jax.experimental.pallas import tpu as pltpu
from jax.sharding import PartitionSpec as P

EPSILON = 1e-05
BF16 = jnp.bfloat16
F32 = jnp.float32
BOTH = ("patch", "feat")
CHUNK = 512
STEPS = 4
TABLE = 896
VMEM_BYTES = 60 * 1024 * 1024


def send(value, dz=0, dx=0, dc=0, dy=0):
    pairs = []
    for z in range(4):
        for x in range(4):
            for c in range(2):
                for y in range(4):
                    source = ((z * 4 + x) * 2 + c) * 4 + y
                    target = (((z + dz) % 4 * 4 + (x + dx) % 4) * 2 + (c ^ dc)) * 4 + (y + dy) % 4
                    pairs.append((source, target))
    return lax.ppermute(value, BOTH, pairs)


def shifted(value, steps):
    return lax.ppermute(value, BOTH, [(k, (k + steps) % 128) for k in range(128)])


def dot(left, right):
    return lax.dot_general(left, right, (((1,), (0,)), ((), ())), preferred_element_type=F32)


def dot_nt(left, right):
    return lax.dot_general(left, right, (((1,), (1,)), ((), ())), preferred_element_type=F32)


def dot_tn(left, right):
    return lax.dot_general(left, right, (((0,), (0,)), ((), ())), preferred_element_type=F32)


def mean(values):
    return jnp.mean(values, axis=-1, keepdims=True)


def normalize(values):
    centre = values - mean(values)
    factor = lax.rsqrt(mean(centre * centre) + EPSILON)
    return centre * factor, factor


def normalize_back(upstream, normed, factor):
    return factor * (upstream - mean(upstream) - normed * mean(upstream * normed))


def swish(pre):
    sigmoid = 0.5 + 0.5 * jnp.tanh(0.5 * pre)
    act = pre * sigmoid
    return act, sigmoid + act * (1.0 - sigmoid)


def hot_tiles(rows, count):
    lanes = lax.broadcasted_iota(jnp.int32, (128, 128), 1)
    spread = jnp.transpose(jnp.broadcast_to(rows, (128, 128)))
    return [jnp.where(spread == lanes + 128 * j, 1.0, 0.0).astype(BF16) for j in range(count)]


def live_rows(step, count):
    place = lax.broadcasted_iota(jnp.int32, (CHUNK, 1), 0) + step * CHUNK
    return jnp.where(place < count, 1.0, 0.0)


def place_weights(co, own_first, own_second, near, far, first, second):
    core, y = co[2], co[3]
    kinds = first.shape[0]
    for s in range(4):
        yy = (y - s) & 3
        columns = pl.ds(pl.multiple_of(yy * 128, 128), 128)
        if s == 0:
            for m in range(kinds):
                first[m, :, columns] = own_first[m]
            second[columns, :] = own_second[...]
            continue
        for part, half in ((near[s - 1], core), (far[s - 1], 1 - core)):
            rows = pl.ds(pl.multiple_of(half * 256, 256), 256)
            for m in range(kinds):
                first[m, rows, columns] = part[m * 256 : (m + 1) * 256, :]
            rows = pl.ds(pl.multiple_of(yy * 128 + half * 64, 64), 64)
            for b in range(4):
                start = kinds * 256 + b * 64
                second[rows, b * 128 : (b + 1) * 128] = part[start : start + 64, :]


def forward_kernel(co, node, prev, after, *refs):
    coarse, refs = refs[:16], refs[16:]
    own_first, own_second = refs[:2]
    near, far = refs[2:5], refs[5:8]
    src, dst, dst_wide, edge = refs[8:12]
    edge_out, incoming, act_out, normed_out, slope_out, factor_out, lookup, first, second = refs[12:21]
    table, total = refs[21:]
    step = pl.program_id(0)

    @pl.when(step == 0)
    def _():
        lookup[0:256, :] = node[...]
        lookup[256:288, :] = prev[...]
        lookup[288:320, :] = after[...]
        lookup[832:896, :] = jnp.zeros((64, 512), BF16)
        for dz in range(4):
            for dx in range(4):
                place = ((co[0] - dz) & 3) * 4 + ((co[1] - dx) & 3)
                rows = pl.ds(pl.multiple_of(320 + place * 32, 32), 32)
                lookup[rows, :] = coarse[dz * 4 + dx][...]
        place_weights(co, own_first, own_second, near, far, first, second)
        table[0:TABLE, :] = dot(lookup[...], first[1]).astype(BF16)
        table[TABLE:, :] = dot(node[...], first[2]).astype(BF16)
        total[...] = jnp.zeros_like(total)

    hots = []
    for r in range(CHUNK // 128):
        row = pl.ds(step * (CHUNK // 128) + r, 1)
        tiles = hot_tiles(src[row, :], TABLE // 128) + hot_tiles(dst[row, :], 2)
        hots.append(jnp.concatenate(tiles, axis=1))
    hot = jnp.concatenate(hots, axis=0)
    rows = edge[...]
    pre = dot(rows, first[0]) + dot(hot, table[...])
    act, slope = swish(pre)
    act = act.astype(BF16)
    act_out[...] = act
    slope_out[...] = slope.astype(BF16)
    normed, factor = normalize(dot(act, second[...]))
    normed_out[...] = normed.astype(BF16)
    factor_out[...] = jnp.broadcast_to(factor, (CHUNK, 128))
    new = (rows.astype(F32) + live_rows(step, co[4]) * normed).astype(BF16)
    edge_out[...] = new
    place = lax.broadcasted_iota(jnp.int32, (256, CHUNK), 1) + step * CHUNK
    node_of = lax.broadcasted_iota(jnp.int32, (256, CHUNK), 0)
    match = (node_of == dst_wide[pl.ds(step, 1), :]) & (place < co[4])
    total[...] += dot(jnp.where(match, 1.0, 0.0).astype(BF16), new)

    @pl.when(step == STEPS - 1)
    def _():
        incoming[...] = total[...].astype(BF16)


def put_columns(co, grad, slot, scratch, keep, give):
    scratch[...] = grad.astype(BF16).reshape(16, 2, 16, 512)
    for target, core in ((keep, co[2]), (give, 1 - co[2])):
        value = scratch[:, pl.ds(core, 1), :, :].reshape(8, 2, 16, 512)
        for y in range(4):
            target[:, :, y, slot * 16 : (slot + 1) * 16, :] = value[:, :, :, y * 128 : (y + 1) * 128]


def put_rows(co, grad, slot, scratch, keep, give):
    for b in range(4):
        scratch[b] = grad[:, b * 128 : (b + 1) * 128].astype(BF16)
    for target, core in ((keep, co[2]), (give, 1 - co[2])):
        for h in range(2):
            value = scratch[2 * h + core].reshape(4, 8, 16, 128)
            for y in range(4):
                target[:, h, y, slot * 16 : (slot + 1) * 16, :] = value[y]


def backward_kernel(co, node, incoming, grad_node, own_first, own_second, *refs):
    near, far, refs = refs[:3], refs[3:6], refs[6:]
    edge_first, edge_second, lookup, dst, src_wide, dst_wide = refs[:6]
    edge, act, normed, slope, factor, grad_edge = refs[6:12]
    node_out, node_total, edge_grad, to_prev, to_next, keep, give = refs[12:19]
    first, second, spread, sum_second, sum_first, sums, columns, rows = refs[19:]
    step = pl.program_id(0)

    @pl.when(step == 0)
    def _():
        place_weights(co, own_first, own_second, near, far, first, second)
        lat, summed = node[...], incoming[...]
        pre = dot(lat, first[0]) + dot(summed, first[1])
        node_act, node_slope = swish(pre)
        node_act = node_act.astype(BF16)
        node_normed, node_factor = normalize(dot(node_act, second[...]))
        node_out[...] = (lat.astype(F32) + node_normed).astype(BF16)
        upstream = grad_node[...].astype(F32)
        delta = normalize_back(upstream, node_normed, node_factor).astype(BF16)
        put_rows(co, dot_tn(node_act, delta), 7, rows, keep, give)
        pre_grad = (dot_nt(delta, second[...]) * node_slope).astype(BF16)
        put_columns(co, dot_tn(lat, pre_grad), 3, columns, keep, give)
        put_columns(co, dot_tn(summed, pre_grad), 4, columns, keep, give)
        node_total[...] = upstream + dot_nt(pre_grad, first[0])
        spread[...] = dot_nt(pre_grad, first[1]).astype(BF16)
        sum_second[...] = jnp.zeros_like(sum_second)
        sum_first[...] = jnp.zeros_like(sum_first)
        sums[...] = jnp.zeros_like(sums)

    hots = []
    for r in range(CHUNK // 128):
        row = pl.ds(step * (CHUNK // 128) + r, 1)
        hots.append(jnp.concatenate(hot_tiles(dst[row, :], 2), axis=1))
    live = live_rows(step, co[4])
    total = grad_edge[...].astype(F32) + live * dot(jnp.concatenate(hots, axis=0), spread[...])
    delta = normalize_back(live * total, normed[...].astype(F32), factor[:, 0:1]).astype(BF16)
    pre_grad = (dot_nt(delta, edge_second[...]) * slope[...].astype(F32)).astype(BF16)
    edge_grad[...] = (total + dot_nt(pre_grad, edge_first[0])).astype(BF16)
    sum_second[...] += dot_tn(act[...], delta)
    sum_first[...] += dot_tn(edge[...], pre_grad)
    place = lax.broadcasted_iota(jnp.int32, (128, CHUNK), 0)
    src_row, dst_row = src_wide[pl.ds(step, 1), :], dst_wide[pl.ds(step, 1), :]
    for j in range(9):
        match = place + 128 * j == src_row if j < 7 else place + 128 * (j - 7) == dst_row
        hot = jnp.where(match, 1.0, 0.0).astype(BF16)
        sums[j * 128 : (j + 1) * 128, :] += dot(hot, pre_grad)

    @pl.when(step == STEPS - 1)
    def _():
        put_rows(co, sum_second[...], 6, rows, keep, give)
        put_columns(co, sum_first[...], 0, columns, keep, give)
        sent = sums[0:TABLE, :].astype(BF16)
        received = sums[TABLE:, :].astype(BF16)
        put_columns(co, dot_tn(lookup[...], sent), 1, columns, keep, give)
        put_columns(co, dot_tn(node[...], received), 2, columns, keep, give)
        back = dot_nt(sent, edge_first[1])
        node_total[...] += back[0:256] + dot_nt(received, edge_first[2])
        to_prev[...] = back[256:288].astype(BF16)
        to_next[...] = back[288:320].astype(BF16)
        put_columns(co, back[320:832], 5, columns, keep, give)


def summed(*values):
    values = [value.astype(F32) for value in values]
    if len(values) == 4:
        return (values[0] + values[2]) + (values[1] + values[3])
    return values[0] + values[1]


def core_kernel(co, keep, got, *outs):
    z, x, y = co[0], co[1], co[3]
    for s in range(4):
        at = (slice(None), slice(None), pl.ds((y + s) & 3, 1), slice(0, 48))
        outs[s][...] = summed(keep[at], got[at]).astype(BF16).reshape(4, 4, 48, 128)
        at = (slice(None), pl.ds((x + s) & 3, 1), slice(None), slice(48, 96))
        outs[4 + s][...] = summed(keep[at], got[at]).astype(BF16).reshape(4, 4, 48, 128)
        at = (pl.ds((z + s) & 3, 1), slice(None), slice(None), slice(96, 128))
        outs[8 + s][...] = summed(keep[at], got[at]).astype(BF16).reshape(4, 4, 32, 128)


def second_kernel(co, *refs):
    one, two, three, outs = refs[:4], refs[4:8], refs[8:12], refs[12:]
    x, y = co[1], co[3]
    for s in range(4):
        at = (slice(None), pl.ds((x + s) & 3, 1))
        outs[s][...] = summed(*[r[at] for r in one]).astype(BF16).reshape(4, 48, 128)
        at = (slice(None), pl.ds((y + s) & 3, 1))
        outs[4 + s][:, 0:48, :] = summed(*[r[at] for r in two]).astype(BF16).reshape(4, 48, 128)
        outs[4 + s][:, 48:80, :] = summed(*[r[at] for r in three]).astype(BF16).reshape(4, 32, 128)


def third_kernel(*refs):
    one, two, (wide, narrow) = refs[:4], refs[4:8], refs[8:]
    wide[:, 0:48, :] = summed(*[r[...] for r in one]).astype(BF16)
    value = summed(*[r[...] for r in two]).astype(BF16)
    wide[:, 48:96, :] = value[:, 0:48]
    narrow[...] = value[:, 48:80]


def fourth_kernel(co, *refs):
    one, two, (wide, narrow, coarse) = refs[:4], refs[4:8], refs[8:]
    wide[...] = summed(*[r[:, 0:80, :] for r in one]).astype(BF16)
    narrow[...] = summed(*[r[...] for r in two]).astype(BF16)
    at = (pl.ds(co[0], 1), slice(80, 96))
    coarse[...] = summed(*[r[at] for r in one]).astype(BF16).reshape(16, 128)


def final_kernel(co, *refs):
    wide, narrow, coarse, refs = refs[:8], refs[8:16], refs[16:20], refs[20:]
    ahead, behind, targets, node_total = refs[:4]
    edge_first, edge_second, node_first, node_second, node_grad = refs[4:9]
    blocks, rows = refs[9:]
    z, x, core, y = co[0], co[1], co[2], co[3]
    for dc in range(2):
        cc = core ^ dc
        for d in range(4):
            piece = wide[dc * 4 + d][...].astype(F32)
            xx = (x - d) & 3
            for m in range(5):
                value = piece[:, m * 16 : (m + 1) * 16].reshape(4, 1, 1, 16, 128)
                target = edge_first if m < 3 else node_first
                target[m if m < 3 else m - 3, :, pl.ds(xx, 1), pl.ds(cc, 1)] = value
            piece = narrow[dc * 4 + d][...].astype(F32)
            zz = (z - d) & 3
            for k in range(2):
                for xs in range(4):
                    value = piece[xs, k * 16 : (k + 1) * 16]
                    blocks[k, zz * 2 + xs // 2, (xs % 2) * 2 + cc] = value
    for k, target in enumerate((edge_second, node_second)):
        for r in range(8):
            for b in range(4):
                target[r * 16 : (r + 1) * 16, b * 128 : (b + 1) * 128] = blocks[k, r, b]
    rows[0:32, :] = ahead[...]
    rows[32:64, :] = behind[...]
    for d in range(4):
        columns = pl.ds(pl.multiple_of(((y - d) & 3) * 128, 128), 128)
        rows[64:80, columns] = coarse[d][...]
    rows[80:128, :] = jnp.zeros((48, 512), BF16)
    match = lax.broadcasted_iota(jnp.int32, (256, 128), 0) == targets[...]
    hot = jnp.where(match, 1.0, 0.0).astype(BF16)
    node_grad[...] = node_total[...] + dot(hot, rows[...])


SMEM = pl.BlockSpec(memory_space=pltpu.SMEM)
WHOLE = pl.BlockSpec(memory_space=pltpu.VMEM)


def shape(*dims, dtype=BF16):
    return jax.ShapeDtypeStruct(dims, dtype)


def plain_call(kernel, scalars, operands, outs, scratch=()):
    return pl.pallas_call(
        kernel,
        in_specs=[SMEM] * len(scalars) + [WHOLE] * len(operands),
        out_specs=[WHOLE] * len(outs),
        out_shape=list(outs),
        scratch_shapes=list(scratch),
        compiler_params=pltpu.CompilerParams(vmem_limit_bytes=VMEM_BYTES),
    )(*scalars, *operands)


def same(*dims):
    return pl.BlockSpec(dims, lambda i: (0,) * len(dims))


def chunk(*dims):
    return pl.BlockSpec(dims, lambda i: (i,) + (0,) * (len(dims) - 1))


def like(value):
    return same(*value.shape)


def halves(first, second, core):
    kinds = first.shape[0]
    top = lax.dynamic_slice_in_dim(first, core * 256, 256, 1).reshape(kinds * 256, 128)
    rest = lax.dynamic_slice_in_dim(second, core * 64, 64, 0)
    rest = rest.reshape(64, 4, 128).transpose(1, 0, 2).reshape(256, 128)
    return jnp.concatenate([top, rest], axis=0)


def shards(
    node_lat,
    edge_lat,
    edge_src,
    edge_dst,
    edge_count,
    halo_send,
    coarse_of,
    edge_w1,
    edge_w2,
    node_w1,
    node_w2,
    grad_node,
    grad_edge,
):
    patch, y = lax.axis_index("patch"), lax.axis_index("feat")
    z, x, core = patch // 8, (patch // 2) % 4, patch % 2
    co = jnp.stack([z, x, core, y, edge_count[0]]).astype(jnp.int32)
    lists, owned = halo_send[0], coarse_of[0]
    mine = jnp.where(jnp.arange(16) // 4 == y, jnp.tile(owned, 4), -1)
    unused = jnp.full((48,), -1, jnp.int32)
    targets = jnp.concatenate([lists[1], lists[0], mine, unused]).reshape(1, 128)

    edge_half = halves(edge_w1, edge_w2, core)
    edge_near = [send(edge_half, dy=s) for s in (1, 2, 3)]
    coarse_own = node_lat[owned]
    others = [(dc, dy) for dc in range(2) for dy in range(4)]
    pieces = [coarse_own if o == (0, 0) else send(coarse_own, dc=o[0], dy=o[1]) for o in others]
    from_prev = shifted(node_lat[lists[1]], 1)
    from_next = shifted(node_lat[lists[0]], -1)
    edge_far = [send(part, dc=1) for part in edge_near]
    place = jnp.arange(32, dtype=jnp.int32)
    wanted = ((place // 16) ^ core) * 16 + ((y - (place // 4) % 4) % 4) * 4 + place % 4
    order = (wanted[:, None] == place[None, :]).astype(BF16)
    block = dot(order, jnp.concatenate(pieces, axis=0)).astype(BF16)
    blocks = [
        block if (dz, dx) == (0, 0) else send(block, dz=dz, dx=dx)
        for dz in range(4)
        for dx in range(4)
    ]
    node_half = halves(node_w1, node_w2, core)
    node_near = [send(node_half, dy=s) for s in (1, 2, 3)]
    node_far = [send(part, dc=1) for part in node_near]

    src, dst = edge_src.reshape(16, 128), edge_dst.reshape(16, 128)
    src_wide, dst_wide = edge_src.reshape(STEPS, CHUNK), edge_dst.reshape(STEPS, CHUNK)
    fixed = [node_lat, from_prev, from_next, *blocks, edge_w1, edge_w2, *edge_near, *edge_far]
    fixed += [src, dst, dst_wide]
    wide = chunk(CHUNK, 512)
    params = pltpu.CompilerParams(vmem_limit_bytes=VMEM_BYTES, dimension_semantics=("arbitrary",))
    edge_out, incoming, act, normed, slope, factor, lookup, first, second = pl.pallas_call(
        forward_kernel,
        grid=(STEPS,),
        in_specs=[SMEM] + [like(v) for v in fixed] + [wide],
        out_specs=[wide, same(256, 512), wide, wide, wide, chunk(CHUNK, 128)]
        + [same(TABLE, 512), same(3, 512, 512), same(512, 512)],
        out_shape=[
            shape(2048, 512),
            shape(256, 512),
            shape(2048, 512),
            shape(2048, 512),
            shape(2048, 512),
            shape(2048, 128, dtype=F32),
            shape(TABLE, 512),
            shape(3, 512, 512),
            shape(512, 512),
        ],
        scratch_shapes=[pltpu.VMEM((TABLE + 256, 512), BF16), pltpu.VMEM((256, 512), F32)],
        compiler_params=params,
        cost_estimate=pl.CostEstimate(
            flops=7_000_000_000, bytes_accessed=18_000_000, transcendentals=1_000_000
        ),
    )(co, *fixed, edge_lat)

    fixed = [node_lat, incoming, grad_node, node_w1, node_w2, *node_near, *node_far]
    fixed += [first, second, lookup, dst, src_wide, dst_wide]
    moving = [edge_lat, act, normed, slope, factor, grad_edge]
    tiles = (8, 2, 4, 128, 128)
    node_out, node_total, edge_grad, to_prev, to_next, keep, give = pl.pallas_call(
        backward_kernel,
        grid=(STEPS,),
        in_specs=[SMEM]
        + [like(v) for v in fixed]
        + [wide, wide, wide, wide, chunk(CHUNK, 128), wide],
        out_specs=[same(256, 512), same(256, 512), wide, same(32, 512), same(32, 512)]
        + [same(*tiles), same(*tiles)],
        out_shape=[
            shape(256, 512),
            shape(256, 512, dtype=F32),
            shape(2048, 512),
            shape(32, 512),
            shape(32, 512),
            shape(*tiles),
            shape(*tiles),
        ],
        scratch_shapes=[
            pltpu.VMEM((2, 512, 512), BF16),
            pltpu.VMEM((512, 512), BF16),
            pltpu.VMEM((256, 512), BF16),
            pltpu.VMEM((512, 512), F32),
            pltpu.VMEM((512, 512), F32),
            pltpu.VMEM((TABLE + 256, 512), F32),
            pltpu.VMEM((16, 2, 16, 512), BF16),
            pltpu.VMEM((4, 512, 128), BF16),
        ],
        compiler_params=params,
        cost_estimate=pl.CostEstimate(
            flops=9_000_000_000, bytes_accessed=24_000_000, transcendentals=100_000
        ),
    )(co, *fixed, *moving)

    ahead = shifted(to_prev, -1)
    behind = shifted(to_next, 1)
    got = send(give, dc=1)
    sizes = [shape(4, 4, rows, 128) for rows in (48, 48, 32) for _ in range(4)]
    cube = (4, 4, 4, 128, 128)
    outs = plain_call(core_kernel, [co], [keep.reshape(cube), got.reshape(cube)], sizes)
    along = (dict(dy=1), dict(dx=1), dict(dz=1))
    held = []
    for part, step in enumerate(along):
        (axis,) = step
        held.append(outs[4 * part])
        held += [send(outs[4 * part + s], **{axis: s}) for s in (1, 2, 3)]
    sizes = [shape(4, rows, 128) for rows in (48, 80) for _ in range(4)]
    outs = plain_call(second_kernel, [co], held, sizes)
    held = [outs[0]] + [send(outs[s], dx=s) for s in (1, 2, 3)]
    held += [outs[4]] + [send(outs[4 + s], dy=s) for s in (1, 2, 3)]
    major, minor = plain_call(third_kernel, [], held, [shape(4, 96, 128), shape(4, 32, 128)])
    held = [major] + [send(major, dz=s) for s in (1, 2, 3)]
    held += [minor] + [send(minor, dx=s) for s in (1, 2, 3)]
    major, minor, coarse = plain_call(
        fourth_kernel, [co], held, [shape(4, 80, 128), shape(4, 32, 128), shape(16, 128)]
    )
    held = [
        major if (dc, d) == (0, 0) else send(major, dc=dc, dx=d)
        for dc in range(2)
        for d in range(4)
    ]
    held += [
        minor if (dc, d) == (0, 0) else send(minor, dc=dc, dz=d)
        for dc in range(2)
        for d in range(4)
    ]
    held += [coarse] + [send(coarse, dy=s) for s in (1, 2, 3)]
    edge_first, edge_second, node_first, node_second, node_grad = plain_call(
        final_kernel,
        [co],
        held + [ahead, behind, targets, node_total],
        [
            shape(3, 4, 4, 2, 16, 128, dtype=F32),
            shape(128, 512, dtype=F32),
            shape(2, 4, 4, 2, 16, 128, dtype=F32),
            shape(128, 512, dtype=F32),
            shape(256, 512, dtype=F32),
        ],
        [
            pltpu.VMEM((2, 8, 4, 16, 128), F32),
            pltpu.VMEM((128, 512), BF16),
        ],
    )
    return (
        edge_out,
        node_out,
        node_grad,
        edge_grad,
        edge_first.reshape(3, 512, 128),
        edge_second,
        node_first.reshape(2, 512, 128),
        node_second,
    )


def solution(mesh):
    rows = P(("patch", "feat"), None)
    flat = P(("patch", "feat"))
    first, second = P(None, None, "feat"), P("feat", None)
    return jax.shard_map(
        shards,
        mesh=mesh,
        in_specs=(
            rows,
            rows,
            flat,
            flat,
            flat,
            P(("patch", "feat"), None, None),
            rows,
            first,
            second,
            first,
            second,
            rows,
            rows,
        ),
        out_specs=(rows, rows, rows, rows, first, second, first, second),
        check_vma=False,
    )
```

time: 350 us -> 245 us (0.70); the launches traced: 349 us -> 240 us
  starting transfers between devices: 7.71 us -> 128 us
  waiting for transfers between devices: 140 us -> 43.9 us
  blocking collectives: 83.2 us -> 0 us
  matrix products: 52.2 us -> 0.19 us
  Pallas kernels: 0 us -> 49 us
  local copies, waits for them, and re-layouts: 35.5 us -> 14.6 us
  other arithmetic: 15.3 us -> 2.12 us
  between operations: 14.9 us -> 2.43 us
    unnamed x4 -> x0, waiting for transfers between devices: 140 us -> none
    ppermute x4 -> x77, starting transfers between devices: 7.59 us -> 128 us  [the longest x73 119 us: send(): return lax.ppermute(value, BOTH, pairs)]
    all_gather x3 -> x0, blocking collectives: 83.2 us -> none  [the longest x1 56.8 us: shards(): lax.all_gather(owned_rows, ('patch', 'feat'), axis=0, tiled=True)]
    dot_general x26 -> x1, matrix products: 52.2 us -> 0.19 us  [dot(): lax.dot_general(left, right, (((1,), (0,)), ((), ())), preferred_element_...]
    pallas_call x0 -> x7, Pallas kernels: none -> 49 us  [the longest x1 21.1 us: shards(): pl.pallas_call(backward_kernel, grid=(STEPS,), in_specs=[SMEM] + [like(v)...]
    ppermute x4 -> x77, waiting for transfers between devices: 0.01 us -> 43.9 us  [the longest x73 43.9 us: send(): return lax.ppermute(value, BOTH, pairs)]
    unnamed x79 -> x156, local copies, waits for them, and re-layouts: 23.3 us -> 5.9 us
    convert_element_type x4 -> x0, other arithmetic: 5.62 us -> none  [the longest x1 4.73 us: local_step(): normalize_back(active * edge_total, edge_normed, edge_factor)]
  transfers between devices with their start and end apart: 7 -> 77, of which waited for: 1 -> 24; matrix products, arithmetic and copies ran while one was open for 12% -> 4% of each run, Pallas kernels for 0% -> 7%
where the time goes in v1:
time: 245 us; the launch traced here: 240 us
  starting transfers between devices  128 us (52%)
  Pallas kernels  49 us (20%)
  waiting for transfers between devices  43.9 us (18%)
  local copies, waits for them, and re-layouts  14.6 us (6%)
    ppermute x73, starting transfers between devices, send(): return lax.ppermute(value, BOTH, pairs)  119 us
    ppermute x73, waiting for transfers between devices, send(): return lax.ppermute(value, BOTH, pairs)  43.9 us
    pallas_call x1, Pallas kernels, shards(): pl.pallas_call(backward_kernel, grid=(STEPS,), in_specs=[SMEM] + [like(v)...  21.1 us
    pallas_call x1, Pallas kernels, shards(): pl.pallas_call(forward_kernel, grid=(STEPS,), in_specs=[SMEM] + [like(v)...  14.7 us
    pallas_call x5, Pallas kernels, plain_call(): pl.pallas_call(kernel, in_specs=[SMEM] * len(scalars) + [WHOLE] * len(ope...  13.3 us
    ppermute x4, starting transfers between devices, shifted(): lax.ppermute(value, BOTH, [(k, (k + steps) % 128) for k in range(128)])  9.45 us
    unnamed x156, local copies, waits for them, and re-layouts  5.9 us
  transfers between devices with their start and end apart: 77, of which 24 were waited for; matrix products, arithmetic and copies ran while one was open for 4% of the time, Pallas kernels for 7%

profile of v1, /device:TPU:1, one launch (start us, length us, event | category | flops | bytes accessed | tf_op | source)
XLA Modules:
  0.0 240.4 jit_solution(11098517925295088848)
XLA Ops:
  2.9 4.2 %collective-permute-start.8 = (bf16[4,512]{1,0:T(4,128)(2,1)S(1)}, bf16[4,512]{1,0:T(4,128)(2,1)S(1)}, u32[]{:S(2)}, u32[]{:S(2)}) collective-permute-start(bf16[4,512]{1,0:T(4,128)(2,1)S(1)} %gather_fusion.2), channel_id=1, source_target_pairs={{0,7},{1,4},{2,5},{3,6},{4,3},{5,0},{6,1},{7,2},{8,15},{9,12},{10,... | collective-permute-start | bytes 12296 | tf_op jit(solution)/shard_map/ppermute | solution.py:27
  8.4 2.0 collective-permute-start.4
  17.0 4.0 %collective-permute-start.1 = (bf16[32,512]{1,0:T(8,128)(2,1)S(1)}, bf16[32,512]{1,0:T(8,128)(2,1)S(1)}, u32[]{:S(2)}, u32[]{:S(2)}) collective-permute-start(bf16[32,512]{1,0:T(8,128)(2,1)S(1)} %gather_fusion.1), channel_id=1, source_target_pairs={{0,127},{1,0},{2,1},{3,2},{4,3},{5,4},{6,5},{7,6},{8,7},{9,8},{10,... | collective-permute-start | bytes 98312 | tf_op jit(solution)/shard_map/ppermute | solution.py:31
  21.3 6.0 %collective-permute-start.23 = (bf16[32,512]{1,0:T(8,128)(2,1)S(1)}, bf16[32,512]{1,0:T(8,128)(2,1)S(1)}, u32[]{:S(2)}, u32[]{:S(2)}) collective-permute-start(bf16[32,512]{1,0:T(8,128)(2,1)S(1)} %convolution_convert_fusion.refs_0_), channel_id=1, source_target_pairs={{0,120},{1,121},{2,122},{3,123},{4,124},{5,125},{6,126},{7,127},{8... | collective-permute-start | bytes 98312 | tf_op jit(solution)/shard_map/ppermute | solution.py:27
  28.8 5.2 %collective-permute-start.19 = (bf16[32,512]{1,0:T(8,128)(2,1)S(1)}, bf16[32,512]{1,0:T(8,128)(2,1)S(1)}, u32[]{:S(2)}, u32[]{:S(2)}) collective-permute-start(bf16[32,512]{1,0:T(8,128)(2,1)S(1)} %convolution_convert_fusion.refs_0_), channel_id=1, source_target_pairs={{0,88},{1,89},{2,90},{3,91},{4,92},{5,93},{6,94},{7,95},{8,64},{9,... | collective-permute-start | bytes 98312 | tf_op jit(solution)/shard_map/ppermute | solution.py:27
  34.6 5.5 %collective-permute-start.26 = (bf16[1024,128]{1,0:T(8,128)(2,1)S(1)}, bf16[1024,128]{1,0:T(8,128)(2,1)S(1)}, u32[]{:S(2)}, u32[]{:S(2)}) collective-permute-start(bf16[1024,128]{1,0:T(8,128)(2,1)S(1)} %pad_maximum_fusion), channel_id=1, source_target_pairs={{0,3},{1,0},{2,1},{3,2},{4,7},{5,4},{6,5},{7,6},{8,11},{9,8},{10,9... | collective-permute-start | bytes 786440 | tf_op jit(solution)/shard_map/ppermute | solution.py:27
  40.8 3.2 %collective-permute-start.17 = (bf16[32,512]{1,0:T(8,128)(2,1)S(1)}, bf16[32,512]{1,0:T(8,128)(2,1)S(1)}, u32[]{:S(2)}, u32[]{:S(2)}) collective-permute-start(bf16[32,512]{1,0:T(8,128)(2,1)S(1)} %convolution_convert_fusion.refs_0_), channel_id=1, source_target_pairs={{0,72},{1,73},{2,74},{3,75},{4,76},{5,77},{6,78},{7,79},{8,80},{9,... | collective-permute-start | bytes 98312 | tf_op jit(solution)/shard_map/ppermute | solution.py:27
  44.8 2.4 %collective-permute-done.17.refs_9_ = bf16[32,512]{1,0:T(8,128)(2,1)S(1)} collective-permute-done((bf16[32,512]{1,0:T(8,128)(2,1)S(1)}, bf16[32,512]{1,0:T(8,128)(2,1)S(1)}, u32[]{:S(2)}, u32[]{:S(2)}) %collective-permute-start.17) | collective-permute-done | bytes 32800 | tf_op jit(solution)/shard_map/ppermute | solution.py:27
  48.8 1.9 collective-permute-start.14
  52.1 2.7 %collective-permute-start.32 = (bf16[768,128]{1,0:T(8,128)(2,1)S(1)}, bf16[768,128]{1,0:T(8,128)(2,1)S(1)}, u32[]{:S(2)}, u32[]{:S(2)}) collective-permute-start(bf16[768,128]{1,0:T(8,128)(2,1)S(1)} %pad_maximum_fusion.1), channel_id=1, source_target_pairs={{0,3},{1,0},{2,1},{3,2},{4,7},{5,4},{6,5},{7,6},{8,11},{9,8},{10,9... | collective-permute-start | bytes 589832 | tf_op jit(solution)/shard_map/ppermute | solution.py:27
  55.1 2.0 collective-permute-start.13
  57.1 4.1 %collective-permute-done.13.refs_5_ = bf16[32,512]{1,0:T(8,128)(2,1)S(1)} collective-permute-done((bf16[32,512]{1,0:T(8,128)(2,1)S(1)}, bf16[32,512]{1,0:T(8,128)(2,1)S(1)}, u32[]{:S(2)}, u32[]{:S(2)}) %collective-permute-start.13) | collective-permute-done | bytes 32800 | tf_op jit(solution)/shard_map/ppermute | solution.py:27
  61.2 4.0 %collective-permute-done.12.refs_4_ = bf16[32,512]{1,0:T(8,128)(2,1)S(1)} collective-permute-done((bf16[32,512]{1,0:T(8,128)(2,1)S(1)}, bf16[32,512]{1,0:T(8,128)(2,1)S(1)}, u32[]{:S(2)}, u32[]{:S(2)}) %collective-permute-start.12) | collective-permute-done | bytes 32800 | tf_op jit(solution)/shard_map/ppermute | solution.py:27
  65.2 1.8 collective-permute-start.11
  69.5 5.3 %collective-permute-start.29 = (bf16[1024,128]{1,0:T(8,128)(2,1)S(1)}, bf16[1024,128]{1,0:T(8,128)(2,1)S(1)}, u32[]{:S(2)}, u32[]{:S(2)}) collective-permute-start(bf16[1024,128]{1,0:T(8,128)(2,1)S(1)} %collective-permute-done.26.refs_20_), channel_id=1, source_target_pairs={{0,4},{1,5},{2,6},{3,7},{4,0},{5,1},{6,2},{7,3},{8,12},{9,13},{10,... | collective-permute-start | bytes 786440 | tf_op jit(solution)/shard_map/ppermute | solution.py:27
  75.4 2.4 collective-permute-start.9
  79.3 2.7 %collective-permute-start.31 = (bf16[768,128]{1,0:T(8,128)(2,1)S(1)}, bf16[768,128]{1,0:T(8,128)(2,1)S(1)}, u32[]{:S(2)}, u32[]{:S(2)}) collective-permute-start(bf16[768,128]{1,0:T(8,128)(2,1)S(1)} %pad_maximum_fusion.1), channel_id=1, source_target_pairs={{0,2},{1,3},{2,0},{3,1},{4,6},{5,7},{6,4},{7,5},{8,10},{9,11},{10,... | collective-permute-start | bytes 589832 | tf_op jit(solution)/shard_map/ppermute | solution.py:27
  85.6 5.7 %collective-permute-start.35 = (bf16[768,128]{1,0:T(8,128)(2,1)S(1)}, bf16[768,128]{1,0:T(8,128)(2,1)S(1)}, u32[]{:S(2)}, u32[]{:S(2)}) collective-permute-start(bf16[768,128]{1,0:T(8,128)(2,1)S(1)} %collective-permute-done.32.refs_2_), channel_id=1, source_target_pairs={{0,4},{1,5},{2,6},{3,7},{4,0},{5,1},{6,2},{7,3},{8,12},{9,13},{10,... | collective-permute-start | bytes 589832 | tf_op jit(solution)/shard_map/ppermute | solution.py:27
  91.3 2.4 %collective-permute-start.34 = (bf16[768,128]{1,0:T(8,128)(2,1)S(1)}, bf16[768,128]{1,0:T(8,128)(2,1)S(1)}, u32[]{:S(2)}, u32[]{:S(2)}) collective-permute-start(bf16[768,128]{1,0:T(8,128)(2,1)S(1)} %collective-permute-done.31.refs_1_), channel_id=1, source_target_pairs={{0,4},{1,5},{2,6},{3,7},{4,0},{5,1},{6,2},{7,3},{8,12},{9,13},{10,... | collective-permute-start | bytes 589832 | tf_op jit(solution)/shard_map/ppermute | solution.py:27
  94.6 14.7 %shard_map.188 = (bf16[2048,512]{1,0:T(8,128)(2,1)}, bf16[256,512]{1,0:T(8,128)(2,1)}, bf16[2048,512]{1,0:T(8,128)(2,1)}, bf16[2048,512]{1,0:T(8,128)(2,1)}, bf1...) custom-call(s32[5]{0:T(128)} %stack.19.co, ...), custom_call_target="tpu_custom_call" | custom-call | flops 7000000000 | bytes 18000000 | tf_op jit(solution)/shard_map/pallas_call | solution.py:400
  110.2 21.1 %shard_map.189 = (bf16[256,512]{1,0:T(8,128)(2,1)}, f32[256,512]{1,0:T(8,128)}, bf16[2048,512]{1,0:T(8,128)(2,1)}, bf16[32,512]{1,0:T(8,128)(2,1)}, bf16[32,512]...) custom-call(s32[5]{0:T(128)} %stack.19.co, bf16[256,512]{1,0:T(8,128)(2,1)} %node.3, ...), custom_call_target="tpu_custom_call" | custom-call | flops 8999999488 | bytes 24000000 | tf_op jit(solution)/shard_map/pallas_call | solution.py:428
  131.8 4.0 %collective-permute-done.36 = bf16[8,2,4,128,128]{4,3,2,1,0:T(8,128)(2,1)S(1)} collective-permute-done((bf16[8,2,4,128,128]{4,3,2,1,0:T(8,128)(2,1)}, bf16[8,2,4,128,128]{4,3,2,1,0:T(8,128)(2,1)S(1)}, u32[]{:S(2)}, u32[]{:S(2)}) %collective-permute-start.36) | collective-permute-done | bytes 2097184 | tf_op jit(solution)/shard_map/ppermute | solution.py:27
  137.1 4.0 %shard_map.190 = (bf16[4,4,48,128]{3,2,1,0:T(8,128)(2,1)}, bf16[4,4,48,128]{3,2,1,0:T(8,128)(2,1)}, bf16[4,4,48,128]{3,2,1,0:T(8,128)(2,1)}, bf16[4,4,48,128]{3,...) custom-call(s32[5]{0:T(128)} %stack.19.co, ...), custom_call_target="tpu_custom_call" | custom-call | tf_op jit(solution)/shard_map/pallas_call | solution.py:320
  141.9 12.0 %collective-permute-start.44 = (bf16[4,4,32,128]{3,2,1,0:T(8,128)(2,1)}, bf16[4,4,32,128]{3,2,1,0:T(8,128)(2,1)S(1)}, u32[]{:S(2)}, u32[]{:S(2)}) collective-permute-start(bf16[4,4,32,128]{3,2,1,0:T(8,128)(2,1)} %get-tuple-element.76), channel_id=1, source_target_pairs={{0,64},{1,65},{2,66},{3,67},{4,68},{5,69},{6,70},{7,71},{8,72},{9,... | collective-permute-start | bytes 393224 | tf_op jit(solution)/shard_map/ppermute | solution.py:27
  158.2 2.6 %collective-permute-done.45.refs_11_ = bf16[4,4,32,128]{3,2,1,0:T(8,128)(2,1)S(1)} collective-permute-done((bf16[4,4,32,128]{3,2,1,0:T(8,128)(2,1)}, bf16[4,4,32,128]{3,2,1,0:T(8,128)(2,1)S(1)}, u32[]{:S(2)}, u32[]{:S(2)}) %collective-permute-start.45) | collective-permute-done | bytes 131104 | tf_op jit(solution)/shard_map/ppermute | solution.py:27
  161.7 1.8 collective-permute-start.42
  163.5 2.5 %collective-permute-done.39.refs_3_ = bf16[4,4,48,128]{3,2,1,0:T(8,128)(2,1)S(1)} collective-permute-done((bf16[4,4,48,128]{3,2,1,0:T(8,128)(2,1)}, bf16[4,4,48,128]{3,2,1,0:T(8,128)(2,1)S(1)}, u32[]{:S(2)}, u32[]{:S(2)}) %collective-permute-start.39) | collective-permute-done | bytes 196640 | tf_op jit(solution)/shard_map/ppermute | solution.py:27
  166.0 3.4 %collective-permute-done.41.refs_6_ = bf16[4,4,48,128]{3,2,1,0:T(8,128)(2,1)S(1)} collective-permute-done((bf16[4,4,48,128]{3,2,1,0:T(8,128)(2,1)}, bf16[4,4,48,128]{3,2,1,0:T(8,128)(2,1)S(1)}, u32[]{:S(2)}, u32[]{:S(2)}) %collective-permute-start.41) | collective-permute-done | bytes 196640 | tf_op jit(solution)/shard_map/ppermute | solution.py:27
  169.4 1.7 collective-permute-done.42.refs_7_
  171.8 2.6 %shard_map.191 = (bf16[4,48,128]{2,1,0:T(8,128)(2,1)}, bf16[4,48,128]{2,1,0:T(8,128)(2,1)}, bf16[4,48,128]{2,1,0:T(8,128)(2,1)}, bf16[4,48,128]{2,1,0:T(8,128)(2...) custom-call(s32[5]{0:T(128)} %stack.19.co, ...), custom_call_target="tpu_custom_call" | custom-call | tf_op jit(solution)/shard_map/pallas_call | solution.py:320
  174.4 2.3 collective-permute-start.46
  176.8 2.8 %collective-permute-start.50 = (bf16[4,80,128]{2,1,0:T(8,128)(2,1)}, bf16[4,80,128]{2,1,0:T(8,128)(2,1)S(1)}, u32[]{:S(2)}, u32[]{:S(2)}) collective-permute-start(bf16[4,80,128]{2,1,0:T(8,128)(2,1)} %get-tuple-element.84), channel_id=1, source_target_pairs={{0,2},{1,3},{2,0},{3,1},{4,6},{5,7},{6,4},{7,5},{8,10},{9,11},{10,... | collective-permute-start | bytes 245768 | tf_op jit(solution)/shard_map/ppermute | solution.py:27
  179.7 2.9 %collective-permute-start.47 = (bf16[4,48,128]{2,1,0:T(8,128)(2,1)}, bf16[4,48,128]{2,1,0:T(8,128)(2,1)S(1)}, u32[]{:S(2)}, u32[]{:S(2)}) collective-permute-start(bf16[4,48,128]{2,1,0:T(8,128)(2,1)} %get-tuple-element.80), channel_id=1, source_target_pairs={{0,16},{1,17},{2,18},{3,19},{4,20},{5,21},{6,22},{7,23},{8,24},{9,... | collective-permute-start | bytes 147464 | tf_op jit(solution)/shard_map/ppermute | solution.py:27
  182.5 2.1 collective-permute-done.47.refs_2_
  186.6 1.8 shard_map.192
  188.4 4.0 %collective-permute-start.54 = (bf16[4,96,128]{2,1,0:T(8,128)(2,1)}, bf16[4,96,128]{2,1,0:T(8,128)(2,1)S(1)}, u32[]{:S(2)}, u32[]{:S(2)}) collective-permute-start(bf16[4,96,128]{2,1,0:T(8,128)(2,1)} %get-tuple-element.86.refs_0_), channel_id=1, source_target_pairs={{0,96},{1,97},{2,98},{3,99},{4,100},{5,101},{6,102},{7,103},{8,104... | collective-permute-start | bytes 294920 | tf_op jit(solution)/shard_map/ppermute | solution.py:27
  194.3 2.0 collective-permute-done.57.refs_7_
  196.3 1.9 collective-permute-done.56.refs_6_
  198.2 5.4 %collective-permute-start.75 = (bf16[32,512]{1,0:T(8,128)(2,1)S(1)}, bf16[32,512]{1,0:T(8,128)(2,1)S(1)}, u32[]{:S(2)}, u32[]{:S(2)}) collective-permute-start(bf16[32,512]{1,0:T(8,128)(2,1)S(1)} %copy-done.65), channel_id=1, source_target_pairs={{0,127},{1,0},{2,1},{3,2},{4,3},{5,4},{6,5},{7,6},{8,7},{9,8},{10,... | collective-permute-start | bytes 98312 | tf_op jit(solution)/shard_map/ppermute | solution.py:31
  205.0 1.8 shard_map.193
  206.8 2.7 %collective-permute-start.74 = (bf16[16,128]{1,0:T(8,128)(2,1)}, bf16[16,128]{1,0:T(8,128)(2,1)S(1)}, u32[]{:S(2)}, u32[]{:S(2)}) collective-permute-start(bf16[16,128]{1,0:T(8,128)(2,1)} %get-tuple-element.90.refs_16_), channel_id=1, source_target_pairs={{0,3},{1,0},{2,1},{3,2},{4,7},{5,4},{6,5},{7,6},{8,11},{9,8},{10,9... | collective-permute-start | bytes 12296 | tf_op jit(solution)/shard_map/ppermute | solution.py:27
  210.1 4.6 %collective-permute-start.71 = (bf16[4,32,128]{2,1,0:T(8,128)(2,1)}, bf16[4,32,128]{2,1,0:T(8,128)(2,1)S(1)}, u32[]{:S(2)}, u32[]{:S(2)}) collective-permute-start(bf16[4,32,128]{2,1,0:T(8,128)(2,1)} %get-tuple-element.89.refs_8_), channel_id=1, source_target_pairs={{0,100},{1,101},{2,102},{3,103},{4,96},{5,97},{6,98},{7,99},{8,108... | collective-permute-start | bytes 98312 | tf_op jit(solution)/shard_map/ppermute | solution.py:27
  217.4 2.5 %collective-permute-start.67 = (bf16[4,32,128]{2,1,0:T(8,128)(2,1)}, bf16[4,32,128]{2,1,0:T(8,128)(2,1)S(1)}, u32[]{:S(2)}, u32[]{:S(2)}) collective-permute-start(bf16[4,32,128]{2,1,0:T(8,128)(2,1)} %get-tuple-element.89.refs_8_), channel_id=1, source_target_pairs={{0,96},{1,97},{2,98},{3,99},{4,100},{5,101},{6,102},{7,103},{8,104... | collective-permute-start | bytes 98312 | tf_op jit(solution)/shard_map/ppermute | solution.py:27
  220.7 3.2 %collective-permute-start.64 = (bf16[4,80,128]{2,1,0:T(8,128)(2,1)}, bf16[4,80,128]{2,1,0:T(8,128)(2,1)S(1)}, u32[]{:S(2)}, u32[]{:S(2)}) collective-permute-start(bf16[4,80,128]{2,1,0:T(8,128)(2,1)} %get-tuple-element.88.refs_0_), channel_id=1, source_target_pairs={{0,28},{1,29},{2,30},{3,31},{4,24},{5,25},{6,26},{7,27},{8,4},{9,5... | collective-permute-start | bytes 245768 | tf_op jit(solution)/shard_map/ppermute | solution.py:27
  224.5 1.8 collective-permute-start.61
  230.0 1.8 collective-permute-start.58
  233.0 3.4 %collective-permute-done.58.refs_1_ = bf16[4,80,128]{2,1,0:T(8,128)(2,1)S(1)} collective-permute-done((bf16[4,80,128]{2,1,0:T(8,128)(2,1)}, bf16[4,80,128]{2,1,0:T(8,128)(2,1)S(1)}, u32[]{:S(2)}, u32[]{:S(2)}) %collective-permute-start.58) | collective-permute-done | bytes 81952 | tf_op jit(solution)/shard_map/ppermute | solution.py:27
  237.0 3.2 %shard_map.194 = (f32[3,4,4,2,16,128]{5,4,3,2,1,0:T(8,128)}, f32[128,512]{1,0:T(8,128)}, f32[2,4,4,2,16,128]{5,4,3,2,1,0:T(8,128)}, f32[128,512]{1,0:T(8,128)}, f32[256,512]{1,0:T(8,128)}) custom-call(s32[5]{0:T(128)} %stack.19.co, bf16[4,80,128]{2,1,0:T(8,128)(2,1)} %get-tuple-element.88.refs_0_, bf16[4,80,128]{2,1,0:T(8,128)(2,1)} %copy-done.19, ...), custom_call_target="tpu_custom_call" | custom-call | tf_op jit(solution)/shard_map/pallas_call | solution.py:320
  (298 shorter events, 50.1 us)
Async XLA Ops:
  2.9 9.3 %collective-permute-start.8 = (bf16[4,512]{1,0:T(4,128)(2,1)S(1)}, bf16[4,512]{1,0:T(4,128)(2,1)S(1)}, u32[]{:S(2)}, u32[]{:S(2)}) collective-permute-start(bf16[4,512]{1,0:T(4,128)(2,1)S(1)} %gather_fusion.2), channel_id=1, source_target_pairs={{0,7},{1,4},{2,5},{3,6},{4,3},{5,0},{6,1},{7,2},{8,15},{9,12},{10,... | collective-permute-start | bytes 12296 | tf_op jit(solution)/shard_map/ppermute | solution.py:27
  7.4 9.6 %collective-permute-start.6 = (bf16[4,512]{1,0:T(4,128)(2,1)S(1)}, bf16[4,512]{1,0:T(4,128)(2,1)S(1)}, u32[]{:S(2)}, u32[]{:S(2)}) collective-permute-start(bf16[4,512]{1,0:T(4,128)(2,1)S(1)} %gather_fusion.2), channel_id=1, source_target_pairs={{0,5},{1,6},{2,7},{3,4},{4,1},{5,2},{6,3},{7,0},{8,13},{9,14},{10,... | collective-permute-start | bytes 12296 | tf_op jit(solution)/shard_map/ppermute | solution.py:27
  8.4 12.5 %collective-permute-start.5 = (bf16[4,512]{1,0:T(4,128)(2,1)S(1)}, bf16[4,512]{1,0:T(4,128)(2,1)S(1)}, u32[]{:S(2)}, u32[]{:S(2)}) collective-permute-start(bf16[4,512]{1,0:T(4,128)(2,1)S(1)} %gather_fusion.2), channel_id=1, source_target_pairs={{0,4},{1,5},{2,6},{3,7},{4,0},{5,1},{6,2},{7,3},{8,12},{9,13},{10,... | collective-permute-start | bytes 12296 | tf_op jit(solution)/shard_map/ppermute | solution.py:27
  8.4 12.5 %collective-permute-start.4 = (bf16[4,512]{1,0:T(4,128)(2,1)S(1)}, bf16[4,512]{1,0:T(4,128)(2,1)S(1)}, u32[]{:S(2)}, u32[]{:S(2)}) collective-permute-start(bf16[4,512]{1,0:T(4,128)(2,1)S(1)} %gather_fusion.2), channel_id=1, source_target_pairs={{0,3},{1,0},{2,1},{3,2},{4,7},{5,4},{6,5},{7,6},{8,11},{9,8},{10,9... | collective-permute-start | bytes 12296 | tf_op jit(solution)/shard_map/ppermute | solution.py:27
  12.2 8.7 %collective-permute-start.3 = (bf16[4,512]{1,0:T(4,128)(2,1)S(1)}, bf16[4,512]{1,0:T(4,128)(2,1)S(1)}, u32[]{:S(2)}, u32[]{:S(2)}) collective-permute-start(bf16[4,512]{1,0:T(4,128)(2,1)S(1)} %gather_fusion.2), channel_id=1, source_target_pairs={{0,2},{1,3},{2,0},{3,1},{4,6},{5,7},{6,4},{7,5},{8,10},{9,11},{10,... | collective-permute-start | bytes 12296 | tf_op jit(solution)/shard_map/ppermute | solution.py:27
  13.7 7.3 %collective-permute-start.2 = (bf16[4,512]{1,0:T(4,128)(2,1)S(1)}, bf16[4,512]{1,0:T(4,128)(2,1)S(1)}, u32[]{:S(2)}, u32[]{:S(2)}) collective-permute-start(bf16[4,512]{1,0:T(4,128)(2,1)S(1)} %gather_fusion.2), channel_id=1, source_target_pairs={{0,1},{1,2},{2,3},{3,0},{4,5},{5,6},{6,7},{7,4},{8,9},{9,10},{10,1... | collective-permute-start | bytes 12296 | tf_op jit(solution)/shard_map/ppermute | solution.py:27
  17.0 11.8 %collective-permute-start.1 = (bf16[32,512]{1,0:T(8,128)(2,1)S(1)}, bf16[32,512]{1,0:T(8,128)(2,1)S(1)}, u32[]{:S(2)}, u32[]{:S(2)}) collective-permute-start(bf16[32,512]{1,0:T(8,128)(2,1)S(1)} %gather_fusion.1), channel_id=1, source_target_pairs={{0,127},{1,0},{2,1},{3,2},{4,3},{5,4},{6,5},{7,6},{8,7},{9,8},{10,... | collective-permute-start | bytes 98312 | tf_op jit(solution)/shard_map/ppermute | solution.py:31
  20.9 7.8 %collective-permute-start = (bf16[32,512]{1,0:T(8,128)(2,1)S(1)}, bf16[32,512]{1,0:T(8,128)(2,1)S(1)}, u32[]{:S(2)}, u32[]{:S(2)}) collective-permute-start(bf16[32,512]{1,0:T(8,128)(2,1)S(1)} %gather_fusion), channel_id=1, source_target_pairs={{0,1},{1,2},{2,3},{3,4},{4,5},{5,6},{6,7},{7,8},{8,9},{9,10},{10,1... | collective-permute-start | bytes 98312 | tf_op jit(solution)/shard_map/ppermute | solution.py:31
  21.3 12.7 %collective-permute-start.23 = (bf16[32,512]{1,0:T(8,128)(2,1)S(1)}, bf16[32,512]{1,0:T(8,128)(2,1)S(1)}, u32[]{:S(2)}, u32[]{:S(2)}) collective-permute-start(bf16[32,512]{1,0:T(8,128)(2,1)S(1)} %convolution_convert_fusion.refs_0_), channel_id=1, source_target_pairs={{0,120},{1,121},{2,122},{3,123},{4,124},{5,125},{6,126},{7,127},{8... | collective-permute-start | bytes 98312 | tf_op jit(solution)/shard_map/ppermute | solution.py:27
  28.6 11.5 %collective-permute-start.21 = (bf16[32,512]{1,0:T(8,128)(2,1)S(1)}, bf16[32,512]{1,0:T(8,128)(2,1)S(1)}, u32[]{:S(2)}, u32[]{:S(2)}) collective-permute-start(bf16[32,512]{1,0:T(8,128)(2,1)S(1)} %convolution_convert_fusion.refs_0_), channel_id=1, source_target_pairs={{0,104},{1,105},{2,106},{3,107},{4,108},{5,109},{6,110},{7,111},{8... | collective-permute-start | bytes 98312 | tf_op jit(solution)/shard_map/ppermute | solution.py:27
  28.8 11.4 %collective-permute-start.20 = (bf16[32,512]{1,0:T(8,128)(2,1)S(1)}, bf16[32,512]{1,0:T(8,128)(2,1)S(1)}, u32[]{:S(2)}, u32[]{:S(2)}) collective-permute-start(bf16[32,512]{1,0:T(8,128)(2,1)S(1)} %convolution_convert_fusion.refs_0_), channel_id=1, source_target_pairs={{0,96},{1,97},{2,98},{3,99},{4,100},{5,101},{6,102},{7,103},{8,104... | collective-permute-start | bytes 98312 | tf_op jit(solution)/shard_map/ppermute | solution.py:27
  28.8 12.0 %collective-permute-start.19 = (bf16[32,512]{1,0:T(8,128)(2,1)S(1)}, bf16[32,512]{1,0:T(8,128)(2,1)S(1)}, u32[]{:S(2)}, u32[]{:S(2)}) collective-permute-start(bf16[32,512]{1,0:T(8,128)(2,1)S(1)} %convolution_convert_fusion.refs_0_), channel_id=1, source_target_pairs={{0,88},{1,89},{2,90},{3,91},{4,92},{5,93},{6,94},{7,95},{8,64},{9,... | collective-permute-start | bytes 98312 | tf_op jit(solution)/shard_map/ppermute | solution.py:27
  34.0 10.0 %collective-permute-start.18 = (bf16[32,512]{1,0:T(8,128)(2,1)S(1)}, bf16[32,512]{1,0:T(8,128)(2,1)S(1)}, u32[]{:S(2)}, u32[]{:S(2)}) collective-permute-start(bf16[32,512]{1,0:T(8,128)(2,1)S(1)} %convolution_convert_fusion.refs_0_), channel_id=1, source_target_pairs={{0,80},{1,81},{2,82},{3,83},{4,84},{5,85},{6,86},{7,87},{8,88},{9,... | collective-permute-start | bytes 98312 | tf_op jit(solution)/shard_map/ppermute | solution.py:27
  34.6 34.9 %collective-permute-start.26 = (bf16[1024,128]{1,0:T(8,128)(2,1)S(1)}, bf16[1024,128]{1,0:T(8,128)(2,1)S(1)}, u32[]{:S(2)}, u32[]{:S(2)}) collective-permute-start(bf16[1024,128]{1,0:T(8,128)(2,1)S(1)} %pad_maximum_fusion), channel_id=1, source_target_pairs={{0,3},{1,0},{2,1},{3,2},{4,7},{5,4},{6,5},{7,6},{8,11},{9,8},{10,9... | collective-permute-start | bytes 786440 | tf_op jit(solution)/shard_map/ppermute | solution.py:27
  40.1 34.7 %collective-permute-start.25 = (bf16[1024,128]{1,0:T(8,128)(2,1)S(1)}, bf16[1024,128]{1,0:T(8,128)(2,1)S(1)}, u32[]{:S(2)}, u32[]{:S(2)}) collective-permute-start(bf16[1024,128]{1,0:T(8,128)(2,1)S(1)} %pad_maximum_fusion), channel_id=1, source_target_pairs={{0,2},{1,3},{2,0},{3,1},{4,6},{5,7},{6,4},{7,5},{8,10},{9,11},{10,... | collective-permute-start | bytes 786440 | tf_op jit(solution)/shard_map/ppermute | solution.py:27
  40.2 34.8 %collective-permute-start.24 = (bf16[1024,128]{1,0:T(8,128)(2,1)S(1)}, bf16[1024,128]{1,0:T(8,128)(2,1)S(1)}, u32[]{:S(2)}, u32[]{:S(2)}) collective-permute-start(bf16[1024,128]{1,0:T(8,128)(2,1)S(1)} %pad_maximum_fusion), channel_id=1, source_target_pairs={{0,1},{1,2},{2,3},{3,0},{4,5},{5,6},{6,7},{7,4},{8,9},{9,10},{10,1... | collective-permute-start | bytes 786440 | tf_op jit(solution)/shard_map/ppermute | solution.py:27
  52.1 29.9 %collective-permute-start.32 = (bf16[768,128]{1,0:T(8,128)(2,1)S(1)}, bf16[768,128]{1,0:T(8,128)(2,1)S(1)}, u32[]{:S(2)}, u32[]{:S(2)}) collective-permute-start(bf16[768,128]{1,0:T(8,128)(2,1)S(1)} %pad_maximum_fusion.1), channel_id=1, source_target_pairs={{0,3},{1,0},{2,1},{3,2},{4,7},{5,4},{6,5},{7,6},{8,11},{9,8},{10,9... | collective-permute-start | bytes 589832 | tf_op jit(solution)/shard_map/ppermute | solution.py:27
  69.5 24.2 %collective-permute-start.29 = (bf16[1024,128]{1,0:T(8,128)(2,1)S(1)}, bf16[1024,128]{1,0:T(8,128)(2,1)S(1)}, u32[]{:S(2)}, u32[]{:S(2)}) collective-permute-start(bf16[1024,128]{1,0:T(8,128)(2,1)S(1)} %collective-permute-done.26.refs_20_), channel_id=1, source_target_pairs={{0,4},{1,5},{2,6},{3,7},{4,0},{5,1},{6,2},{7,3},{8,12},{9,13},{10,... | collective-permute-start | bytes 786440 | tf_op jit(solution)/shard_map/ppermute | solution.py:27
  74.8 19.0 %collective-permute-start.28 = (bf16[1024,128]{1,0:T(8,128)(2,1)S(1)}, bf16[1024,128]{1,0:T(8,128)(2,1)S(1)}, u32[]{:S(2)}, u32[]{:S(2)}) collective-permute-start(bf16[1024,128]{1,0:T(8,128)(2,1)S(1)} %collective-permute-done.25.refs_19_), channel_id=1, source_target_pairs={{0,4},{1,5},{2,6},{3,7},{4,0},{5,1},{6,2},{7,3},{8,12},{9,13},{10,... | collective-permute-start | bytes 786440 | tf_op jit(solution)/shard_map/ppermute | solution.py:27
  74.9 18.9 %collective-permute-start.27 = (bf16[1024,128]{1,0:T(8,128)(2,1)S(1)}, bf16[1024,128]{1,0:T(8,128)(2,1)S(1)}, u32[]{:S(2)}, u32[]{:S(2)}) collective-permute-start(bf16[1024,128]{1,0:T(8,128)(2,1)S(1)} %collective-permute-done.24.refs_18_), channel_id=1, source_target_pairs={{0,4},{1,5},{2,6},{3,7},{4,0},{5,1},{6,2},{7,3},{8,12},{9,13},{10,... | collective-permute-start | bytes 786440 | tf_op jit(solution)/shard_map/ppermute | solution.py:27
  82.0 9.3 %collective-permute-start.30 = (bf16[768,128]{1,0:T(8,128)(2,1)S(1)}, bf16[768,128]{1,0:T(8,128)(2,1)S(1)}, u32[]{:S(2)}, u32[]{:S(2)}) collective-permute-start(bf16[768,128]{1,0:T(8,128)(2,1)S(1)} %pad_maximum_fusion.1), channel_id=1, source_target_pairs={{0,1},{1,2},{2,3},{3,0},{4,5},{5,6},{6,7},{7,4},{8,9},{9,10},{10,1... | collective-permute-start | bytes 589832 | tf_op jit(solution)/shard_map/ppermute | solution.py:27
  85.6 23.8 %collective-permute-start.35 = (bf16[768,128]{1,0:T(8,128)(2,1)S(1)}, bf16[768,128]{1,0:T(8,128)(2,1)S(1)}, u32[]{:S(2)}, u32[]{:S(2)}) collective-permute-start(bf16[768,128]{1,0:T(8,128)(2,1)S(1)} %collective-permute-done.32.refs_2_), channel_id=1, source_target_pairs={{0,4},{1,5},{2,6},{3,7},{4,0},{5,1},{6,2},{7,3},{8,12},{9,13},{10,... | collective-permute-start | bytes 589832 | tf_op jit(solution)/shard_map/ppermute | solution.py:27
  91.3 18.0 %collective-permute-start.34 = (bf16[768,128]{1,0:T(8,128)(2,1)S(1)}, bf16[768,128]{1,0:T(8,128)(2,1)S(1)}, u32[]{:S(2)}, u32[]{:S(2)}) collective-permute-start(bf16[768,128]{1,0:T(8,128)(2,1)S(1)} %collective-permute-done.31.refs_1_), channel_id=1, source_target_pairs={{0,4},{1,5},{2,6},{3,7},{4,0},{5,1},{6,2},{7,3},{8,12},{9,13},{10,... | collective-permute-start | bytes 589832 | tf_op jit(solution)/shard_map/ppermute | solution.py:27
  93.8 15.6 %collective-permute-start.33 = (bf16[768,128]{1,0:T(8,128)(2,1)S(1)}, bf16[768,128]{1,0:T(8,128)(2,1)S(1)}, u32[]{:S(2)}, u32[]{:S(2)}) collective-permute-start(bf16[768,128]{1,0:T(8,128)(2,1)S(1)} %collective-permute-done.30.refs_0_), channel_id=1, source_target_pairs={{0,4},{1,5},{2,6},{3,7},{4,0},{5,1},{6,2},{7,3},{8,12},{9,13},{10,... | collective-permute-start | bytes 589832 | tf_op jit(solution)/shard_map/ppermute | solution.py:27
  141.1 20.6 %collective-permute-start.37 = (bf16[4,4,48,128]{3,2,1,0:T(8,128)(2,1)}, bf16[4,4,48,128]{3,2,1,0:T(8,128)(2,1)S(1)}, u32[]{:S(2)}, u32[]{:S(2)}) collective-permute-start(bf16[4,4,48,128]{3,2,1,0:T(8,128)(2,1)} %get-tuple-element.67), channel_id=1, source_target_pairs={{0,1},{1,2},{2,3},{3,0},{4,5},{5,6},{6,7},{7,4},{8,9},{9,10},{10,1... | collective-permute-start | bytes 589832 | tf_op jit(solution)/shard_map/ppermute | solution.py:27
  141.9 14.2 %collective-permute-start.43 = (bf16[4,4,32,128]{3,2,1,0:T(8,128)(2,1)}, bf16[4,4,32,128]{3,2,1,0:T(8,128)(2,1)S(1)}, u32[]{:S(2)}, u32[]{:S(2)}) collective-permute-start(bf16[4,4,32,128]{3,2,1,0:T(8,128)(2,1)} %get-tuple-element.75), channel_id=1, source_target_pairs={{0,32},{1,33},{2,34},{3,35},{4,36},{5,37},{6,38},{7,39},{8,40},{9,... | collective-permute-start | bytes 393224 | tf_op jit(solution)/shard_map/ppermute | solution.py:27
  141.9 16.0 %collective-permute-start.44 = (bf16[4,4,32,128]{3,2,1,0:T(8,128)(2,1)}, bf16[4,4,32,128]{3,2,1,0:T(8,128)(2,1)S(1)}, u32[]{:S(2)}, u32[]{:S(2)}) collective-permute-start(bf16[4,4,32,128]{3,2,1,0:T(8,128)(2,1)} %get-tuple-element.76), channel_id=1, source_target_pairs={{0,64},{1,65},{2,66},{3,67},{4,68},{5,69},{6,70},{7,71},{8,72},{9,... | collective-permute-start | bytes 393224 | tf_op jit(solution)/shard_map/ppermute | solution.py:27
  154.6 8.9 %collective-permute-start.38 = (bf16[4,4,48,128]{3,2,1,0:T(8,128)(2,1)}, bf16[4,4,48,128]{3,2,1,0:T(8,128)(2,1)S(1)}, u32[]{:S(2)}, u32[]{:S(2)}) collective-permute-start(bf16[4,4,48,128]{3,2,1,0:T(8,128)(2,1)} %get-tuple-element.68), channel_id=1, source_target_pairs={{0,2},{1,3},{2,0},{3,1},{4,6},{5,7},{6,4},{7,5},{8,10},{9,11},{10,... | collective-permute-start | bytes 589832 | tf_op jit(solution)/shard_map/ppermute | solution.py:27
  156.0 10.0 %collective-permute-start.39 = (bf16[4,4,48,128]{3,2,1,0:T(8,128)(2,1)}, bf16[4,4,48,128]{3,2,1,0:T(8,128)(2,1)S(1)}, u32[]{:S(2)}, u32[]{:S(2)}) collective-permute-start(bf16[4,4,48,128]{3,2,1,0:T(8,128)(2,1)} %get-tuple-element.69), channel_id=1, source_target_pairs={{0,3},{1,0},{2,1},{3,2},{4,7},{5,4},{6,5},{7,6},{8,11},{9,8},{10,9... | collective-permute-start | bytes 589832 | tf_op jit(solution)/shard_map/ppermute | solution.py:27
  157.8 8.2 %collective-permute-start.40 = (bf16[4,4,48,128]{3,2,1,0:T(8,128)(2,1)}, bf16[4,4,48,128]{3,2,1,0:T(8,128)(2,1)S(1)}, u32[]{:S(2)}, u32[]{:S(2)}) collective-permute-start(bf16[4,4,48,128]{3,2,1,0:T(8,128)(2,1)} %get-tuple-element.71), channel_id=1, source_target_pairs={{0,8},{1,9},{2,10},{3,11},{4,12},{5,13},{6,14},{7,15},{8,16},{9,17... | collective-permute-start | bytes 589832 | tf_op jit(solution)/shard_map/ppermute | solution.py:27
  160.8 8.6 %collective-permute-start.41 = (bf16[4,4,48,128]{3,2,1,0:T(8,128)(2,1)}, bf16[4,4,48,128]{3,2,1,0:T(8,128)(2,1)S(1)}, u32[]{:S(2)}, u32[]{:S(2)}) collective-permute-start(bf16[4,4,48,128]{3,2,1,0:T(8,128)(2,1)} %get-tuple-element.72), channel_id=1, source_target_pairs={{0,16},{1,17},{2,18},{3,19},{4,20},{5,21},{6,22},{7,23},{8,24},{9,... | collective-permute-start | bytes 589832 | tf_op jit(solution)/shard_map/ppermute | solution.py:27
  161.7 9.5 %collective-permute-start.42 = (bf16[4,4,48,128]{3,2,1,0:T(8,128)(2,1)}, bf16[4,4,48,128]{3,2,1,0:T(8,128)(2,1)S(1)}, u32[]{:S(2)}, u32[]{:S(2)}) collective-permute-start(bf16[4,4,48,128]{3,2,1,0:T(8,128)(2,1)} %get-tuple-element.73), channel_id=1, source_target_pairs={{0,24},{1,25},{2,26},{3,27},{4,28},{5,29},{6,30},{7,31},{8,0},{9,1... | collective-permute-start | bytes 589832 | tf_op jit(solution)/shard_map/ppermute | solution.py:27
  174.4 8.2 %collective-permute-start.46 = (bf16[4,48,128]{2,1,0:T(8,128)(2,1)}, bf16[4,48,128]{2,1,0:T(8,128)(2,1)S(1)}, u32[]{:S(2)}, u32[]{:S(2)}) collective-permute-start(bf16[4,48,128]{2,1,0:T(8,128)(2,1)} %get-tuple-element.79), channel_id=1, source_target_pairs={{0,8},{1,9},{2,10},{3,11},{4,12},{5,13},{6,14},{7,15},{8,16},{9,17... | collective-permute-start | bytes 147464 | tf_op jit(solution)/shard_map/ppermute | solution.py:27
  176.6 9.2 %collective-permute-start.49 = (bf16[4,80,128]{2,1,0:T(8,128)(2,1)}, bf16[4,80,128]{2,1,0:T(8,128)(2,1)S(1)}, u32[]{:S(2)}, u32[]{:S(2)}) collective-permute-start(bf16[4,80,128]{2,1,0:T(8,128)(2,1)} %get-tuple-element.83), channel_id=1, source_target_pairs={{0,1},{1,2},{2,3},{3,0},{4,5},{5,6},{6,7},{7,4},{8,9},{9,10},{10,1... | collective-permute-start | bytes 245768 | tf_op jit(solution)/shard_map/ppermute | solution.py:27
  176.8 9.0 %collective-permute-start.50 = (bf16[4,80,128]{2,1,0:T(8,128)(2,1)}, bf16[4,80,128]{2,1,0:T(8,128)(2,1)S(1)}, u32[]{:S(2)}, u32[]{:S(2)}) collective-permute-start(bf16[4,80,128]{2,1,0:T(8,128)(2,1)} %get-tuple-element.84), channel_id=1, source_target_pairs={{0,2},{1,3},{2,0},{3,1},{4,6},{5,7},{6,4},{7,5},{8,10},{9,11},{10,... | collective-permute-start | bytes 245768 | tf_op jit(solution)/shard_map/ppermute | solution.py:27
  188.4 15.3 %collective-permute-start.54 = (bf16[4,96,128]{2,1,0:T(8,128)(2,1)}, bf16[4,96,128]{2,1,0:T(8,128)(2,1)S(1)}, u32[]{:S(2)}, u32[]{:S(2)}) collective-permute-start(bf16[4,96,128]{2,1,0:T(8,128)(2,1)} %get-tuple-element.86.refs_0_), channel_id=1, source_target_pairs={{0,96},{1,97},{2,98},{3,99},{4,100},{5,101},{6,102},{7,103},{8,104... | collective-permute-start | bytes 294920 | tf_op jit(solution)/shard_map/ppermute | solution.py:27
  192.4 11.3 %collective-permute-start.53 = (bf16[4,96,128]{2,1,0:T(8,128)(2,1)}, bf16[4,96,128]{2,1,0:T(8,128)(2,1)S(1)}, u32[]{:S(2)}, u32[]{:S(2)}) collective-permute-start(bf16[4,96,128]{2,1,0:T(8,128)(2,1)} %get-tuple-element.86.refs_0_), channel_id=1, source_target_pairs={{0,64},{1,65},{2,66},{3,67},{4,68},{5,69},{6,70},{7,71},{8,72},{9,... | collective-permute-start | bytes 294920 | tf_op jit(solution)/shard_map/ppermute | solution.py:27
  192.4 11.3 %collective-permute-start.52 = (bf16[4,96,128]{2,1,0:T(8,128)(2,1)}, bf16[4,96,128]{2,1,0:T(8,128)(2,1)S(1)}, u32[]{:S(2)}, u32[]{:S(2)}) collective-permute-start(bf16[4,96,128]{2,1,0:T(8,128)(2,1)} %get-tuple-element.86.refs_0_), channel_id=1, source_target_pairs={{0,32},{1,33},{2,34},{3,35},{4,36},{5,37},{6,38},{7,39},{8,40},{9,... | collective-permute-start | bytes 294920 | tf_op jit(solution)/shard_map/ppermute | solution.py:27
  196.2 7.3 %collective-permute-start.55 = (bf16[4,32,128]{2,1,0:T(8,128)(2,1)}, bf16[4,32,128]{2,1,0:T(8,128)(2,1)S(1)}, u32[]{:S(2)}, u32[]{:S(2)}) collective-permute-start(bf16[4,32,128]{2,1,0:T(8,128)(2,1)} %get-tuple-element.87.refs_4_), channel_id=1, source_target_pairs={{0,8},{1,9},{2,10},{3,11},{4,12},{5,13},{6,14},{7,15},{8,16},{9,17... | collective-permute-start | bytes 98312 | tf_op jit(solution)/shard_map/ppermute | solution.py:27
  198.2 11.9 %collective-permute-start.75 = (bf16[32,512]{1,0:T(8,128)(2,1)S(1)}, bf16[32,512]{1,0:T(8,128)(2,1)S(1)}, u32[]{:S(2)}, u32[]{:S(2)}) collective-permute-start(bf16[32,512]{1,0:T(8,128)(2,1)S(1)} %copy-done.65), channel_id=1, source_target_pairs={{0,127},{1,0},{2,1},{3,2},{4,3},{5,4},{6,5},{7,6},{8,7},{9,8},{10,... | collective-permute-start | bytes 98312 | tf_op jit(solution)/shard_map/ppermute | solution.py:31
  203.6 11.2 %collective-permute-start.76 = (bf16[32,512]{1,0:T(8,128)(2,1)S(1)}, bf16[32,512]{1,0:T(8,128)(2,1)S(1)}, u32[]{:S(2)}, u32[]{:S(2)}) collective-permute-start(bf16[32,512]{1,0:T(8,128)(2,1)S(1)} %copy-done.63), channel_id=1, source_target_pairs={{0,1},{1,2},{2,3},{3,4},{4,5},{5,6},{6,7},{7,8},{8,9},{9,10},{10,1... | collective-permute-start | bytes 98312 | tf_op jit(solution)/shard_map/ppermute | solution.py:31
  206.8 8.6 %collective-permute-start.74 = (bf16[16,128]{1,0:T(8,128)(2,1)}, bf16[16,128]{1,0:T(8,128)(2,1)S(1)}, u32[]{:S(2)}, u32[]{:S(2)}) collective-permute-start(bf16[16,128]{1,0:T(8,128)(2,1)} %get-tuple-element.90.refs_16_), channel_id=1, source_target_pairs={{0,3},{1,0},{2,1},{3,2},{4,7},{5,4},{6,5},{7,6},{8,11},{9,8},{10,9... | collective-permute-start | bytes 12296 | tf_op jit(solution)/shard_map/ppermute | solution.py:27
  209.5 8.0 %collective-permute-start.72 = (bf16[16,128]{1,0:T(8,128)(2,1)}, bf16[16,128]{1,0:T(8,128)(2,1)S(1)}, u32[]{:S(2)}, u32[]{:S(2)}) collective-permute-start(bf16[16,128]{1,0:T(8,128)(2,1)} %get-tuple-element.90.refs_16_), channel_id=1, source_target_pairs={{0,1},{1,2},{2,3},{3,0},{4,5},{5,6},{6,7},{7,4},{8,9},{9,10},{10,1... | collective-permute-start | bytes 12296 | tf_op jit(solution)/shard_map/ppermute | solution.py:27
  210.1 9.8 %collective-permute-start.71 = (bf16[4,32,128]{2,1,0:T(8,128)(2,1)}, bf16[4,32,128]{2,1,0:T(8,128)(2,1)S(1)}, u32[]{:S(2)}, u32[]{:S(2)}) collective-permute-start(bf16[4,32,128]{2,1,0:T(8,128)(2,1)} %get-tuple-element.89.refs_8_), channel_id=1, source_target_pairs={{0,100},{1,101},{2,102},{3,103},{4,96},{5,97},{6,98},{7,99},{8,108... | collective-permute-start | bytes 98312 | tf_op jit(solution)/shard_map/ppermute | solution.py:27
  216.4 7.5 %collective-permute-start.68 = (bf16[4,32,128]{2,1,0:T(8,128)(2,1)}, bf16[4,32,128]{2,1,0:T(8,128)(2,1)S(1)}, u32[]{:S(2)}, u32[]{:S(2)}) collective-permute-start(bf16[4,32,128]{2,1,0:T(8,128)(2,1)} %get-tuple-element.89.refs_8_), channel_id=1, source_target_pairs={{0,4},{1,5},{2,6},{3,7},{4,0},{5,1},{6,2},{7,3},{8,12},{9,13},{10,... | collective-permute-start | bytes 98312 | tf_op jit(solution)/shard_map/ppermute | solution.py:27
  220.7 7.4 %collective-permute-start.64 = (bf16[4,80,128]{2,1,0:T(8,128)(2,1)}, bf16[4,80,128]{2,1,0:T(8,128)(2,1)S(1)}, u32[]{:S(2)}, u32[]{:S(2)}) collective-permute-start(bf16[4,80,128]{2,1,0:T(8,128)(2,1)} %get-tuple-element.88.refs_0_), channel_id=1, source_target_pairs={{0,28},{1,29},{2,30},{3,31},{4,24},{5,25},{6,26},{7,27},{8,4},{9,5... | collective-permute-start | bytes 245768 | tf_op jit(solution)/shard_map/ppermute | solution.py:27
  223.9 8.4 %collective-permute-start.62 = (bf16[4,80,128]{2,1,0:T(8,128)(2,1)}, bf16[4,80,128]{2,1,0:T(8,128)(2,1)S(1)}, u32[]{:S(2)}, u32[]{:S(2)}) collective-permute-start(bf16[4,80,128]{2,1,0:T(8,128)(2,1)} %get-tuple-element.88.refs_0_), channel_id=1, source_target_pairs={{0,12},{1,13},{2,14},{3,15},{4,8},{5,9},{6,10},{7,11},{8,20},{9,21... | collective-permute-start | bytes 245768 | tf_op jit(solution)/shard_map/ppermute | solution.py:27
  224.5 7.8 %collective-permute-start.61 = (bf16[4,80,128]{2,1,0:T(8,128)(2,1)}, bf16[4,80,128]{2,1,0:T(8,128)(2,1)S(1)}, u32[]{:S(2)}, u32[]{:S(2)}) collective-permute-start(bf16[4,80,128]{2,1,0:T(8,128)(2,1)} %get-tuple-element.88.refs_0_), channel_id=1, source_target_pairs={{0,4},{1,5},{2,6},{3,7},{4,0},{5,1},{6,2},{7,3},{8,12},{9,13},{10,... | collective-permute-start | bytes 245768 | tf_op jit(solution)/shard_map/ppermute | solution.py:27
  (107 other events, 1930.1 us)

commit v2 on v1

v2 whole, which is shorter than its diff:
```python
import jax
import jax.numpy as jnp
from jax import lax
from jax.experimental import pallas as pl
from jax.experimental.pallas import tpu as pltpu
from jax.sharding import Mesh
from jax.sharding import PartitionSpec as P

EPSILON = 1e-05
BF16 = jnp.bfloat16
F32 = jnp.float32
BOTH = ("z", "x", "core", "feat")
CHUNK = 512
STEPS = 4
TABLE = 896
VMEM_BYTES = 60 * 1024 * 1024


def other_core(value):
    return lax.ppermute(value, "core", [(0, 1), (1, 0)])


def shifted(value, steps):
    return lax.ppermute(value, BOTH, [(k, (k + steps) % 128) for k in range(128)])


def exchange(value, axes):
    return lax.all_to_all(value, axes, 0, 0, tiled=True)


def repeated(value, count):
    return jnp.broadcast_to(value[None], (count,) + value.shape)


def dot(left, right):
    return lax.dot_general(left, right, (((1,), (0,)), ((), ())), preferred_element_type=F32)


def dot_nt(left, right):
    return lax.dot_general(left, right, (((1,), (1,)), ((), ())), preferred_element_type=F32)


def dot_tn(left, right):
    return lax.dot_general(left, right, (((0,), (0,)), ((), ())), preferred_element_type=F32)


def mean(values):
    return jnp.mean(values, axis=-1, keepdims=True)


def normalize(values):
    centre = values - mean(values)
    factor = lax.rsqrt(mean(centre * centre) + EPSILON)
    return centre * factor, factor


def normalize_back(upstream, normed, factor):
    return factor * (upstream - mean(upstream) - normed * mean(upstream * normed))


def swish(pre):
    sigmoid = 0.5 + 0.5 * jnp.tanh(0.5 * pre)
    act = pre * sigmoid
    return act, sigmoid + act * (1.0 - sigmoid)


def hot_tiles(rows, count):
    lanes = lax.broadcasted_iota(jnp.int32, (128, 128), 1)
    spread = jnp.transpose(jnp.broadcast_to(rows, (128, 128)))
    return [jnp.where(spread == lanes + 128 * j, 1.0, 0.0).astype(BF16) for j in range(count)]


def live_rows(step, count):
    place = lax.broadcasted_iota(jnp.int32, (CHUNK, 1), 0) + step * CHUNK
    return jnp.where(place < count, 1.0, 0.0)


def place_weights(core, near, far, first, second):
    kinds = first.shape[0]
    for part, half in ((near, core), (far, 1 - core)):
        for y in range(4):
            rows = pl.ds(pl.multiple_of(half * 256, 256), 256)
            for m in range(kinds):
                first[m, rows, y * 128 : (y + 1) * 128] = part[y, m * 256 : (m + 1) * 256, :]
            rows = pl.ds(pl.multiple_of(y * 128 + half * 64, 64), 64)
            for b in range(4):
                start = kinds * 256 + b * 64
                second[rows, b * 128 : (b + 1) * 128] = part[y, start : start + 64, :]


def forward_kernel(co, node, prev, after, coarse, near, far, src, dst, dst_wide, edge, *refs):
    edge_out, incoming, act_out, normed_out, slope_out, factor_out, lookup, first, second = refs[:9]
    table, total = refs[9:]
    step = pl.program_id(0)

    @pl.when(step == 0)
    def _():
        lookup[0:256, :] = node[...]
        lookup[256:288, :] = prev[...]
        lookup[288:320, :] = after[...]
        lookup[832:896, :] = jnp.zeros((64, 512), BF16)
        lookup[320:832, :] = coarse[...]
        place_weights(co[2], near, far, first, second)
        table[0:TABLE, :] = dot(lookup[...], first[1]).astype(BF16)
        table[TABLE:, :] = dot(node[...], first[2]).astype(BF16)
        total[...] = jnp.zeros_like(total)

    hots = []
    for r in range(CHUNK // 128):
        row = pl.ds(step * (CHUNK // 128) + r, 1)
        tiles = hot_tiles(src[row, :], TABLE // 128) + hot_tiles(dst[row, :], 2)
        hots.append(jnp.concatenate(tiles, axis=1))
    hot = jnp.concatenate(hots, axis=0)
    rows = edge[...]
    pre = dot(rows, first[0]) + dot(hot, table[...])
    act, slope = swish(pre)
    act = act.astype(BF16)
    act_out[...] = act
    slope_out[...] = slope.astype(BF16)
    normed, factor = normalize(dot(act, second[...]))
    normed_out[...] = normed.astype(BF16)
    factor_out[...] = jnp.broadcast_to(factor, (CHUNK, 128))
    new = (rows.astype(F32) + live_rows(step, co[4]) * normed).astype(BF16)
    edge_out[...] = new
    place = lax.broadcasted_iota(jnp.int32, (256, CHUNK), 1) + step * CHUNK
    node_of = lax.broadcasted_iota(jnp.int32, (256, CHUNK), 0)
    match = (node_of == dst_wide[pl.ds(step, 1), :]) & (place < co[4])
    total[...] += dot(jnp.where(match, 1.0, 0.0).astype(BF16), new)

    @pl.when(step == STEPS - 1)
    def _():
        incoming[...] = total[...].astype(BF16)


def put_columns(co, grad, slot, scratch, keep, give):
    scratch[...] = grad.astype(BF16).reshape(16, 2, 16, 512)
    for target, core in ((keep, co[2]), (give, 1 - co[2])):
        value = scratch[:, pl.ds(core, 1), :, :].reshape(8, 2, 16, 512)
        for y in range(4):
            target[:, :, y, slot * 16 : (slot + 1) * 16, :] = value[:, :, :, y * 128 : (y + 1) * 128]


def put_rows(co, grad, slot, scratch, keep, give):
    for b in range(4):
        scratch[b] = grad[:, b * 128 : (b + 1) * 128].astype(BF16)
    for target, core in ((keep, co[2]), (give, 1 - co[2])):
        for h in range(2):
            value = scratch[2 * h + core].reshape(4, 8, 16, 128)
            for y in range(4):
                target[:, h, y, slot * 16 : (slot + 1) * 16, :] = value[y]


def put_owned(co, grad, scratch, keep, give):
    rows = grad.reshape(64, 8, 512)
    turned = pltpu.roll(rows, 4, 1)
    low = lax.broadcasted_iota(jnp.int32, (64, 8, 128), 1) < 4
    for odd in range(2):
        left, right = (turned, rows) if odd else (rows, turned)
        parts = [
            jnp.where(low, left[:, :, b : b + 128], right[:, :, b + 128 : b + 256]) for b in (0, 256)
        ]
        tile = jnp.concatenate(parts, axis=1).astype(BF16).reshape(16, 2, 2, 16, 128)
        for pair in range(2):
            scratch[:, :, pair * 2 + odd] = tile[:, :, pair]
    for target, core in ((keep, co[2]), (give, 1 - co[2])):
        value = scratch[:, pl.ds(core, 1)].reshape(8, 2, 4, 16, 128)
        target[:, :, :, 112:128, :] = value


def backward_kernel(co, node, incoming, grad_node, near, far, *refs):
    edge_first, edge_second, lookup, dst, src_wide, dst_wide = refs[:6]
    edge, act, normed, slope, factor, grad_edge = refs[6:12]
    node_out, node_total, edge_grad, to_prev, to_next, keep, give = refs[12:19]
    first, second, spread, sum_second, sum_first, sums, columns, rows, owned = refs[19:]
    step = pl.program_id(0)

    @pl.when(step == 0)
    def _():
        place_weights(co[2], near, far, first, second)
        lat, summed = node[...], incoming[...]
        pre = dot(lat, first[0]) + dot(summed, first[1])
        node_act, node_slope = swish(pre)
        node_act = node_act.astype(BF16)
        node_normed, node_factor = normalize(dot(node_act, second[...]))
        node_out[...] = (lat.astype(F32) + node_normed).astype(BF16)
        upstream = grad_node[...].astype(F32)
        delta = normalize_back(upstream, node_normed, node_factor).astype(BF16)
        put_rows(co, dot_tn(node_act, delta), 6, rows, keep, give)
        pre_grad = (dot_nt(delta, second[...]) * node_slope).astype(BF16)
        put_columns(co, dot_tn(lat, pre_grad), 3, columns, keep, give)
        put_columns(co, dot_tn(summed, pre_grad), 4, columns, keep, give)
        node_total[...] = upstream + dot_nt(pre_grad, first[0])
        spread[...] = dot_nt(pre_grad, first[1]).astype(BF16)
        sum_second[...] = jnp.zeros_like(sum_second)
        sum_first[...] = jnp.zeros_like(sum_first)
        sums[...] = jnp.zeros_like(sums)

    hots = []
    for r in range(CHUNK // 128):
        row = pl.ds(step * (CHUNK // 128) + r, 1)
        hots.append(jnp.concatenate(hot_tiles(dst[row, :], 2), axis=1))
    live = live_rows(step, co[4])
    total = grad_edge[...].astype(F32) + live * dot(jnp.concatenate(hots, axis=0), spread[...])
    delta = normalize_back(live * total, normed[...].astype(F32), factor[:, 0:1]).astype(BF16)
    pre_grad = (dot_nt(delta, edge_second[...]) * slope[...].astype(F32)).astype(BF16)
    edge_grad[...] = (total + dot_nt(pre_grad, edge_first[0])).astype(BF16)
    sum_second[...] += dot_tn(act[...], delta)
    sum_first[...] += dot_tn(edge[...], pre_grad)
    place = lax.broadcasted_iota(jnp.int32, (128, CHUNK), 0)
    src_row, dst_row = src_wide[pl.ds(step, 1), :], dst_wide[pl.ds(step, 1), :]
    for j in range(9):
        match = place + 128 * j == src_row if j < 7 else place + 128 * (j - 7) == dst_row
        hot = jnp.where(match, 1.0, 0.0).astype(BF16)
        sums[j * 128 : (j + 1) * 128, :] += dot(hot, pre_grad)

    @pl.when(step == STEPS - 1)
    def _():
        put_rows(co, sum_second[...], 5, rows, keep, give)
        put_columns(co, sum_first[...], 0, columns, keep, give)
        sent = sums[0:TABLE, :].astype(BF16)
        received = sums[TABLE:, :].astype(BF16)
        put_columns(co, dot_tn(lookup[...], sent), 1, columns, keep, give)
        put_columns(co, dot_tn(node[...], received), 2, columns, keep, give)
        back = dot_nt(sent, edge_first[1])
        node_total[...] += back[0:256] + dot_nt(received, edge_first[2])
        to_prev[...] = back[256:288].astype(BF16)
        to_next[...] = back[288:320].astype(BF16)
        put_owned(co, back[320:832], owned, keep, give)


def final_kernel(tiles, own, ahead, behind, targets, node_total, *refs):
    edge_first, edge_second, node_first, node_second, node_grad, rows = refs
    for m in range(5):
        value = tiles[:, m * 16 : (m + 1) * 16, :].astype(F32)
        if m < 3:
            edge_first[m] = value
        else:
            node_first[m - 3] = value
    for p in range(32):
        r, b = p // 4 * 16, p % 4 * 128
        edge_second[r : r + 16, b : b + 128] = tiles[p, 80:96, :].astype(F32)
        node_second[r : r + 16, b : b + 128] = tiles[p, 96:112, :].astype(F32)
    rows[0:32, :] = ahead[...]
    rows[32:64, :] = behind[...]
    group = lax.broadcasted_iota(jnp.int32, (16, 128), 0) // 4
    for b in range(4):
        value = jnp.where(group == b, own[112:128, :].astype(F32), 0.0)
        rows[64:80, b * 128 : (b + 1) * 128] = value.astype(BF16)
    rows[80:128, :] = jnp.zeros((48, 512), BF16)
    match = lax.broadcasted_iota(jnp.int32, (256, 128), 0) == targets[...]
    hot = jnp.where(match, 1.0, 0.0).astype(BF16)
    node_grad[...] = node_total[...] + dot(hot, rows[...])


SMEM = pl.BlockSpec(memory_space=pltpu.SMEM)
WHOLE = pl.BlockSpec(memory_space=pltpu.VMEM)


def shape(*dims, dtype=BF16):
    return jax.ShapeDtypeStruct(dims, dtype)


def plain_call(kernel, scalars, operands, outs, scratch=()):
    return pl.pallas_call(
        kernel,
        in_specs=[SMEM] * len(scalars) + [WHOLE] * len(operands),
        out_specs=[WHOLE] * len(outs),
        out_shape=list(outs),
        scratch_shapes=list(scratch),
        compiler_params=pltpu.CompilerParams(vmem_limit_bytes=VMEM_BYTES),
    )(*scalars, *operands)


def same(*dims):
    return pl.BlockSpec(dims, lambda i: (0,) * len(dims))


def chunk(*dims):
    return pl.BlockSpec(dims, lambda i: (i,) + (0,) * (len(dims) - 1))


def like(value):
    return same(*value.shape)


def halves(first, second, core):
    kinds = first.shape[0]
    top = lax.dynamic_slice_in_dim(first, core * 256, 256, 1).reshape(kinds * 256, 128)
    rest = lax.dynamic_slice_in_dim(second, core * 64, 64, 0)
    rest = rest.reshape(64, 4, 128).transpose(1, 0, 2).reshape(256, 128)
    return jnp.concatenate([top, rest], axis=0)


def shards(
    node_lat,
    edge_lat,
    edge_src,
    edge_dst,
    edge_count,
    halo_send,
    coarse_of,
    edge_w1,
    edge_w2,
    node_w1,
    node_w2,
    grad_node,
    grad_edge,
):
    core = lax.axis_index("core")
    co = jnp.stack([core, core, core, core, edge_count[0]]).astype(jnp.int32)
    lists, owned = halo_send[0], coarse_of[0]
    unused = jnp.full((48,), -1, jnp.int32)
    targets = jnp.concatenate([lists[1], lists[0], jnp.tile(owned, 4), unused]).reshape(1, 128)

    edge_near = exchange(repeated(halves(edge_w1, edge_w2, core), 4), "feat")
    from_prev = shifted(node_lat[lists[1]], 1)
    from_next = shifted(node_lat[lists[0]], -1)
    edge_far = other_core(edge_near)
    coarse = exchange(repeated(node_lat[owned], 128), BOTH).reshape(512, 512)
    node_near = exchange(repeated(halves(node_w1, node_w2, core), 4), "feat")
    node_far = other_core(node_near)

    src, dst = edge_src.reshape(16, 128), edge_dst.reshape(16, 128)
    src_wide, dst_wide = edge_src.reshape(STEPS, CHUNK), edge_dst.reshape(STEPS, CHUNK)
    fixed = [node_lat, from_prev, from_next, coarse, edge_near, edge_far]
    fixed += [src, dst, dst_wide]
    wide = chunk(CHUNK, 512)
    params = pltpu.CompilerParams(vmem_limit_bytes=VMEM_BYTES, dimension_semantics=("arbitrary",))
    edge_out, incoming, act, normed, slope, factor, lookup, first, second = pl.pallas_call(
        forward_kernel,
        grid=(STEPS,),
        in_specs=[SMEM] + [like(v) for v in fixed] + [wide],
        out_specs=[wide, same(256, 512), wide, wide, wide, chunk(CHUNK, 128)]
        + [same(TABLE, 512), same(3, 512, 512), same(512, 512)],
        out_shape=[
            shape(2048, 512),
            shape(256, 512),
            shape(2048, 512),
            shape(2048, 512),
            shape(2048, 512),
            shape(2048, 128, dtype=F32),
            shape(TABLE, 512),
            shape(3, 512, 512),
            shape(512, 512),
        ],
        scratch_shapes=[pltpu.VMEM((TABLE + 256, 512), BF16), pltpu.VMEM((256, 512), F32)],
        compiler_params=params,
        cost_estimate=pl.CostEstimate(
            flops=7_000_000_000, bytes_accessed=18_000_000, transcendentals=1_000_000
        ),
    )(co, *fixed, edge_lat)

    fixed = [node_lat, incoming, grad_node, node_near, node_far]
    fixed += [first, second, lookup, dst, src_wide, dst_wide]
    moving = [edge_lat, act, normed, slope, factor, grad_edge]
    tiles = (8, 2, 4, 128, 128)
    node_out, node_total, edge_grad, to_prev, to_next, keep, give = pl.pallas_call(
        backward_kernel,
        grid=(STEPS,),
        in_specs=[SMEM]
        + [like(v) for v in fixed]
        + [wide, wide, wide, wide, chunk(CHUNK, 128), wide],
        out_specs=[same(256, 512), same(256, 512), wide, same(32, 512), same(32, 512)]
        + [same(*tiles), same(*tiles)],
        out_shape=[
            shape(256, 512),
            shape(256, 512, dtype=F32),
            shape(2048, 512),
            shape(32, 512),
            shape(32, 512),
            shape(*tiles),
            shape(*tiles),
        ],
        scratch_shapes=[
            pltpu.VMEM((2, 512, 512), BF16),
            pltpu.VMEM((512, 512), BF16),
            pltpu.VMEM((256, 512), BF16),
            pltpu.VMEM((512, 512), F32),
            pltpu.VMEM((512, 512), F32),
            pltpu.VMEM((TABLE + 256, 512), F32),
            pltpu.VMEM((16, 2, 16, 512), BF16),
            pltpu.VMEM((4, 512, 128), BF16),
            pltpu.VMEM((16, 2, 4, 16, 128), BF16),
        ],
        compiler_params=params,
        cost_estimate=pl.CostEstimate(
            flops=9_000_000_000, bytes_accessed=24_000_000, transcendentals=100_000
        ),
    )(co, *fixed, *moving)

    ahead = shifted(to_prev, -1)
    behind = shifted(to_next, 1)
    pair = (keep.astype(F32) + other_core(give).astype(F32)).astype(BF16).reshape(64, 128, 128)
    own = jnp.sum(exchange(pair, ("z", "x", "feat")).astype(F32), axis=0).astype(BF16)
    tiles = exchange(repeated(own[:112], 32), ("z", "x", "core"))
    edge_first, edge_second, node_first, node_second, node_grad = plain_call(
        final_kernel,
        [],
        [tiles, own, ahead, behind, targets, node_total],
        [
            shape(3, 32, 16, 128, dtype=F32),
            shape(128, 512, dtype=F32),
            shape(2, 32, 16, 128, dtype=F32),
            shape(128, 512, dtype=F32),
            shape(256, 512, dtype=F32),
        ],
        [pltpu.VMEM((128, 512), BF16)],
    )
    return (
        edge_out,
        node_out,
        node_grad,
        edge_grad,
        edge_first.reshape(3, 512, 128),
        edge_second,
        node_first.reshape(2, 512, 128),
        node_second,
    )


def solution(mesh):
    cube = Mesh(mesh.devices.reshape(4, 4, 2, 4), BOTH)
    rows = P(BOTH, None)
    flat = P(BOTH)
    first, second = P(None, None, "feat"), P("feat", None)
    return jax.shard_map(
        shards,
        mesh=cube,
        in_specs=(
            rows,
            rows,
            flat,
            flat,
            flat,
            P(BOTH, None, None),
            rows,
            first,
            second,
            first,
            second,
            rows,
            rows,
        ),
        out_specs=(rows, rows, rows, rows, first, second, first, second),
        check_vma=False,
    )
```

time: 245 us -> 170 us (0.69); the launches traced: 240 us -> 169 us
  starting transfers between devices: 128 us -> 34.8 us
  blocking collectives: 0 us -> 34.4 us
  Pallas kernels: 49 us -> 38.5 us
  local copies, waits for them, and re-layouts: 14.6 us -> 11.6 us
    ppermute x73 -> x3, starting transfers between devices: 119 us -> 3.09 us  [other_core(): return lax.ppermute(value, 'core', [(0, 1), (1, 0)])]
    ppermute x73 -> x3, waiting for transfers between devices: 43.9 us -> 4 us  [other_core(): return lax.ppermute(value, 'core', [(0, 1), (1, 0)])]
    all_to_all x0 -> x4, waiting for transfers between devices: none -> 37 us  [exchange(): return lax.all_to_all(value, axes, 0, 0, tiled=True)]
    all_to_all x0 -> x1, blocking collectives: none -> 34.4 us  [exchange(): return lax.all_to_all(value, axes, 0, 0, tiled=True)]
    all_to_all x0 -> x4, starting transfers between devices: none -> 26 us  [exchange(): return lax.all_to_all(value, axes, 0, 0, tiled=True)]
    pallas_call x5 -> x1, Pallas kernels: 13.3 us -> 2.93 us  [plain_call(): pl.pallas_call(kernel, in_specs=[SMEM] * len(scalars) + [WHOLE] * len(ope...]
    broadcast_in_dim x0 -> x4, local copies, waits for them, and re-layouts: none -> 4.31 us  [repeated(): return jnp.broadcast_to(value[None], (count,) + value.shape)]
    unnamed x156 -> x34, local copies, waits for them, and re-layouts: 5.9 us -> 1.65 us
  transfers between devices with their start and end apart: 77 -> 11, of which waited for: 24 -> 7; matrix products, arithmetic and copies ran while one was open for 4% -> 4% of each run, Pallas kernels for 7% -> 9%
where the time goes in v2:
time: 170 us; the launch traced here: 169 us
  waiting for transfers between devices  44.7 us (26%)
  Pallas kernels  38.5 us (23%)
  starting transfers between devices  34.8 us (20%)
  blocking collectives  34.4 us (20%)
  local copies, waits for them, and re-layouts  11.6 us (7%)
  other arithmetic  3.4 us (2%)
    all_to_all x4, waiting for transfers between devices, exchange(): return lax.all_to_all(value, axes, 0, 0, tiled=True)  37 us
    all_to_all x1, blocking collectives, exchange(): return lax.all_to_all(value, axes, 0, 0, tiled=True)  34.4 us
    all_to_all x4, starting transfers between devices, exchange(): return lax.all_to_all(value, axes, 0, 0, tiled=True)  26 us
    pallas_call x1, Pallas kernels, shards(): pl.pallas_call(backward_kernel, grid=(STEPS,), in_specs=[SMEM] + [like(v)...  21.1 us
    pallas_call x1, Pallas kernels, shards(): pl.pallas_call(forward_kernel, grid=(STEPS,), in_specs=[SMEM] + [like(v)...  14.5 us
    ppermute x4, starting transfers between devices, shifted(): lax.ppermute(value, BOTH, [(k, (k + steps) % 128) for k in range(128)])  5.65 us
    broadcast_in_dim x4, local copies, waits for them, and re-layouts, repeated(): return jnp.broadcast_to(value[None], (count,) + value.shape)  4.31 us
    ppermute x3, waiting for transfers between devices, other_core(): return lax.ppermute(value, 'core', [(0, 1), (1, 0)])  4 us
  transfers between devices with their start and end apart: 11, of which 7 were waited for; matrix products, arithmetic and copies ran while one was open for 4% of the time, Pallas kernels for 9%

profile of v2, /device:TPU:1, one launch (start us, length us, event | category | flops | bytes accessed | tf_op | source)
XLA Modules:
  0.0 169.0 jit_solution(17198721098020623530)
XLA Ops:
  0.6 0.0 copy-start
  0.7 0.9 constant_dynamic-slice_fusion
  1.6 0.1 copy-done
  1.7 0.0 copy-start.6
  1.8 1.1 broadcast_in_dim.11
  2.9 5.0 %all-to-all-start.1 = ((bf16[4,1024,128]{2,1,0:T(8,128)(2,1)}), bf16[4,1024,128]{2,1,0:T(8,128)(2,1)S(1)}, u32[]{:S(2)}, u32[]{:S(2)}) async-start(bf16[4,1024,128]{2,1,0:T(8,128)(2,1)} %broadcast_in_dim.11), calls=%async_computation.1 | async-start | bytes 2097152 | tf_op jit(solution)/shard_map/all_to_all | solution.py:28
  8.0 0.0 copy-start.11
  8.0 14.1 %all-to-all-done.1.near = bf16[4,1024,128]{2,1,0:T(8,128)(2,1)S(1)} async-done(((bf16[4,1024,128]{2,1,0:T(8,128)(2,1)}), bf16[4,1024,128]{2,1,0:T(8,128)(2,1)S(1)}, u32[]{:S(2)}, u32[]{:S(2)}) %all-to-all-start.1) | async-done | bytes 1048608 | tf_op jit(solution)/shard_map/all_to_all | solution.py:28
  22.1 1.1 broadcast_in_dim.12
  23.2 3.6 %all-to-all-start.2 = ((bf16[4,768,128]{2,1,0:T(8,128)(2,1)}), bf16[4,768,128]{2,1,0:T(8,128)(2,1)S(1)}, u32[]{:S(2)}, u32[]{:S(2)}) async-start(bf16[4,768,128]{2,1,0:T(8,128)(2,1)} %broadcast_in_dim.12), calls=%async_computation.2 | async-start | bytes 1572864 | tf_op jit(solution)/shard_map/all_to_all | solution.py:28
  26.8 1.9 %collective-permute-start.2 = (bf16[4,1024,128]{2,1,0:T(8,128)(2,1)S(1)}, bf16[4,1024,128]{2,1,0:T(8,128)(2,1)}, u32[]{:S(2)}, u32[]{:S(2)}) collective-permute-start(bf16[4,1024,128]{2,1,0:T(8,128)(2,1)S(1)} %all-to-all-done.1.near), channel_id=1, source_target_pairs={{0,4},{4,0},{1,5},{5,1},{2,6},{6,2},{3,7},{7,3},{8,12},{12,8},{9,1... | collective-permute-start | bytes 3145736 | tf_op jit(solution)/shard_map/ppermute | solution.py:20
  28.8 0.6 gather_fusion.2
  29.3 7.6 %all-to-all-done.2.near = bf16[4,768,128]{2,1,0:T(8,128)(2,1)S(1)} async-done(((bf16[4,768,128]{2,1,0:T(8,128)(2,1)}), bf16[4,768,128]{2,1,0:T(8,128)(2,1)S(1)}, u32[]{:S(2)}, u32[]{:S(2)}) %all-to-all-start.2) | async-done | bytes 786464 | tf_op jit(solution)/shard_map/all_to_all | solution.py:28
  36.9 1.0 broadcast_in_dim.10
  38.0 11.0 %all-to-all-start = ((bf16[128,4,512]{2,1,0:T(4,128)(2,1)}), bf16[128,4,512]{2,1,0:T(4,128)(2,1)S(1)}, u32[]{:S(2)}, u32[]{:S(2)}) async-start(bf16[128,4,512]{2,1,0:T(4,128)(2,1)} %broadcast_in_dim.10), calls=%async_computation | async-start | bytes 1048576 | tf_op jit(solution)/shard_map/all_to_all | solution.py:28
  49.1 0.6 gather_fusion
  49.7 1.5 collective-permute-start
  51.2 0.6 collective-permute-start.3
  51.8 0.6 gather_fusion.1
  52.4 2.6 %collective-permute-start.1 = (bf16[32,512]{1,0:T(8,128)(2,1)S(1)}, bf16[32,512]{1,0:T(8,128)(2,1)S(1)}, u32[]{:S(2)}, u32[]{:S(2)}) collective-permute-start(bf16[32,512]{1,0:T(8,128)(2,1)S(1)} %gather_fusion.1), channel_id=1, source_target_pairs={{0,127},{1,0},{2,1},{3,2},{4,3},{5,4},{6,5},{7,6},{8,7},{9,8},{10,... | collective-permute-start | bytes 98312 | tf_op jit(solution)/shard_map/ppermute | solution.py:24
  55.7 0.6 reshape.159.dst_wide.refs_5_
  56.4 0.6 reshape.163.refs_4_
  57.0 0.6 stack.10.co
  57.5 5.4 %all-to-all-done = bf16[128,4,512]{2,1,0:T(4,128)(2,1)S(1)} async-done(((bf16[128,4,512]{2,1,0:T(4,128)(2,1)}), bf16[128,4,512]{2,1,0:T(4,128)(2,1)S(1)}, u32[]{:S(2)}, u32[]{:S(2)}) %all-to-all-start) | async-done | bytes 524320 | tf_op jit(solution)/shard_map/all_to_all | solution.py:28
  62.9 0.9 reshape.153.coarse
  63.8 0.0 collective-permute-done.prev
  63.8 0.0 collective-permute-done.1.after
  63.8 0.0 copy-start.16
  63.9 0.6 copy-done.15
  64.4 0.0 copy-done.16
  64.5 14.5 %shard_map.188 = (bf16[2048,512]{1,0:T(8,128)(2,1)}, bf16[256,512]{1,0:T(8,128)(2,1)}, bf16[2048,512]{1,0:T(8,128)(2,1)}, bf16[2048,512]{1,0:T(8,128)(2,1)}, bf1...) custom-call(s32[5]{0:T(128)} %stack.10.co, ...), custom_call_target="tpu_custom_call" | custom-call | flops 7000000000 | bytes 18000000 | tf_op jit(solution)/shard_map/pallas_call | solution.py:329
  79.0 21.1 %shard_map.189 = (bf16[256,512]{1,0:T(8,128)(2,1)}, f32[256,512]{1,0:T(8,128)}, bf16[2048,512]{1,0:T(8,128)(2,1)}, bf16[32,512]{1,0:T(8,128)(2,1)}, bf16[32,512]...) custom-call(s32[5]{0:T(128)} %stack.10.co, bf16[256,512]{1,0:T(8,128)(2,1)} %node.3, ...), custom_call_target="tpu_custom_call" | custom-call | flops 8999999488 | bytes 24000000 | tf_op jit(solution)/shard_map/pallas_call | solution.py:357
  100.1 0.5 collective-permute-start.4
  100.6 4.0 %collective-permute-done.4 = bf16[8,2,4,128,128]{4,3,2,1,0:T(8,128)(2,1)S(1)} collective-permute-done((bf16[8,2,4,128,128]{4,3,2,1,0:T(8,128)(2,1)}, bf16[8,2,4,128,128]{4,3,2,1,0:T(8,128)(2,1)S(1)}, u32[]{:S(2)}, u32[]{:S(2)}) %collective-permute-start.4) | collective-permute-done | bytes 2097184 | tf_op jit(solution)/shard_map/ppermute | solution.py:20
  104.6 2.4 %add_convert_fusion = bf16[8,2,4,128,128]{4,3,2,1,0:T(8,128)(2,1)S(1)} fusion(bf16[8,2,4,128,128]{4,3,2,1,0:T(8,128)(2,1)S(1)} %collective-permute-done.4, bf16[8,2,4,128,128]{4,3,2,1,0:T(8,128)(2,1)} %get-tuple-element.39), kind=kLoop, calls=%fused_computation.3 | loop fusion | flops 4194304 | bytes 6291456 | tf_op jit(solution)/shard_map/convert_element_type | solution.py:393
  107.0 34.4 %all_to_all.25 = bf16[64,128,128]{2,1,0:T(8,128)(2,1)S(1)} all-to-all(bf16[64,128,128]{2,1,0:T(8,128)(2,1)S(1)} %bitcast.31), channel_id=1, replica_groups=mesh['z'=4,'x'=4,'core'=2,'feat'=4] {'z','x','feat'}, dimensions={0} | all-to-all | bytes 4194304 | tf_op jit(solution)/shard_map/all_to_all | solution.py:28
  141.5 0.3 reduce_sum.12.own
  141.8 1.1 broadcast_in_dim.13
  142.8 6.3 %all-to-all-start.4 = ((bf16[32,112,128]{2,1,0:T(8,128)(2,1)}), bf16[32,112,128]{2,1,0:T(8,128)(2,1)S(1)}, u32[]{:S(2)}, u32[]{:S(2)}) async-start(bf16[32,112,128]{2,1,0:T(8,128)(2,1)} %broadcast_in_dim.13), calls=%async_computation.4 | async-start | bytes 1835008 | tf_op jit(solution)/shard_map/all_to_all | solution.py:28
  149.2 0.1 tile.12
  149.3 1.0 collective-permute-start.5
  150.3 0.6 collective-permute-start.6
  150.8 0.6 add_bitcast_fusion.targets
  151.5 0.8 collective-permute-done.5.ahead
  152.2 2.9 %collective-permute-done.6.behind = bf16[32,512]{1,0:T(8,128)(2,1)S(1)} collective-permute-done((bf16[32,512]{1,0:T(8,128)(2,1)S(1)}, bf16[32,512]{1,0:T(8,128)(2,1)S(1)}, u32[]{:S(2)}, u32[]{:S(2)}) %collective-permute-start.6) | collective-permute-done | bytes 32800 | tf_op jit(solution)/shard_map/ppermute | solution.py:24
  155.1 10.0 %all-to-all-done.4.tiles = bf16[32,112,128]{2,1,0:T(8,128)(2,1)S(1)} async-done(((bf16[32,112,128]{2,1,0:T(8,128)(2,1)}), bf16[32,112,128]{2,1,0:T(8,128)(2,1)S(1)}, u32[]{:S(2)}, u32[]{:S(2)}) %all-to-all-start.4) | async-done | bytes 917536 | tf_op jit(solution)/shard_map/all_to_all | solution.py:28
  165.2 0.9 copy-done.1
  166.1 2.9 %shard_map.190 = (f32[3,32,16,128]{3,2,1,0:T(8,128)}, f32[128,512]{1,0:T(8,128)}, f32[2,32,16,128]{3,2,1,0:T(8,128)}, f32[128,512]{1,0:T(8,128)}, f32[256,512]{1,0:T(8,128)}) custom-call(bf16[32,112,128]{2,1,0:T(8,128)(2,1)} %copy-done.1, bf16[128,128]{1,0:T(8,128)(2,1)} %copy-done.5, bf16[32,512]{1,0:T(8,128)(2,1)} %copy-done.7, bf16[32,512]{1,0:T(8,128)(2,1)} %copy-done.8, ...), custom_call_target="tpu_custom_call" | custom-call | tf_op jit(solution)/shard_map/pallas_call | solution.py:264
  (45 shorter events, 0.2 us)
Async XLA Ops:
  0.6 1.1 copy-start
  1.7 6.2 %copy-start.6 = (bf16[2,512,128]{2,1,0:T(8,128)(2,1)S(1)}, bf16[2,512,128]{2,1,0:T(8,128)(2,1)}, u32[]{:S(2)}) copy-start(bf16[2,512,128]{2,1,0:T(8,128)(2,1)} %param.22) | copy-start | bytes 786436
  2.9 19.2 %all-to-all-start.1 = ((bf16[4,1024,128]{2,1,0:T(8,128)(2,1)}), bf16[4,1024,128]{2,1,0:T(8,128)(2,1)S(1)}, u32[]{:S(2)}, u32[]{:S(2)}) async-start(bf16[4,1024,128]{2,1,0:T(8,128)(2,1)} %broadcast_in_dim.11), calls=%async_computation.1 | async-start | bytes 2097152 | tf_op jit(solution)/shard_map/all_to_all | solution.py:28
  7.9 20.9 %copy-start.12 = (s32[1,4]{1,0:T(1,128)S(1)}, s32[1,4]{1,0:T(1,128)}, u32[]{:S(2)}) copy-start(s32[1,4]{1,0:T(1,128)} %param.19) | copy-start | bytes 52
  7.9 20.9 %copy-start.2 = (bf16[256,512]{1,0:T(8,128)(2,1)S(1)}, bf16[256,512]{1,0:T(8,128)(2,1)}, u32[]{:S(2)}) copy-start(bf16[256,512]{1,0:T(8,128)(2,1)} %node.3) | copy-start | bytes 786436
  8.0 41.0 %copy-start.11 = (s32[1,2,32]{2,1,0:T(2,128)S(1)}, s32[1,2,32]{2,1,0:T(2,128)}, u32[]{:S(2)}) copy-start(s32[1,2,32]{2,1,0:T(2,128)} %param.18) | copy-start | bytes 772
  22.1 27.6 %copy-start.3 = (bf16[4,1024,128]{2,1,0:T(8,128)(2,1)}, bf16[4,1024,128]{2,1,0:T(8,128)(2,1)S(1)}, u32[]{:S(2)}) copy-start(bf16[4,1024,128]{2,1,0:T(8,128)(2,1)S(1)} %all-to-all-done.1.near) | copy-start | bytes 3145732
  23.2 32.6 %copy-start.10 = (s32[2048]{0:T(1024)S(1)}, s32[2048]{0:T(1024)}, u32[]{:S(2)}) copy-start(s32[2048]{0:T(1024)} %param.16) | copy-start | bytes 24580
  23.2 33.2 %copy-start.9 = (s32[2048]{0:T(1024)S(1)}, s32[2048]{0:T(1024)}, u32[]{:S(2)}) copy-start(s32[2048]{0:T(1024)} %param.15) | copy-start | bytes 24580
  23.2 13.8 %all-to-all-start.2 = ((bf16[4,768,128]{2,1,0:T(8,128)(2,1)}), bf16[4,768,128]{2,1,0:T(8,128)(2,1)S(1)}, u32[]{:S(2)}, u32[]{:S(2)}) async-start(bf16[4,768,128]{2,1,0:T(8,128)(2,1)} %broadcast_in_dim.12), calls=%async_computation.2 | async-start | bytes 1572864 | tf_op jit(solution)/shard_map/all_to_all | solution.py:28
  26.8 37.1 %collective-permute-start.2 = (bf16[4,1024,128]{2,1,0:T(8,128)(2,1)S(1)}, bf16[4,1024,128]{2,1,0:T(8,128)(2,1)}, u32[]{:S(2)}, u32[]{:S(2)}) collective-permute-start(bf16[4,1024,128]{2,1,0:T(8,128)(2,1)S(1)} %all-to-all-done.1.near), channel_id=1, source_target_pairs={{0,4},{4,0},{1,5},{5,1},{2,6},{6,2},{3,7},{7,3},{8,12},{12,8},{9,1... | collective-permute-start | bytes 3145736 | tf_op jit(solution)/shard_map/ppermute | solution.py:20
  36.9 42.0 %copy-start.4 = (bf16[4,768,128]{2,1,0:T(8,128)(2,1)}, bf16[4,768,128]{2,1,0:T(8,128)(2,1)S(1)}, u32[]{:S(2)}) copy-start(bf16[4,768,128]{2,1,0:T(8,128)(2,1)S(1)} %all-to-all-done.2.near) | copy-start | bytes 2359300
  38.0 24.9 %all-to-all-start = ((bf16[128,4,512]{2,1,0:T(4,128)(2,1)}), bf16[128,4,512]{2,1,0:T(4,128)(2,1)S(1)}, u32[]{:S(2)}, u32[]{:S(2)}) async-start(bf16[128,4,512]{2,1,0:T(4,128)(2,1)} %broadcast_in_dim.10), calls=%async_computation | async-start | bytes 1048576 | tf_op jit(solution)/shard_map/all_to_all | solution.py:28
  49.7 14.1 %collective-permute-start = (bf16[32,512]{1,0:T(8,128)(2,1)S(1)}, bf16[32,512]{1,0:T(8,128)(2,1)S(1)}, u32[]{:S(2)}, u32[]{:S(2)}) collective-permute-start(bf16[32,512]{1,0:T(8,128)(2,1)S(1)} %gather_fusion), channel_id=1, source_target_pairs={{0,1},{1,2},{2,3},{3,4},{4,5},{5,6},{6,7},{7,8},{8,9},{9,10},{10,1... | collective-permute-start | bytes 98312 | tf_op jit(solution)/shard_map/ppermute | solution.py:24
  51.2 27.8 %collective-permute-start.3 = (bf16[4,768,128]{2,1,0:T(8,128)(2,1)S(1)}, bf16[4,768,128]{2,1,0:T(8,128)(2,1)}, u32[]{:S(2)}, u32[]{:S(2)}) collective-permute-start(bf16[4,768,128]{2,1,0:T(8,128)(2,1)S(1)} %all-to-all-done.2.near), channel_id=1, source_target_pairs={{0,4},{4,0},{1,5},{5,1},{2,6},{6,2},{3,7},{7,3},{8,12},{12,8},{9,1... | collective-permute-start | bytes 2359304 | tf_op jit(solution)/shard_map/ppermute | solution.py:20
  52.4 11.4 %collective-permute-start.1 = (bf16[32,512]{1,0:T(8,128)(2,1)S(1)}, bf16[32,512]{1,0:T(8,128)(2,1)S(1)}, u32[]{:S(2)}, u32[]{:S(2)}) collective-permute-start(bf16[32,512]{1,0:T(8,128)(2,1)S(1)} %gather_fusion.1), channel_id=1, source_target_pairs={{0,127},{1,0},{2,1},{3,2},{4,3},{5,4},{6,5},{7,6},{8,7},{9,8},{10,... | collective-permute-start | bytes 98312 | tf_op jit(solution)/shard_map/ppermute | solution.py:24
  63.8 0.6 copy-start.15
  63.8 0.6 copy-start.16
  100.1 4.5 %collective-permute-start.4 = (bf16[8,2,4,128,128]{4,3,2,1,0:T(8,128)(2,1)}, bf16[8,2,4,128,128]{4,3,2,1,0:T(8,128)(2,1)S(1)}, u32[]{:S(2)}, u32[]{:S(2)}) collective-permute-start(bf16[8,2,4,128,128]{4,3,2,1,0:T(8,128)(2,1)} %get-tuple-element.40), channel_id=1, source_target_pairs={{0,4},{4,0},{1,5},{5,1},{2,6},{6,2},{3,7},{7,3},{8,12},{12,8},{9,1... | collective-permute-start | bytes 6291464 | tf_op jit(solution)/shard_map/ppermute | solution.py:20
  141.5 7.8 %copy-start.14 = (bf16[32,512]{1,0:T(8,128)(2,1)S(1)}, bf16[32,512]{1,0:T(8,128)(2,1)}, u32[]{:S(2)}) copy-start(bf16[32,512]{1,0:T(8,128)(2,1)} %get-tuple-element.41) | copy-start | bytes 98308
  141.5 8.8 %copy-start.13 = (bf16[32,512]{1,0:T(8,128)(2,1)S(1)}, bf16[32,512]{1,0:T(8,128)(2,1)}, u32[]{:S(2)}) copy-start(bf16[32,512]{1,0:T(8,128)(2,1)} %get-tuple-element.42) | copy-start | bytes 98308
  141.8 23.4 %copy-start.5 = (bf16[128,128]{1,0:T(8,128)(2,1)}, bf16[128,128]{1,0:T(8,128)(2,1)S(1)}, u32[]{:S(2)}) copy-start(bf16[128,128]{1,0:T(8,128)(2,1)S(1)} %reduce_sum.12.own) | copy-start | bytes 98308
  142.8 22.3 %all-to-all-start.4 = ((bf16[32,112,128]{2,1,0:T(8,128)(2,1)}), bf16[32,112,128]{2,1,0:T(8,128)(2,1)S(1)}, u32[]{:S(2)}, u32[]{:S(2)}) async-start(bf16[32,112,128]{2,1,0:T(8,128)(2,1)} %broadcast_in_dim.13), calls=%async_computation.4 | async-start | bytes 1835008 | tf_op jit(solution)/shard_map/all_to_all | solution.py:28
  149.3 2.9 %collective-permute-start.5 = (bf16[32,512]{1,0:T(8,128)(2,1)S(1)}, bf16[32,512]{1,0:T(8,128)(2,1)S(1)}, u32[]{:S(2)}, u32[]{:S(2)}) collective-permute-start(bf16[32,512]{1,0:T(8,128)(2,1)S(1)} %copy-done.14), channel_id=1, source_target_pairs={{0,127},{1,0},{2,1},{3,2},{4,3},{5,4},{6,5},{7,6},{8,7},{9,8},{10,... | collective-permute-start | bytes 98312 | tf_op jit(solution)/shard_map/ppermute | solution.py:24
  150.3 4.8 %collective-permute-start.6 = (bf16[32,512]{1,0:T(8,128)(2,1)S(1)}, bf16[32,512]{1,0:T(8,128)(2,1)S(1)}, u32[]{:S(2)}, u32[]{:S(2)}) collective-permute-start(bf16[32,512]{1,0:T(8,128)(2,1)S(1)} %copy-done.13), channel_id=1, source_target_pairs={{0,1},{1,2},{2,3},{3,4},{4,5},{5,6},{6,7},{7,8},{8,9},{9,10},{10,1... | collective-permute-start | bytes 98312 | tf_op jit(solution)/shard_map/ppermute | solution.py:24
  152.2 12.9 %copy-start.7 = (bf16[32,512]{1,0:T(8,128)(2,1)}, bf16[32,512]{1,0:T(8,128)(2,1)S(1)}, u32[]{:S(2)}) copy-start(bf16[32,512]{1,0:T(8,128)(2,1)S(1)} %collective-permute-done.5.ahead) | copy-start | bytes 98308
  155.1 10.0 %copy-start.8 = (bf16[32,512]{1,0:T(8,128)(2,1)}, bf16[32,512]{1,0:T(8,128)(2,1)S(1)}, u32[]{:S(2)}) copy-start(bf16[32,512]{1,0:T(8,128)(2,1)S(1)} %collective-permute-done.6.behind) | copy-start | bytes 98308
  165.2 0.9 copy-start.1

commit v3 on v2

--- a/solution.py
+++ b/solution.py
@@ -26,6 +26,10 @@
 
 def exchange(value, axes):
     return lax.all_to_all(value, axes, 0, 0, tiled=True)
+
+
+def after(value, *earlier):
+    return lax.optimization_barrier((value, *earlier))[0]
 
 
 def repeated(value, count):
@@ -88,21 +92,46 @@
                 second[rows, b * 128 : (b + 1) * 128] = part[y, start : start + 64, :]
 
 
-def forward_kernel(co, node, prev, after, coarse, near, far, src, dst, dst_wide, edge, *refs):
+def whole(first, m):
+    return first[m].reshape(512, 512)
+
+
+def place_tiles(own_core, near, far, lookup, first, second, coarse):
+    for part, core in ((near, own_core), (far, 1 - own_core)):
+        for y in range(4):
+            block = slice(y * 128, (y + 1) * 128)
+            for m in range(3):
+                value = part[:, y, m * 16 : (m + 1) * 16, :].reshape(16, 1, 16, 128)
+                first[m, :, pl.ds(core, 1), :, block] = value
+            for k in range(16):
+                rows = slice(y * 128 + k // 2 * 16, y * 128 + k // 2 * 16 + 16)
+                columns = pl.ds(pl.multiple_of((k % 2 * 2 + core) * 128, 128), 128)
+                second[rows, columns] = part[k, y, 48:64, :]
+            coarse[:, pl.ds(core, 1), y] = part[:, y, 64:80, :].reshape(16, 1, 16, 128)
+    low = lax.broadcasted_iota(jnp.int32, (64, 8, 128), 1) < 4
+    pairs = coarse[...].reshape(64, 2, 16, 128).astype(F32)
+    for half in range(2):
+        even, odd = pairs[:, 0, half * 8 : half * 8 + 8], pairs[:, 1, half * 8 : half * 8 + 8]
+        first_block = jnp.where(low, even, pltpu.roll(odd, 4, 1)).reshape(512, 128)
+        other_block = jnp.where(low, pltpu.roll(even, 4, 1), odd).reshape(512, 128)
+        lookup[320:832, half * 256 : half * 256 + 128] = first_block.astype(BF16)
+        lookup[320:832, half * 256 + 128 : half * 256 + 256] = other_block.astype(BF16)
+
+
+def forward_kernel(co, node, prev, following, near, far, src, dst, dst_wide, edge, *refs):
     edge_out, incoming, act_out, normed_out, slope_out, factor_out, lookup, first, second = refs[:9]
-    table, total = refs[9:]
+    table, total, coarse = refs[9:]
     step = pl.program_id(0)
 
     @pl.when(step == 0)
     def _():
         lookup[0:256, :] = node[...]
         lookup[256:288, :] = prev[...]
-        lookup[288:320, :] = after[...]
+        lookup[288:320, :] = following[...]
         lookup[832:896, :] = jnp.zeros((64, 512), BF16)
-        lookup[320:832, :] = coarse[...]
-        place_weights(co[2], near, far, first, second)
-        table[0:TABLE, :] = dot(lookup[...], first[1]).astype(BF16)
-        table[TABLE:, :] = dot(node[...], first[2]).astype(BF16)
+        place_tiles(co[2], near, far, lookup, first, second, coarse)
+        table[0:TABLE, :] = dot(lookup[...], whole(first, 1)).astype(BF16)
+        table[TABLE:, :] = dot(node[...], whole(first, 2)).astype(BF16)
         total[...] = jnp.zeros_like(total)
 
     hots = []
@@ -112,7 +141,7 @@
         hots.append(jnp.concatenate(tiles, axis=1))
     hot = jnp.concatenate(hots, axis=0)
     rows = edge[...]
-    pre = dot(rows, first[0]) + dot(hot, table[...])
+    pre = dot(rows, whole(first, 0)) + dot(hot, table[...])
     act, slope = swish(pre)
     act = act.astype(BF16)
     act_out[...] = act
@@ -203,7 +232,7 @@
     total = grad_edge[...].astype(F32) + live * dot(jnp.concatenate(hots, axis=0), spread[...])
     delta = normalize_back(live * total, normed[...].astype(F32), factor[:, 0:1]).astype(BF16)
     pre_grad = (dot_nt(delta, edge_second[...]) * slope[...].astype(F32)).astype(BF16)
-    edge_grad[...] = (total + dot_nt(pre_grad, edge_first[0])).astype(BF16)
+    edge_grad[...] = (total + dot_nt(pre_grad, whole(edge_first, 0))).astype(BF16)
     sum_second[...] += dot_tn(act[...], delta)
     sum_first[...] += dot_tn(edge[...], pre_grad)
     place = lax.broadcasted_iota(jnp.int32, (128, CHUNK), 0)
@@ -221,25 +250,27 @@
         received = sums[TABLE:, :].astype(BF16)
         put_columns(co, dot_tn(lookup[...], sent), 1, columns, keep, give)
         put_columns(co, dot_tn(node[...], received), 2, columns, keep, give)
-        back = dot_nt(sent, edge_first[1])
-        node_total[...] += back[0:256] + dot_nt(received, edge_first[2])
+        back = dot_nt(sent, whole(edge_first, 1))
+        node_total[...] += back[0:256] + dot_nt(received, whole(edge_first, 2))
         to_prev[...] = back[256:288].astype(BF16)
         to_next[...] = back[288:320].astype(BF16)
         put_owned(co, back[320:832], owned, keep, give)
 
 
-def final_kernel(tiles, own, ahead, behind, targets, node_total, *refs):
+def final_kernel(co, tiles, far, own, ahead, behind, targets, node_total, *refs):
     edge_first, edge_second, node_first, node_second, node_grad, rows = refs
-    for m in range(5):
-        value = tiles[:, m * 16 : (m + 1) * 16, :].astype(F32)
-        if m < 3:
-            edge_first[m] = value
-        else:
-            node_first[m - 3] = value
-    for p in range(32):
-        r, b = p // 4 * 16, p % 4 * 128
-        edge_second[r : r + 16, b : b + 128] = tiles[p, 80:96, :].astype(F32)
-        node_second[r : r + 16, b : b + 128] = tiles[p, 96:112, :].astype(F32)
+    for part, core in ((tiles, co[2]), (far, 1 - co[2])):
+        for m in range(3):
+            value = part[:, m * 16 : (m + 1) * 16, :].astype(F32)
+            edge_first[m, :, pl.ds(core, 1)] = value.reshape(16, 1, 16, 128)
+        for m in range(2):
+            value = part[:, 48 + m * 16 : 64 + m * 16, :].astype(F32)
+            node_first[m, :, pl.ds(core, 1)] = value.reshape(16, 1, 16, 128)
+        for k in range(16):
+            r = k // 2 * 16
+            b = pl.ds(pl.multiple_of((k % 2 * 2 + core) * 128, 128), 128)
+            edge_second[r : r + 16, b] = part[k, 80:96, :].astype(F32)
+            node_second[r : r + 16, b] = part[k, 96:112, :].astype(F32)
     rows[0:32, :] = ahead[...]
     rows[32:64, :] = behind[...]
     group = lax.broadcasted_iota(jnp.int32, (16, 128), 0) // 4
@@ -307,22 +338,27 @@
     grad_edge,
 ):
     core = lax.axis_index("core")
+    patch = (lax.axis_index("z") * 4 + lax.axis_index("x")) * 2 + core
     co = jnp.stack([core, core, core, core, edge_count[0]]).astype(jnp.int32)
     lists, owned = halo_send[0], coarse_of[0]
     unused = jnp.full((48,), -1, jnp.int32)
     targets = jnp.concatenate([lists[1], lists[0], jnp.tile(owned, 4), unused]).reshape(1, 128)
 
-    edge_near = exchange(repeated(halves(edge_w1, edge_w2, core), 4), "feat")
+    first_part = lax.dynamic_slice_in_dim(edge_w1, patch * 16, 16, 1).reshape(48, 128)
+    second_part = lax.dynamic_slice(edge_w2, (patch // 4 * 16, patch % 4 * 128), (16, 128))
+    coarse_own = node_lat[owned].reshape(4, 4, 128).transpose(1, 0, 2).reshape(16, 128)
+    tile = jnp.concatenate([first_part, second_part, coarse_own], axis=0)
     from_prev = shifted(node_lat[lists[1]], 1)
     from_next = shifted(node_lat[lists[0]], -1)
-    edge_far = other_core(edge_near)
-    coarse = exchange(repeated(node_lat[owned], 128), BOTH).reshape(512, 512)
-    node_near = exchange(repeated(halves(node_w1, node_w2, core), 4), "feat")
-    node_far = other_core(node_near)
+    near = exchange(repeated(tile, 64), ("z", "x", "feat")).reshape(16, 4, 80, 128)
+    near = after(near, from_prev, from_next)
+    far = other_core(near)
+    node_half = after(repeated(halves(node_w1, node_w2, core), 4), near, far)
+    node_near = exchange(node_half, "feat")
 
     src, dst = edge_src.reshape(16, 128), edge_dst.reshape(16, 128)
     src_wide, dst_wide = edge_src.reshape(STEPS, CHUNK), edge_dst.reshape(STEPS, CHUNK)
-    fixed = [node_lat, from_prev, from_next, coarse, edge_near, edge_far]
+    fixed = [node_lat, from_prev, from_next, near, far]
     fixed += [src, dst, dst_wide]
     wide = chunk(CHUNK, 512)
     params = pltpu.CompilerParams(vmem_limit_bytes=VMEM_BYTES, dimension_semantics=("arbitrary",))
@@ -331,7 +367,7 @@
         grid=(STEPS,),
         in_specs=[SMEM] + [like(v) for v in fixed] + [wide],
         out_specs=[wide, same(256, 512), wide, wide, wide, chunk(CHUNK, 128)]
-        + [same(TABLE, 512), same(3, 512, 512), same(512, 512)],
+        + [same(TABLE, 512), same(3, 16, 2, 16, 512), same(512, 512)],
         out_shape=[
             shape(2048, 512),
             shape(256, 512),
@@ -340,16 +376,22 @@
             shape(2048, 512),
             shape(2048, 128, dtype=F32),
             shape(TABLE, 512),
-            shape(3, 512, 512),
+            shape(3, 16, 2, 16, 512),
             shape(512, 512),
         ],
-        scratch_shapes=[pltpu.VMEM((TABLE + 256, 512), BF16), pltpu.VMEM((256, 512), F32)],
+        scratch_shapes=[
+            pltpu.VMEM((TABLE + 256, 512), BF16),
+            pltpu.VMEM((256, 512), F32),
+            pltpu.VMEM((16, 2, 4, 16, 128), BF16),
+        ],
         compiler_params=params,
         cost_estimate=pl.CostEstimate(
             flops=7_000_000_000, bytes_accessed=18_000_000, transcendentals=1_000_000
         ),
     )(co, *fixed, edge_lat)
 
+    node_near = after(node_near, incoming)
+    node_far = other_core(node_near)
     fixed = [node_lat, incoming, grad_node, node_near, node_far]
     fixed += [first, second, lookup, dst, src_wide, dst_wide]
     moving = [edge_lat, act, normed, slope, factor, grad_edge]
@@ -388,19 +430,21 @@
         ),
     )(co, *fixed, *moving)
 
-    ahead = shifted(to_prev, -1)
-    behind = shifted(to_next, 1)
     pair = (keep.astype(F32) + other_core(give).astype(F32)).astype(BF16).reshape(64, 128, 128)
+    ahead = shifted(after(to_prev, pair), -1)
+    behind = shifted(after(to_next, pair), 1)
     own = jnp.sum(exchange(pair, ("z", "x", "feat")).astype(F32), axis=0).astype(BF16)
-    tiles = exchange(repeated(own[:112], 32), ("z", "x", "core"))
+    own = after(own, ahead, behind)
+    tiles = exchange(repeated(own[:112], 16), ("z", "x"))
+    far_tiles = other_core(tiles)
     edge_first, edge_second, node_first, node_second, node_grad = plain_call(
         final_kernel,
-        [],
-        [tiles, own, ahead, behind, targets, node_total],
+        [co],
+        [tiles, far_tiles, own, ahead, behind, targets, node_total],
         [
-            shape(3, 32, 16, 128, dtype=F32),
+            shape(3, 16, 2, 16, 128, dtype=F32),
             shape(128, 512, dtype=F32),
-            shape(2, 32, 16, 128, dtype=F32),
+            shape(2, 16, 2, 16, 128, dtype=F32),
             shape(128, 512, dtype=F32),
             shape(256, 512, dtype=F32),
         ],

time: 170 us -> 152 us (0.89)
  blocking collectives: 34.4 us -> 13.8 us
  local copies, waits for them, and re-layouts: 11.6 us -> 9.49 us
  other arithmetic: 3.4 us -> 5.46 us
  waiting for transfers between devices: 44.7 us -> 46.7 us
    all_to_all x1, blocking collectives: 34.4 us -> 13.8 us  [exchange(): return lax.all_to_all(value, axes, 0, 0, tiled=True)]
    ppermute x3 -> x4, starting transfers between devices: 3.09 us -> 6.58 us  [other_core(): return lax.ppermute(value, 'core', [(0, 1), (1, 0)])]
    all_to_all x4 -> x3, starting transfers between devices: 26 us -> 22.9 us  [exchange(): return lax.all_to_all(value, axes, 0, 0, tiled=True)]
    all_to_all x4 -> x3, waiting for transfers between devices: 37 us -> 34 us  [exchange(): return lax.all_to_all(value, axes, 0, 0, tiled=True)]
    ppermute x3 -> x4, waiting for transfers between devices: 4 us -> 6.86 us  [other_core(): return lax.ppermute(value, 'core', [(0, 1), (1, 0)])]
    ppermute x4, waiting for transfers between devices: 3.68 us -> 5.91 us  [shifted(): lax.ppermute(value, BOTH, [(k, (k + steps) % 128) for k in range(128)])]
    broadcast_in_dim x4 -> x3, local copies, waits for them, and re-layouts: 4.31 us -> 2.27 us  [repeated(): return jnp.broadcast_to(value[None], (count,) + value.shape)]
  transfers between devices with their start and end apart: 11 -> 11, of which waited for: 7 -> 7; matrix products, arithmetic and copies ran while one was open for 4% -> 3% of each run, Pallas kernels for 9% -> 10%
where the time goes in v3:
time: 152 us
  waiting for transfers between devices  46.7 us (31%)
  Pallas kernels  38.6 us (25%)
  starting transfers between devices  36.1 us (24%)
  blocking collectives  13.8 us (9%)
  local copies, waits for them, and re-layouts  9.49 us (6%)
  other arithmetic  5.46 us (4%)
  between operations  1.63 us (1%)
    all_to_all x3, waiting for transfers between devices, exchange(): return lax.all_to_all(value, axes, 0, 0, tiled=True)  34 us
    all_to_all x3, starting transfers between devices, exchange(): return lax.all_to_all(value, axes, 0, 0, tiled=True)  22.9 us
    pallas_call x1, Pallas kernels, shards(): pl.pallas_call(backward_kernel, grid=(STEPS,), in_specs=[SMEM] + [like(v)...  21.1 us
    pallas_call x1, Pallas kernels, shards(): pl.pallas_call(forward_kernel, grid=(STEPS,), in_specs=[SMEM] + [like(v)...  14.5 us
    all_to_all x1, blocking collectives, exchange(): return lax.all_to_all(value, axes, 0, 0, tiled=True)  13.8 us
    ppermute x4, waiting for transfers between devices, other_core(): return lax.ppermute(value, 'core', [(0, 1), (1, 0)])  6.86 us
    ppermute x4, starting transfers between devices, shifted(): lax.ppermute(value, BOTH, [(k, (k + steps) % 128) for k in range(128)])  6.63 us
    ppermute x4, starting transfers between devices, other_core(): return lax.ppermute(value, 'core', [(0, 1), (1, 0)])  6.58 us
  transfers between devices with their start and end apart: 11, of which 7 were waited for; matrix products, arithmetic and copies ran while one was open for 3% of the time, Pallas kernels for 10%

profile of v3, /device:TPU:1, one launch (start us, length us, event | category | flops | bytes accessed | tf_op | source)
XLA Modules:
  0.0 151.8 jit_solution(9009835921411577369)
XLA Ops:
  0.6 0.0 copy-start
  0.6 0.0 copy-start.3
  0.7 0.7 fusion.2
  1.4 1.6 %gather_fusion.2 = bf16[4,512]{1,0:T(4,128)(2,1)S(1)} fusion(bf16[256,512]{1,0:T(8,128)(2,1)} %node.3, s32[1024]{0:T(1024)S(1)} %pad_clamp_fusion), kind=kCustom, calls=%fused_computation.2 | custom fusion | bytes 8208 | tf_op jit(solution)/shard_map/gather | solution.py:349
  3.0 0.7 dynamic_slice.13
  3.7 1.2 broadcast_in_dim.8
  5.0 12.1 %all-to-all-start = ((bf16[64,80,128]{2,1,0:T(8,128)(2,1)}), bf16[64,80,128]{2,1,0:T(8,128)(2,1)S(1)}, u32[]{:S(2)}, u32[]{:S(2)}) async-start(bf16[64,80,128]{2,1,0:T(8,128)(2,1)} %broadcast_in_dim.8), calls=%async_computation | async-start | bytes 2621440 | tf_op jit(solution)/shard_map/all_to_all | solution.py:28
  17.1 0.6 gather_fusion
  17.7 1.1 collective-permute-start
  18.8 0.6 gather_fusion.1
  19.5 2.4 %collective-permute-start.1 = (bf16[32,512]{1,0:T(8,128)(2,1)S(1)}, bf16[32,512]{1,0:T(8,128)(2,1)S(1)}, u32[]{:S(2)}, u32[]{:S(2)}) collective-permute-start(bf16[32,512]{1,0:T(8,128)(2,1)S(1)} %gather_fusion.1), channel_id=1, source_target_pairs={{0,127},{1,0},{2,1},{3,2},{4,3},{5,4},{6,5},{7,6},{8,7},{9,8},{10,... | collective-permute-start | bytes 98312 | tf_op jit(solution)/shard_map/ppermute | solution.py:24
  21.9 5.9 %collective-permute-done.prev = bf16[32,512]{1,0:T(8,128)(2,1)S(1)} collective-permute-done((bf16[32,512]{1,0:T(8,128)(2,1)S(1)}, bf16[32,512]{1,0:T(8,128)(2,1)S(1)}, u32[]{:S(2)}, u32[]{:S(2)}) %collective-permute-start) | collective-permute-done | bytes 32800 | tf_op jit(solution)/shard_map/ppermute | solution.py:24
  27.8 0.0 collective-permute-done.1.following
  27.8 9.1 %all-to-all-done = bf16[64,80,128]{2,1,0:T(8,128)(2,1)S(1)} async-done(((bf16[64,80,128]{2,1,0:T(8,128)(2,1)}), bf16[64,80,128]{2,1,0:T(8,128)(2,1)S(1)}, u32[]{:S(2)}, u32[]{:S(2)}) %all-to-all-start) | async-done | bytes 1310752 | tf_op jit(solution)/shard_map/all_to_all | solution.py:28
  36.9 2.6 %collective-permute-start.2 = (bf16[16,4,80,128]{3,2,1,0:T(8,128)(2,1)S(1)}, bf16[16,4,80,128]{3,2,1,0:T(8,128)(2,1)}, u32[]{:S(2)}, u32[]{:S(2)}) collective-permute-start(bf16[16,4,80,128]{3,2,1,0:T(8,128)(2,1)S(1)} %bitcast.35), channel_id=1, source_target_pairs={{0,4},{4,0},{1,5},{5,1},{2,6},{6,2},{3,7},{7,3},{8,12},{12,8},{9,1... | collective-permute-start | bytes 3932168 | tf_op jit(solution)/shard_map/ppermute | solution.py:20
  40.1 0.6 reshape.158.dst_wide.refs_5_
  40.8 0.6 stack.10.co
  41.4 0.8 collective-permute-done.2.far
  42.2 1.0 broadcast_in_dim.9
  43.2 3.5 %all-to-all-start.1 = ((bf16[4,768,128]{2,1,0:T(8,128)(2,1)}), bf16[4,768,128]{2,1,0:T(8,128)(2,1)S(1)}, u32[]{:S(2)}, u32[]{:S(2)}) async-start(bf16[4,768,128]{2,1,0:T(8,128)(2,1)} %broadcast_in_dim.9), calls=%async_computation.1 | async-start | bytes 1572864 | tf_op jit(solution)/shard_map/all_to_all | solution.py:28
  46.8 0.0 copy-start.11
  46.8 14.5 %shard_map.188 = (bf16[2048,512]{1,0:T(8,128)(2,1)}, bf16[256,512]{1,0:T(8,128)(2,1)}, bf16[2048,512]{1,0:T(8,128)(2,1)}, bf16[2048,512]{1,0:T(8,128)(2,1)}, bf1...) custom-call(s32[5]{0:T(128)} %stack.10.co, ...), custom_call_target="tpu_custom_call" | custom-call | flops 7000000000 | bytes 18000000 | tf_op jit(solution)/shard_map/pallas_call | solution.py:365
  61.3 0.0 all-to-all-done.1.near
  61.3 0.0 copy-start.4
  61.3 0.6 collective-permute-start.3
  62.0 0.6 reshape.162.refs_4_
  62.6 1.3 collective-permute-done.3.far
  63.9 0.9 copy-done.15
  64.8 21.1 %shard_map.189 = (bf16[256,512]{1,0:T(8,128)(2,1)}, f32[256,512]{1,0:T(8,128)}, bf16[2048,512]{1,0:T(8,128)(2,1)}, bf16[32,512]{1,0:T(8,128)(2,1)}, bf16[32,512]...) custom-call(s32[5]{0:T(128)} %stack.10.co, bf16[256,512]{1,0:T(8,128)(2,1)} %node.3, ...), custom_call_target="tpu_custom_call" | custom-call | flops 8999999488 | bytes 24000000 | tf_op jit(solution)/shard_map/pallas_call | solution.py:399
  85.9 0.5 collective-permute-start.4
  86.4 4.0 %collective-permute-done.4 = bf16[8,2,4,128,128]{4,3,2,1,0:T(8,128)(2,1)S(1)} collective-permute-done((bf16[8,2,4,128,128]{4,3,2,1,0:T(8,128)(2,1)}, bf16[8,2,4,128,128]{4,3,2,1,0:T(8,128)(2,1)S(1)}, u32[]{:S(2)}, u32[]{:S(2)}) %collective-permute-start.4) | collective-permute-done | bytes 2097184 | tf_op jit(solution)/shard_map/ppermute | solution.py:20
  90.4 3.8 %add_convert_fusion = bf16[8,2,4,128,128]{4,3,2,1,0:T(8,128)(2,1)} fusion(bf16[8,2,4,128,128]{4,3,2,1,0:T(8,128)(2,1)S(1)} %collective-permute-done.4, bf16[8,2,4,128,128]{4,3,2,1,0:T(8,128)(2,1)} %get-tuple-element.48), kind=kLoop, calls=%fused_computation.3 | loop fusion | flops 4194304 | bytes 6291456 | tf_op jit(solution)/shard_map/convert_element_type | solution.py:433
  94.1 7.3 %all-to-all-start.2 = ((bf16[64,128,128]{2,1,0:T(8,128)(2,1)}), bf16[64,128,128]{2,1,0:T(8,128)(2,1)S(1)}, u32[]{:S(2)}, u32[]{:S(2)}) async-start(bf16[64,128,128]{2,1,0:T(8,128)(2,1)} %bitcast.17), calls=%async_computation.2 | async-start | bytes 4194304 | tf_op jit(solution)/shard_map/all_to_all | solution.py:28
  101.4 0.0 copy-start.14
  101.5 3.1 %collective-permute-start.5 = (bf16[32,512]{1,0:T(8,128)(2,1)S(1)}, bf16[32,512]{1,0:T(8,128)(2,1)S(1)}, u32[]{:S(2)}, u32[]{:S(2)}) collective-permute-start(bf16[32,512]{1,0:T(8,128)(2,1)S(1)} %copy-done.19), channel_id=1, source_target_pairs={{0,127},{1,0},{2,1},{3,2},{4,3},{5,4},{6,5},{7,6},{8,7},{9,8},{10,... | collective-permute-start | bytes 98312 | tf_op jit(solution)/shard_map/ppermute | solution.py:24
  104.6 0.0 collective-permute-start.6
  104.6 24.9 %all-to-all-done.2 = bf16[64,128,128]{2,1,0:T(8,128)(2,1)S(1)} async-done(((bf16[64,128,128]{2,1,0:T(8,128)(2,1)}), bf16[64,128,128]{2,1,0:T(8,128)(2,1)S(1)}, u32[]{:S(2)}, u32[]{:S(2)}) %all-to-all-start.2) | async-done | bytes 2097184 | tf_op jit(solution)/shard_map/all_to_all | solution.py:28
  129.5 0.3 reduce_sum.12.own
  129.8 0.0 collective-permute-done.5.ahead
  129.8 0.0 collective-permute-done.6.behind
  129.9 0.1 broadcast_in_dim.10
  129.9 13.8 %all_to_all.20.tiles = bf16[16,112,128]{2,1,0:T(8,128)(2,1)S(1)} all-to-all(bf16[16,112,128]{2,1,0:T(8,128)(2,1)S(1)} %broadcast_in_dim.10), channel_id=1, replica_groups=mesh['z'=4,'x'=4,'core'=2,'feat'=4] {'z','x'}, dimensions={0} | all-to-all | bytes 917504 | tf_op jit(solution)/shard_map/all_to_all | solution.py:28
  143.7 2.9 %collective-permute-start.7 = (bf16[16,112,128]{2,1,0:T(8,128)(2,1)S(1)}, bf16[16,112,128]{2,1,0:T(8,128)(2,1)S(1)}, u32[]{:S(2)}, u32[]{:S(2)}) collective-permute-start(bf16[16,112,128]{2,1,0:T(8,128)(2,1)S(1)} %all_to_all.20.tiles), channel_id=1, source_target_pairs={{0,4},{4,0},{1,5},{5,1},{2,6},{6,2},{3,7},{7,3},{8,12},{12,8},{9,1... | collective-permute-start | bytes 1376264 | tf_op jit(solution)/shard_map/ppermute | solution.py:20
  146.6 0.1 tile.12
  146.7 0.6 add_bitcast_fusion.targets
  147.3 0.7 collective-permute-done.7.far
  148.1 0.8 copy-done.5
  148.9 2.9 %shard_map.190 = (f32[3,16,2,16,128]{4,3,2,1,0:T(8,128)}, f32[128,512]{1,0:T(8,128)}, f32[2,16,2,16,128]{4,3,2,1,0:T(8,128)}, f32[128,512]{1,0:T(8,128)}, f32[256,512]{1,0:T(8,128)}) custom-call(s32[5]{0:T(128)} %stack.10.co, bf16[16,112,128]{2,1,0:T(8,128)(2,1)} %copy-done.1, bf16[16,112,128]{2,1,0:T(8,128)(2,1)} %copy-done.5, bf16[128,128]{1,0:T(8,128)(2,1)} %copy-done.6, ...), custom_call_target="tpu_custom_call" | custom-call | tf_op jit(solution)/shard_map/pallas_call | solution.py:295
  (48 shorter events, 0.2 us)
Async XLA Ops:
  0.6 2.4 %copy-start = (bf16[3,512,128]{2,1,0:T(8,128)(2,1)S(1)}, bf16[3,512,128]{2,1,0:T(8,128)(2,1)}, u32[]{:S(2)}) copy-start(bf16[3,512,128]{2,1,0:T(8,128)(2,1)} %param.20) | copy-start | bytes 1179652
  0.6 16.4 %copy-start.3 = (bf16[256,512]{1,0:T(8,128)(2,1)S(1)}, bf16[256,512]{1,0:T(8,128)(2,1)}, u32[]{:S(2)}) copy-start(bf16[256,512]{1,0:T(8,128)(2,1)} %node.3) | copy-start | bytes 786436
  0.7 16.4 %copy-start.13 = (s32[1,2,32]{2,1,0:T(2,128)S(1)}, s32[1,2,32]{2,1,0:T(2,128)}, u32[]{:S(2)}) copy-start(s32[1,2,32]{2,1,0:T(2,128)} %param.18) | copy-start | bytes 772
  3.7 36.4 %copy-start.12 = (s32[2048]{0:T(1024)S(1)}, s32[2048]{0:T(1024)}, u32[]{:S(2)}) copy-start(s32[2048]{0:T(1024)} %param.16) | copy-start | bytes 24580
  3.7 37.0 %copy-start.8 = (bf16[128,512]{1,0:T(8,128)(2,1)S(1)}, bf16[128,512]{1,0:T(8,128)(2,1)}, u32[]{:S(2)}) copy-start(bf16[128,512]{1,0:T(8,128)(2,1)} %param.23) | copy-start | bytes 393220
  5.0 36.4 %copy-start.7 = (bf16[2,512,128]{2,1,0:T(8,128)(2,1)S(1)}, bf16[2,512,128]{2,1,0:T(8,128)(2,1)}, u32[]{:S(2)}) copy-start(bf16[2,512,128]{2,1,0:T(8,128)(2,1)} %param.22) | copy-start | bytes 786436
  5.0 31.9 %all-to-all-start = ((bf16[64,80,128]{2,1,0:T(8,128)(2,1)}), bf16[64,80,128]{2,1,0:T(8,128)(2,1)S(1)}, u32[]{:S(2)}, u32[]{:S(2)}) async-start(bf16[64,80,128]{2,1,0:T(8,128)(2,1)} %broadcast_in_dim.8), calls=%async_computation | async-start | bytes 2621440 | tf_op jit(solution)/shard_map/all_to_all | solution.py:28
  17.7 10.1 %collective-permute-start = (bf16[32,512]{1,0:T(8,128)(2,1)S(1)}, bf16[32,512]{1,0:T(8,128)(2,1)S(1)}, u32[]{:S(2)}, u32[]{:S(2)}) collective-permute-start(bf16[32,512]{1,0:T(8,128)(2,1)S(1)} %gather_fusion), channel_id=1, source_target_pairs={{0,1},{1,2},{2,3},{3,4},{4,5},{5,6},{6,7},{7,8},{8,9},{9,10},{10,1... | collective-permute-start | bytes 98312 | tf_op jit(solution)/shard_map/ppermute | solution.py:24
  19.5 8.3 %collective-permute-start.1 = (bf16[32,512]{1,0:T(8,128)(2,1)S(1)}, bf16[32,512]{1,0:T(8,128)(2,1)S(1)}, u32[]{:S(2)}, u32[]{:S(2)}) collective-permute-start(bf16[32,512]{1,0:T(8,128)(2,1)S(1)} %gather_fusion.1), channel_id=1, source_target_pairs={{0,127},{1,0},{2,1},{3,2},{4,3},{5,4},{6,5},{7,6},{8,7},{9,8},{10,... | collective-permute-start | bytes 98312 | tf_op jit(solution)/shard_map/ppermute | solution.py:24
  27.8 18.9 %copy-start.16 = (bf16[32,512]{1,0:T(8,128)(2,1)}, bf16[32,512]{1,0:T(8,128)(2,1)S(1)}, u32[]{:S(2)}) copy-start(bf16[32,512]{1,0:T(8,128)(2,1)S(1)} %collective-permute-done.prev) | copy-start | bytes 98308
  27.8 18.9 %copy-start.17 = (bf16[32,512]{1,0:T(8,128)(2,1)}, bf16[32,512]{1,0:T(8,128)(2,1)S(1)}, u32[]{:S(2)}) copy-start(bf16[32,512]{1,0:T(8,128)(2,1)S(1)} %collective-permute-done.1.following) | copy-start | bytes 98308
  36.9 9.9 %copy-start.2 = (bf16[64,80,128]{2,1,0:T(8,128)(2,1)}, bf16[64,80,128]{2,1,0:T(8,128)(2,1)S(1)}, u32[]{:S(2)}) copy-start(bf16[64,80,128]{2,1,0:T(8,128)(2,1)S(1)} %all-to-all-done) | copy-start | bytes 3932164
  36.9 5.4 %collective-permute-start.2 = (bf16[16,4,80,128]{3,2,1,0:T(8,128)(2,1)S(1)}, bf16[16,4,80,128]{3,2,1,0:T(8,128)(2,1)}, u32[]{:S(2)}, u32[]{:S(2)}) collective-permute-start(bf16[16,4,80,128]{3,2,1,0:T(8,128)(2,1)S(1)} %bitcast.35), channel_id=1, source_target_pairs={{0,4},{4,0},{1,5},{5,1},{2,6},{6,2},{3,7},{7,3},{8,12},{12,8},{9,1... | collective-permute-start | bytes 3932168 | tf_op jit(solution)/shard_map/ppermute | solution.py:20
  43.2 18.1 %all-to-all-start.1 = ((bf16[4,768,128]{2,1,0:T(8,128)(2,1)}), bf16[4,768,128]{2,1,0:T(8,128)(2,1)S(1)}, u32[]{:S(2)}, u32[]{:S(2)}) async-start(bf16[4,768,128]{2,1,0:T(8,128)(2,1)} %broadcast_in_dim.9), calls=%async_computation.1 | async-start | bytes 1572864 | tf_op jit(solution)/shard_map/all_to_all | solution.py:28
  46.8 15.2 %copy-start.11 = (s32[2048]{0:T(1024)S(1)}, s32[2048]{0:T(1024)}, u32[]{:S(2)}) copy-start(s32[2048]{0:T(1024)} %param.15) | copy-start | bytes 24580
  61.3 2.6 %copy-start.4 = (bf16[4,768,128]{2,1,0:T(8,128)(2,1)}, bf16[4,768,128]{2,1,0:T(8,128)(2,1)S(1)}, u32[]{:S(2)}) copy-start(bf16[4,768,128]{2,1,0:T(8,128)(2,1)S(1)} %all-to-all-done.1.near) | copy-start | bytes 2359300
  61.3 2.6 %collective-permute-start.3 = (bf16[4,768,128]{2,1,0:T(8,128)(2,1)S(1)}, bf16[4,768,128]{2,1,0:T(8,128)(2,1)S(1)}, u32[]{:S(2)}, u32[]{:S(2)}) collective-permute-start(bf16[4,768,128]{2,1,0:T(8,128)(2,1)S(1)} %all-to-all-done.1.near), channel_id=1, source_target_pairs={{0,4},{4,0},{1,5},{5,1},{2,6},{6,2},{3,7},{7,3},{8,12},{12,8},{9,1... | collective-permute-start | bytes 2359304 | tf_op jit(solution)/shard_map/ppermute | solution.py:20
  63.9 0.9 copy-start.15
  85.9 4.5 %collective-permute-start.4 = (bf16[8,2,4,128,128]{4,3,2,1,0:T(8,128)(2,1)}, bf16[8,2,4,128,128]{4,3,2,1,0:T(8,128)(2,1)S(1)}, u32[]{:S(2)}, u32[]{:S(2)}) collective-permute-start(bf16[8,2,4,128,128]{4,3,2,1,0:T(8,128)(2,1)} %get-tuple-element.49), channel_id=1, source_target_pairs={{0,4},{4,0},{1,5},{5,1},{2,6},{6,2},{3,7},{7,3},{8,12},{12,8},{9,1... | collective-permute-start | bytes 6291464 | tf_op jit(solution)/shard_map/ppermute | solution.py:20
  94.1 7.3 %copy-start.19 = (bf16[32,512]{1,0:T(8,128)(2,1)S(1)}, bf16[32,512]{1,0:T(8,128)(2,1)}, u32[]{:S(2)}) copy-start(bf16[32,512]{1,0:T(8,128)(2,1)} %get-tuple-element.51) | copy-start | bytes 98308
  94.1 10.4 %copy-start.18 = (bf16[32,512]{1,0:T(8,128)(2,1)S(1)}, bf16[32,512]{1,0:T(8,128)(2,1)}, u32[]{:S(2)}) copy-start(bf16[32,512]{1,0:T(8,128)(2,1)} %get-tuple-element.53) | copy-start | bytes 98308
  94.1 35.3 %all-to-all-start.2 = ((bf16[64,128,128]{2,1,0:T(8,128)(2,1)}), bf16[64,128,128]{2,1,0:T(8,128)(2,1)S(1)}, u32[]{:S(2)}, u32[]{:S(2)}) async-start(bf16[64,128,128]{2,1,0:T(8,128)(2,1)} %bitcast.17), calls=%async_computation.2 | async-start | bytes 4194304 | tf_op jit(solution)/shard_map/all_to_all | solution.py:28
  101.4 45.2 %copy-start.14 = (s32[1,4]{1,0:T(1,128)S(1)}, s32[1,4]{1,0:T(1,128)}, u32[]{:S(2)}) copy-start(s32[1,4]{1,0:T(1,128)} %param.19) | copy-start | bytes 52
  101.5 28.3 %collective-permute-start.5 = (bf16[32,512]{1,0:T(8,128)(2,1)S(1)}, bf16[32,512]{1,0:T(8,128)(2,1)S(1)}, u32[]{:S(2)}, u32[]{:S(2)}) collective-permute-start(bf16[32,512]{1,0:T(8,128)(2,1)S(1)} %copy-done.19), channel_id=1, source_target_pairs={{0,127},{1,0},{2,1},{3,2},{4,3},{5,4},{6,5},{7,6},{8,7},{9,8},{10,... | collective-permute-start | bytes 98312 | tf_op jit(solution)/shard_map/ppermute | solution.py:24
  104.6 25.3 %collective-permute-start.6 = (bf16[32,512]{1,0:T(8,128)(2,1)S(1)}, bf16[32,512]{1,0:T(8,128)(2,1)S(1)}, u32[]{:S(2)}, u32[]{:S(2)}) collective-permute-start(bf16[32,512]{1,0:T(8,128)(2,1)S(1)} %copy-done.18), channel_id=1, source_target_pairs={{0,1},{1,2},{2,3},{3,4},{4,5},{5,6},{6,7},{7,8},{8,9},{9,10},{10,1... | collective-permute-start | bytes 98312 | tf_op jit(solution)/shard_map/ppermute | solution.py:24
  129.8 18.3 %copy-start.6 = (bf16[128,128]{1,0:T(8,128)(2,1)}, bf16[128,128]{1,0:T(8,128)(2,1)S(1)}, u32[]{:S(2)}) copy-start(bf16[128,128]{1,0:T(8,128)(2,1)S(1)} %reduce_sum.12.own) | copy-start | bytes 98308
  129.8 18.3 %copy-start.9 = (bf16[32,512]{1,0:T(8,128)(2,1)}, bf16[32,512]{1,0:T(8,128)(2,1)S(1)}, u32[]{:S(2)}) copy-start(bf16[32,512]{1,0:T(8,128)(2,1)S(1)} %collective-permute-done.5.ahead) | copy-start | bytes 98308
  129.8 18.2 %copy-start.10 = (bf16[32,512]{1,0:T(8,128)(2,1)}, bf16[32,512]{1,0:T(8,128)(2,1)S(1)}, u32[]{:S(2)}) copy-start(bf16[32,512]{1,0:T(8,128)(2,1)S(1)} %collective-permute-done.6.behind) | copy-start | bytes 98308
  143.7 4.4 %copy-start.1 = (bf16[16,112,128]{2,1,0:T(8,128)(2,1)}, bf16[16,112,128]{2,1,0:T(8,128)(2,1)S(1)}, u32[]{:S(2)}) copy-start(bf16[16,112,128]{2,1,0:T(8,128)(2,1)S(1)} %all_to_all.20.tiles) | copy-start | bytes 1376260
  143.7 4.3 %collective-permute-start.7 = (bf16[16,112,128]{2,1,0:T(8,128)(2,1)S(1)}, bf16[16,112,128]{2,1,0:T(8,128)(2,1)S(1)}, u32[]{:S(2)}, u32[]{:S(2)}) collective-permute-start(bf16[16,112,128]{2,1,0:T(8,128)(2,1)S(1)} %all_to_all.20.tiles), channel_id=1, source_target_pairs={{0,4},{4,0},{1,5},{5,1},{2,6},{6,2},{3,7},{7,3},{8,12},{12,8},{9,1... | collective-permute-start | bytes 1376264 | tf_op jit(solution)/shard_map/ppermute | solution.py:20
  148.1 0.8 copy-start.5

commit v4 on v3

--- a/solution.py
+++ b/solution.py
@@ -63,9 +63,10 @@
 
 
 def swish(pre):
-    sigmoid = 0.5 + 0.5 * jnp.tanh(0.5 * pre)
-    act = pre * sigmoid
-    return act, sigmoid + act * (1.0 - sigmoid)
+    half = 0.5 * pre
+    tanh = jnp.tanh(half)
+    act = half + half * tanh
+    return act, 0.5 * (1.0 + act + tanh * (1.0 - act))
 
 
 def hot_tiles(rows, count):
@@ -74,9 +75,49 @@
     return [jnp.where(spread == lanes + 128 * j, 1.0, 0.0).astype(BF16) for j in range(count)]
 
 
+def hot_kernel(co, src, dst, src_wide, dst_wide, hot, turned):
+    step = pl.program_id(0)
+    lanes = lax.broadcasted_iota(jnp.int32, (1, 128), 1)
+    for r in range(CHUNK // 128):
+        row = pl.ds(step * (CHUNK // 128) + r, 1)
+        live = lanes + step * CHUNK + r * 128 < co[4]
+        tiles = hot_tiles(jnp.where(live, dst[row, :], -1), 2) + hot_tiles(src[row, :], 7)
+        hot[r * 128 : (r + 1) * 128, :] = jnp.concatenate(tiles, axis=1)
+    place = lax.broadcasted_iota(jnp.int32, (128, CHUNK), 0)
+    lanes = lax.broadcasted_iota(jnp.int32, (1, CHUNK), 1)
+    src_row = src_wide[pl.ds(step, 1), :]
+    dst_row = jnp.where(lanes + step * CHUNK < co[4], dst_wide[pl.ds(step, 1), :], -1)
+    for j in range(9):
+        match = place + 128 * j == dst_row if j < 2 else place + 128 * (j - 2) == src_row
+        turned[j * 128 : (j + 1) * 128, :] = jnp.where(match, 1.0, 0.0).astype(BF16)
+
+
+def pack_kernel(co, node, targets, edge_first, edge_second, tiles, to_next, to_prev):
+    match = lax.broadcasted_iota(jnp.int32, (256, 128), 0) == targets[...]
+    rows = dot_tn(jnp.where(match, 1.0, 0.0).astype(BF16), node[...])
+    to_next[...] = rows[0:32].astype(BF16)
+    to_prev[...] = rows[32:64].astype(BF16)
+    group = lax.broadcasted_iota(jnp.int32, (16, 128), 0) // 4
+    coarse = jnp.zeros((16, 128), F32)
+    for b in range(4):
+        coarse = jnp.where(group == b, rows[64:80, b * 128 : (b + 1) * 128], coarse)
+    patch = co[0]
+    at = pl.ds(pl.multiple_of(patch * 16, 16), 16)
+    parts = [edge_first[m, at, :] for m in range(3)]
+    row = pl.ds(pl.multiple_of(patch // 4 * 16, 16), 16)
+    parts.append(edge_second[row, pl.ds(pl.multiple_of(patch % 4 * 128, 128), 128)])
+    parts.append(coarse.astype(BF16))
+    tile = jnp.concatenate(parts, axis=0)
+    for k in range(64):
+        tiles[k] = tile
+
+
 def live_rows(step, count):
     place = lax.broadcasted_iota(jnp.int32, (CHUNK, 1), 0) + step * CHUNK
     return jnp.where(place < count, 1.0, 0.0)
+
+
+HALVES = (slice(0, CHUNK // 2), slice(CHUNK // 2, CHUNK))
 
 
 def place_weights(core, near, far, first, second):
@@ -118,7 +159,7 @@
         lookup[320:832, half * 256 + 128 : half * 256 + 256] = other_block.astype(BF16)
 
 
-def forward_kernel(co, node, prev, following, near, far, src, dst, dst_wide, edge, *refs):
+def forward_kernel(co, node, prev, following, near, far, edge, hot, turned, *refs):
     edge_out, incoming, act_out, normed_out, slope_out, factor_out, lookup, first, second = refs[:9]
     table, total, coarse = refs[9:]
     step = pl.program_id(0)
@@ -130,31 +171,27 @@
         lookup[288:320, :] = following[...]
         lookup[832:896, :] = jnp.zeros((64, 512), BF16)
         place_tiles(co[2], near, far, lookup, first, second, coarse)
-        table[0:TABLE, :] = dot(lookup[...], whole(first, 1)).astype(BF16)
-        table[TABLE:, :] = dot(node[...], whole(first, 2)).astype(BF16)
+        table[0:256, :] = dot(node[...], whole(first, 2)).astype(BF16)
+        table[256:, :] = dot(lookup[...], whole(first, 1)).astype(BF16)
         total[...] = jnp.zeros_like(total)
 
-    hots = []
-    for r in range(CHUNK // 128):
-        row = pl.ds(step * (CHUNK // 128) + r, 1)
-        tiles = hot_tiles(src[row, :], TABLE // 128) + hot_tiles(dst[row, :], 2)
-        hots.append(jnp.concatenate(tiles, axis=1))
-    hot = jnp.concatenate(hots, axis=0)
-    rows = edge[...]
-    pre = dot(rows, whole(first, 0)) + dot(hot, table[...])
-    act, slope = swish(pre)
-    act = act.astype(BF16)
-    act_out[...] = act
-    slope_out[...] = slope.astype(BF16)
-    normed, factor = normalize(dot(act, second[...]))
-    normed_out[...] = normed.astype(BF16)
-    factor_out[...] = jnp.broadcast_to(factor, (CHUNK, 128))
-    new = (rows.astype(F32) + live_rows(step, co[4]) * normed).astype(BF16)
-    edge_out[...] = new
-    place = lax.broadcasted_iota(jnp.int32, (256, CHUNK), 1) + step * CHUNK
-    node_of = lax.broadcasted_iota(jnp.int32, (256, CHUNK), 0)
-    match = (node_of == dst_wide[pl.ds(step, 1), :]) & (place < co[4])
-    total[...] += dot(jnp.where(match, 1.0, 0.0).astype(BF16), new)
+    live = live_rows(step, co[4])
+    pres = [dot(edge[h, :], whole(first, 0)) + dot(hot[h, :], table[...]) for h in HALVES]
+    acts = []
+    for h, pre in zip(HALVES, pres):
+        act, slope = swish(pre)
+        acts.append(act.astype(BF16))
+        act_out[h, :] = acts[-1]
+        slope_out[h, :] = slope.astype(BF16)
+    values = [dot(act, second[...]) for act in acts]
+    for h, value in zip(HALVES, values):
+        centre = value - mean(value)
+        factor = lax.rsqrt(mean(centre * centre) + EPSILON) * live[h]
+        normed = centre * factor
+        normed_out[h, :] = normed.astype(BF16)
+        factor_out[h, :] = jnp.broadcast_to(factor, (CHUNK // 2, 128))
+        edge_out[h, :] = (edge[h, :].astype(F32) + normed).astype(BF16)
+    total[...] += dot(turned[...], edge_out[...])
 
     @pl.when(step == STEPS - 1)
     def _():
@@ -197,10 +234,10 @@
 
 
 def backward_kernel(co, node, incoming, grad_node, near, far, *refs):
-    edge_first, edge_second, lookup, dst, src_wide, dst_wide = refs[:6]
-    edge, act, normed, slope, factor, grad_edge = refs[6:12]
-    node_out, node_total, edge_grad, to_prev, to_next, keep, give = refs[12:19]
-    first, second, spread, sum_second, sum_first, sums, columns, rows, owned = refs[19:]
+    edge_first, edge_second, lookup = refs[:3]
+    edge, act, normed, slope, factor, grad_edge, hot, turned = refs[3:11]
+    node_out, node_total, edge_grad, to_prev, to_next, keep, give = refs[11:18]
+    first, second, spread, sum_second, sum_first, sums, columns, rows, owned = refs[18:]
     step = pl.program_id(0)
 
     @pl.when(step == 0)
@@ -224,30 +261,26 @@
         sum_first[...] = jnp.zeros_like(sum_first)
         sums[...] = jnp.zeros_like(sums)
 
-    hots = []
-    for r in range(CHUNK // 128):
-        row = pl.ds(step * (CHUNK // 128) + r, 1)
-        hots.append(jnp.concatenate(hot_tiles(dst[row, :], 2), axis=1))
-    live = live_rows(step, co[4])
-    total = grad_edge[...].astype(F32) + live * dot(jnp.concatenate(hots, axis=0), spread[...])
-    delta = normalize_back(live * total, normed[...].astype(F32), factor[:, 0:1]).astype(BF16)
-    pre_grad = (dot_nt(delta, edge_second[...]) * slope[...].astype(F32)).astype(BF16)
-    edge_grad[...] = (total + dot_nt(pre_grad, whole(edge_first, 0))).astype(BF16)
-    sum_second[...] += dot_tn(act[...], delta)
+    totals = [grad_edge[h, :].astype(F32) + dot(hot[h, :], spread[...]) for h in HALVES]
+    deltas = []
+    for h, total in zip(HALVES, totals):
+        delta = normalize_back(total, normed[h, :].astype(F32), factor[h, 0:1])
+        deltas.append(delta.astype(BF16))
+    grads = [dot_nt(delta, edge_second[...]) for delta in deltas]
+    pre_grads = [(g * slope[h, :].astype(F32)).astype(BF16) for h, g in zip(HALVES, grads)]
+    for h, total, pre_grad in zip(HALVES, totals, pre_grads):
+        edge_grad[h, :] = (total + dot_nt(pre_grad, whole(edge_first, 0))).astype(BF16)
+    pre_grad = jnp.concatenate(pre_grads, axis=0)
+    sum_second[...] += dot_tn(act[...], jnp.concatenate(deltas, axis=0))
     sum_first[...] += dot_tn(edge[...], pre_grad)
-    place = lax.broadcasted_iota(jnp.int32, (128, CHUNK), 0)
-    src_row, dst_row = src_wide[pl.ds(step, 1), :], dst_wide[pl.ds(step, 1), :]
-    for j in range(9):
-        match = place + 128 * j == src_row if j < 7 else place + 128 * (j - 7) == dst_row
-        hot = jnp.where(match, 1.0, 0.0).astype(BF16)
-        sums[j * 128 : (j + 1) * 128, :] += dot(hot, pre_grad)
+    sums[...] += dot(turned[...], pre_grad)
 
     @pl.when(step == STEPS - 1)
     def _():
         put_rows(co, sum_second[...], 5, rows, keep, give)
         put_columns(co, sum_first[...], 0, columns, keep, give)
-        sent = sums[0:TABLE, :].astype(BF16)
-        received = sums[TABLE:, :].astype(BF16)
+        received = sums[0:256, :].astype(BF16)
+        sent = sums[256:, :].astype(BF16)
         put_columns(co, dot_tn(lookup[...], sent), 1, columns, keep, give)
         put_columns(co, dot_tn(node[...], received), 2, columns, keep, give)
         back = dot_nt(sent, whole(edge_first, 1))
@@ -339,33 +372,49 @@
 ):
     core = lax.axis_index("core")
     patch = (lax.axis_index("z") * 4 + lax.axis_index("x")) * 2 + core
-    co = jnp.stack([core, core, core, core, edge_count[0]]).astype(jnp.int32)
+    co = jnp.stack([patch, patch, core, core, edge_count[0]]).astype(jnp.int32)
     lists, owned = halo_send[0], coarse_of[0]
     unused = jnp.full((48,), -1, jnp.int32)
     targets = jnp.concatenate([lists[1], lists[0], jnp.tile(owned, 4), unused]).reshape(1, 128)
 
-    first_part = lax.dynamic_slice_in_dim(edge_w1, patch * 16, 16, 1).reshape(48, 128)
-    second_part = lax.dynamic_slice(edge_w2, (patch // 4 * 16, patch % 4 * 128), (16, 128))
-    coarse_own = node_lat[owned].reshape(4, 4, 128).transpose(1, 0, 2).reshape(16, 128)
-    tile = jnp.concatenate([first_part, second_part, coarse_own], axis=0)
-    from_prev = shifted(node_lat[lists[1]], 1)
-    from_next = shifted(node_lat[lists[0]], -1)
-    near = exchange(repeated(tile, 64), ("z", "x", "feat")).reshape(16, 4, 80, 128)
-    near = after(near, from_prev, from_next)
+    packed, to_next, to_prev = plain_call(
+        pack_kernel,
+        [co],
+        [node_lat, targets, edge_w1, edge_w2],
+        [shape(64, 80, 128), shape(32, 512), shape(32, 512)],
+    )
+    from_prev = shifted(to_next, 1)
+    from_next = shifted(to_prev, -1)
+    near = exchange(packed, ("z", "x", "feat")).reshape(16, 4, 80, 128)
+    indices = [edge_src.reshape(16, 128), edge_dst.reshape(16, 128)]
+    indices += [edge_src.reshape(STEPS, CHUNK), edge_dst.reshape(STEPS, CHUNK)]
+    indices = [after(value, packed) for value in indices]
+    params = pltpu.CompilerParams(vmem_limit_bytes=VMEM_BYTES, dimension_semantics=("arbitrary",))
+    high = TABLE + 256
+    hot, turned = pl.pallas_call(
+        hot_kernel,
+        grid=(STEPS,),
+        in_specs=[SMEM] + [like(v) for v in indices],
+        out_specs=[chunk(CHUNK, high), pl.BlockSpec((high, CHUNK), lambda i: (0, i))],
+        out_shape=[shape(2048, high), shape(high, 2048)],
+        compiler_params=params,
+        cost_estimate=pl.CostEstimate(
+            flops=20_000_000, bytes_accessed=10_000_000, transcendentals=0
+        ),
+    )(co, *indices)
+    near = after(near, from_prev, from_next, hot)
     far = other_core(near)
     node_half = after(repeated(halves(node_w1, node_w2, core), 4), near, far)
     node_near = exchange(node_half, "feat")
 
-    src, dst = edge_src.reshape(16, 128), edge_dst.reshape(16, 128)
-    src_wide, dst_wide = edge_src.reshape(STEPS, CHUNK), edge_dst.reshape(STEPS, CHUNK)
     fixed = [node_lat, from_prev, from_next, near, far]
-    fixed += [src, dst, dst_wide]
     wide = chunk(CHUNK, 512)
-    params = pltpu.CompilerParams(vmem_limit_bytes=VMEM_BYTES, dimension_semantics=("arbitrary",))
     edge_out, incoming, act, normed, slope, factor, lookup, first, second = pl.pallas_call(
         forward_kernel,
         grid=(STEPS,),
-        in_specs=[SMEM] + [like(v) for v in fixed] + [wide],
+        in_specs=[SMEM]
+        + [like(v) for v in fixed]
+        + [wide, chunk(CHUNK, high), pl.BlockSpec((256, CHUNK), lambda i: (0, i))],
         out_specs=[wide, same(256, 512), wide, wide, wide, chunk(CHUNK, 128)]
         + [same(TABLE, 512), same(3, 16, 2, 16, 512), same(512, 512)],
         out_shape=[
@@ -388,20 +437,21 @@
         cost_estimate=pl.CostEstimate(
             flops=7_000_000_000, bytes_accessed=18_000_000, transcendentals=1_000_000
         ),
-    )(co, *fixed, edge_lat)
+    )(co, *fixed, edge_lat, hot, turned)
 
     node_near = after(node_near, incoming)
     node_far = other_core(node_near)
     fixed = [node_lat, incoming, grad_node, node_near, node_far]
-    fixed += [first, second, lookup, dst, src_wide, dst_wide]
-    moving = [edge_lat, act, normed, slope, factor, grad_edge]
+    fixed += [first, second, lookup]
+    moving = [edge_lat, act, normed, slope, factor, grad_edge, hot, turned]
     tiles = (8, 2, 4, 128, 128)
     node_out, node_total, edge_grad, to_prev, to_next, keep, give = pl.pallas_call(
         backward_kernel,
         grid=(STEPS,),
         in_specs=[SMEM]
         + [like(v) for v in fixed]
-        + [wide, wide, wide, wide, chunk(CHUNK, 128), wide],
+        + [wide, wide, wide, wide, chunk(CHUNK, 128), wide, chunk(CHUNK, 256)]
+        + [pl.BlockSpec((high, CHUNK), lambda i: (0, i))],
         out_specs=[same(256, 512), same(256, 512), wide, same(32, 512), same(32, 512)]
         + [same(*tiles), same(*tiles)],
         out_shape=[

time: 152 us -> 155 us (1.020)
  Pallas kernels: 38.6 us -> 46.4 us
  local copies, waits for them, and re-layouts: 9.49 us -> 6.56 us
  waiting for transfers between devices: 46.7 us -> 44.8 us
    pallas_call x0 -> x1, Pallas kernels: none -> 5.12 us  [shards(): pl.pallas_call(hot_kernel, grid=(STEPS,), in_specs=[SMEM] + [like(v) for...]
    ppermute x4, waiting for transfers between devices: 5.91 us -> 0.88 us  [shifted(): lax.ppermute(value, BOTH, [(k, (k + steps) % 128) for k in range(128)])]
    ppermute x4, waiting for transfers between devices: 6.86 us -> 9.9 us  [other_core(): return lax.ppermute(value, 'core', [(0, 1), (1, 0)])]
    gather x3 -> x0, local copies, waits for them, and re-layouts: 2.8 us -> none  [the longest x1 1.55 us: shards(): node_lat[owned].reshape(4, 4, 128).transpose(1, 0, 2).reshape(16, 128)]
    pallas_call x1 -> x2, Pallas kernels: 2.92 us -> 5.31 us  [plain_call(): pl.pallas_call(kernel, in_specs=[SMEM] * len(scalars) + [WHOLE] * len(ope...]
  transfers between devices with their start and end apart: 11 -> 11, of which waited for: 7 -> 7; matrix products, arithmetic and copies ran while one was open for 3% -> 1% of each run, Pallas kernels for 10% -> 13%
where the time goes in v4:
time: 155 us; the launch traced here: 154 us
  Pallas kernels  46.4 us (30%)
  waiting for transfers between devices  44.8 us (29%)
  starting transfers between devices  36.1 us (23%)
  blocking collectives  13.8 us (9%)
  local copies, waits for them, and re-layouts  6.56 us (4%)
  other arithmetic  4.65 us (3%)
  between operations  1.58 us (1%)
    all_to_all x3, waiting for transfers between devices, exchange(): return lax.all_to_all(value, axes, 0, 0, tiled=True)  34 us
    all_to_all x3, starting transfers between devices, exchange(): return lax.all_to_all(value, axes, 0, 0, tiled=True)  22.9 us
    pallas_call x1, Pallas kernels, shards(): pl.pallas_call(backward_kernel, grid=(STEPS,), in_specs=[SMEM] + [like(v)...  20.9 us
    pallas_call x1, Pallas kernels, shards(): pl.pallas_call(forward_kernel, grid=(STEPS,), in_specs=[SMEM] + [like(v)...  15.1 us
    all_to_all x1, blocking collectives, exchange(): return lax.all_to_all(value, axes, 0, 0, tiled=True)  13.8 us
    ppermute x4, waiting for transfers between devices, other_core(): return lax.ppermute(value, 'core', [(0, 1), (1, 0)])  9.9 us
    ppermute x4, starting transfers between devices, shifted(): lax.ppermute(value, BOTH, [(k, (k + steps) % 128) for k in range(128)])  6.62 us
    ppermute x4, starting transfers between devices, other_core(): return lax.ppermute(value, 'core', [(0, 1), (1, 0)])  6.59 us
  transfers between devices with their start and end apart: 11, of which 7 were waited for; matrix products, arithmetic and copies ran while one was open for 1% of the time, Pallas kernels for 13%

profile of v4, /device:TPU:1, one launch (start us, length us, event | category | flops | bytes accessed | tf_op | source)
XLA Modules:
  0.0 153.9 jit_solution(17986858528724739502)
XLA Ops:
  0.6 0.0 copy-start
  0.6 0.0 copy-start.9
  0.7 0.0 copy-start.10
  0.7 0.0 copy-start.6
  1.4 0.8 slice_bitcast_fusion.1
  2.1 0.7 tile.11
  2.8 0.1 tile.12
  2.9 0.6 stack.13.co
  3.5 0.6 add_bitcast_fusion.targets
  4.0 2.4 %shard_map.188 = (bf16[64,80,128]{2,1,0:T(8,128)(2,1)}, bf16[32,512]{1,0:T(8,128)(2,1)}, bf16[32,512]{1,0:T(8,128)(2,1)}) custom-call(s32[5]{0:T(128)} %stack.13.co, bf16[256,512]{1,0:T(8,128)(2,1)} %node.5, s32[1,128]{1,0:T(1,128)} %add_bitcast_fusion.targets, bf16[3,512,128]{2,1,0:T(8,128)(2,1)} %edge_first.1, bf16[128,512]{1,0:T(8,128)(2,1)} %edge_second.1), custom_call_target="tpu_custom_call" | custom-call | tf_op jit(solution)/shard_map/pallas_call | solution.py:328
  6.4 12.1 %all-to-all-start = ((bf16[64,80,128]{2,1,0:T(8,128)(2,1)}), bf16[64,80,128]{2,1,0:T(8,128)(2,1)S(1)}, u32[]{:S(2)}, u32[]{:S(2)}) async-start(bf16[64,80,128]{2,1,0:T(8,128)(2,1)} %get-tuple-element.46), calls=%async_computation | async-start | bytes 2621440 | tf_op jit(solution)/shard_map/all_to_all | solution.py:28
  18.6 1.1 collective-permute-start
  19.7 2.4 %collective-permute-start.1 = (bf16[32,512]{1,0:T(8,128)(2,1)S(1)}, bf16[32,512]{1,0:T(8,128)(2,1)S(1)}, u32[]{:S(2)}, u32[]{:S(2)}) collective-permute-start(bf16[32,512]{1,0:T(8,128)(2,1)S(1)} %copy-done.17), channel_id=1, source_target_pairs={{0,127},{1,0},{2,1},{3,2},{4,3},{5,4},{6,5},{7,6},{8,7},{9,8},{10,... | collective-permute-start | bytes 98312 | tf_op jit(solution)/shard_map/ppermute | solution.py:24
  22.1 0.6 reshape.62.src_wide
  22.7 0.0 copy-done.10
  22.7 0.6 reshape.63.dst_wide
  23.3 5.1 %shard_map.189 = (bf16[2048,1152]{1,0:T(8,128)(2,1)}, bf16[1152,2048]{1,0:T(8,128)(2,1)}) custom-call(s32[5]{0:T(128)} %stack.13.co, s32[16,128]{1,0:T(8,128)} %bitcast.23, s32[16,128]{1,0:T(8,128)} %bitcast.24, s32[4,512]{1,0:T(4,128)} %reshape.62.src_wide, s32[4,512]{1,0:T(4,128)} %reshape.63.dst_wide), custom_call_target="tpu_custom_call" | custom-call | flops 20000000 | bytes 10000000 | tf_op jit(solution)/shard_map/pallas_call | solution.py:394
  28.4 0.9 collective-permute-done.prev
  29.3 0.0 collective-permute-done.1.following
  29.3 9.1 %all-to-all-done = bf16[64,80,128]{2,1,0:T(8,128)(2,1)S(1)} async-done(((bf16[64,80,128]{2,1,0:T(8,128)(2,1)}), bf16[64,80,128]{2,1,0:T(8,128)(2,1)S(1)}, u32[]{:S(2)}, u32[]{:S(2)}) %all-to-all-start) | async-done | bytes 1310752 | tf_op jit(solution)/shard_map/all_to_all | solution.py:28
  38.4 2.6 %collective-permute-start.2 = (bf16[16,4,80,128]{3,2,1,0:T(8,128)(2,1)S(1)}, bf16[16,4,80,128]{3,2,1,0:T(8,128)(2,1)S(1)}, u32[]{:S(2)}, u32[]{:S(2)}) collective-permute-start(bf16[16,4,80,128]{3,2,1,0:T(8,128)(2,1)S(1)} %bitcast.18), channel_id=1, source_target_pairs={{0,4},{4,0},{1,5},{5,1},{2,6},{6,2},{3,7},{7,3},{8,12},{12,8},{9,1... | collective-permute-start | bytes 3932168 | tf_op jit(solution)/shard_map/ppermute | solution.py:20
  41.1 2.5 %collective-permute-done.2.far = bf16[16,4,80,128]{3,2,1,0:T(8,128)(2,1)S(1)} collective-permute-done((bf16[16,4,80,128]{3,2,1,0:T(8,128)(2,1)S(1)}, bf16[16,4,80,128]{3,2,1,0:T(8,128)(2,1)S(1)}, u32[]{:S(2)}, u32[]{:S(2)}) %collective-permute-start.2) | collective-permute-done | bytes 1310752 | tf_op jit(solution)/shard_map/ppermute | solution.py:20
  43.6 1.1 broadcast_in_dim.7
  44.7 0.3 copy-done.11
  45.0 3.5 %all-to-all-start.1 = ((bf16[4,768,128]{2,1,0:T(8,128)(2,1)}), bf16[4,768,128]{2,1,0:T(8,128)(2,1)S(1)}, u32[]{:S(2)}, u32[]{:S(2)}) async-start(bf16[4,768,128]{2,1,0:T(8,128)(2,1)} %broadcast_in_dim.7), calls=%async_computation.1 | async-start | bytes 1572864 | tf_op jit(solution)/shard_map/all_to_all | solution.py:28
  48.5 15.1 %shard_map.190 = (bf16[2048,512]{1,0:T(8,128)(2,1)}, bf16[256,512]{1,0:T(8,128)(2,1)}, bf16[2048,512]{1,0:T(8,128)(2,1)}, bf16[2048,512]{1,0:T(8,128)(2,1)}, bf1...) custom-call(s32[5]{0:T(128)} %stack.13.co, ...), custom_call_target="tpu_custom_call" | custom-call | flops 7000000000 | bytes 18000000 | tf_op jit(solution)/shard_map/pallas_call | solution.py:412
  63.6 0.0 all-to-all-done.1.near
  63.7 0.0 copy-start.3
  63.7 0.6 collective-permute-start.3
  64.3 1.9 %collective-permute-done.3.far = bf16[4,768,128]{2,1,0:T(8,128)(2,1)S(1)} collective-permute-done((bf16[4,768,128]{2,1,0:T(8,128)(2,1)S(1)}, bf16[4,768,128]{2,1,0:T(8,128)(2,1)S(1)}, u32[]{:S(2)}, u32[]{:S(2)}) %collective-permute-start.3) | collective-permute-done | bytes 786464 | tf_op jit(solution)/shard_map/ppermute | solution.py:20
  66.2 0.9 copy-done.12
  67.1 20.9 %shard_map.191 = (bf16[256,512]{1,0:T(8,128)(2,1)}, f32[256,512]{1,0:T(8,128)}, bf16[2048,512]{1,0:T(8,128)(2,1)}, bf16[32,512]{1,0:T(8,128)(2,1)}, bf16[32,512]...) custom-call(s32[5]{0:T(128)} %stack.13.co, bf16[256,512]{1,0:T(8,128)(2,1)} %node.5, ...), custom_call_target="tpu_custom_call" | custom-call | flops 8999999488 | bytes 24000000 | tf_op jit(solution)/shard_map/pallas_call | solution.py:448
  88.0 0.5 collective-permute-start.4
  88.4 4.0 %collective-permute-done.4 = bf16[8,2,4,128,128]{4,3,2,1,0:T(8,128)(2,1)S(1)} collective-permute-done((bf16[8,2,4,128,128]{4,3,2,1,0:T(8,128)(2,1)}, bf16[8,2,4,128,128]{4,3,2,1,0:T(8,128)(2,1)S(1)}, u32[]{:S(2)}, u32[]{:S(2)}) %collective-permute-start.4) | collective-permute-done | bytes 2097184 | tf_op jit(solution)/shard_map/ppermute | solution.py:20
  92.4 3.8 %add_convert_fusion = bf16[8,2,4,128,128]{4,3,2,1,0:T(8,128)(2,1)} fusion(bf16[8,2,4,128,128]{4,3,2,1,0:T(8,128)(2,1)S(1)} %collective-permute-done.4, bf16[8,2,4,128,128]{4,3,2,1,0:T(8,128)(2,1)} %get-tuple-element.66), kind=kLoop, calls=%fused_computation | loop fusion | flops 4194304 | bytes 6291456 | tf_op jit(solution)/shard_map/convert_element_type | solution.py:483
  96.2 7.3 %all-to-all-start.2 = ((bf16[64,128,128]{2,1,0:T(8,128)(2,1)}), bf16[64,128,128]{2,1,0:T(8,128)(2,1)S(1)}, u32[]{:S(2)}, u32[]{:S(2)}) async-start(bf16[64,128,128]{2,1,0:T(8,128)(2,1)} %bitcast.12), calls=%async_computation.2 | async-start | bytes 4194304 | tf_op jit(solution)/shard_map/all_to_all | solution.py:28
  103.5 3.1 %collective-permute-start.5 = (bf16[32,512]{1,0:T(8,128)(2,1)S(1)}, bf16[32,512]{1,0:T(8,128)(2,1)S(1)}, u32[]{:S(2)}, u32[]{:S(2)}) collective-permute-start(bf16[32,512]{1,0:T(8,128)(2,1)S(1)} %copy-done.16), channel_id=1, source_target_pairs={{0,127},{1,0},{2,1},{3,2},{4,3},{5,4},{6,5},{7,6},{8,7},{9,8},{10,... | collective-permute-start | bytes 98312 | tf_op jit(solution)/shard_map/ppermute | solution.py:24
  106.6 0.0 collective-permute-start.6
  106.6 24.9 %all-to-all-done.2 = bf16[64,128,128]{2,1,0:T(8,128)(2,1)S(1)} async-done(((bf16[64,128,128]{2,1,0:T(8,128)(2,1)}), bf16[64,128,128]{2,1,0:T(8,128)(2,1)S(1)}, u32[]{:S(2)}, u32[]{:S(2)}) %all-to-all-start.2) | async-done | bytes 2097184 | tf_op jit(solution)/shard_map/all_to_all | solution.py:28
  131.6 0.3 reduce_sum.12.own
  131.9 0.0 collective-permute-done.5.ahead
  131.9 0.0 collective-permute-done.6.behind
  131.9 0.1 broadcast_in_dim.8
  132.0 13.8 %all_to_all.20.tiles = bf16[16,112,128]{2,1,0:T(8,128)(2,1)S(1)} all-to-all(bf16[16,112,128]{2,1,0:T(8,128)(2,1)S(1)} %broadcast_in_dim.8), channel_id=1, replica_groups=mesh['z'=4,'x'=4,'core'=2,'feat'=4] {'z','x'}, dimensions={0} | all-to-all | bytes 917504 | tf_op jit(solution)/shard_map/all_to_all | solution.py:28
  145.8 2.9 %collective-permute-start.7 = (bf16[16,112,128]{2,1,0:T(8,128)(2,1)S(1)}, bf16[16,112,128]{2,1,0:T(8,128)(2,1)S(1)}, u32[]{:S(2)}, u32[]{:S(2)}) collective-permute-start(bf16[16,112,128]{2,1,0:T(8,128)(2,1)S(1)} %all_to_all.20.tiles), channel_id=1, source_target_pairs={{0,4},{4,0},{1,5},{5,1},{2,6},{6,2},{3,7},{7,3},{8,12},{12,8},{9,1... | collective-permute-start | bytes 1376264 | tf_op jit(solution)/shard_map/ppermute | solution.py:20
  148.7 1.4 collective-permute-done.7.far
  150.2 0.8 copy-done.4
  150.9 2.9 %shard_map.192 = (f32[3,16,2,16,128]{4,3,2,1,0:T(8,128)}, f32[128,512]{1,0:T(8,128)}, f32[2,16,2,16,128]{4,3,2,1,0:T(8,128)}, f32[128,512]{1,0:T(8,128)}, f32[256,512]{1,0:T(8,128)}) custom-call(s32[5]{0:T(128)} %stack.13.co, bf16[16,112,128]{2,1,0:T(8,128)(2,1)} %copy-done.1, bf16[16,112,128]{2,1,0:T(8,128)(2,1)} %copy-done.4, bf16[128,128]{1,0:T(8,128)(2,1)} %copy-done.5, ...), custom_call_target="tpu_custom_call" | custom-call | tf_op jit(solution)/shard_map/pallas_call | solution.py:328
  (36 shorter events, 0.1 us)
Async XLA Ops:
  0.6 40.4 %copy-start = (bf16[2,512,128]{2,1,0:T(8,128)(2,1)S(1)}, bf16[2,512,128]{2,1,0:T(8,128)(2,1)}, u32[]{:S(2)}) copy-start(bf16[2,512,128]{2,1,0:T(8,128)(2,1)} %param.22) | copy-start | bytes 786436
  0.6 21.4 %copy-start.9 = (s32[2048]{0:T(1024)S(1)}, s32[2048]{0:T(1024)}, u32[]{:S(2)}) copy-start(s32[2048]{0:T(1024)} %param.15) | copy-start | bytes 24580
  0.7 22.0 %copy-start.10 = (s32[2048]{0:T(1024)S(1)}, s32[2048]{0:T(1024)}, u32[]{:S(2)}) copy-start(s32[2048]{0:T(1024)} %param.16) | copy-start | bytes 24580
  0.7 40.3 %copy-start.6 = (bf16[128,512]{1,0:T(8,128)(2,1)S(1)}, bf16[128,512]{1,0:T(8,128)(2,1)}, u32[]{:S(2)}) copy-start(bf16[128,512]{1,0:T(8,128)(2,1)} %param.23) | copy-start | bytes 393220
  6.4 12.1 %copy-start.18 = (bf16[32,512]{1,0:T(8,128)(2,1)S(1)}, bf16[32,512]{1,0:T(8,128)(2,1)}, u32[]{:S(2)}) copy-start(bf16[32,512]{1,0:T(8,128)(2,1)} %get-tuple-element.44) | copy-start | bytes 98308
  6.4 13.2 %copy-start.17 = (bf16[32,512]{1,0:T(8,128)(2,1)S(1)}, bf16[32,512]{1,0:T(8,128)(2,1)}, u32[]{:S(2)}) copy-start(bf16[32,512]{1,0:T(8,128)(2,1)} %get-tuple-element.45) | copy-start | bytes 98308
  6.4 31.9 %all-to-all-start = ((bf16[64,80,128]{2,1,0:T(8,128)(2,1)}), bf16[64,80,128]{2,1,0:T(8,128)(2,1)S(1)}, u32[]{:S(2)}, u32[]{:S(2)}) async-start(bf16[64,80,128]{2,1,0:T(8,128)(2,1)} %get-tuple-element.46), calls=%async_computation | async-start | bytes 2621440 | tf_op jit(solution)/shard_map/all_to_all | solution.py:28
  18.6 10.7 %collective-permute-start = (bf16[32,512]{1,0:T(8,128)(2,1)S(1)}, bf16[32,512]{1,0:T(8,128)(2,1)S(1)}, u32[]{:S(2)}, u32[]{:S(2)}) collective-permute-start(bf16[32,512]{1,0:T(8,128)(2,1)S(1)} %copy-done.18), channel_id=1, source_target_pairs={{0,1},{1,2},{2,3},{3,4},{4,5},{5,6},{6,7},{7,8},{8,9},{9,10},{10,1... | collective-permute-start | bytes 98312 | tf_op jit(solution)/shard_map/ppermute | solution.py:24
  19.7 9.6 %collective-permute-start.1 = (bf16[32,512]{1,0:T(8,128)(2,1)S(1)}, bf16[32,512]{1,0:T(8,128)(2,1)S(1)}, u32[]{:S(2)}, u32[]{:S(2)}) collective-permute-start(bf16[32,512]{1,0:T(8,128)(2,1)S(1)} %copy-done.17), channel_id=1, source_target_pairs={{0,127},{1,0},{2,1},{3,2},{4,3},{5,4},{6,5},{7,6},{8,7},{9,8},{10,... | collective-permute-start | bytes 98312 | tf_op jit(solution)/shard_map/ppermute | solution.py:24
  29.3 19.2 %copy-start.13 = (bf16[32,512]{1,0:T(8,128)(2,1)}, bf16[32,512]{1,0:T(8,128)(2,1)S(1)}, u32[]{:S(2)}) copy-start(bf16[32,512]{1,0:T(8,128)(2,1)S(1)} %collective-permute-done.prev) | copy-start | bytes 98308
  29.3 19.2 %copy-start.14 = (bf16[32,512]{1,0:T(8,128)(2,1)}, bf16[32,512]{1,0:T(8,128)(2,1)S(1)}, u32[]{:S(2)}) copy-start(bf16[32,512]{1,0:T(8,128)(2,1)S(1)} %collective-permute-done.1.following) | copy-start | bytes 98308
  38.4 10.2 %copy-start.2 = (bf16[64,80,128]{2,1,0:T(8,128)(2,1)}, bf16[64,80,128]{2,1,0:T(8,128)(2,1)S(1)}, u32[]{:S(2)}) copy-start(bf16[64,80,128]{2,1,0:T(8,128)(2,1)S(1)} %all-to-all-done) | copy-start | bytes 3932164
  38.4 5.3 %collective-permute-start.2 = (bf16[16,4,80,128]{3,2,1,0:T(8,128)(2,1)S(1)}, bf16[16,4,80,128]{3,2,1,0:T(8,128)(2,1)S(1)}, u32[]{:S(2)}, u32[]{:S(2)}) collective-permute-start(bf16[16,4,80,128]{3,2,1,0:T(8,128)(2,1)S(1)} %bitcast.18), channel_id=1, source_target_pairs={{0,4},{4,0},{1,5},{5,1},{2,6},{6,2},{3,7},{7,3},{8,12},{12,8},{9,1... | collective-permute-start | bytes 3932168 | tf_op jit(solution)/shard_map/ppermute | solution.py:20
  43.6 1.4 copy-start.11
  45.0 18.6 %all-to-all-start.1 = ((bf16[4,768,128]{2,1,0:T(8,128)(2,1)}), bf16[4,768,128]{2,1,0:T(8,128)(2,1)S(1)}, u32[]{:S(2)}, u32[]{:S(2)}) async-start(bf16[4,768,128]{2,1,0:T(8,128)(2,1)} %broadcast_in_dim.7), calls=%async_computation.1 | async-start | bytes 1572864 | tf_op jit(solution)/shard_map/all_to_all | solution.py:28
  63.7 2.6 %copy-start.3 = (bf16[4,768,128]{2,1,0:T(8,128)(2,1)}, bf16[4,768,128]{2,1,0:T(8,128)(2,1)S(1)}, u32[]{:S(2)}) copy-start(bf16[4,768,128]{2,1,0:T(8,128)(2,1)S(1)} %all-to-all-done.1.near) | copy-start | bytes 2359300
  63.7 2.6 %collective-permute-start.3 = (bf16[4,768,128]{2,1,0:T(8,128)(2,1)S(1)}, bf16[4,768,128]{2,1,0:T(8,128)(2,1)S(1)}, u32[]{:S(2)}, u32[]{:S(2)}) collective-permute-start(bf16[4,768,128]{2,1,0:T(8,128)(2,1)S(1)} %all-to-all-done.1.near), channel_id=1, source_target_pairs={{0,4},{4,0},{1,5},{5,1},{2,6},{6,2},{3,7},{7,3},{8,12},{12,8},{9,1... | collective-permute-start | bytes 2359304 | tf_op jit(solution)/shard_map/ppermute | solution.py:20
  66.2 0.9 copy-start.12
  88.0 4.5 %collective-permute-start.4 = (bf16[8,2,4,128,128]{4,3,2,1,0:T(8,128)(2,1)}, bf16[8,2,4,128,128]{4,3,2,1,0:T(8,128)(2,1)S(1)}, u32[]{:S(2)}, u32[]{:S(2)}) collective-permute-start(bf16[8,2,4,128,128]{4,3,2,1,0:T(8,128)(2,1)} %get-tuple-element.67), channel_id=1, source_target_pairs={{0,4},{4,0},{1,5},{5,1},{2,6},{6,2},{3,7},{7,3},{8,12},{12,8},{9,1... | collective-permute-start | bytes 6291464 | tf_op jit(solution)/shard_map/ppermute | solution.py:20
  96.2 7.3 %copy-start.16 = (bf16[32,512]{1,0:T(8,128)(2,1)S(1)}, bf16[32,512]{1,0:T(8,128)(2,1)}, u32[]{:S(2)}) copy-start(bf16[32,512]{1,0:T(8,128)(2,1)} %get-tuple-element.69) | copy-start | bytes 98308
  96.2 10.4 %copy-start.15 = (bf16[32,512]{1,0:T(8,128)(2,1)S(1)}, bf16[32,512]{1,0:T(8,128)(2,1)}, u32[]{:S(2)}) copy-start(bf16[32,512]{1,0:T(8,128)(2,1)} %get-tuple-element.71) | copy-start | bytes 98308
  96.2 35.4 %all-to-all-start.2 = ((bf16[64,128,128]{2,1,0:T(8,128)(2,1)}), bf16[64,128,128]{2,1,0:T(8,128)(2,1)S(1)}, u32[]{:S(2)}, u32[]{:S(2)}) async-start(bf16[64,128,128]{2,1,0:T(8,128)(2,1)} %bitcast.12), calls=%async_computation.2 | async-start | bytes 4194304 | tf_op jit(solution)/shard_map/all_to_all | solution.py:28
  103.5 28.4 %collective-permute-start.5 = (bf16[32,512]{1,0:T(8,128)(2,1)S(1)}, bf16[32,512]{1,0:T(8,128)(2,1)S(1)}, u32[]{:S(2)}, u32[]{:S(2)}) collective-permute-start(bf16[32,512]{1,0:T(8,128)(2,1)S(1)} %copy-done.16), channel_id=1, source_target_pairs={{0,127},{1,0},{2,1},{3,2},{4,3},{5,4},{6,5},{7,6},{8,7},{9,8},{10,... | collective-permute-start | bytes 98312 | tf_op jit(solution)/shard_map/ppermute | solution.py:24
  106.6 25.3 %collective-permute-start.6 = (bf16[32,512]{1,0:T(8,128)(2,1)S(1)}, bf16[32,512]{1,0:T(8,128)(2,1)S(1)}, u32[]{:S(2)}, u32[]{:S(2)}) collective-permute-start(bf16[32,512]{1,0:T(8,128)(2,1)S(1)} %copy-done.15), channel_id=1, source_target_pairs={{0,1},{1,2},{2,3},{3,4},{4,5},{5,6},{6,7},{7,8},{8,9},{9,10},{10,1... | collective-permute-start | bytes 98312 | tf_op jit(solution)/shard_map/ppermute | solution.py:24
  131.9 18.3 %copy-start.5 = (bf16[128,128]{1,0:T(8,128)(2,1)}, bf16[128,128]{1,0:T(8,128)(2,1)S(1)}, u32[]{:S(2)}) copy-start(bf16[128,128]{1,0:T(8,128)(2,1)S(1)} %reduce_sum.12.own) | copy-start | bytes 98308
  131.9 18.3 %copy-start.7 = (bf16[32,512]{1,0:T(8,128)(2,1)}, bf16[32,512]{1,0:T(8,128)(2,1)S(1)}, u32[]{:S(2)}) copy-start(bf16[32,512]{1,0:T(8,128)(2,1)S(1)} %collective-permute-done.5.ahead) | copy-start | bytes 98308
  131.9 18.2 %copy-start.8 = (bf16[32,512]{1,0:T(8,128)(2,1)}, bf16[32,512]{1,0:T(8,128)(2,1)S(1)}, u32[]{:S(2)}) copy-start(bf16[32,512]{1,0:T(8,128)(2,1)S(1)} %collective-permute-done.6.behind) | copy-start | bytes 98308
  145.8 4.4 %copy-start.1 = (bf16[16,112,128]{2,1,0:T(8,128)(2,1)}, bf16[16,112,128]{2,1,0:T(8,128)(2,1)S(1)}, u32[]{:S(2)}) copy-start(bf16[16,112,128]{2,1,0:T(8,128)(2,1)S(1)} %all_to_all.20.tiles) | copy-start | bytes 1376260
  145.8 4.3 %collective-permute-start.7 = (bf16[16,112,128]{2,1,0:T(8,128)(2,1)S(1)}, bf16[16,112,128]{2,1,0:T(8,128)(2,1)S(1)}, u32[]{:S(2)}, u32[]{:S(2)}) collective-permute-start(bf16[16,112,128]{2,1,0:T(8,128)(2,1)S(1)} %all_to_all.20.tiles), channel_id=1, source_target_pairs={{0,4},{4,0},{1,5},{5,1},{2,6},{6,2},{3,7},{7,3},{8,12},{12,8},{9,1... | collective-permute-start | bytes 1376264 | tf_op jit(solution)/shard_map/ppermute | solution.py:20
  150.2 0.8 copy-start.4

commit v5 on v4

--- a/solution.py
+++ b/solution.py
@@ -10,8 +10,8 @@
 BF16 = jnp.bfloat16
 F32 = jnp.float32
 BOTH = ("z", "x", "core", "feat")
-CHUNK = 512
-STEPS = 4
+CHUNK = 1024
+STEPS = 2
 TABLE = 896
 VMEM_BYTES = 60 * 1024 * 1024
 
@@ -75,8 +75,9 @@
     return [jnp.where(spread == lanes + 128 * j, 1.0, 0.0).astype(BF16) for j in range(count)]
 
 
-def hot_kernel(co, src, dst, src_wide, dst_wide, hot, turned):
+def hot_kernel(co, src, dst, src_wide, dst_wide, edge, hot, turned, edge_turned):
     step = pl.program_id(0)
+    edge_turned[...] = jnp.transpose(edge[...])
     lanes = lax.broadcasted_iota(jnp.int32, (1, 128), 1)
     for r in range(CHUNK // 128):
         row = pl.ds(step * (CHUNK // 128) + r, 1)
@@ -92,7 +93,8 @@
         turned[j * 128 : (j + 1) * 128, :] = jnp.where(match, 1.0, 0.0).astype(BF16)
 
 
-def pack_kernel(co, node, targets, edge_first, edge_second, tiles, to_next, to_prev):
+def pack_kernel(co, node, targets, edge_first, edge_second, first, second, *outs):
+    tiles, to_next, to_prev, packed = outs
     match = lax.broadcasted_iota(jnp.int32, (256, 128), 0) == targets[...]
     rows = dot_tn(jnp.where(match, 1.0, 0.0).astype(BF16), node[...])
     to_next[...] = rows[0:32].astype(BF16)
@@ -110,6 +112,14 @@
     tile = jnp.concatenate(parts, axis=0)
     for k in range(64):
         tiles[k] = tile
+    at = pl.ds(pl.multiple_of(co[2] * 256, 256), 256)
+    row = pl.ds(pl.multiple_of(co[2] * 64, 64), 64)
+    for y in range(4):
+        for m in range(2):
+            packed[y, m * 256 : (m + 1) * 256, :] = first[m, at, :]
+        for b in range(4):
+            rows = slice(512 + b * 64, 576 + b * 64)
+            packed[y, rows, :] = second[row, b * 128 : (b + 1) * 128]
 
 
 def live_rows(step, count):
@@ -235,7 +245,7 @@
 
 def backward_kernel(co, node, incoming, grad_node, near, far, *refs):
     edge_first, edge_second, lookup = refs[:3]
-    edge, act, normed, slope, factor, grad_edge, hot, turned = refs[3:11]
+    edge_turned, act, normed, slope, factor, grad_edge, hot, turned = refs[3:11]
     node_out, node_total, edge_grad, to_prev, to_next, keep, give = refs[11:18]
     first, second, spread, sum_second, sum_first, sums, columns, rows, owned = refs[18:]
     step = pl.program_id(0)
@@ -272,7 +282,7 @@
         edge_grad[h, :] = (total + dot_nt(pre_grad, whole(edge_first, 0))).astype(BF16)
     pre_grad = jnp.concatenate(pre_grads, axis=0)
     sum_second[...] += dot_tn(act[...], jnp.concatenate(deltas, axis=0))
-    sum_first[...] += dot_tn(edge[...], pre_grad)
+    sum_first[...] += dot(edge_turned[...], pre_grad)
     sums[...] += dot(turned[...], pre_grad)
 
     @pl.when(step == STEPS - 1)
@@ -343,16 +353,14 @@
     return pl.BlockSpec(dims, lambda i: (i,) + (0,) * (len(dims) - 1))
 
 
+def column(*dims):
+    return pl.BlockSpec(dims, lambda i: (0, i))
+
+
 def like(value):
-    return same(*value.shape)
-
-
-def halves(first, second, core):
-    kinds = first.shape[0]
-    top = lax.dynamic_slice_in_dim(first, core * 256, 256, 1).reshape(kinds * 256, 128)
-    rest = lax.dynamic_slice_in_dim(second, core * 64, 64, 0)
-    rest = rest.reshape(64, 4, 128).transpose(1, 0, 2).reshape(256, 128)
-    return jnp.concatenate([top, rest], axis=0)
+    dims = value.shape
+    once = pl.Buffered(buffer_count=1)
+    return pl.BlockSpec(dims, lambda i: (0,) * len(dims), pipeline_mode=once)
 
 
 def shards(
@@ -377,11 +385,11 @@
     unused = jnp.full((48,), -1, jnp.int32)
     targets = jnp.concatenate([lists[1], lists[0], jnp.tile(owned, 4), unused]).reshape(1, 128)
 
-    packed, to_next, to_prev = plain_call(
+    packed, to_next, to_prev, node_half = plain_call(
         pack_kernel,
         [co],
-        [node_lat, targets, edge_w1, edge_w2],
-        [shape(64, 80, 128), shape(32, 512), shape(32, 512)],
+        [node_lat, targets, edge_w1, edge_w2, node_w1, node_w2],
+        [shape(64, 80, 128), shape(32, 512), shape(32, 512), shape(4, 768, 128)],
     )
     from_prev = shifted(to_next, 1)
     from_next = shifted(to_prev, -1)
@@ -391,21 +399,21 @@
     indices = [after(value, packed) for value in indices]
     params = pltpu.CompilerParams(vmem_limit_bytes=VMEM_BYTES, dimension_semantics=("arbitrary",))
     high = TABLE + 256
-    hot, turned = pl.pallas_call(
+    wide = chunk(CHUNK, 512)
+    hot, turned, edge_turned = pl.pallas_call(
         hot_kernel,
         grid=(STEPS,),
-        in_specs=[SMEM] + [like(v) for v in indices],
-        out_specs=[chunk(CHUNK, high), pl.BlockSpec((high, CHUNK), lambda i: (0, i))],
-        out_shape=[shape(2048, high), shape(high, 2048)],
+        in_specs=[SMEM] + [like(v) for v in indices] + [wide],
+        out_specs=[chunk(CHUNK, high), column(high, CHUNK), column(512, CHUNK)],
+        out_shape=[shape(2048, high), shape(high, 2048), shape(512, 2048)],
         compiler_params=params,
         cost_estimate=pl.CostEstimate(
-            flops=20_000_000, bytes_accessed=10_000_000, transcendentals=0
+            flops=20_000_000, bytes_accessed=14_000_000, transcendentals=0
         ),
-    )(co, *indices)
+    )(co, *indices, edge_lat)
     near = after(near, from_prev, from_next, hot)
     far = other_core(near)
-    node_half = after(repeated(halves(node_w1, node_w2, core), 4), near, far)
-    node_near = exchange(node_half, "feat")
+    node_near = exchange(after(node_half, near, far), "feat")
 
     fixed = [node_lat, from_prev, from_next, near, far]
     wide = chunk(CHUNK, 512)
@@ -414,7 +422,7 @@
         grid=(STEPS,),
         in_specs=[SMEM]
         + [like(v) for v in fixed]
-        + [wide, chunk(CHUNK, high), pl.BlockSpec((256, CHUNK), lambda i: (0, i))],
+        + [wide, chunk(CHUNK, high), column(256, CHUNK)],
         out_specs=[wide, same(256, 512), wide, wide, wide, chunk(CHUNK, 128)]
         + [same(TABLE, 512), same(3, 16, 2, 16, 512), same(512, 512)],
         out_shape=[
@@ -443,15 +451,15 @@
     node_far = other_core(node_near)
     fixed = [node_lat, incoming, grad_node, node_near, node_far]
     fixed += [first, second, lookup]
-    moving = [edge_lat, act, normed, slope, factor, grad_edge, hot, turned]
+    moving = [edge_turned, act, normed, slope, factor, grad_edge, hot, turned]
     tiles = (8, 2, 4, 128, 128)
     node_out, node_total, edge_grad, to_prev, to_next, keep, give = pl.pallas_call(
         backward_kernel,
         grid=(STEPS,),
         in_specs=[SMEM]
         + [like(v) for v in fixed]
-        + [wide, wide, wide, wide, chunk(CHUNK, 128), wide, chunk(CHUNK, 256)]
-        + [pl.BlockSpec((high, CHUNK), lambda i: (0, i))],
+        + [column(512, CHUNK), wide, wide, wide, chunk(CHUNK, 128), wide, chunk(CHUNK, 256)]
+        + [column(high, CHUNK)],
         out_specs=[same(256, 512), same(256, 512), wide, same(32, 512), same(32, 512)]
         + [same(*tiles), same(*tiles)],
         out_shape=[

time: 155 us -> 155 us (level)
  Pallas kernels: 46.4 us -> 49.8 us
  transfers between devices with their start and end apart: 11 -> 11, of which waited for: 7 -> 6; matrix products, arithmetic and copies ran while one was open for 1% -> 1% of each run, Pallas kernels for 13% -> 14%
where the time goes in v5:
time: 155 us
  Pallas kernels  49.8 us (32%)
  waiting for transfers between devices  43.6 us (28%)
  starting transfers between devices  36.1 us (23%)
  blocking collectives  13.8 us (9%)
  local copies, waits for them, and re-layouts  5.09 us (3%)
  other arithmetic  4.68 us (3%)
    all_to_all x3, waiting for transfers between devices, exchange(): return lax.all_to_all(value, axes, 0, 0, tiled=True)  33.6 us
    all_to_all x3, starting transfers between devices, exchange(): return lax.all_to_all(value, axes, 0, 0, tiled=True)  22.9 us
    pallas_call x1, Pallas kernels, shards(): pl.pallas_call(backward_kernel, grid=(STEPS,), in_specs=[SMEM] + [like(v)...  22 us
    pallas_call x1, Pallas kernels, shards(): pl.pallas_call(forward_kernel, grid=(STEPS,), in_specs=[SMEM] + [like(v)...  15.7 us
    all_to_all x1, blocking collectives, exchange(): return lax.all_to_all(value, axes, 0, 0, tiled=True)  13.8 us
    ppermute x4, waiting for transfers between devices, other_core(): return lax.ppermute(value, 'core', [(0, 1), (1, 0)])  10 us
    ppermute x4, starting transfers between devices, shifted(): lax.ppermute(value, BOTH, [(k, (k + steps) % 128) for k in range(128)])  6.62 us
    ppermute x4, starting transfers between devices, other_core(): return lax.ppermute(value, 'core', [(0, 1), (1, 0)])  6.55 us
  transfers between devices with their start and end apart: 11, of which 6 were waited for; matrix products, arithmetic and copies ran while one was open for 1% of the time, Pallas kernels for 14%

profile of v5, /device:TPU:1, one launch (start us, length us, event | category | flops | bytes accessed | tf_op | source)
XLA Modules:
  0.0 154.7 jit_solution(15017335528170463794)
XLA Ops:
  0.6 0.0 copy-start.5
  0.6 0.0 copy-start.6
  1.3 0.8 slice_bitcast_fusion.1
  2.1 0.7 tile.11
  2.7 0.1 tile.12
  2.8 0.6 stack.13.co
  3.4 0.6 add_bitcast_fusion.targets
  4.0 2.9 %shard_map.188 = (bf16[64,80,128]{2,1,0:T(8,128)(2,1)}, bf16[32,512]{1,0:T(8,128)(2,1)}, bf16[32,512]{1,0:T(8,128)(2,1)}, bf16[4,768,128]{2,1,0:T(8,128)(2,1)}) custom-call(s32[5]{0:T(128)} %stack.13.co, bf16[256,512]{1,0:T(8,128)(2,1)} %node.5, s32[1,128]{1,0:T(1,128)} %add_bitcast_fusion.targets, bf16[3,512,128]{2,1,0:T(8,128)(2,1)} %edge_first.1, ...), custom_call_target="tpu_custom_call" | custom-call | tf_op jit(solution)/shard_map/pallas_call | solution.py:338
  6.9 12.1 %all-to-all-start = ((bf16[64,80,128]{2,1,0:T(8,128)(2,1)}), bf16[64,80,128]{2,1,0:T(8,128)(2,1)S(1)}, u32[]{:S(2)}, u32[]{:S(2)}) async-start(bf16[64,80,128]{2,1,0:T(8,128)(2,1)} %get-tuple-element.48), calls=%async_computation | async-start | bytes 2621440 | tf_op jit(solution)/shard_map/all_to_all | solution.py:28
  19.0 1.1 collective-permute-start
  20.1 2.4 %collective-permute-start.1 = (bf16[32,512]{1,0:T(8,128)(2,1)S(1)}, bf16[32,512]{1,0:T(8,128)(2,1)S(1)}, u32[]{:S(2)}, u32[]{:S(2)}) collective-permute-start(bf16[32,512]{1,0:T(8,128)(2,1)S(1)} %copy-done.15), channel_id=1, source_target_pairs={{0,127},{1,0},{2,1},{3,2},{4,3},{5,4},{6,5},{7,6},{8,7},{9,8},{10,... | collective-permute-start | bytes 98312 | tf_op jit(solution)/shard_map/ppermute | solution.py:24
  22.5 0.6 reshape.52.src_wide
  23.1 0.0 copy-done.6
  23.2 0.6 reshape.53.dst_wide
  23.8 6.4 %shard_map.189 = (bf16[2048,1152]{1,0:T(8,128)(2,1)}, bf16[1152,2048]{1,0:T(8,128)(2,1)}, bf16[512,2048]{1,0:T(8,128)(2,1)}) custom-call(s32[5]{0:T(128)} %stack.13.co, s32[16,128]{1,0:T(8,128)} %bitcast.17, s32[16,128]{1,0:T(8,128)} %bitcast.18, s32[2,1024]{1,0:T(2,128)} %reshape.52.src_wide, s32[2,1024]{1,0:T(2,128)} %reshape.53.dst_wide, ...), custom_call_target="tpu_custom_call" | custom-call | flops 20000000 | bytes 14000000 | tf_op jit(solution)/shard_map/pallas_call | solution.py:403
  30.1 0.0 collective-permute-done.prev
  30.1 0.0 collective-permute-done.1.following
  30.1 0.0 copy-start.14
  30.1 8.7 %all-to-all-done = bf16[64,80,128]{2,1,0:T(8,128)(2,1)S(1)} async-done(((bf16[64,80,128]{2,1,0:T(8,128)(2,1)}), bf16[64,80,128]{2,1,0:T(8,128)(2,1)S(1)}, u32[]{:S(2)}, u32[]{:S(2)}) %all-to-all-start) | async-done | bytes 1310752 | tf_op jit(solution)/shard_map/all_to_all | solution.py:28
  38.8 2.6 %collective-permute-start.2 = (bf16[16,4,80,128]{3,2,1,0:T(8,128)(2,1)S(1)}, bf16[16,4,80,128]{3,2,1,0:T(8,128)(2,1)S(1)}, u32[]{:S(2)}, u32[]{:S(2)}) collective-permute-start(bf16[16,4,80,128]{3,2,1,0:T(8,128)(2,1)S(1)} %bitcast.15), channel_id=1, source_target_pairs={{0,4},{4,0},{1,5},{5,1},{2,6},{6,2},{3,7},{7,3},{8,12},{12,8},{9,1... | collective-permute-start | bytes 3932168 | tf_op jit(solution)/shard_map/ppermute | solution.py:20
  41.4 2.7 %collective-permute-done.2.far = bf16[16,4,80,128]{3,2,1,0:T(8,128)(2,1)S(1)} collective-permute-done((bf16[16,4,80,128]{3,2,1,0:T(8,128)(2,1)S(1)}, bf16[16,4,80,128]{3,2,1,0:T(8,128)(2,1)S(1)}, u32[]{:S(2)}, u32[]{:S(2)}) %collective-permute-start.2) | collective-permute-done | bytes 1310752 | tf_op jit(solution)/shard_map/ppermute | solution.py:20
  44.1 3.5 %all-to-all-start.1 = ((bf16[4,768,128]{2,1,0:T(8,128)(2,1)}), bf16[4,768,128]{2,1,0:T(8,128)(2,1)S(1)}, u32[]{:S(2)}, u32[]{:S(2)}) async-start(bf16[4,768,128]{2,1,0:T(8,128)(2,1)} %get-tuple-element.59), calls=%async_computation.1 | async-start | bytes 1572864 | tf_op jit(solution)/shard_map/all_to_all | solution.py:28
  47.6 0.0 copy-done.13
  47.6 0.0 copy-done.14
  47.6 0.0 copy-done.1
  47.6 15.7 %shard_map.190 = (bf16[2048,512]{1,0:T(8,128)(2,1)}, bf16[256,512]{1,0:T(8,128)(2,1)}, bf16[2048,512]{1,0:T(8,128)(2,1)}, bf16[2048,512]{1,0:T(8,128)(2,1)}, bf1...) custom-call(s32[5]{0:T(128)} %stack.13.co, ...), custom_call_target="tpu_custom_call" | custom-call | flops 7000000000 | bytes 18000000 | tf_op jit(solution)/shard_map/pallas_call | solution.py:420
  63.3 0.0 all-to-all-done.1.near
  63.3 0.0 copy-start.2
  63.3 0.6 collective-permute-start.3
  64.0 1.9 %collective-permute-done.3.far = bf16[4,768,128]{2,1,0:T(8,128)(2,1)S(1)} collective-permute-done((bf16[4,768,128]{2,1,0:T(8,128)(2,1)S(1)}, bf16[4,768,128]{2,1,0:T(8,128)(2,1)S(1)}, u32[]{:S(2)}, u32[]{:S(2)}) %collective-permute-start.3) | collective-permute-done | bytes 786464 | tf_op jit(solution)/shard_map/ppermute | solution.py:20
  65.9 0.9 copy-done.10
  66.8 22.0 %shard_map.191 = (bf16[256,512]{1,0:T(8,128)(2,1)}, f32[256,512]{1,0:T(8,128)}, bf16[2048,512]{1,0:T(8,128)(2,1)}, bf16[32,512]{1,0:T(8,128)(2,1)}, bf16[32,512]...) custom-call(s32[5]{0:T(128)} %stack.13.co, bf16[256,512]{1,0:T(8,128)(2,1)} %node.5, ...), custom_call_target="tpu_custom_call" | custom-call | flops 8999999488 | bytes 24000000 | tf_op jit(solution)/shard_map/pallas_call | solution.py:456
  88.8 0.4 collective-permute-start.4
  89.2 4.0 %collective-permute-done.4 = bf16[8,2,4,128,128]{4,3,2,1,0:T(8,128)(2,1)S(1)} collective-permute-done((bf16[8,2,4,128,128]{4,3,2,1,0:T(8,128)(2,1)}, bf16[8,2,4,128,128]{4,3,2,1,0:T(8,128)(2,1)S(1)}, u32[]{:S(2)}, u32[]{:S(2)}) %collective-permute-start.4) | collective-permute-done | bytes 2097184 | tf_op jit(solution)/shard_map/ppermute | solution.py:20
  93.2 3.8 %add_convert_fusion = bf16[8,2,4,128,128]{4,3,2,1,0:T(8,128)(2,1)} fusion(bf16[8,2,4,128,128]{4,3,2,1,0:T(8,128)(2,1)S(1)} %collective-permute-done.4, bf16[8,2,4,128,128]{4,3,2,1,0:T(8,128)(2,1)} %get-tuple-element.70), kind=kLoop, calls=%fused_computation | loop fusion | flops 4194304 | bytes 6291456 | tf_op jit(solution)/shard_map/convert_element_type | solution.py:491
  97.0 7.3 %all-to-all-start.2 = ((bf16[64,128,128]{2,1,0:T(8,128)(2,1)}), bf16[64,128,128]{2,1,0:T(8,128)(2,1)S(1)}, u32[]{:S(2)}, u32[]{:S(2)}) async-start(bf16[64,128,128]{2,1,0:T(8,128)(2,1)} %bitcast.9), calls=%async_computation.2 | async-start | bytes 4194304 | tf_op jit(solution)/shard_map/all_to_all | solution.py:28
  104.3 3.1 %collective-permute-start.5 = (bf16[32,512]{1,0:T(8,128)(2,1)S(1)}, bf16[32,512]{1,0:T(8,128)(2,1)S(1)}, u32[]{:S(2)}, u32[]{:S(2)}) collective-permute-start(bf16[32,512]{1,0:T(8,128)(2,1)S(1)} %copy-done.12), channel_id=1, source_target_pairs={{0,127},{1,0},{2,1},{3,2},{4,3},{5,4},{6,5},{7,6},{8,7},{9,8},{10,... | collective-permute-start | bytes 98312 | tf_op jit(solution)/shard_map/ppermute | solution.py:24
  107.4 0.0 collective-permute-start.6
  107.4 24.9 %all-to-all-done.2 = bf16[64,128,128]{2,1,0:T(8,128)(2,1)S(1)} async-done(((bf16[64,128,128]{2,1,0:T(8,128)(2,1)}), bf16[64,128,128]{2,1,0:T(8,128)(2,1)S(1)}, u32[]{:S(2)}, u32[]{:S(2)}) %all-to-all-start.2) | async-done | bytes 2097184 | tf_op jit(solution)/shard_map/all_to_all | solution.py:28
  132.3 0.3 reduce_sum.12.own
  132.7 0.0 collective-permute-done.5.ahead
  132.7 0.0 collective-permute-done.6.behind
  132.7 0.1 broadcast_in_dim.10
  132.8 13.8 %all_to_all.20.tiles = bf16[16,112,128]{2,1,0:T(8,128)(2,1)S(1)} all-to-all(bf16[16,112,128]{2,1,0:T(8,128)(2,1)S(1)} %broadcast_in_dim.10), channel_id=1, replica_groups=mesh['z'=4,'x'=4,'core'=2,'feat'=4] {'z','x'}, dimensions={0} | all-to-all | bytes 917504 | tf_op jit(solution)/shard_map/all_to_all | solution.py:28
  146.6 2.9 %collective-permute-start.7 = (bf16[16,112,128]{2,1,0:T(8,128)(2,1)S(1)}, bf16[16,112,128]{2,1,0:T(8,128)(2,1)S(1)}, u32[]{:S(2)}, u32[]{:S(2)}) collective-permute-start(bf16[16,112,128]{2,1,0:T(8,128)(2,1)S(1)} %all_to_all.20.tiles), channel_id=1, source_target_pairs={{0,4},{4,0},{1,5},{5,1},{2,6},{6,2},{3,7},{7,3},{8,12},{12,8},{9,1... | collective-permute-start | bytes 1376264 | tf_op jit(solution)/shard_map/ppermute | solution.py:20
  149.5 1.4 collective-permute-done.7.far
  151.0 0.8 copy-done.3
  151.7 2.9 %shard_map.192 = (f32[3,16,2,16,128]{4,3,2,1,0:T(8,128)}, f32[128,512]{1,0:T(8,128)}, f32[2,16,2,16,128]{4,3,2,1,0:T(8,128)}, f32[128,512]{1,0:T(8,128)}, f32[256,512]{1,0:T(8,128)}) custom-call(s32[5]{0:T(128)} %stack.13.co, bf16[16,112,128]{2,1,0:T(8,128)(2,1)} %copy-done, bf16[16,112,128]{2,1,0:T(8,128)(2,1)} %copy-done.3, bf16[128,128]{1,0:T(8,128)(2,1)} %copy-done.4, ...), custom_call_target="tpu_custom_call" | custom-call | tf_op jit(solution)/shard_map/pallas_call | solution.py:338
  (26 shorter events, 0.1 us)
Async XLA Ops:
  0.6 21.9 %copy-start.5 = (s32[2048]{0:T(1024)S(1)}, s32[2048]{0:T(1024)}, u32[]{:S(2)}) copy-start(s32[2048]{0:T(1024)} %param.15) | copy-start | bytes 24580
  0.6 22.5 %copy-start.6 = (s32[2048]{0:T(1024)S(1)}, s32[2048]{0:T(1024)}, u32[]{:S(2)}) copy-start(s32[2048]{0:T(1024)} %param.16) | copy-start | bytes 24580
  6.9 12.1 %copy-start.16 = (bf16[32,512]{1,0:T(8,128)(2,1)S(1)}, bf16[32,512]{1,0:T(8,128)(2,1)}, u32[]{:S(2)}) copy-start(bf16[32,512]{1,0:T(8,128)(2,1)} %get-tuple-element.46) | copy-start | bytes 98308
  6.9 13.2 %copy-start.15 = (bf16[32,512]{1,0:T(8,128)(2,1)S(1)}, bf16[32,512]{1,0:T(8,128)(2,1)}, u32[]{:S(2)}) copy-start(bf16[32,512]{1,0:T(8,128)(2,1)} %get-tuple-element.47) | copy-start | bytes 98308
  6.9 31.9 %all-to-all-start = ((bf16[64,80,128]{2,1,0:T(8,128)(2,1)}), bf16[64,80,128]{2,1,0:T(8,128)(2,1)S(1)}, u32[]{:S(2)}, u32[]{:S(2)}) async-start(bf16[64,80,128]{2,1,0:T(8,128)(2,1)} %get-tuple-element.48), calls=%async_computation | async-start | bytes 2621440 | tf_op jit(solution)/shard_map/all_to_all | solution.py:28
  19.0 11.1 %collective-permute-start = (bf16[32,512]{1,0:T(8,128)(2,1)S(1)}, bf16[32,512]{1,0:T(8,128)(2,1)S(1)}, u32[]{:S(2)}, u32[]{:S(2)}) collective-permute-start(bf16[32,512]{1,0:T(8,128)(2,1)S(1)} %copy-done.16), channel_id=1, source_target_pairs={{0,1},{1,2},{2,3},{3,4},{4,5},{5,6},{6,7},{7,8},{8,9},{9,10},{10,1... | collective-permute-start | bytes 98312 | tf_op jit(solution)/shard_map/ppermute | solution.py:24
  20.1 10.0 %collective-permute-start.1 = (bf16[32,512]{1,0:T(8,128)(2,1)S(1)}, bf16[32,512]{1,0:T(8,128)(2,1)S(1)}, u32[]{:S(2)}, u32[]{:S(2)}) collective-permute-start(bf16[32,512]{1,0:T(8,128)(2,1)S(1)} %copy-done.15), channel_id=1, source_target_pairs={{0,127},{1,0},{2,1},{3,2},{4,3},{5,4},{6,5},{7,6},{8,7},{9,8},{10,... | collective-permute-start | bytes 98312 | tf_op jit(solution)/shard_map/ppermute | solution.py:24
  30.1 17.5 %copy-start.13 = (bf16[32,512]{1,0:T(8,128)(2,1)}, bf16[32,512]{1,0:T(8,128)(2,1)S(1)}, u32[]{:S(2)}) copy-start(bf16[32,512]{1,0:T(8,128)(2,1)S(1)} %collective-permute-done.prev) | copy-start | bytes 98308
  30.1 17.5 %copy-start.14 = (bf16[32,512]{1,0:T(8,128)(2,1)}, bf16[32,512]{1,0:T(8,128)(2,1)S(1)}, u32[]{:S(2)}) copy-start(bf16[32,512]{1,0:T(8,128)(2,1)S(1)} %collective-permute-done.1.following) | copy-start | bytes 98308
  38.8 8.8 %copy-start.1 = (bf16[64,80,128]{2,1,0:T(8,128)(2,1)}, bf16[64,80,128]{2,1,0:T(8,128)(2,1)S(1)}, u32[]{:S(2)}) copy-start(bf16[64,80,128]{2,1,0:T(8,128)(2,1)S(1)} %all-to-all-done) | copy-start | bytes 3932164
  38.8 5.3 %collective-permute-start.2 = (bf16[16,4,80,128]{3,2,1,0:T(8,128)(2,1)S(1)}, bf16[16,4,80,128]{3,2,1,0:T(8,128)(2,1)S(1)}, u32[]{:S(2)}, u32[]{:S(2)}) collective-permute-start(bf16[16,4,80,128]{3,2,1,0:T(8,128)(2,1)S(1)} %bitcast.15), channel_id=1, source_target_pairs={{0,4},{4,0},{1,5},{5,1},{2,6},{6,2},{3,7},{7,3},{8,12},{12,8},{9,1... | collective-permute-start | bytes 3932168 | tf_op jit(solution)/shard_map/ppermute | solution.py:20
  44.1 3.5 %copy-start.9 = (bf16[16,4,80,128]{3,2,1,0:T(8,128)(2,1)}, bf16[16,4,80,128]{3,2,1,0:T(8,128)(2,1)S(1)}, u32[]{:S(2)}) copy-start(bf16[16,4,80,128]{3,2,1,0:T(8,128)(2,1)S(1)} %collective-permute-done.2.far) | copy-start | bytes 3932164
  44.1 19.2 %all-to-all-start.1 = ((bf16[4,768,128]{2,1,0:T(8,128)(2,1)}), bf16[4,768,128]{2,1,0:T(8,128)(2,1)S(1)}, u32[]{:S(2)}, u32[]{:S(2)}) async-start(bf16[4,768,128]{2,1,0:T(8,128)(2,1)} %get-tuple-element.59), calls=%async_computation.1 | async-start | bytes 1572864 | tf_op jit(solution)/shard_map/all_to_all | solution.py:28
  63.3 2.6 %copy-start.2 = (bf16[4,768,128]{2,1,0:T(8,128)(2,1)}, bf16[4,768,128]{2,1,0:T(8,128)(2,1)S(1)}, u32[]{:S(2)}) copy-start(bf16[4,768,128]{2,1,0:T(8,128)(2,1)S(1)} %all-to-all-done.1.near) | copy-start | bytes 2359300
  63.3 2.5 %collective-permute-start.3 = (bf16[4,768,128]{2,1,0:T(8,128)(2,1)S(1)}, bf16[4,768,128]{2,1,0:T(8,128)(2,1)S(1)}, u32[]{:S(2)}, u32[]{:S(2)}) collective-permute-start(bf16[4,768,128]{2,1,0:T(8,128)(2,1)S(1)} %all-to-all-done.1.near), channel_id=1, source_target_pairs={{0,4},{4,0},{1,5},{5,1},{2,6},{6,2},{3,7},{7,3},{8,12},{12,8},{9,1... | collective-permute-start | bytes 2359304 | tf_op jit(solution)/shard_map/ppermute | solution.py:20
  65.9 0.9 copy-start.10
  88.8 4.5 %collective-permute-start.4 = (bf16[8,2,4,128,128]{4,3,2,1,0:T(8,128)(2,1)}, bf16[8,2,4,128,128]{4,3,2,1,0:T(8,128)(2,1)S(1)}, u32[]{:S(2)}, u32[]{:S(2)}) collective-permute-start(bf16[8,2,4,128,128]{4,3,2,1,0:T(8,128)(2,1)} %get-tuple-element.71), channel_id=1, source_target_pairs={{0,4},{4,0},{1,5},{5,1},{2,6},{6,2},{3,7},{7,3},{8,12},{12,8},{9,1... | collective-permute-start | bytes 6291464 | tf_op jit(solution)/shard_map/ppermute | solution.py:20
  97.0 7.3 %copy-start.12 = (bf16[32,512]{1,0:T(8,128)(2,1)S(1)}, bf16[32,512]{1,0:T(8,128)(2,1)}, u32[]{:S(2)}) copy-start(bf16[32,512]{1,0:T(8,128)(2,1)} %get-tuple-element.73) | copy-start | bytes 98308
  97.0 10.4 %copy-start.11 = (bf16[32,512]{1,0:T(8,128)(2,1)S(1)}, bf16[32,512]{1,0:T(8,128)(2,1)}, u32[]{:S(2)}) copy-start(bf16[32,512]{1,0:T(8,128)(2,1)} %get-tuple-element.75) | copy-start | bytes 98308
  97.0 35.3 %all-to-all-start.2 = ((bf16[64,128,128]{2,1,0:T(8,128)(2,1)}), bf16[64,128,128]{2,1,0:T(8,128)(2,1)S(1)}, u32[]{:S(2)}, u32[]{:S(2)}) async-start(bf16[64,128,128]{2,1,0:T(8,128)(2,1)} %bitcast.9), calls=%async_computation.2 | async-start | bytes 4194304 | tf_op jit(solution)/shard_map/all_to_all | solution.py:28
  104.3 28.3 %collective-permute-start.5 = (bf16[32,512]{1,0:T(8,128)(2,1)S(1)}, bf16[32,512]{1,0:T(8,128)(2,1)S(1)}, u32[]{:S(2)}, u32[]{:S(2)}) collective-permute-start(bf16[32,512]{1,0:T(8,128)(2,1)S(1)} %copy-done.12), channel_id=1, source_target_pairs={{0,127},{1,0},{2,1},{3,2},{4,3},{5,4},{6,5},{7,6},{8,7},{9,8},{10,... | collective-permute-start | bytes 98312 | tf_op jit(solution)/shard_map/ppermute | solution.py:24
  107.4 25.2 %collective-permute-start.6 = (bf16[32,512]{1,0:T(8,128)(2,1)S(1)}, bf16[32,512]{1,0:T(8,128)(2,1)S(1)}, u32[]{:S(2)}, u32[]{:S(2)}) collective-permute-start(bf16[32,512]{1,0:T(8,128)(2,1)S(1)} %copy-done.11), channel_id=1, source_target_pairs={{0,1},{1,2},{2,3},{3,4},{4,5},{5,6},{6,7},{7,8},{8,9},{9,10},{10,1... | collective-permute-start | bytes 98312 | tf_op jit(solution)/shard_map/ppermute | solution.py:24
  132.7 18.3 %copy-start.4 = (bf16[128,128]{1,0:T(8,128)(2,1)}, bf16[128,128]{1,0:T(8,128)(2,1)S(1)}, u32[]{:S(2)}) copy-start(bf16[128,128]{1,0:T(8,128)(2,1)S(1)} %reduce_sum.12.own) | copy-start | bytes 98308
  132.7 18.3 %copy-start.7 = (bf16[32,512]{1,0:T(8,128)(2,1)}, bf16[32,512]{1,0:T(8,128)(2,1)S(1)}, u32[]{:S(2)}) copy-start(bf16[32,512]{1,0:T(8,128)(2,1)S(1)} %collective-permute-done.5.ahead) | copy-start | bytes 98308
  132.7 18.3 %copy-start.8 = (bf16[32,512]{1,0:T(8,128)(2,1)}, bf16[32,512]{1,0:T(8,128)(2,1)S(1)}, u32[]{:S(2)}) copy-start(bf16[32,512]{1,0:T(8,128)(2,1)S(1)} %collective-permute-done.6.behind) | copy-start | bytes 98308
  146.6 4.3 %copy-start = (bf16[16,112,128]{2,1,0:T(8,128)(2,1)}, bf16[16,112,128]{2,1,0:T(8,128)(2,1)S(1)}, u32[]{:S(2)}) copy-start(bf16[16,112,128]{2,1,0:T(8,128)(2,1)S(1)} %all_to_all.20.tiles) | copy-start | bytes 1376260
  146.6 4.3 %collective-permute-start.7 = (bf16[16,112,128]{2,1,0:T(8,128)(2,1)S(1)}, bf16[16,112,128]{2,1,0:T(8,128)(2,1)S(1)}, u32[]{:S(2)}, u32[]{:S(2)}) collective-permute-start(bf16[16,112,128]{2,1,0:T(8,128)(2,1)S(1)} %all_to_all.20.tiles), channel_id=1, source_target_pairs={{0,4},{4,0},{1,5},{5,1},{2,6},{6,2},{3,7},{7,3},{8,12},{12,8},{9,1... | collective-permute-start | bytes 1376264 | tf_op jit(solution)/shard_map/ppermute | solution.py:20
  150.9 0.8 copy-start.3

commit v6 on v5

--- a/solution.py
+++ b/solution.py
@@ -10,10 +10,10 @@
 BF16 = jnp.bfloat16
 F32 = jnp.float32
 BOTH = ("z", "x", "core", "feat")
-CHUNK = 1024
-STEPS = 2
+CHUNK = 512
+STEPS = 4
 TABLE = 896
-VMEM_BYTES = 60 * 1024 * 1024
+MIB = 1024 * 1024
 
 
 def other_core(value):
@@ -334,33 +334,38 @@
     return jax.ShapeDtypeStruct(dims, dtype)
 
 
-def plain_call(kernel, scalars, operands, outs, scratch=()):
+def plain_call(kernel, scalars, operands, outs, scratch=(), mib=16):
     return pl.pallas_call(
         kernel,
         in_specs=[SMEM] * len(scalars) + [WHOLE] * len(operands),
         out_specs=[WHOLE] * len(outs),
         out_shape=list(outs),
         scratch_shapes=list(scratch),
-        compiler_params=pltpu.CompilerParams(vmem_limit_bytes=VMEM_BYTES),
+        compiler_params=pltpu.CompilerParams(vmem_limit_bytes=mib * MIB),
     )(*scalars, *operands)
 
 
 def same(*dims):
-    return pl.BlockSpec(dims, lambda i: (0,) * len(dims))
+    once = pl.Buffered(buffer_count=1)
+    return pl.BlockSpec(dims, lambda i: (0,) * len(dims), pipeline_mode=once)
 
 
 def chunk(*dims):
     return pl.BlockSpec(dims, lambda i: (i,) + (0,) * (len(dims) - 1))
 
 
+def limit(mib):
+    return pltpu.CompilerParams(
+        vmem_limit_bytes=mib * MIB, dimension_semantics=("arbitrary",)
+    )
+
+
 def column(*dims):
     return pl.BlockSpec(dims, lambda i: (0, i))
 
 
 def like(value):
-    dims = value.shape
-    once = pl.Buffered(buffer_count=1)
-    return pl.BlockSpec(dims, lambda i: (0,) * len(dims), pipeline_mode=once)
+    return same(*value.shape)
 
 
 def shards(
@@ -397,7 +402,6 @@
     indices = [edge_src.reshape(16, 128), edge_dst.reshape(16, 128)]
     indices += [edge_src.reshape(STEPS, CHUNK), edge_dst.reshape(STEPS, CHUNK)]
     indices = [after(value, packed) for value in indices]
-    params = pltpu.CompilerParams(vmem_limit_bytes=VMEM_BYTES, dimension_semantics=("arbitrary",))
     high = TABLE + 256
     wide = chunk(CHUNK, 512)
     hot, turned, edge_turned = pl.pallas_call(
@@ -406,7 +410,7 @@
         in_specs=[SMEM] + [like(v) for v in indices] + [wide],
         out_specs=[chunk(CHUNK, high), column(high, CHUNK), column(512, CHUNK)],
         out_shape=[shape(2048, high), shape(high, 2048), shape(512, 2048)],
-        compiler_params=params,
+        compiler_params=limit(10),
         cost_estimate=pl.CostEstimate(
             flops=20_000_000, bytes_accessed=14_000_000, transcendentals=0
         ),
@@ -441,7 +445,7 @@
             pltpu.VMEM((256, 512), F32),
             pltpu.VMEM((16, 2, 4, 16, 128), BF16),
         ],
-        compiler_params=params,
+        compiler_params=limit(16),
         cost_estimate=pl.CostEstimate(
             flops=7_000_000_000, bytes_accessed=18_000_000, transcendentals=1_000_000
         ),
@@ -482,7 +486,7 @@
             pltpu.VMEM((4, 512, 128), BF16),
             pltpu.VMEM((16, 2, 4, 16, 128), BF16),
         ],
-        compiler_params=params,
+        compiler_params=limit(24),
         cost_estimate=pl.CostEstimate(
             flops=9_000_000_000, bytes_accessed=24_000_000, transcendentals=100_000
         ),

time: 155 us -> 184 us (1.19)
  local copies, waits for them, and re-layouts: 5.09 us -> 50.8 us
  Pallas kernels: 49.8 us -> 34.7 us
    unnamed x34 -> x80, local copies, waits for them, and re-layouts: 1.72 us -> 49.2 us
    pallas_call x1, Pallas kernels: 22 us -> 16.6 us  [shards(): pl.pallas_call(backward_kernel, grid=(STEPS,), in_specs=[SMEM] + [like(v)...]
    pallas_call x1, Pallas kernels: 15.7 us -> 11 us  [shards(): pl.pallas_call(forward_kernel, grid=(STEPS,), in_specs=[SMEM] + [like(v)...]
    pallas_call x1, Pallas kernels: 6.35 us -> 3.59 us  [shards(): pl.pallas_call(hot_kernel, grid=(STEPS,), in_specs=[SMEM] + [like(v) for...]
    pallas_call x2, Pallas kernels: 5.8 us -> 3.51 us  [plain_call(): pl.pallas_call(kernel, in_specs=[SMEM] * len(scalars) + [WHOLE] * len(ope...]
  transfers between devices with their start and end apart: 11 -> 11, of which waited for: 6 -> 6; matrix products, arithmetic and copies ran while one was open for 1% -> 1% of each run, Pallas kernels for 14% -> 8%
where the time goes in v6:
time: 184 us; the launch traced here: 183 us
  local copies, waits for them, and re-layouts  50.8 us (28%)
  waiting for transfers between devices  41.8 us (23%)
  starting transfers between devices  36.6 us (20%)
  Pallas kernels  34.7 us (19%)
  blocking collectives  13.4 us (7%)
  other arithmetic  4.12 us (2%)
    unnamed x80, local copies, waits for them, and re-layouts  49.2 us
    all_to_all x3, waiting for transfers between devices, exchange(): return lax.all_to_all(value, axes, 0, 0, tiled=True)  31.8 us
    all_to_all x3, starting transfers between devices, exchange(): return lax.all_to_all(value, axes, 0, 0, tiled=True)  23.6 us
    pallas_call x1, Pallas kernels, shards(): pl.pallas_call(backward_kernel, grid=(STEPS,), in_specs=[SMEM] + [like(v)...  16.6 us
    all_to_all x1, blocking collectives, exchange(): return lax.all_to_all(value, axes, 0, 0, tiled=True)  13.4 us
    pallas_call x1, Pallas kernels, shards(): pl.pallas_call(forward_kernel, grid=(STEPS,), in_specs=[SMEM] + [like(v)...  11 us
    ppermute x4, waiting for transfers between devices, other_core(): return lax.ppermute(value, 'core', [(0, 1), (1, 0)])  10 us
    ppermute x4, starting transfers between devices, shifted(): lax.ppermute(value, BOTH, [(k, (k + steps) % 128) for k in range(128)])  6.54 us
  transfers between devices with their start and end apart: 11, of which 6 were waited for; matrix products, arithmetic and copies ran while one was open for 1% of the time, Pallas kernels for 8%

profile of v6, /device:TPU:1, one launch (start us, length us, event | category | flops | bytes accessed | tf_op | source)
XLA Modules:
  0.0 183.1 jit_solution(3886682233178181556)
XLA Ops:
  3.1 1.0 copy-done.3
  7.8 1.4 shard_map.188
  9.3 1.1 copy-done.1
  11.2 12.0 %all-to-all-start = ((bf16[64,80,128]{2,1,0:T(8,128)(2,1)}), bf16[64,80,128]{2,1,0:T(8,128)(2,1)S(1)}, u32[]{:S(2)}, u32[]{:S(2)}) async-start(bf16[64,80,128]{2,1,0:T(8,128)(2,1)} %copy-done.1), calls=%async_computation | async-start | bytes 2621440 | tf_op jit(solution)/shard_map/all_to_all | solution.py:28
  23.2 1.1 collective-permute-start
  24.2 2.4 %collective-permute-start.1 = (bf16[32,512]{1,0:T(8,128)(2,1)S(1)}, bf16[32,512]{1,0:T(8,128)(2,1)S(1)}, u32[]{:S(2)}, u32[]{:S(2)}) collective-permute-start(bf16[32,512]{1,0:T(8,128)(2,1)S(1)} %get-tuple-element.47), channel_id=1, source_target_pairs={{0,127},{1,0},{2,1},{3,2},{4,3},{5,4},{6,5},{7,6},{8,7},{9,8},{10,... | collective-permute-start | bytes 98312 | tf_op jit(solution)/shard_map/ppermute | solution.py:24
  26.7 3.6 %shard_map.189 = (bf16[2048,1152]{1,0:T(8,128)(2,1)S(1)}, bf16[1152,2048]{1,0:T(8,128)(2,1)S(1)}, bf16[512,2048]{1,0:T(8,128)(2,1)S(1)}) custom-call(s32[5]{0:T(128)S(1)} %stack.13.co, s32[16,128]{1,0:T(8,128)S(1)} %bitcast.17, s32[16,128]{1,0:T(8,128)S(1)} %bitcast.18, s32[4,512]{1,0:T(4,128)S(1)} %reshape.52.src_wide, s32[4,512]{1,0:T(4,128)S(1)} %reshape.53.dst_wide, ...), custom_call_target="tpu_custom_call" | custom-call | flops 20000000 | bytes 14000000 | tf_op jit(solution)/shard_map/pallas_call | solution.py:407
  30.3 2.2 %copy-done.12 = bf16[2048,1152]{1,0:T(8,128)(2,1)} copy-done((bf16[2048,1152]{1,0:T(8,128)(2,1)}, bf16[2048,1152]{1,0:T(8,128)(2,1)S(1)}, u32[]{:S(2)}) %copy-start.12) | copy-done | bytes 4718616
  32.5 2.2 %copy-done.15 = bf16[1152,2048]{1,0:T(8,128)(2,1)} copy-done((bf16[1152,2048]{1,0:T(8,128)(2,1)}, bf16[1152,2048]{1,0:T(8,128)(2,1)S(1)}, u32[]{:S(2)}) %copy-start.15) | copy-done | bytes 4718616
  34.7 1.3 copy-done.19
  36.0 7.0 %all-to-all-done = bf16[64,80,128]{2,1,0:T(8,128)(2,1)S(1)} async-done(((bf16[64,80,128]{2,1,0:T(8,128)(2,1)}), bf16[64,80,128]{2,1,0:T(8,128)(2,1)S(1)}, u32[]{:S(2)}, u32[]{:S(2)}) %all-to-all-start) | async-done | bytes 1310752 | tf_op jit(solution)/shard_map/all_to_all | solution.py:28
  43.0 2.6 %collective-permute-start.2 = (bf16[16,4,80,128]{3,2,1,0:T(8,128)(2,1)S(1)}, bf16[16,4,80,128]{3,2,1,0:T(8,128)(2,1)S(1)}, u32[]{:S(2)}, u32[]{:S(2)}) collective-permute-start(bf16[16,4,80,128]{3,2,1,0:T(8,128)(2,1)S(1)} %bitcast.15), channel_id=1, source_target_pairs={{0,4},{4,0},{1,5},{5,1},{2,6},{6,2},{3,7},{7,3},{8,12},{12,8},{9,1... | collective-permute-start | bytes 3932168 | tf_op jit(solution)/shard_map/ppermute | solution.py:20
  45.6 2.7 %collective-permute-done.2.far = bf16[16,4,80,128]{3,2,1,0:T(8,128)(2,1)S(1)} collective-permute-done((bf16[16,4,80,128]{3,2,1,0:T(8,128)(2,1)S(1)}, bf16[16,4,80,128]{3,2,1,0:T(8,128)(2,1)S(1)}, u32[]{:S(2)}, u32[]{:S(2)}) %collective-permute-start.2) | collective-permute-done | bytes 1310752 | tf_op jit(solution)/shard_map/ppermute | solution.py:20
  48.2 1.1 copy-done.21
  49.3 4.2 %all-to-all-start.1 = ((bf16[4,768,128]{2,1,0:T(8,128)(2,1)}), bf16[4,768,128]{2,1,0:T(8,128)(2,1)}, u32[]{:S(2)}, u32[]{:S(2)}) async-start(bf16[4,768,128]{2,1,0:T(8,128)(2,1)} %copy-done.2), calls=%async_computation.1 | async-start | bytes 1572864 | tf_op jit(solution)/shard_map/all_to_all | solution.py:28
  54.4 2.3 %copy-done.13 = bf16[2048,1152]{1,0:T(8,128)(2,1)S(1)} copy-done((bf16[2048,1152]{1,0:T(8,128)(2,1)S(1)}, bf16[2048,1152]{1,0:T(8,128)(2,1)}, u32[]{:S(2)}) %copy-start.13) | copy-done | bytes 4718616
  56.8 2.3 %copy-done.16 = bf16[1152,2048]{1,0:T(8,128)(2,1)S(1)} copy-done((bf16[1152,2048]{1,0:T(8,128)(2,1)S(1)}, bf16[1152,2048]{1,0:T(8,128)(2,1)}, u32[]{:S(2)}) %copy-start.16) | copy-done | bytes 4718616
  59.1 1.3 copy-done.22
  60.4 11.0 %shard_map.190 = (bf16[2048,512]{1,0:T(8,128)(2,1)}, bf16[256,512]{1,0:T(8,128)(2,1)S(1)}, bf16[2048,512]{1,0:T(8,128)(2,1)S(1)}, bf16[2048,512]{1,0:T(8,128)(2,...) custom-call(s32[5]{0:T(128)S(1)} %stack.13.co, ...), custom_call_target="tpu_custom_call" | custom-call | flops 7000000000 | bytes 18000000 | tf_op jit(solution)/shard_map/pallas_call | solution.py:424
  71.5 1.3 copy-done.24
  72.7 1.4 copy-done.26
  74.1 1.3 copy-done.28
  75.4 1.2 copy-done.30
  76.6 1.0 copy-done.32
  80.4 2.1 %collective-permute-done.3.far = bf16[4,768,128]{2,1,0:T(8,128)(2,1)S(1)} collective-permute-done((bf16[4,768,128]{2,1,0:T(8,128)(2,1)}, bf16[4,768,128]{2,1,0:T(8,128)(2,1)S(1)}, u32[]{:S(2)}, u32[]{:S(2)}) %collective-permute-start.3) | collective-permute-done | bytes 786464 | tf_op jit(solution)/shard_map/ppermute | solution.py:20
  82.5 0.9 copy-done.7
  83.4 2.3 %copy-done.14 = bf16[2048,1152]{1,0:T(8,128)(2,1)S(1)} copy-done((bf16[2048,1152]{1,0:T(8,128)(2,1)S(1)}, bf16[2048,1152]{1,0:T(8,128)(2,1)}, u32[]{:S(2)}) %copy-start.14) | copy-done | bytes 4718616
  85.8 2.3 %copy-done.17 = bf16[1152,2048]{1,0:T(8,128)(2,1)S(1)} copy-done((bf16[1152,2048]{1,0:T(8,128)(2,1)S(1)}, bf16[1152,2048]{1,0:T(8,128)(2,1)}, u32[]{:S(2)}) %copy-start.17) | copy-done | bytes 4718616
  88.1 1.6 copy-done.18
  89.7 1.6 copy-done.20
  92.3 1.6 copy-done.25
  93.8 1.6 copy-done.27
  95.4 1.6 copy-done.29
  97.0 1.4 copy-done.31
  98.4 1.2 copy-done.33
  99.7 1.2 copy-done.35
  100.8 1.0 copy-done.37
  102.8 16.6 %shard_map.191 = (bf16[256,512]{1,0:T(8,128)(2,1)}, f32[256,512]{1,0:T(8,128)S(1)}, bf16[2048,512]{1,0:T(8,128)(2,1)}, bf16[32,512]{1,0:T(8,128)(2,1)S(1)}, bf16...) custom-call(s32[5]{0:T(128)S(1)} %stack.13.co, ...), custom_call_target="tpu_custom_call" | custom-call | flops 8999999488 | bytes 24000000 | tf_op jit(solution)/shard_map/pallas_call | solution.py:460
  119.8 3.8 %collective-permute-done.4 = bf16[8,2,4,128,128]{4,3,2,1,0:T(8,128)(2,1)S(1)} collective-permute-done((bf16[8,2,4,128,128]{4,3,2,1,0:T(8,128)(2,1)S(1)}, bf16[8,2,4,128,128]{4,3,2,1,0:T(8,128)(2,1)S(1)}, u32[]{:S(2)}, u32[]{:S(2)}) %collective-permute-start.4) | collective-permute-done | bytes 2097184 | tf_op jit(solution)/shard_map/ppermute | solution.py:20
  123.6 2.1 %add_convert_fusion = bf16[8,2,4,128,128]{4,3,2,1,0:T(8,128)(2,1)} fusion(bf16[8,2,4,128,128]{4,3,2,1,0:T(8,128)(2,1)S(1)} %collective-permute-done.4, bf16[8,2,4,128,128]{4,3,2,1,0:T(8,128)(2,1)S(1)} %get-tuple-element.70), kind=kLoop, calls=%fused_computation | loop fusion | flops 4194304 | bytes 6291456 | tf_op jit(solution)/shard_map/convert_element_type | solution.py:495
  125.7 7.4 %all-to-all-start.2 = ((bf16[64,128,128]{2,1,0:T(8,128)(2,1)}), bf16[64,128,128]{2,1,0:T(8,128)(2,1)}, u32[]{:S(2)}, u32[]{:S(2)}) async-start(bf16[64,128,128]{2,1,0:T(8,128)(2,1)} %bitcast.19), calls=%async_computation.2 | async-start | bytes 4194304 | tf_op jit(solution)/shard_map/all_to_all | solution.py:28
  133.2 3.0 %collective-permute-start.5 = (bf16[32,512]{1,0:T(8,128)(2,1)S(1)}, bf16[32,512]{1,0:T(8,128)(2,1)S(1)}, u32[]{:S(2)}, u32[]{:S(2)}) collective-permute-start(bf16[32,512]{1,0:T(8,128)(2,1)S(1)} %get-tuple-element.73), channel_id=1, source_target_pairs={{0,127},{1,0},{2,1},{3,2},{4,3},{5,4},{6,5},{7,6},{8,7},{9,8},{10,... | collective-permute-start | bytes 98312 | tf_op jit(solution)/shard_map/ppermute | solution.py:24
  136.2 24.8 %all-to-all-done.2 = bf16[64,128,128]{2,1,0:T(8,128)(2,1)} async-done(((bf16[64,128,128]{2,1,0:T(8,128)(2,1)}), bf16[64,128,128]{2,1,0:T(8,128)(2,1)}, u32[]{:S(2)}, u32[]{:S(2)}) %all-to-all-start.2) | async-done | bytes 2097184 | tf_op jit(solution)/shard_map/all_to_all | solution.py:28
  161.1 1.9 %reduce_sum.12.own = bf16[128,128]{1,0:T(8,128)(2,1)S(1)} reduce(bf16[64,128,128]{2,1,0:T(8,128)(2,1)} %all-to-all-done.2, bf16[]{:T(256)} %constant.22.clone.1), dimensions={0}, to_apply=%region_0.0 | reduce | flops 1032192 | bytes 2129922 | tf_op jit(solution)/shard_map/reduce_sum | solution.py:498
  163.1 13.4 %all_to_all.20.tiles = bf16[16,112,128]{2,1,0:T(8,128)(2,1)S(1)} all-to-all(bf16[16,112,128]{2,1,0:T(8,128)(2,1)S(1)} %broadcast_in_dim.10), channel_id=1, replica_groups=mesh['z'=4,'x'=4,'core'=2,'feat'=4] {'z','x'}, dimensions={0} | all-to-all | bytes 917504 | tf_op jit(solution)/shard_map/all_to_all | solution.py:28
  176.5 3.1 %collective-permute-start.7 = (bf16[16,112,128]{2,1,0:T(8,128)(2,1)S(1)}, bf16[16,112,128]{2,1,0:T(8,128)(2,1)S(1)}, u32[]{:S(2)}, u32[]{:S(2)}) collective-permute-start(bf16[16,112,128]{2,1,0:T(8,128)(2,1)S(1)} %all_to_all.20.tiles), channel_id=1, source_target_pairs={{0,4},{4,0},{1,5},{5,1},{2,6},{6,2},{3,7},{7,3},{8,12},{12,8},{9,1... | collective-permute-start | bytes 1376264 | tf_op jit(solution)/shard_map/ppermute | solution.py:20
  179.6 1.4 collective-permute-done.7.far
  181.0 2.1 %shard_map.192 = (f32[3,16,2,16,128]{4,3,2,1,0:T(8,128)}, f32[128,512]{1,0:T(8,128)}, f32[2,16,2,16,128]{4,3,2,1,0:T(8,128)}, f32[128,512]{1,0:T(8,128)}, f32[256,512]{1,0:T(8,128)}) custom-call(s32[5]{0:T(128)S(1)} %stack.13.co, bf16[16,112,128]{2,1,0:T(8,128)(2,1)S(1)} %all_to_all.20.tiles, bf16[16,112,128]{2,1,0:T(8,128)(2,1)S(1)} %collective-permute-done.7.far, ...), custom_call_target="tpu_custom_call" | custom-call | tf_op jit(solution)/shard_map/pallas_call | solution.py:338
  (72 shorter events, 12.4 us)
Async XLA Ops:
  0.6 26.1 %copy-start = (bf16[2048,512]{1,0:T(8,128)(2,1)S(1)}, bf16[2048,512]{1,0:T(8,128)(2,1)}, u32[]{:S(2)}) copy-start(bf16[2048,512]{1,0:T(8,128)(2,1)} %edge.3) | copy-start | bytes 6291460
  3.1 1.0 copy-start.3
  4.1 0.9 copy-start.4
  5.1 0.9 copy-start.5
  6.0 0.9 copy-start.8
  6.9 0.9 copy-start.9
  7.8 18.8 %copy-start.10 = (s32[2048]{0:T(1024)S(1)}, s32[2048]{0:T(1024)}, u32[]{:S(2)}) copy-start(s32[2048]{0:T(1024)} %param.15) | copy-start | bytes 24580
  7.8 18.9 %copy-start.11 = (s32[2048]{0:T(1024)S(1)}, s32[2048]{0:T(1024)}, u32[]{:S(2)}) copy-start(s32[2048]{0:T(1024)} %param.16) | copy-start | bytes 24580
  9.3 1.1 copy-start.1
  11.2 31.8 %all-to-all-start = ((bf16[64,80,128]{2,1,0:T(8,128)(2,1)}), bf16[64,80,128]{2,1,0:T(8,128)(2,1)S(1)}, u32[]{:S(2)}, u32[]{:S(2)}) async-start(bf16[64,80,128]{2,1,0:T(8,128)(2,1)} %copy-done.1), calls=%async_computation | async-start | bytes 2621440 | tf_op jit(solution)/shard_map/all_to_all | solution.py:28
  23.2 12.8 %collective-permute-start = (bf16[32,512]{1,0:T(8,128)(2,1)}, bf16[32,512]{1,0:T(8,128)(2,1)S(1)}, u32[]{:S(2)}, u32[]{:S(2)}) collective-permute-start(bf16[32,512]{1,0:T(8,128)(2,1)} %get-tuple-element.46), channel_id=1, source_target_pairs={{0,1},{1,2},{2,3},{3,4},{4,5},{5,6},{6,7},{7,8},{8,9},{9,10},{10,1... | collective-permute-start | bytes 98312 | tf_op jit(solution)/shard_map/ppermute | solution.py:24
  24.2 11.7 %collective-permute-start.1 = (bf16[32,512]{1,0:T(8,128)(2,1)S(1)}, bf16[32,512]{1,0:T(8,128)(2,1)S(1)}, u32[]{:S(2)}, u32[]{:S(2)}) collective-permute-start(bf16[32,512]{1,0:T(8,128)(2,1)S(1)} %get-tuple-element.47), channel_id=1, source_target_pairs={{0,127},{1,0},{2,1},{3,2},{4,3},{5,4},{6,5},{7,6},{8,7},{9,8},{10,... | collective-permute-start | bytes 98312 | tf_op jit(solution)/shard_map/ppermute | solution.py:24
  30.3 2.2 %copy-start.12 = (bf16[2048,1152]{1,0:T(8,128)(2,1)}, bf16[2048,1152]{1,0:T(8,128)(2,1)S(1)}, u32[]{:S(2)}) copy-start(bf16[2048,1152]{1,0:T(8,128)(2,1)S(1)} %get-tuple-element.53.hot.refs_9_) | copy-start | bytes 14155780
  32.5 2.2 %copy-start.15 = (bf16[1152,2048]{1,0:T(8,128)(2,1)}, bf16[1152,2048]{1,0:T(8,128)(2,1)S(1)}, u32[]{:S(2)}) copy-start(bf16[1152,2048]{1,0:T(8,128)(2,1)S(1)} %get-tuple-element.55.turned.refs_10_) | copy-start | bytes 14155780
  34.7 1.3 copy-start.19
  43.0 5.3 %collective-permute-start.2 = (bf16[16,4,80,128]{3,2,1,0:T(8,128)(2,1)S(1)}, bf16[16,4,80,128]{3,2,1,0:T(8,128)(2,1)S(1)}, u32[]{:S(2)}, u32[]{:S(2)}) collective-permute-start(bf16[16,4,80,128]{3,2,1,0:T(8,128)(2,1)S(1)} %bitcast.15), channel_id=1, source_target_pairs={{0,4},{4,0},{1,5},{5,1},{2,6},{6,2},{3,7},{7,3},{8,12},{12,8},{9,1... | collective-permute-start | bytes 3932168 | tf_op jit(solution)/shard_map/ppermute | solution.py:20
  48.2 1.1 copy-start.21
  49.3 30.7 %all-to-all-start.1 = ((bf16[4,768,128]{2,1,0:T(8,128)(2,1)}), bf16[4,768,128]{2,1,0:T(8,128)(2,1)}, u32[]{:S(2)}, u32[]{:S(2)}) async-start(bf16[4,768,128]{2,1,0:T(8,128)(2,1)} %copy-done.2), calls=%async_computation.1 | async-start | bytes 1572864 | tf_op jit(solution)/shard_map/all_to_all | solution.py:28
  53.5 1.0 copy-start.6
  54.4 2.3 %copy-start.13 = (bf16[2048,1152]{1,0:T(8,128)(2,1)S(1)}, bf16[2048,1152]{1,0:T(8,128)(2,1)}, u32[]{:S(2)}) copy-start(bf16[2048,1152]{1,0:T(8,128)(2,1)} %copy-done.12) | copy-start | bytes 14155780
  56.8 2.3 %copy-start.16 = (bf16[1152,2048]{1,0:T(8,128)(2,1)S(1)}, bf16[1152,2048]{1,0:T(8,128)(2,1)}, u32[]{:S(2)}) copy-start(bf16[1152,2048]{1,0:T(8,128)(2,1)} %copy-done.15) | copy-start | bytes 14155780
  59.1 1.3 copy-start.22
  71.5 1.3 copy-start.24
  72.7 1.4 copy-start.26
  74.1 1.3 copy-start.28
  75.4 1.2 copy-start.30
  76.6 1.0 copy-start.32
  77.6 0.9 copy-start.34
  80.0 2.5 %collective-permute-start.3 = (bf16[4,768,128]{2,1,0:T(8,128)(2,1)}, bf16[4,768,128]{2,1,0:T(8,128)(2,1)S(1)}, u32[]{:S(2)}, u32[]{:S(2)}) collective-permute-start(bf16[4,768,128]{2,1,0:T(8,128)(2,1)} %all-to-all-done.1.near), channel_id=1, source_target_pairs={{0,4},{4,0},{1,5},{5,1},{2,6},{6,2},{3,7},{7,3},{8,12},{12,8},{9,1... | collective-permute-start | bytes 2359304 | tf_op jit(solution)/shard_map/ppermute | solution.py:20
  82.5 1.0 copy-start.7
  83.4 2.3 %copy-start.14 = (bf16[2048,1152]{1,0:T(8,128)(2,1)S(1)}, bf16[2048,1152]{1,0:T(8,128)(2,1)}, u32[]{:S(2)}) copy-start(bf16[2048,1152]{1,0:T(8,128)(2,1)} %copy-done.12) | copy-start | bytes 14155780
  85.8 2.3 %copy-start.17 = (bf16[1152,2048]{1,0:T(8,128)(2,1)S(1)}, bf16[1152,2048]{1,0:T(8,128)(2,1)}, u32[]{:S(2)}) copy-start(bf16[1152,2048]{1,0:T(8,128)(2,1)} %copy-done.15) | copy-start | bytes 14155780
  88.1 1.6 copy-start.18
  89.7 1.6 copy-start.20
  91.3 0.9 copy-start.23
  92.3 1.6 copy-start.25
  93.8 1.6 copy-start.27
  95.4 1.6 copy-start.29
  97.0 1.4 copy-start.31
  98.4 1.2 copy-start.33
  99.7 1.2 copy-start.35
  100.8 1.0 copy-start.37
  101.9 0.9 copy-start.39
  119.4 4.2 %collective-permute-start.4 = (bf16[8,2,4,128,128]{4,3,2,1,0:T(8,128)(2,1)S(1)}, bf16[8,2,4,128,128]{4,3,2,1,0:T(8,128)(2,1)S(1)}, u32[]{:S(2)}, u32[]{:S(2)}) collective-permute-start(bf16[8,2,4,128,128]{4,3,2,1,0:T(8,128)(2,1)S(1)} %get-tuple-element.71), channel_id=1, source_target_pairs={{0,4},{4,0},{1,5},{5,1},{2,6},{6,2},{3,7},{7,3},{8,12},{12,8},{9,1... | collective-permute-start | bytes 6291464 | tf_op jit(solution)/shard_map/ppermute | solution.py:20
  125.7 35.3 %all-to-all-start.2 = ((bf16[64,128,128]{2,1,0:T(8,128)(2,1)}), bf16[64,128,128]{2,1,0:T(8,128)(2,1)}, u32[]{:S(2)}, u32[]{:S(2)}) async-start(bf16[64,128,128]{2,1,0:T(8,128)(2,1)} %bitcast.19), calls=%async_computation.2 | async-start | bytes 4194304 | tf_op jit(solution)/shard_map/all_to_all | solution.py:28
  133.2 29.8 %collective-permute-start.5 = (bf16[32,512]{1,0:T(8,128)(2,1)S(1)}, bf16[32,512]{1,0:T(8,128)(2,1)S(1)}, u32[]{:S(2)}, u32[]{:S(2)}) collective-permute-start(bf16[32,512]{1,0:T(8,128)(2,1)S(1)} %get-tuple-element.73), channel_id=1, source_target_pairs={{0,127},{1,0},{2,1},{3,2},{4,3},{5,4},{6,5},{7,6},{8,7},{9,8},{10,... | collective-permute-start | bytes 98312 | tf_op jit(solution)/shard_map/ppermute | solution.py:24
  136.2 26.7 %collective-permute-start.6 = (bf16[32,512]{1,0:T(8,128)(2,1)S(1)}, bf16[32,512]{1,0:T(8,128)(2,1)S(1)}, u32[]{:S(2)}, u32[]{:S(2)}) collective-permute-start(bf16[32,512]{1,0:T(8,128)(2,1)S(1)} %get-tuple-element.75), channel_id=1, source_target_pairs={{0,1},{1,2},{2,3},{3,4},{4,5},{5,6},{6,7},{7,8},{8,9},{9,10},{10,1... | collective-permute-start | bytes 98312 | tf_op jit(solution)/shard_map/ppermute | solution.py:24
  176.5 4.5 %collective-permute-start.7 = (bf16[16,112,128]{2,1,0:T(8,128)(2,1)S(1)}, bf16[16,112,128]{2,1,0:T(8,128)(2,1)S(1)}, u32[]{:S(2)}, u32[]{:S(2)}) collective-permute-start(bf16[16,112,128]{2,1,0:T(8,128)(2,1)S(1)} %all_to_all.20.tiles), channel_id=1, source_target_pairs={{0,4},{4,0},{1,5},{5,1},{2,6},{6,2},{3,7},{7,3},{8,12},{12,8},{9,1... | collective-permute-start | bytes 1376264 | tf_op jit(solution)/shard_map/ppermute | solution.py:20
  (3 other events, 2.4 us)

commit v7 on v6

--- a/solution.py
+++ b/solution.py
@@ -75,22 +75,30 @@
     return [jnp.where(spread == lanes + 128 * j, 1.0, 0.0).astype(BF16) for j in range(count)]
 
 
-def hot_kernel(co, src, dst, src_wide, dst_wide, edge, hot, turned, edge_turned):
+def turned_rows(row, count):
+    place = lax.broadcasted_iota(jnp.int32, (128, CHUNK), 0)
+    return [jnp.where(place + 128 * j == row, 1.0, 0.0).astype(BF16) for j in range(count)]
+
+
+def live_targets(step, row, count):
+    lanes = lax.broadcasted_iota(jnp.int32, row.shape, 1)
+    return jnp.where(lanes + step * CHUNK < count, row, -1)
+
+
+def hot_kernel(co, dst, src_wide, dst_wide, edge, hot, turned, edge_turned):
     step = pl.program_id(0)
     edge_turned[...] = jnp.transpose(edge[...])
     lanes = lax.broadcasted_iota(jnp.int32, (1, 128), 1)
     for r in range(CHUNK // 128):
         row = pl.ds(step * (CHUNK // 128) + r, 1)
         live = lanes + step * CHUNK + r * 128 < co[4]
-        tiles = hot_tiles(jnp.where(live, dst[row, :], -1), 2) + hot_tiles(src[row, :], 7)
+        tiles = hot_tiles(jnp.where(live, dst[row, :], -1), 2)
         hot[r * 128 : (r + 1) * 128, :] = jnp.concatenate(tiles, axis=1)
-    place = lax.broadcasted_iota(jnp.int32, (128, CHUNK), 0)
-    lanes = lax.broadcasted_iota(jnp.int32, (1, CHUNK), 1)
-    src_row = src_wide[pl.ds(step, 1), :]
-    dst_row = jnp.where(lanes + step * CHUNK < co[4], dst_wide[pl.ds(step, 1), :], -1)
-    for j in range(9):
-        match = place + 128 * j == dst_row if j < 2 else place + 128 * (j - 2) == src_row
-        turned[j * 128 : (j + 1) * 128, :] = jnp.where(match, 1.0, 0.0).astype(BF16)
+    at = pl.ds(step, 1)
+    blocks = turned_rows(live_targets(step, dst_wide[at, :], co[4]), 2)
+    blocks += turned_rows(src_wide[at, :], 7)
+    for j, block in enumerate(blocks):
+        turned[j * 128 : (j + 1) * 128, :] = block
 
 
 def pack_kernel(co, node, targets, edge_first, edge_second, first, second, *outs):
@@ -114,12 +122,10 @@
         tiles[k] = tile
     at = pl.ds(pl.multiple_of(co[2] * 256, 256), 256)
     row = pl.ds(pl.multiple_of(co[2] * 64, 64), 64)
-    for y in range(4):
-        for m in range(2):
-            packed[y, m * 256 : (m + 1) * 256, :] = first[m, at, :]
-        for b in range(4):
-            rows = slice(512 + b * 64, 576 + b * 64)
-            packed[y, rows, :] = second[row, b * 128 : (b + 1) * 128]
+    for m in range(2):
+        packed[m * 256 : (m + 1) * 256, :] = first[m, at, :]
+    for b in range(4):
+        packed[512 + b * 64 : 576 + b * 64, :] = second[row, b * 128 : (b + 1) * 128]
 
 
 def live_rows(step, count):
@@ -130,17 +136,24 @@
 HALVES = (slice(0, CHUNK // 2), slice(CHUNK // 2, CHUNK))
 
 
-def place_weights(core, near, far, first, second):
-    kinds = first.shape[0]
-    for part, half in ((near, core), (far, 1 - core)):
-        for y in range(4):
+def place_weights(co, own_first, own_second, near, far, first, second):
+    core, y = co[2], co[3]
+    for s in range(4):
+        yy = (y - s) & 3
+        columns = pl.ds(pl.multiple_of(yy * 128, 128), 128)
+        if s == 0:
+            for m in range(2):
+                first[m, :, columns] = own_first[m]
+            second[columns, :] = own_second[...]
+            continue
+        for part, half in ((near[s - 1], core), (far[s - 1], 1 - core)):
             rows = pl.ds(pl.multiple_of(half * 256, 256), 256)
-            for m in range(kinds):
-                first[m, rows, y * 128 : (y + 1) * 128] = part[y, m * 256 : (m + 1) * 256, :]
-            rows = pl.ds(pl.multiple_of(y * 128 + half * 64, 64), 64)
+            for m in range(2):
+                first[m, rows, columns] = part[m * 256 : (m + 1) * 256, :]
+            rows = pl.ds(pl.multiple_of(yy * 128 + half * 64, 64), 64)
             for b in range(4):
-                start = kinds * 256 + b * 64
-                second[rows, b * 128 : (b + 1) * 128] = part[y, start : start + 64, :]
+                start = 512 + b * 64
+                second[rows, b * 128 : (b + 1) * 128] = part[start : start + 64, :]
 
 
 def whole(first, m):
@@ -169,7 +182,7 @@
         lookup[320:832, half * 256 + 128 : half * 256 + 256] = other_block.astype(BF16)
 
 
-def forward_kernel(co, node, prev, following, near, far, edge, hot, turned, *refs):
+def forward_kernel(co, node, prev, following, near, far, src, dst, dst_wide, edge, *refs):
     edge_out, incoming, act_out, normed_out, slope_out, factor_out, lookup, first, second = refs[:9]
     table, total, coarse = refs[9:]
     step = pl.program_id(0)
@@ -185,6 +198,14 @@
         table[256:, :] = dot(lookup[...], whole(first, 1)).astype(BF16)
         total[...] = jnp.zeros_like(total)
 
+    hots = []
+    for r in range(CHUNK // 128):
+        row = pl.ds(step * (CHUNK // 128) + r, 1)
+        tiles = hot_tiles(dst[row, :], 2) + hot_tiles(src[row, :], 7)
+        hots.append(jnp.concatenate(tiles, axis=1))
+    hot = jnp.concatenate(hots, axis=0)
+    turned = turned_rows(live_targets(step, dst_wide[pl.ds(step, 1), :], co[4]), 2)
+    turned = jnp.concatenate(turned, axis=0)
     live = live_rows(step, co[4])
     pres = [dot(edge[h, :], whole(first, 0)) + dot(hot[h, :], table[...]) for h in HALVES]
     acts = []
@@ -201,7 +222,7 @@
         normed_out[h, :] = normed.astype(BF16)
         factor_out[h, :] = jnp.broadcast_to(factor, (CHUNK // 2, 128))
         edge_out[h, :] = (edge[h, :].astype(F32) + normed).astype(BF16)
-    total[...] += dot(turned[...], edge_out[...])
+    total[...] += dot(turned, edge_out[...])
 
     @pl.when(step == STEPS - 1)
     def _():
@@ -243,7 +264,8 @@
         target[:, :, :, 112:128, :] = value
 
 
-def backward_kernel(co, node, incoming, grad_node, near, far, *refs):
+def backward_kernel(co, node, incoming, grad_node, own_first, own_second, *refs):
+    near, far, refs = refs[:3], refs[3:6], refs[6:]
     edge_first, edge_second, lookup = refs[:3]
     edge_turned, act, normed, slope, factor, grad_edge, hot, turned = refs[3:11]
     node_out, node_total, edge_grad, to_prev, to_next, keep, give = refs[11:18]
@@ -252,7 +274,7 @@
 
     @pl.when(step == 0)
     def _():
-        place_weights(co[2], near, far, first, second)
+        place_weights(co, own_first, own_second, near, far, first, second)
         lat, summed = node[...], incoming[...]
         pre = dot(lat, first[0]) + dot(summed, first[1])
         node_act, node_slope = swish(pre)
@@ -385,7 +407,7 @@
 ):
     core = lax.axis_index("core")
     patch = (lax.axis_index("z") * 4 + lax.axis_index("x")) * 2 + core
-    co = jnp.stack([patch, patch, core, core, edge_count[0]]).astype(jnp.int32)
+    co = jnp.stack([patch, patch, core, lax.axis_index("feat"), edge_count[0]]).astype(jnp.int32)
     lists, owned = halo_send[0], coarse_of[0]
     unused = jnp.full((48,), -1, jnp.int32)
     targets = jnp.concatenate([lists[1], lists[0], jnp.tile(owned, 4), unused]).reshape(1, 128)
@@ -394,13 +416,15 @@
         pack_kernel,
         [co],
         [node_lat, targets, edge_w1, edge_w2, node_w1, node_w2],
-        [shape(64, 80, 128), shape(32, 512), shape(32, 512), shape(4, 768, 128)],
+        [shape(64, 80, 128), shape(32, 512), shape(32, 512), shape(768, 128)],
+        mib=60,
     )
     from_prev = shifted(to_next, 1)
     from_next = shifted(to_prev, -1)
     near = exchange(packed, ("z", "x", "feat")).reshape(16, 4, 80, 128)
-    indices = [edge_src.reshape(16, 128), edge_dst.reshape(16, 128)]
-    indices += [edge_src.reshape(STEPS, CHUNK), edge_dst.reshape(STEPS, CHUNK)]
+    src, dst = edge_src.reshape(16, 128), edge_dst.reshape(16, 128)
+    dst_wide = edge_dst.reshape(STEPS, CHUNK)
+    indices = [dst, edge_src.reshape(STEPS, CHUNK), dst_wide]
     indices = [after(value, packed) for value in indices]
     high = TABLE + 256
     wide = chunk(CHUNK, 512)
@@ -408,25 +432,28 @@
         hot_kernel,
         grid=(STEPS,),
         in_specs=[SMEM] + [like(v) for v in indices] + [wide],
-        out_specs=[chunk(CHUNK, high), column(high, CHUNK), column(512, CHUNK)],
-        out_shape=[shape(2048, high), shape(high, 2048), shape(512, 2048)],
-        compiler_params=limit(10),
+        out_specs=[chunk(CHUNK, 256), column(high, CHUNK), column(512, CHUNK)],
+        out_shape=[shape(2048, 256), shape(high, 2048), shape(512, 2048)],
+        compiler_params=limit(60),
         cost_estimate=pl.CostEstimate(
             flops=20_000_000, bytes_accessed=14_000_000, transcendentals=0
         ),
     )(co, *indices, edge_lat)
     near = after(near, from_prev, from_next, hot)
     far = other_core(near)
-    node_near = exchange(after(node_half, near, far), "feat")
-
-    fixed = [node_lat, from_prev, from_next, near, far]
+    node_half = after(node_half, near, far)
+    node_near = [
+        lax.ppermute(node_half, "feat", [(k, (k + s) % 4) for k in range(4)]) for s in (1, 2, 3)
+    ]
+
+    fixed = [node_lat, from_prev, from_next, near, far, src, dst, dst_wide]
     wide = chunk(CHUNK, 512)
     edge_out, incoming, act, normed, slope, factor, lookup, first, second = pl.pallas_call(
         forward_kernel,
         grid=(STEPS,),
         in_specs=[SMEM]
         + [like(v) for v in fixed]
-        + [wide, chunk(CHUNK, high), column(256, CHUNK)],
+        + [wide],
         out_specs=[wide, same(256, 512), wide, wide, wide, chunk(CHUNK, 128)]
         + [same(TABLE, 512), same(3, 16, 2, 16, 512), same(512, 512)],
         out_shape=[
@@ -449,11 +476,11 @@
         cost_estimate=pl.CostEstimate(
             flops=7_000_000_000, bytes_accessed=18_000_000, transcendentals=1_000_000
         ),
-    )(co, *fixed, edge_lat, hot, turned)
-
-    node_near = after(node_near, incoming)
-    node_far = other_core(node_near)
-    fixed = [node_lat, incoming, grad_node, node_near, node_far]
+    )(co, *fixed, edge_lat)
+
+    node_near = [after(part, incoming) for part in node_near]
+    node_far = [other_core(part) for part in node_near]
+    fixed = [node_lat, incoming, grad_node, node_w1, node_w2, *node_near, *node_far]
     fixed += [first, second, lookup]
     moving = [edge_turned, act, normed, slope, factor, grad_edge, hot, turned]
     tiles = (8, 2, 4, 128, 128)

time: 184 us -> 141 us (0.77)
  local copies, waits for them, and re-layouts: 50.8 us -> 4.4 us
  Pallas kernels: 34.7 us -> 38.6 us
    unnamed x80 -> x34, local copies, waits for them, and re-layouts: 49.2 us -> 1.02 us
    all_to_all x3 -> x2, starting transfers between devices: 23.6 us -> 18.7 us  [exchange(): return lax.all_to_all(value, axes, 0, 0, tiled=True)]
    ppermute x0 -> x3, starting transfers between devices: none -> 2.65 us  [shards(): lax.ppermute(node_half, 'feat', [(k, (k + s) % 4) for k in range(4)])]
    all_to_all x3 -> x2, waiting for transfers between devices: 31.8 us -> 34.2 us  [exchange(): return lax.all_to_all(value, axes, 0, 0, tiled=True)]
    pallas_call x1, Pallas kernels: 3.59 us -> 5.83 us  [shards(): pl.pallas_call(hot_kernel, grid=(STEPS,), in_specs=[SMEM] + [like(v) for...]
    ppermute x4 -> x6, waiting for transfers between devices: 10 us -> 9.19 us  [other_core(): return lax.ppermute(value, 'core', [(0, 1), (1, 0)])]
    ppermute x4 -> x6, starting transfers between devices: 6.46 us -> 7.24 us  [other_core(): return lax.ppermute(value, 'core', [(0, 1), (1, 0)])]
  transfers between devices with their start and end apart: 11 -> 15, of which waited for: 6 -> 9; matrix products, arithmetic and copies ran while one was open for 1% -> 1% of each run, Pallas kernels for 8% -> 12%
where the time goes in v7:
time: 141 us; the launch traced here: 140 us
  waiting for transfers between devices  43.5 us (31%)
  Pallas kernels  38.6 us (27%)
  starting transfers between devices  35.2 us (25%)
  blocking collectives  13.8 us (10%)
  local copies, waits for them, and re-layouts  4.4 us (3%)
  other arithmetic  3.36 us (2%)
  between operations  1.52 us (1%)
    all_to_all x2, waiting for transfers between devices, exchange(): return lax.all_to_all(value, axes, 0, 0, tiled=True)  34.2 us
    all_to_all x2, starting transfers between devices, exchange(): return lax.all_to_all(value, axes, 0, 0, tiled=True)  18.7 us
    pallas_call x1, Pallas kernels, shards(): pl.pallas_call(backward_kernel, grid=(STEPS,), in_specs=[SMEM] + [like(v)...  16.4 us
    all_to_all x1, blocking collectives, exchange(): return lax.all_to_all(value, axes, 0, 0, tiled=True)  13.8 us
    pallas_call x1, Pallas kernels, shards(): pl.pallas_call(forward_kernel, grid=(STEPS,), in_specs=[SMEM] + [like(v)...  11.7 us
    ppermute x6, waiting for transfers between devices, other_core(): return lax.ppermute(value, 'core', [(0, 1), (1, 0)])  9.19 us
    ppermute x6, starting transfers between devices, other_core(): return lax.ppermute(value, 'core', [(0, 1), (1, 0)])  7.24 us
    ppermute x4, starting transfers between devices, shifted(): lax.ppermute(value, BOTH, [(k, (k + steps) % 128) for k in range(128)])  6.54 us
  transfers between devices with their start and end apart: 15, of which 9 were waited for; matrix products, arithmetic and copies ran while one was open for 1% of the time, Pallas kernels for 12%

profile of v7, /device:TPU:1, one launch (start us, length us, event | category | flops | bytes accessed | tf_op | source)
XLA Modules:
  0.0 140.4 jit_solution(13226499628244493175)
XLA Ops:
  0.6 0.0 copy-start.5
  1.3 0.8 slice_bitcast_fusion.1
  2.1 0.7 tile.11
  2.7 0.1 tile.12
  2.8 0.6 stack.16.co
  3.4 0.6 add_bitcast_fusion.targets
  4.0 2.6 %shard_map.188 = (bf16[64,80,128]{2,1,0:T(8,128)(2,1)}, bf16[32,512]{1,0:T(8,128)(2,1)}, bf16[32,512]{1,0:T(8,128)(2,1)}, bf16[768,128]{1,0:T(8,128)(2,1)}) custom-call(s32[5]{0:T(128)} %stack.16.co, bf16[256,512]{1,0:T(8,128)(2,1)} %node.5, s32[1,128]{1,0:T(1,128)} %add_bitcast_fusion.targets, bf16[3,512,128]{2,1,0:T(8,128)(2,1)} %edge_first.1, ...), custom_call_target="tpu_custom_call" | custom-call | tf_op jit(solution)/shard_map/pallas_call | solution.py:360
  6.6 0.0 copy-start.6
  6.6 0.0 copy-start.8
  6.7 12.1 %all-to-all-start = ((bf16[64,80,128]{2,1,0:T(8,128)(2,1)}), bf16[64,80,128]{2,1,0:T(8,128)(2,1)S(1)}, u32[]{:S(2)}, u32[]{:S(2)}) async-start(bf16[64,80,128]{2,1,0:T(8,128)(2,1)} %get-tuple-element.49), calls=%async_computation | async-start | bytes 2621440 | tf_op jit(solution)/shard_map/all_to_all | solution.py:28
  18.8 1.1 collective-permute-start
  19.9 2.4 %collective-permute-start.1 = (bf16[32,512]{1,0:T(8,128)(2,1)S(1)}, bf16[32,512]{1,0:T(8,128)(2,1)S(1)}, u32[]{:S(2)}, u32[]{:S(2)}) collective-permute-start(bf16[32,512]{1,0:T(8,128)(2,1)S(1)} %copy-done.16), channel_id=1, source_target_pairs={{0,127},{1,0},{2,1},{3,2},{4,3},{5,4},{6,5},{7,6},{8,7},{9,8},{10,... | collective-permute-start | bytes 98312 | tf_op jit(solution)/shard_map/ppermute | solution.py:24
  22.3 0.6 reshape.52.dst_wide
  22.9 0.6 reshape.51.src_wide
  23.5 5.8 %shard_map.189 = (bf16[2048,256]{1,0:T(8,128)(2,1)}, bf16[1152,2048]{1,0:T(8,128)(2,1)}, bf16[512,2048]{1,0:T(8,128)(2,1)}) custom-call(s32[5]{0:T(128)} %stack.16.co, s32[16,128]{1,0:T(8,128)} %bitcast.18, s32[4,512]{1,0:T(4,128)} %reshape.51.src_wide, s32[4,512]{1,0:T(4,128)} %reshape.52.dst_wide, bf16[2048,512]{1,0:T(8,128)(2,1)} %edge.3), custom_call_target="tpu_custom_call" | custom-call | flops 20000000 | bytes 14000000 | tf_op jit(solution)/shard_map/pallas_call | solution.py:431
  29.3 0.2 collective-permute-done.prev
  29.5 9.1 %all-to-all-done = bf16[64,80,128]{2,1,0:T(8,128)(2,1)S(1)} async-done(((bf16[64,80,128]{2,1,0:T(8,128)(2,1)}), bf16[64,80,128]{2,1,0:T(8,128)(2,1)S(1)}, u32[]{:S(2)}, u32[]{:S(2)}) %all-to-all-start) | async-done | bytes 1310752 | tf_op jit(solution)/shard_map/all_to_all | solution.py:28
  38.6 2.6 %collective-permute-start.2 = (bf16[16,4,80,128]{3,2,1,0:T(8,128)(2,1)S(1)}, bf16[16,4,80,128]{3,2,1,0:T(8,128)(2,1)S(1)}, u32[]{:S(2)}, u32[]{:S(2)}) collective-permute-start(bf16[16,4,80,128]{3,2,1,0:T(8,128)(2,1)S(1)} %bitcast.16), channel_id=1, source_target_pairs={{0,4},{4,0},{1,5},{5,1},{2,6},{6,2},{3,7},{7,3},{8,12},{12,8},{9,1... | collective-permute-start | bytes 3932168 | tf_op jit(solution)/shard_map/ppermute | solution.py:20
  41.2 2.7 %collective-permute-done.2.far = bf16[16,4,80,128]{3,2,1,0:T(8,128)(2,1)S(1)} collective-permute-done((bf16[16,4,80,128]{3,2,1,0:T(8,128)(2,1)S(1)}, bf16[16,4,80,128]{3,2,1,0:T(8,128)(2,1)S(1)}, u32[]{:S(2)}, u32[]{:S(2)}) %collective-permute-start.2) | collective-permute-done | bytes 1310752 | tf_op jit(solution)/shard_map/ppermute | solution.py:20
  43.8 0.4 collective-permute-start.5
  44.2 2.3 %collective-permute-start.4 = (bf16[768,128]{1,0:T(8,128)(2,1)}, bf16[768,128]{1,0:T(8,128)(2,1)S(1)}, u32[]{:S(2)}, u32[]{:S(2)}) collective-permute-start(bf16[768,128]{1,0:T(8,128)(2,1)} %get-tuple-element.58), channel_id=1, source_target_pairs={{0,2},{1,3},{2,0},{3,1},{4,6},{5,7},{6,4},{7,5},{8,10},{9,11},{10,... | collective-permute-start | bytes 589832 | tf_op jit(solution)/shard_map/ppermute | solution.py:446
  46.5 0.0 collective-permute-start.3
  46.5 0.0 copy-start.1
  46.5 0.9 copy-done.1
  47.5 0.0 copy-start.12
  47.5 0.0 copy-start.13
  47.5 0.0 copy-start.15
  47.5 11.7 %shard_map.190 = (bf16[2048,512]{1,0:T(8,128)(2,1)}, bf16[256,512]{1,0:T(8,128)(2,1)S(1)}, bf16[2048,512]{1,0:T(8,128)(2,1)S(1)}, bf16[2048,512]{1,0:T(8,128)(2,...) custom-call(s32[5]{0:T(128)S(1)} %copy-done.8, ...), custom_call_target="tpu_custom_call" | custom-call | flops 7000000000 | bytes 18000000 | tf_op jit(solution)/shard_map/pallas_call | solution.py:451
  59.2 1.0 collective-permute-start.6
  60.2 0.1 collective-permute-start.7
  60.3 0.4 collective-permute-start.8
  60.7 0.6 collective-permute-done.6.refs_3_
  61.3 0.4 collective-permute-done.7.refs_4_
  61.6 0.3 collective-permute-done.8.refs_5_
  62.0 16.4 %shard_map.191 = (bf16[256,512]{1,0:T(8,128)(2,1)}, f32[256,512]{1,0:T(8,128)S(1)}, bf16[2048,512]{1,0:T(8,128)(2,1)}, bf16[32,512]{1,0:T(8,128)(2,1)S(1)}, bf16...) custom-call(s32[5]{0:T(128)S(1)} %copy-done.8, ...), custom_call_target="tpu_custom_call" | custom-call | flops 8999999488 | bytes 24000000 | tf_op jit(solution)/shard_map/pallas_call | solution.py:487
  78.4 0.3 collective-permute-start.9
  78.7 3.9 %collective-permute-done.9 = bf16[8,2,4,128,128]{4,3,2,1,0:T(8,128)(2,1)S(1)} collective-permute-done((bf16[8,2,4,128,128]{4,3,2,1,0:T(8,128)(2,1)S(1)}, bf16[8,2,4,128,128]{4,3,2,1,0:T(8,128)(2,1)S(1)}, u32[]{:S(2)}, u32[]{:S(2)}) %collective-permute-start.9) | collective-permute-done | bytes 2097184 | tf_op jit(solution)/shard_map/ppermute | solution.py:20
  82.6 2.5 %add_convert_fusion = bf16[8,2,4,128,128]{4,3,2,1,0:T(8,128)(2,1)} fusion(bf16[8,2,4,128,128]{4,3,2,1,0:T(8,128)(2,1)S(1)} %collective-permute-done.9, bf16[8,2,4,128,128]{4,3,2,1,0:T(8,128)(2,1)S(1)} %get-tuple-element.72), kind=kLoop, calls=%fused_computation | loop fusion | flops 4194304 | bytes 6291456 | tf_op jit(solution)/shard_map/convert_element_type | solution.py:522
  85.0 6.6 %all-to-all-start.1 = ((bf16[64,128,128]{2,1,0:T(8,128)(2,1)}), bf16[64,128,128]{2,1,0:T(8,128)(2,1)S(1)}, u32[]{:S(2)}, u32[]{:S(2)}) async-start(bf16[64,128,128]{2,1,0:T(8,128)(2,1)} %bitcast.10), calls=%async_computation.1 | async-start | bytes 4194304 | tf_op jit(solution)/shard_map/all_to_all | solution.py:28
  91.7 0.0 copy-start.10
  91.7 3.0 %collective-permute-start.10 = (bf16[32,512]{1,0:T(8,128)(2,1)S(1)}, bf16[32,512]{1,0:T(8,128)(2,1)S(1)}, u32[]{:S(2)}, u32[]{:S(2)}) collective-permute-start(bf16[32,512]{1,0:T(8,128)(2,1)S(1)} %get-tuple-element.75), channel_id=1, source_target_pairs={{0,127},{1,0},{2,1},{3,2},{4,3},{5,4},{6,5},{7,6},{8,7},{9,8},{10,... | collective-permute-start | bytes 98312 | tf_op jit(solution)/shard_map/ppermute | solution.py:24
  94.7 25.1 %all-to-all-done.1 = bf16[64,128,128]{2,1,0:T(8,128)(2,1)S(1)} async-done(((bf16[64,128,128]{2,1,0:T(8,128)(2,1)}), bf16[64,128,128]{2,1,0:T(8,128)(2,1)S(1)}, u32[]{:S(2)}, u32[]{:S(2)}) %all-to-all-start.1) | async-done | bytes 2097184 | tf_op jit(solution)/shard_map/all_to_all | solution.py:28
  119.8 0.3 reduce_sum.12.own
  120.1 0.1 broadcast_in_dim.10
  120.2 13.8 %all_to_all.15.tiles = bf16[16,112,128]{2,1,0:T(8,128)(2,1)S(1)} all-to-all(bf16[16,112,128]{2,1,0:T(8,128)(2,1)S(1)} %broadcast_in_dim.10), channel_id=1, replica_groups=mesh['z'=4,'x'=4,'core'=2,'feat'=4] {'z','x'}, dimensions={0} | all-to-all | bytes 917504 | tf_op jit(solution)/shard_map/all_to_all | solution.py:28
  134.0 2.8 %collective-permute-start.12 = (bf16[16,112,128]{2,1,0:T(8,128)(2,1)S(1)}, bf16[16,112,128]{2,1,0:T(8,128)(2,1)S(1)}, u32[]{:S(2)}, u32[]{:S(2)}) collective-permute-start(bf16[16,112,128]{2,1,0:T(8,128)(2,1)S(1)} %all_to_all.15.tiles), channel_id=1, source_target_pairs={{0,4},{4,0},{1,5},{5,1},{2,6},{6,2},{3,7},{7,3},{8,12},{12,8},{9,1... | collective-permute-start | bytes 1376264 | tf_op jit(solution)/shard_map/ppermute | solution.py:20
  136.8 1.4 %collective-permute-done.12.far = bf16[16,112,128]{2,1,0:T(8,128)(2,1)S(1)} collective-permute-done((bf16[16,112,128]{2,1,0:T(8,128)(2,1)S(1)}, bf16[16,112,128]{2,1,0:T(8,128)(2,1)S(1)}, u32[]{:S(2)}, u32[]{:S(2)}) %collective-permute-start.12) | collective-permute-done | bytes 458784 | tf_op jit(solution)/shard_map/ppermute | solution.py:20
  138.3 2.1 %shard_map.192 = (f32[3,16,2,16,128]{4,3,2,1,0:T(8,128)}, f32[128,512]{1,0:T(8,128)}, f32[2,16,2,16,128]{4,3,2,1,0:T(8,128)}, f32[128,512]{1,0:T(8,128)}, f32[256,512]{1,0:T(8,128)}) custom-call(s32[5]{0:T(128)S(1)} %copy-done.8, bf16[16,112,128]{2,1,0:T(8,128)(2,1)S(1)} %all_to_all.15.tiles, bf16[16,112,128]{2,1,0:T(8,128)(2,1)S(1)} %collective-permute-done.12.far, ...), custom_call_target="tpu_custom_call" | custom-call | tf_op jit(solution)/shard_map/pallas_call | solution.py:360
  (34 shorter events, 0.1 us)
Async XLA Ops:
  0.6 21.7 %copy-start.5 = (s32[2048]{0:T(1024)S(1)}, s32[2048]{0:T(1024)}, u32[]{:S(2)}) copy-start(s32[2048]{0:T(1024)} %param.16) | copy-start | bytes 24580
  0.6 22.2 %copy-start.9 = (s32[2048]{0:T(1024)S(1)}, s32[2048]{0:T(1024)}, u32[]{:S(2)}) copy-start(s32[2048]{0:T(1024)} %param.15) | copy-start | bytes 24580
  6.6 13.2 %copy-start.16 = (bf16[32,512]{1,0:T(8,128)(2,1)S(1)}, bf16[32,512]{1,0:T(8,128)(2,1)}, u32[]{:S(2)}) copy-start(bf16[32,512]{1,0:T(8,128)(2,1)} %get-tuple-element.48) | copy-start | bytes 98308
  6.6 39.9 %copy-start = (bf16[2048,512]{1,0:T(8,128)(2,1)S(1)}, bf16[2048,512]{1,0:T(8,128)(2,1)}, u32[]{:S(2)}) copy-start(bf16[2048,512]{1,0:T(8,128)(2,1)} %edge.3) | copy-start | bytes 6291460
  6.6 39.9 %copy-start.6 = (s32[2048]{0:T(1024)S(1)}, s32[2048]{0:T(1024)}, u32[]{:S(2)}) copy-start(s32[2048]{0:T(1024)} %param.16) | copy-start | bytes 24580
  6.6 39.8 %copy-start.8 = (s32[5]{0:T(128)S(1)}, s32[5]{0:T(128)}, u32[]{:S(2)}) copy-start(s32[5]{0:T(128)} %stack.16.co) | copy-start | bytes 64
  6.7 31.9 %all-to-all-start = ((bf16[64,80,128]{2,1,0:T(8,128)(2,1)}), bf16[64,80,128]{2,1,0:T(8,128)(2,1)S(1)}, u32[]{:S(2)}, u32[]{:S(2)}) async-start(bf16[64,80,128]{2,1,0:T(8,128)(2,1)} %get-tuple-element.49), calls=%async_computation | async-start | bytes 2621440 | tf_op jit(solution)/shard_map/all_to_all | solution.py:28
  18.8 10.7 %collective-permute-start = (bf16[32,512]{1,0:T(8,128)(2,1)}, bf16[32,512]{1,0:T(8,128)(2,1)S(1)}, u32[]{:S(2)}, u32[]{:S(2)}) collective-permute-start(bf16[32,512]{1,0:T(8,128)(2,1)} %get-tuple-element.47), channel_id=1, source_target_pairs={{0,1},{1,2},{2,3},{3,4},{4,5},{5,6},{6,7},{7,8},{8,9},{9,10},{10,1... | collective-permute-start | bytes 98312 | tf_op jit(solution)/shard_map/ppermute | solution.py:24
  19.9 9.6 %collective-permute-start.1 = (bf16[32,512]{1,0:T(8,128)(2,1)S(1)}, bf16[32,512]{1,0:T(8,128)(2,1)S(1)}, u32[]{:S(2)}, u32[]{:S(2)}) collective-permute-start(bf16[32,512]{1,0:T(8,128)(2,1)S(1)} %copy-done.16), channel_id=1, source_target_pairs={{0,127},{1,0},{2,1},{3,2},{4,3},{5,4},{6,5},{7,6},{8,7},{9,8},{10,... | collective-permute-start | bytes 98312 | tf_op jit(solution)/shard_map/ppermute | solution.py:24
  22.9 23.6 %copy-start.7 = (s32[4,512]{1,0:T(4,128)S(1)}, s32[4,512]{1,0:T(4,128)}, u32[]{:S(2)}) copy-start(s32[4,512]{1,0:T(4,128)} %reshape.52.dst_wide) | copy-start | bytes 24580
  38.6 5.3 %collective-permute-start.2 = (bf16[16,4,80,128]{3,2,1,0:T(8,128)(2,1)S(1)}, bf16[16,4,80,128]{3,2,1,0:T(8,128)(2,1)S(1)}, u32[]{:S(2)}, u32[]{:S(2)}) collective-permute-start(bf16[16,4,80,128]{3,2,1,0:T(8,128)(2,1)S(1)} %bitcast.16), channel_id=1, source_target_pairs={{0,4},{4,0},{1,5},{5,1},{2,6},{6,2},{3,7},{7,3},{8,12},{12,8},{9,1... | collective-permute-start | bytes 3932168 | tf_op jit(solution)/shard_map/ppermute | solution.py:20
  43.8 15.3 %collective-permute-start.5 = (bf16[768,128]{1,0:T(8,128)(2,1)}, bf16[768,128]{1,0:T(8,128)(2,1)S(1)}, u32[]{:S(2)}, u32[]{:S(2)}) collective-permute-start(bf16[768,128]{1,0:T(8,128)(2,1)} %get-tuple-element.58), channel_id=1, source_target_pairs={{0,3},{1,0},{2,1},{3,2},{4,7},{5,4},{6,5},{7,6},{8,11},{9,8},{10,9... | collective-permute-start | bytes 589832 | tf_op jit(solution)/shard_map/ppermute | solution.py:446
  44.2 15.0 %collective-permute-start.4 = (bf16[768,128]{1,0:T(8,128)(2,1)}, bf16[768,128]{1,0:T(8,128)(2,1)S(1)}, u32[]{:S(2)}, u32[]{:S(2)}) collective-permute-start(bf16[768,128]{1,0:T(8,128)(2,1)} %get-tuple-element.58), channel_id=1, source_target_pairs={{0,2},{1,3},{2,0},{3,1},{4,6},{5,7},{6,4},{7,5},{8,10},{9,11},{10,... | collective-permute-start | bytes 589832 | tf_op jit(solution)/shard_map/ppermute | solution.py:446
  46.5 12.7 %collective-permute-start.3 = (bf16[768,128]{1,0:T(8,128)(2,1)}, bf16[768,128]{1,0:T(8,128)(2,1)S(1)}, u32[]{:S(2)}, u32[]{:S(2)}) collective-permute-start(bf16[768,128]{1,0:T(8,128)(2,1)} %get-tuple-element.58), channel_id=1, source_target_pairs={{0,1},{1,2},{2,3},{3,0},{4,5},{5,6},{6,7},{7,4},{8,9},{9,10},{10,1... | collective-permute-start | bytes 589832 | tf_op jit(solution)/shard_map/ppermute | solution.py:446
  46.5 1.0 copy-start.1
  47.5 14.5 %copy-start.2 = (bf16[256,512]{1,0:T(8,128)(2,1)S(1)}, bf16[256,512]{1,0:T(8,128)(2,1)}, u32[]{:S(2)}) copy-start(bf16[256,512]{1,0:T(8,128)(2,1)} %node.5) | copy-start | bytes 786436
  47.5 14.5 %copy-start.3 = (bf16[2,512,128]{2,1,0:T(8,128)(2,1)S(1)}, bf16[2,512,128]{2,1,0:T(8,128)(2,1)}, u32[]{:S(2)}) copy-start(bf16[2,512,128]{2,1,0:T(8,128)(2,1)} %own_first.1) | copy-start | bytes 786436
  47.5 14.5 %copy-start.4 = (bf16[128,512]{1,0:T(8,128)(2,1)S(1)}, bf16[128,512]{1,0:T(8,128)(2,1)}, u32[]{:S(2)}) copy-start(bf16[128,512]{1,0:T(8,128)(2,1)} %own_second.1) | copy-start | bytes 393220
  47.5 14.5 %copy-start.11 = (bf16[1152,2048]{1,0:T(8,128)(2,1)S(1)}, bf16[1152,2048]{1,0:T(8,128)(2,1)}, u32[]{:S(2)}) copy-start(bf16[1152,2048]{1,0:T(8,128)(2,1)} %get-tuple-element.70.refs_16_) | copy-start | bytes 14155780
  47.5 14.5 %copy-start.12 = (bf16[2048,512]{1,0:T(8,128)(2,1)S(1)}, bf16[2048,512]{1,0:T(8,128)(2,1)}, u32[]{:S(2)}) copy-start(bf16[2048,512]{1,0:T(8,128)(2,1)} %refs_14_.1) | copy-start | bytes 6291460
  47.5 14.5 %copy-start.13 = (bf16[512,2048]{1,0:T(8,128)(2,1)S(1)}, bf16[512,2048]{1,0:T(8,128)(2,1)}, u32[]{:S(2)}) copy-start(bf16[512,2048]{1,0:T(8,128)(2,1)} %get-tuple-element.65.refs_9_) | copy-start | bytes 6291460
  47.5 14.5 %copy-start.14 = (bf16[2048,256]{1,0:T(8,128)(2,1)S(1)}, bf16[2048,256]{1,0:T(8,128)(2,1)}, u32[]{:S(2)}) copy-start(bf16[2048,256]{1,0:T(8,128)(2,1)} %get-tuple-element.53.refs_15_) | copy-start | bytes 3145732
  47.5 14.5 %copy-start.15 = (bf16[256,512]{1,0:T(8,128)(2,1)S(1)}, bf16[256,512]{1,0:T(8,128)(2,1)}, u32[]{:S(2)}) copy-start(bf16[256,512]{1,0:T(8,128)(2,1)} %grad_node.1) | copy-start | bytes 786436
  59.2 2.1 %collective-permute-start.6 = (bf16[768,128]{1,0:T(8,128)(2,1)S(1)}, bf16[768,128]{1,0:T(8,128)(2,1)S(1)}, u32[]{:S(2)}, u32[]{:S(2)}) collective-permute-start(bf16[768,128]{1,0:T(8,128)(2,1)S(1)} %collective-permute-done.3.refs_0_), channel_id=1, source_target_pairs={{0,4},{4,0},{1,5},{5,1},{2,6},{6,2},{3,7},{7,3},{8,12},{12,8},{9,1... | collective-permute-start | bytes 589832 | tf_op jit(solution)/shard_map/ppermute | solution.py:20
  60.2 1.4 %collective-permute-start.7 = (bf16[768,128]{1,0:T(8,128)(2,1)S(1)}, bf16[768,128]{1,0:T(8,128)(2,1)S(1)}, u32[]{:S(2)}, u32[]{:S(2)}) collective-permute-start(bf16[768,128]{1,0:T(8,128)(2,1)S(1)} %collective-permute-done.4.refs_1_), channel_id=1, source_target_pairs={{0,4},{4,0},{1,5},{5,1},{2,6},{6,2},{3,7},{7,3},{8,12},{12,8},{9,1... | collective-permute-start | bytes 589832 | tf_op jit(solution)/shard_map/ppermute | solution.py:20
  60.3 1.6 %collective-permute-start.8 = (bf16[768,128]{1,0:T(8,128)(2,1)S(1)}, bf16[768,128]{1,0:T(8,128)(2,1)S(1)}, u32[]{:S(2)}, u32[]{:S(2)}) collective-permute-start(bf16[768,128]{1,0:T(8,128)(2,1)S(1)} %collective-permute-done.5.refs_2_), channel_id=1, source_target_pairs={{0,4},{4,0},{1,5},{5,1},{2,6},{6,2},{3,7},{7,3},{8,12},{12,8},{9,1... | collective-permute-start | bytes 589832 | tf_op jit(solution)/shard_map/ppermute | solution.py:20
  78.4 4.2 %collective-permute-start.9 = (bf16[8,2,4,128,128]{4,3,2,1,0:T(8,128)(2,1)S(1)}, bf16[8,2,4,128,128]{4,3,2,1,0:T(8,128)(2,1)S(1)}, u32[]{:S(2)}, u32[]{:S(2)}) collective-permute-start(bf16[8,2,4,128,128]{4,3,2,1,0:T(8,128)(2,1)S(1)} %get-tuple-element.73), channel_id=1, source_target_pairs={{0,4},{4,0},{1,5},{5,1},{2,6},{6,2},{3,7},{7,3},{8,12},{12,8},{9,1... | collective-permute-start | bytes 6291464 | tf_op jit(solution)/shard_map/ppermute | solution.py:20
  85.0 34.8 %all-to-all-start.1 = ((bf16[64,128,128]{2,1,0:T(8,128)(2,1)}), bf16[64,128,128]{2,1,0:T(8,128)(2,1)S(1)}, u32[]{:S(2)}, u32[]{:S(2)}) async-start(bf16[64,128,128]{2,1,0:T(8,128)(2,1)} %bitcast.10), calls=%async_computation.1 | async-start | bytes 4194304 | tf_op jit(solution)/shard_map/all_to_all | solution.py:28
  91.7 46.6 %copy-start.10 = (s32[1,128]{1,0:T(1,128)S(1)}, s32[1,128]{1,0:T(1,128)}, u32[]{:S(2)}) copy-start(s32[1,128]{1,0:T(1,128)} %add_bitcast_fusion.targets) | copy-start | bytes 1540
  91.7 28.5 %collective-permute-start.10 = (bf16[32,512]{1,0:T(8,128)(2,1)S(1)}, bf16[32,512]{1,0:T(8,128)(2,1)S(1)}, u32[]{:S(2)}, u32[]{:S(2)}) collective-permute-start(bf16[32,512]{1,0:T(8,128)(2,1)S(1)} %get-tuple-element.75), channel_id=1, source_target_pairs={{0,127},{1,0},{2,1},{3,2},{4,3},{5,4},{6,5},{7,6},{8,7},{9,8},{10,... | collective-permute-start | bytes 98312 | tf_op jit(solution)/shard_map/ppermute | solution.py:24
  94.7 25.4 %collective-permute-start.11 = (bf16[32,512]{1,0:T(8,128)(2,1)S(1)}, bf16[32,512]{1,0:T(8,128)(2,1)S(1)}, u32[]{:S(2)}, u32[]{:S(2)}) collective-permute-start(bf16[32,512]{1,0:T(8,128)(2,1)S(1)} %get-tuple-element.77), channel_id=1, source_target_pairs={{0,1},{1,2},{2,3},{3,4},{4,5},{5,6},{6,7},{7,8},{8,9},{9,10},{10,1... | collective-permute-start | bytes 98312 | tf_op jit(solution)/shard_map/ppermute | solution.py:24
  134.0 4.3 %collective-permute-start.12 = (bf16[16,112,128]{2,1,0:T(8,128)(2,1)S(1)}, bf16[16,112,128]{2,1,0:T(8,128)(2,1)S(1)}, u32[]{:S(2)}, u32[]{:S(2)}) collective-permute-start(bf16[16,112,128]{2,1,0:T(8,128)(2,1)S(1)} %all_to_all.15.tiles), channel_id=1, source_target_pairs={{0,4},{4,0},{1,5},{5,1},{2,6},{6,2},{3,7},{7,3},{8,12},{12,8},{9,1... | collective-permute-start | bytes 1376264 | tf_op jit(solution)/shard_map/ppermute | solution.py:20

commit v8 on v7

--- a/solution.py
+++ b/solution.py
@@ -22,6 +22,10 @@
 
 def shifted(value, steps):
     return lax.ppermute(value, BOTH, [(k, (k + steps) % 128) for k in range(128)])
+
+
+def around(value, steps):
+    return lax.ppermute(value, "feat", [(k, (k + steps) % 4) for k in range(4)])
 
 
 def exchange(value, axes):
@@ -101,8 +105,19 @@
         turned[j * 128 : (j + 1) * 128, :] = block
 
 
+def pack_half(core, first, second, packed):
+    kinds = first.shape[0]
+    at = pl.ds(pl.multiple_of(core * 256, 256), 256)
+    row = pl.ds(pl.multiple_of(core * 64, 64), 64)
+    for m in range(kinds):
+        packed[m * 256 : (m + 1) * 256, :] = first[m, at, :]
+    for b in range(4):
+        start = kinds * 256 + b * 64
+        packed[start : start + 64, :] = second[row, b * 128 : (b + 1) * 128]
+
+
 def pack_kernel(co, node, targets, edge_first, edge_second, first, second, *outs):
-    tiles, to_next, to_prev, packed = outs
+    edge_half, node_half, coarse_out, to_next, to_prev = outs
     match = lax.broadcasted_iota(jnp.int32, (256, 128), 0) == targets[...]
     rows = dot_tn(jnp.where(match, 1.0, 0.0).astype(BF16), node[...])
     to_next[...] = rows[0:32].astype(BF16)
@@ -111,21 +126,9 @@
     coarse = jnp.zeros((16, 128), F32)
     for b in range(4):
         coarse = jnp.where(group == b, rows[64:80, b * 128 : (b + 1) * 128], coarse)
-    patch = co[0]
-    at = pl.ds(pl.multiple_of(patch * 16, 16), 16)
-    parts = [edge_first[m, at, :] for m in range(3)]
-    row = pl.ds(pl.multiple_of(patch // 4 * 16, 16), 16)
-    parts.append(edge_second[row, pl.ds(pl.multiple_of(patch % 4 * 128, 128), 128)])
-    parts.append(coarse.astype(BF16))
-    tile = jnp.concatenate(parts, axis=0)
-    for k in range(64):
-        tiles[k] = tile
-    at = pl.ds(pl.multiple_of(co[2] * 256, 256), 256)
-    row = pl.ds(pl.multiple_of(co[2] * 64, 64), 64)
-    for m in range(2):
-        packed[m * 256 : (m + 1) * 256, :] = first[m, at, :]
-    for b in range(4):
-        packed[512 + b * 64 : 576 + b * 64, :] = second[row, b * 128 : (b + 1) * 128]
+    coarse_out[...] = coarse.astype(BF16)
+    pack_half(co[2], edge_first, edge_second, edge_half)
+    pack_half(co[2], first, second, node_half)
 
 
 def live_rows(step, count):
@@ -136,42 +139,40 @@
 HALVES = (slice(0, CHUNK // 2), slice(CHUNK // 2, CHUNK))
 
 
+def place_half(part, half, yy, first, second, start=0):
+    kinds = first.shape[0]
+    columns = pl.ds(pl.multiple_of(yy * 128, 128), 128)
+    rows = pl.ds(pl.multiple_of(half * 256, 256), 256)
+    for m in range(kinds):
+        at = m * 256 - start
+        if 0 <= at < part.shape[0]:
+            first[m, rows, columns] = part[at : at + 256, :]
+    rows = pl.ds(pl.multiple_of(yy * 128 + half * 64, 64), 64)
+    for b in range(4):
+        at = kinds * 256 + b * 64 - start
+        if 0 <= at < part.shape[0]:
+            second[rows, b * 128 : (b + 1) * 128] = part[at : at + 64, :]
+
+
+def place_own(co, own_first, own_second, first, second):
+    columns = pl.ds(pl.multiple_of(co[3] * 128, 128), 128)
+    for m in range(first.shape[0]):
+        first[m, :, columns] = own_first[m]
+    second[columns, :] = own_second[...]
+
+
 def place_weights(co, own_first, own_second, near, far, first, second):
-    core, y = co[2], co[3]
-    for s in range(4):
-        yy = (y - s) & 3
-        columns = pl.ds(pl.multiple_of(yy * 128, 128), 128)
-        if s == 0:
-            for m in range(2):
-                first[m, :, columns] = own_first[m]
-            second[columns, :] = own_second[...]
-            continue
-        for part, half in ((near[s - 1], core), (far[s - 1], 1 - core)):
-            rows = pl.ds(pl.multiple_of(half * 256, 256), 256)
-            for m in range(2):
-                first[m, rows, columns] = part[m * 256 : (m + 1) * 256, :]
-            rows = pl.ds(pl.multiple_of(yy * 128 + half * 64, 64), 64)
-            for b in range(4):
-                start = 512 + b * 64
-                second[rows, b * 128 : (b + 1) * 128] = part[start : start + 64, :]
-
-
-def whole(first, m):
-    return first[m].reshape(512, 512)
-
-
-def place_tiles(own_core, near, far, lookup, first, second, coarse):
-    for part, core in ((near, own_core), (far, 1 - own_core)):
-        for y in range(4):
-            block = slice(y * 128, (y + 1) * 128)
-            for m in range(3):
-                value = part[:, y, m * 16 : (m + 1) * 16, :].reshape(16, 1, 16, 128)
-                first[m, :, pl.ds(core, 1), :, block] = value
-            for k in range(16):
-                rows = slice(y * 128 + k // 2 * 16, y * 128 + k // 2 * 16 + 16)
-                columns = pl.ds(pl.multiple_of((k % 2 * 2 + core) * 128, 128), 128)
-                second[rows, columns] = part[k, y, 48:64, :]
-            coarse[:, pl.ds(core, 1), y] = part[:, y, 64:80, :].reshape(16, 1, 16, 128)
+    place_own(co, own_first, own_second, first, second)
+    for s in (1, 2, 3):
+        place_half(near[s - 1], co[2], (co[3] - s) & 3, first, second)
+        place_half(far[s - 1], 1 - co[2], (co[3] - s) & 3, first, second)
+
+
+def place_coarse(co, near, far, lookup, coarse):
+    for part, core in ((near, co[2]), (far, 1 - co[2])):
+        for s in range(4):
+            value = part[:, s * 16 : (s + 1) * 16, :].reshape(16, 1, 1, 16, 128)
+            coarse[:, pl.ds(core, 1), pl.ds((co[3] - s) & 3, 1)] = value
     low = lax.broadcasted_iota(jnp.int32, (64, 8, 128), 1) < 4
     pairs = coarse[...].reshape(64, 2, 16, 128).astype(F32)
     for half in range(2):
@@ -182,7 +183,9 @@
         lookup[320:832, half * 256 + 128 : half * 256 + 256] = other_block.astype(BF16)
 
 
-def forward_kernel(co, node, prev, following, near, far, src, dst, dst_wide, edge, *refs):
+def forward_kernel(co, node, prev, following, own_first, own_second, *refs):
+    near, far, refs = refs[:5], refs[5:10], refs[10:]
+    src, dst, dst_wide, edge, refs = refs[0], refs[1], refs[2], refs[3], refs[4:]
     edge_out, incoming, act_out, normed_out, slope_out, factor_out, lookup, first, second = refs[:9]
     table, total, coarse = refs[9:]
     step = pl.program_id(0)
@@ -193,9 +196,15 @@
         lookup[256:288, :] = prev[...]
         lookup[288:320, :] = following[...]
         lookup[832:896, :] = jnp.zeros((64, 512), BF16)
-        place_tiles(co[2], near, far, lookup, first, second, coarse)
-        table[0:256, :] = dot(node[...], whole(first, 2)).astype(BF16)
-        table[256:, :] = dot(lookup[...], whole(first, 1)).astype(BF16)
+        place_own(co, own_first, own_second, first, second)
+        for part, half in ((near, co[2]), (far, 1 - co[2])):
+            place_half(part[0], half, (co[3] - 1) & 3, first, second)
+            place_half(part[1], half, (co[3] + 1) & 3, first, second)
+            place_half(part[2], half, (co[3] + 2) & 3, first, second)
+            place_half(part[3], half, (co[3] + 2) & 3, first, second, 512)
+        place_coarse(co, near[4], far[4], lookup, coarse)
+        table[0:256, :] = dot(node[...], first[2]).astype(BF16)
+        table[256:, :] = dot(lookup[...], first[1]).astype(BF16)
         total[...] = jnp.zeros_like(total)
 
     hots = []
@@ -207,7 +216,7 @@
     turned = turned_rows(live_targets(step, dst_wide[pl.ds(step, 1), :], co[4]), 2)
     turned = jnp.concatenate(turned, axis=0)
     live = live_rows(step, co[4])
-    pres = [dot(edge[h, :], whole(first, 0)) + dot(hot[h, :], table[...]) for h in HALVES]
+    pres = [dot(edge[h, :], first[0]) + dot(hot[h, :], table[...]) for h in HALVES]
     acts = []
     for h, pre in zip(HALVES, pres):
         act, slope = swish(pre)
@@ -301,7 +310,7 @@
     grads = [dot_nt(delta, edge_second[...]) for delta in deltas]
     pre_grads = [(g * slope[h, :].astype(F32)).astype(BF16) for h, g in zip(HALVES, grads)]
     for h, total, pre_grad in zip(HALVES, totals, pre_grads):
-        edge_grad[h, :] = (total + dot_nt(pre_grad, whole(edge_first, 0))).astype(BF16)
+        edge_grad[h, :] = (total + dot_nt(pre_grad, edge_first[0])).astype(BF16)
     pre_grad = jnp.concatenate(pre_grads, axis=0)
     sum_second[...] += dot_tn(act[...], jnp.concatenate(deltas, axis=0))
     sum_first[...] += dot(edge_turned[...], pre_grad)
@@ -315,8 +324,8 @@
         sent = sums[256:, :].astype(BF16)
         put_columns(co, dot_tn(lookup[...], sent), 1, columns, keep, give)
         put_columns(co, dot_tn(node[...], received), 2, columns, keep, give)
-        back = dot_nt(sent, whole(edge_first, 1))
-        node_total[...] += back[0:256] + dot_nt(received, whole(edge_first, 2))
+        back = dot_nt(sent, edge_first[1])
+        node_total[...] += back[0:256] + dot_nt(received, edge_first[2])
         to_prev[...] = back[256:288].astype(BF16)
         to_next[...] = back[288:320].astype(BF16)
         put_owned(co, back[320:832], owned, keep, give)
@@ -412,20 +421,25 @@
     unused = jnp.full((48,), -1, jnp.int32)
     targets = jnp.concatenate([lists[1], lists[0], jnp.tile(owned, 4), unused]).reshape(1, 128)
 
-    packed, to_next, to_prev, node_half = plain_call(
+    edge_half, node_half, coarse_own, to_next, to_prev = plain_call(
         pack_kernel,
         [co],
         [node_lat, targets, edge_w1, edge_w2, node_w1, node_w2],
-        [shape(64, 80, 128), shape(32, 512), shape(32, 512), shape(768, 128)],
+        [shape(1024, 128), shape(768, 128), shape(16, 128), shape(32, 512), shape(32, 512)],
         mib=60,
     )
+    coarse_four = [coarse_own] + [around(coarse_own, s) for s in (1, 2, 3)]
     from_prev = shifted(to_next, 1)
     from_next = shifted(to_prev, -1)
-    near = exchange(packed, ("z", "x", "feat")).reshape(16, 4, 80, 128)
+    up, down = around(edge_half, 1), around(edge_half, 3)
+    coarse_four = jnp.concatenate(coarse_four, axis=0)
+    coarse_near = exchange(repeated(coarse_four, 16), ("z", "x"))
+    half_down, half_up = around(down[:512], 3), around(up[512:], 1)
+    near = [up, down, half_down, half_up, coarse_near]
     src, dst = edge_src.reshape(16, 128), edge_dst.reshape(16, 128)
     dst_wide = edge_dst.reshape(STEPS, CHUNK)
     indices = [dst, edge_src.reshape(STEPS, CHUNK), dst_wide]
-    indices = [after(value, packed) for value in indices]
+    indices = [after(value, edge_half) for value in indices]
     high = TABLE + 256
     wide = chunk(CHUNK, 512)
     hot, turned, edge_turned = pl.pallas_call(
@@ -439,14 +453,11 @@
             flops=20_000_000, bytes_accessed=14_000_000, transcendentals=0
         ),
     )(co, *indices, edge_lat)
-    near = after(near, from_prev, from_next, hot)
-    far = other_core(near)
-    node_half = after(node_half, near, far)
-    node_near = [
-        lax.ppermute(node_half, "feat", [(k, (k + s) % 4) for k in range(4)]) for s in (1, 2, 3)
-    ]
-
-    fixed = [node_lat, from_prev, from_next, near, far, src, dst, dst_wide]
+    far = [other_core(part) for part in near]
+    node_half = after(node_half, hot, from_prev, from_next, *far)
+    node_near = [around(node_half, s) for s in (1, 2, 3)]
+
+    fixed = [node_lat, from_prev, from_next, edge_w1, edge_w2, *near, *far, src, dst, dst_wide]
     wide = chunk(CHUNK, 512)
     edge_out, incoming, act, normed, slope, factor, lookup, first, second = pl.pallas_call(
         forward_kernel,
@@ -455,7 +466,7 @@
         + [like(v) for v in fixed]
         + [wide],
         out_specs=[wide, same(256, 512), wide, wide, wide, chunk(CHUNK, 128)]
-        + [same(TABLE, 512), same(3, 16, 2, 16, 512), same(512, 512)],
+        + [same(TABLE, 512), same(3, 512, 512), same(512, 512)],
         out_shape=[
             shape(2048, 512),
             shape(256, 512),
@@ -464,7 +475,7 @@
             shape(2048, 512),
             shape(2048, 128, dtype=F32),
             shape(TABLE, 512),
-            shape(3, 16, 2, 16, 512),
+            shape(3, 512, 512),
             shape(512, 512),
         ],
         scratch_shapes=[

time: 141 us -> 149 us (1.057)
  starting transfers between devices: 35.2 us -> 42.2 us
  waiting for transfers between devices: 43.5 us -> 41 us
  other arithmetic: 3.36 us -> 5.68 us
    ppermute x3 -> x10, starting transfers between devices: 2.65 us -> 9.72 us  [around(): return lax.ppermute(value, 'feat', [(k, (k + steps) % 4) for k in range(4)])]
    ppermute x3 -> x10, waiting for transfers between devices: 0.01 us -> 5.61 us  [around(): return lax.ppermute(value, 'feat', [(k, (k + steps) % 4) for k in range(4)])]
    all_to_all x2, waiting for transfers between devices: 34.2 us -> 28.8 us  [exchange(): return lax.all_to_all(value, axes, 0, 0, tiled=True)]
    all_to_all x2, starting transfers between devices: 18.7 us -> 15.1 us  [exchange(): return lax.all_to_all(value, axes, 0, 0, tiled=True)]
    ppermute x6 -> x10, starting transfers between devices: 7.24 us -> 10.5 us  [other_core(): return lax.ppermute(value, 'core', [(0, 1), (1, 0)])]
    ppermute x6 -> x10, waiting for transfers between devices: 9.19 us -> 6.55 us  [other_core(): return lax.ppermute(value, 'core', [(0, 1), (1, 0)])]
    reduce_sum x1, other arithmetic: 0.32 us -> 1.9 us  [shards(): jnp.sum(exchange(pair, ('z', 'x', 'feat')).astype(F32), axis=0).astype(BF16)]
  transfers between devices with their start and end apart: 15 -> 26, of which waited for: 9 -> 11; matrix products, arithmetic and copies ran while one was open for 1% -> 4% of each run, Pallas kernels for 12% -> 13%
where the time goes in v8:
time: 149 us
  starting transfers between devices  42.2 us (28%)
  waiting for transfers between devices  41 us (28%)
  Pallas kernels  39.4 us (26%)
  blocking collectives  13.8 us (9%)
  other arithmetic  5.68 us (4%)
  local copies, waits for them, and re-layouts  5.15 us (3%)
  between operations  1.62 us (1%)
    all_to_all x2, waiting for transfers between devices, exchange(): return lax.all_to_all(value, axes, 0, 0, tiled=True)  28.8 us
    pallas_call x1, Pallas kernels, shards(): pl.pallas_call(backward_kernel, grid=(STEPS,), in_specs=[SMEM] + [like(v)...  16.4 us
    all_to_all x2, starting transfers between devices, exchange(): return lax.all_to_all(value, axes, 0, 0, tiled=True)  15.1 us
    all_to_all x1, blocking collectives, exchange(): return lax.all_to_all(value, axes, 0, 0, tiled=True)  13.8 us
    pallas_call x1, Pallas kernels, shards(): pl.pallas_call(forward_kernel, grid=(STEPS,), in_specs=[SMEM] + [like(v)...  12.8 us
    ppermute x10, starting transfers between devices, other_core(): return lax.ppermute(value, 'core', [(0, 1), (1, 0)])  10.5 us
    ppermute x10, starting transfers between devices, around(): return lax.ppermute(value, 'feat', [(k, (k + steps) % 4) for k in range(4)])  9.72 us
    ppermute x4, starting transfers between devices, shifted(): lax.ppermute(value, BOTH, [(k, (k + steps) % 128) for k in range(128)])  6.83 us
  transfers between devices with their start and end apart: 26, of which 11 were waited for; matrix products, arithmetic and copies ran while one was open for 4% of the time, Pallas kernels for 13%

profile of v8, /device:TPU:1, one launch (start us, length us, event | category | flops | bytes accessed | tf_op | source)
XLA Modules:
  0.0 148.9 jit_solution(4761188038343749801)
XLA Ops:
  1.3 0.8 slice_bitcast_fusion.1
  2.1 0.7 tile.11
  2.8 0.6 stack.16.co
  3.4 0.7 add_bitcast_fusion.targets
  4.1 2.3 %shard_map.188 = (bf16[1024,128]{1,0:T(8,128)(2,1)}, bf16[768,128]{1,0:T(8,128)(2,1)}, bf16[16,128]{1,0:T(8,128)(2,1)}, bf16[32,512]{1,0:T(8,128)(2,1)}, bf16[32,512]{1,0:T(8,128)(2,1)}) custom-call(s32[5]{0:T(128)} %stack.16.co, bf16[256,512]{1,0:T(8,128)(2,1)} %node.5, s32[1,128]{1,0:T(1,128)} %add_bitcast_fusion.targets, bf16[3,512,128]{2,1,0:T(8,128)(2,1)} %own_first.2, ...), custom_call_target="tpu_custom_call" | custom-call | tf_op jit(solution)/shard_map/pallas_call | solution.py:369
  6.4 3.6 %collective-permute-start.8 = (bf16[16,128]{1,0:T(8,128)(2,1)}, bf16[16,128]{1,0:T(8,128)(2,1)S(1)}, u32[]{:S(2)}, u32[]{:S(2)}) collective-permute-start(bf16[16,128]{1,0:T(8,128)(2,1)} %get-tuple-element.50), channel_id=1, source_target_pairs={{0,3},{1,0},{2,1},{3,2},{4,7},{5,4},{6,5},{7,6},{8,11},{9,8},{10,9... | collective-permute-start | bytes 12296 | tf_op jit(solution)/shard_map/ppermute | solution.py:28
  10.0 0.3 collective-permute-start.7
  10.3 0.7 collective-permute-start.6
  11.0 2.0 %collective-permute-start.3 = (bf16[1024,128]{1,0:T(8,128)(2,1)}, bf16[1024,128]{1,0:T(8,128)(2,1)S(1)}, u32[]{:S(2)}, u32[]{:S(2)}) collective-permute-start(bf16[1024,128]{1,0:T(8,128)(2,1)} %get-tuple-element.49), channel_id=1, source_target_pairs={{0,3},{1,0},{2,1},{3,2},{4,7},{5,4},{6,5},{7,6},{8,11},{9,8},{10,9... | collective-permute-start | bytes 786440 | tf_op jit(solution)/shard_map/ppermute | solution.py:28
  13.0 1.1 collective-permute-done.7
  14.2 0.7 pad_maximum_fusion
  14.9 0.8 broadcast_in_dim.7
  15.6 7.6 %all-to-all-start = ((bf16[16,64,128]{2,1,0:T(8,128)(2,1)}), bf16[16,64,128]{2,1,0:T(8,128)(2,1)S(1)}, u32[]{:S(2)}, u32[]{:S(2)}) async-start(bf16[16,64,128]{2,1,0:T(8,128)(2,1)} %broadcast_in_dim.7), calls=%async_computation | async-start | bytes 524288 | tf_op jit(solution)/shard_map/all_to_all | solution.py:32
  23.3 3.8 %collective-permute-start.1 = (bf16[32,512]{1,0:T(8,128)(2,1)}, bf16[32,512]{1,0:T(8,128)(2,1)S(1)}, u32[]{:S(2)}, u32[]{:S(2)}) collective-permute-start(bf16[32,512]{1,0:T(8,128)(2,1)} %get-tuple-element.48), channel_id=1, source_target_pairs={{0,127},{1,0},{2,1},{3,2},{4,3},{5,4},{6,5},{7,6},{8,7},{9,8},{10,... | collective-permute-start | bytes 98312 | tf_op jit(solution)/shard_map/ppermute | solution.py:24
  27.1 3.8 %all-to-all-done.refs_4_ = bf16[16,64,128]{2,1,0:T(8,128)(2,1)S(1)} async-done(((bf16[16,64,128]{2,1,0:T(8,128)(2,1)}), bf16[16,64,128]{2,1,0:T(8,128)(2,1)S(1)}, u32[]{:S(2)}, u32[]{:S(2)}) %all-to-all-start) | async-done | bytes 262176 | tf_op jit(solution)/shard_map/all_to_all | solution.py:32
  30.9 3.7 %collective-permute-start.13 = (bf16[16,64,128]{2,1,0:T(8,128)(2,1)S(1)}, bf16[16,64,128]{2,1,0:T(8,128)(2,1)}, u32[]{:S(2)}, u32[]{:S(2)}) collective-permute-start(bf16[16,64,128]{2,1,0:T(8,128)(2,1)S(1)} %all-to-all-done.refs_4_), channel_id=1, source_target_pairs={{0,4},{4,0},{1,5},{5,1},{2,6},{6,2},{3,7},{7,3},{8,12},{12,8},{9,1... | collective-permute-start | bytes 786440 | tf_op jit(solution)/shard_map/ppermute | solution.py:20
  34.6 1.2 collective-permute-start.4
  35.9 0.9 slice.23
  36.8 0.4 collective-permute-start.5
  37.1 0.6 collective-permute-start.10
  37.8 2.1 %collective-permute-done.4.refs_2_ = bf16[512,128]{1,0:T(8,128)(2,1)} collective-permute-done((bf16[512,128]{1,0:T(8,128)(2,1)S(1)}, bf16[512,128]{1,0:T(8,128)(2,1)}, u32[]{:S(2)}, u32[]{:S(2)}) %collective-permute-start.4) | collective-permute-done | bytes 131104 | tf_op jit(solution)/shard_map/ppermute | solution.py:28
  39.9 0.8 collective-permute-start.11
  40.7 2.3 %collective-permute-done.5.refs_3_ = bf16[512,128]{1,0:T(8,128)(2,1)} collective-permute-done((bf16[512,128]{1,0:T(8,128)(2,1)S(1)}, bf16[512,128]{1,0:T(8,128)(2,1)}, u32[]{:S(2)}, u32[]{:S(2)}) %collective-permute-start.5) | collective-permute-done | bytes 131104 | tf_op jit(solution)/shard_map/ppermute | solution.py:28
  43.0 1.1 collective-permute-start.12
  44.1 0.6 reshape.49.refs_12_.dst_wide
  44.7 0.6 reshape.50.src_wide
  45.3 5.9 %shard_map.190 = (bf16[2048,256]{1,0:T(8,128)(2,1)}, bf16[1152,2048]{1,0:T(8,128)(2,1)}, bf16[512,2048]{1,0:T(8,128)(2,1)}) custom-call(s32[5]{0:T(128)} %stack.16.co, s32[16,128]{1,0:T(8,128)} %bitcast.15, s32[4,512]{1,0:T(4,128)} %reshape.50.src_wide, s32[4,512]{1,0:T(4,128)} %reshape.49.refs_12_.dst_wide, bf16[2048,512]{1,0:T(8,128)(2,1)} %edge.1), custom_call_target="tpu_custom_call" | custom-call | flops 20000000 | bytes 14000000 | tf_op jit(solution)/shard_map/pallas_call | solution.py:445
  51.3 0.8 collective-permute-start.15
  52.2 0.6 collective-permute-start.14
  52.9 12.8 %shard_map.189 = (bf16[2048,512]{1,0:T(8,128)(2,1)}, bf16[256,512]{1,0:T(8,128)(2,1)S(1)}, bf16[2048,512]{1,0:T(8,128)(2,1)S(1)}, bf16[2048,512]{1,0:T(8,128)(2,...) custom-call(s32[5]{0:T(128)S(1)} %copy-done.9, ...), custom_call_target="tpu_custom_call" | custom-call | flops 7000000000 | bytes 18000000 | tf_op jit(solution)/shard_map/pallas_call | solution.py:462
  65.7 0.6 collective-permute-start.17
  66.4 0.1 collective-permute-start.18
  66.5 0.4 collective-permute-start.19
  66.9 0.6 collective-permute-done.17.refs_3_
  67.4 0.4 collective-permute-done.18.refs_4_
  67.8 0.3 collective-permute-done.19.refs_5_
  68.1 16.4 %shard_map.191 = (bf16[256,512]{1,0:T(8,128)(2,1)}, f32[256,512]{1,0:T(8,128)S(1)}, bf16[2048,512]{1,0:T(8,128)(2,1)}, bf16[32,512]{1,0:T(8,128)(2,1)S(1)}, bf16...) custom-call(s32[5]{0:T(128)S(1)} %copy-done.9, ...), custom_call_target="tpu_custom_call" | custom-call | flops 8999999488 | bytes 24000000 | tf_op jit(solution)/shard_map/pallas_call | solution.py:498
  84.5 0.3 collective-permute-start.20
  84.8 3.9 %collective-permute-done.20 = bf16[8,2,4,128,128]{4,3,2,1,0:T(8,128)(2,1)S(1)} collective-permute-done((bf16[8,2,4,128,128]{4,3,2,1,0:T(8,128)(2,1)S(1)}, bf16[8,2,4,128,128]{4,3,2,1,0:T(8,128)(2,1)S(1)}, u32[]{:S(2)}, u32[]{:S(2)}) %collective-permute-start.20) | collective-permute-done | bytes 2097184 | tf_op jit(solution)/shard_map/ppermute | solution.py:20
  88.7 2.4 %add_convert_fusion = bf16[8,2,4,128,128]{4,3,2,1,0:T(8,128)(2,1)} fusion(bf16[8,2,4,128,128]{4,3,2,1,0:T(8,128)(2,1)S(1)} %collective-permute-done.20, bf16[8,2,4,128,128]{4,3,2,1,0:T(8,128)(2,1)S(1)} %get-tuple-element.72), kind=kLoop, calls=%fused_computation | loop fusion | flops 4194304 | bytes 6291456 | tf_op jit(solution)/shard_map/convert_element_type | solution.py:533
  91.1 7.5 %all-to-all-start.1 = ((bf16[64,128,128]{2,1,0:T(8,128)(2,1)}), bf16[64,128,128]{2,1,0:T(8,128)(2,1)}, u32[]{:S(2)}, u32[]{:S(2)}) async-start(bf16[64,128,128]{2,1,0:T(8,128)(2,1)} %bitcast.9), calls=%async_computation.1 | async-start | bytes 4194304 | tf_op jit(solution)/shard_map/all_to_all | solution.py:32
  98.7 2.9 %collective-permute-start.21 = (bf16[32,512]{1,0:T(8,128)(2,1)S(1)}, bf16[32,512]{1,0:T(8,128)(2,1)S(1)}, u32[]{:S(2)}, u32[]{:S(2)}) collective-permute-start(bf16[32,512]{1,0:T(8,128)(2,1)S(1)} %get-tuple-element.75), channel_id=1, source_target_pairs={{0,127},{1,0},{2,1},{3,2},{4,3},{5,4},{6,5},{7,6},{8,7},{9,8},{10,... | collective-permute-start | bytes 98312 | tf_op jit(solution)/shard_map/ppermute | solution.py:24
  101.6 25.0 %all-to-all-done.1 = bf16[64,128,128]{2,1,0:T(8,128)(2,1)} async-done(((bf16[64,128,128]{2,1,0:T(8,128)(2,1)}), bf16[64,128,128]{2,1,0:T(8,128)(2,1)}, u32[]{:S(2)}, u32[]{:S(2)}) %all-to-all-start.1) | async-done | bytes 2097184 | tf_op jit(solution)/shard_map/all_to_all | solution.py:32
  126.7 1.9 %reduce_sum.12.own = bf16[128,128]{1,0:T(8,128)(2,1)S(1)} reduce(bf16[64,128,128]{2,1,0:T(8,128)(2,1)} %all-to-all-done.1, bf16[]{:T(256)} %constant.24.clone.1), dimensions={0}, to_apply=%region_0.0 | reduce | flops 1032192 | bytes 2129922 | tf_op jit(solution)/shard_map/reduce_sum | solution.py:536
  128.7 13.8 %all_to_all.15.tiles = bf16[16,112,128]{2,1,0:T(8,128)(2,1)S(1)} all-to-all(bf16[16,112,128]{2,1,0:T(8,128)(2,1)S(1)} %broadcast_in_dim.8), channel_id=1, replica_groups=mesh['z'=4,'x'=4,'core'=2,'feat'=4] {'z','x'}, dimensions={0} | all-to-all | bytes 917504 | tf_op jit(solution)/shard_map/all_to_all | solution.py:32
  142.5 2.8 %collective-permute-start.23 = (bf16[16,112,128]{2,1,0:T(8,128)(2,1)S(1)}, bf16[16,112,128]{2,1,0:T(8,128)(2,1)S(1)}, u32[]{:S(2)}, u32[]{:S(2)}) collective-permute-start(bf16[16,112,128]{2,1,0:T(8,128)(2,1)S(1)} %all_to_all.15.tiles), channel_id=1, source_target_pairs={{0,4},{4,0},{1,5},{5,1},{2,6},{6,2},{3,7},{7,3},{8,12},{12,8},{9,1... | collective-permute-start | bytes 1376264 | tf_op jit(solution)/shard_map/ppermute | solution.py:20
  145.3 1.4 collective-permute-done.23.far
  146.8 2.1 %shard_map.192 = (f32[3,16,2,16,128]{4,3,2,1,0:T(8,128)}, f32[128,512]{1,0:T(8,128)}, f32[2,16,2,16,128]{4,3,2,1,0:T(8,128)}, f32[128,512]{1,0:T(8,128)}, f32[256,512]{1,0:T(8,128)}) custom-call(s32[5]{0:T(128)S(1)} %copy-done.9, bf16[16,112,128]{2,1,0:T(8,128)(2,1)S(1)} %all_to_all.15.tiles, bf16[16,112,128]{2,1,0:T(8,128)(2,1)S(1)} %collective-permute-done.23.far, ...), custom_call_target="tpu_custom_call" | custom-call | tf_op jit(solution)/shard_map/pallas_call | solution.py:369
  (62 shorter events, 0.6 us)
Async XLA Ops:
  0.6 43.5 %copy-start.6 = (s32[2048]{0:T(1024)S(1)}, s32[2048]{0:T(1024)}, u32[]{:S(2)}) copy-start(s32[2048]{0:T(1024)} %param.16) | copy-start | bytes 24580
  0.6 44.1 %copy-start.10 = (s32[2048]{0:T(1024)S(1)}, s32[2048]{0:T(1024)}, u32[]{:S(2)}) copy-start(s32[2048]{0:T(1024)} %param.15) | copy-start | bytes 24580
  4.1 48.7 %copy-start = (bf16[2048,512]{1,0:T(8,128)(2,1)S(1)}, bf16[2048,512]{1,0:T(8,128)(2,1)}, u32[]{:S(2)}) copy-start(bf16[2048,512]{1,0:T(8,128)(2,1)} %edge.1) | copy-start | bytes 6291460
  4.1 48.7 %copy-start.1 = (bf16[3,512,128]{2,1,0:T(8,128)(2,1)S(1)}, bf16[3,512,128]{2,1,0:T(8,128)(2,1)}, u32[]{:S(2)}) copy-start(bf16[3,512,128]{2,1,0:T(8,128)(2,1)} %own_first.2) | copy-start | bytes 1179652
  4.1 48.7 %copy-start.2 = (bf16[256,512]{1,0:T(8,128)(2,1)S(1)}, bf16[256,512]{1,0:T(8,128)(2,1)}, u32[]{:S(2)}) copy-start(bf16[256,512]{1,0:T(8,128)(2,1)} %node.5) | copy-start | bytes 786436
  4.1 48.7 %copy-start.4 = (bf16[128,512]{1,0:T(8,128)(2,1)S(1)}, bf16[128,512]{1,0:T(8,128)(2,1)}, u32[]{:S(2)}) copy-start(bf16[128,512]{1,0:T(8,128)(2,1)} %own_second.2) | copy-start | bytes 393220
  4.1 48.7 %copy-start.7 = (s32[2048]{0:T(1024)S(1)}, s32[2048]{0:T(1024)}, u32[]{:S(2)}) copy-start(s32[2048]{0:T(1024)} %param.16) | copy-start | bytes 24580
  4.1 48.7 %copy-start.9 = (s32[5]{0:T(128)S(1)}, s32[5]{0:T(128)}, u32[]{:S(2)}) copy-start(s32[5]{0:T(128)} %stack.16.co) | copy-start | bytes 64
  6.4 6.6 %collective-permute-start.8 = (bf16[16,128]{1,0:T(8,128)(2,1)}, bf16[16,128]{1,0:T(8,128)(2,1)S(1)}, u32[]{:S(2)}, u32[]{:S(2)}) collective-permute-start(bf16[16,128]{1,0:T(8,128)(2,1)} %get-tuple-element.50), channel_id=1, source_target_pairs={{0,3},{1,0},{2,1},{3,2},{4,7},{5,4},{6,5},{7,6},{8,11},{9,8},{10,9... | collective-permute-start | bytes 12296 | tf_op jit(solution)/shard_map/ppermute | solution.py:28
  10.0 4.2 %collective-permute-start.7 = (bf16[16,128]{1,0:T(8,128)(2,1)}, bf16[16,128]{1,0:T(8,128)(2,1)S(1)}, u32[]{:S(2)}, u32[]{:S(2)}) collective-permute-start(bf16[16,128]{1,0:T(8,128)(2,1)} %get-tuple-element.50), channel_id=1, source_target_pairs={{0,2},{1,3},{2,0},{3,1},{4,6},{5,7},{6,4},{7,5},{8,10},{9,11},{10,... | collective-permute-start | bytes 12296 | tf_op jit(solution)/shard_map/ppermute | solution.py:28
  10.3 3.9 %collective-permute-start.6 = (bf16[16,128]{1,0:T(8,128)(2,1)}, bf16[16,128]{1,0:T(8,128)(2,1)S(1)}, u32[]{:S(2)}, u32[]{:S(2)}) collective-permute-start(bf16[16,128]{1,0:T(8,128)(2,1)} %get-tuple-element.50), channel_id=1, source_target_pairs={{0,1},{1,2},{2,3},{3,0},{4,5},{5,6},{6,7},{7,4},{8,9},{9,10},{10,1... | collective-permute-start | bytes 12296 | tf_op jit(solution)/shard_map/ppermute | solution.py:28
  11.0 23.6 %collective-permute-start.3 = (bf16[1024,128]{1,0:T(8,128)(2,1)}, bf16[1024,128]{1,0:T(8,128)(2,1)S(1)}, u32[]{:S(2)}, u32[]{:S(2)}) collective-permute-start(bf16[1024,128]{1,0:T(8,128)(2,1)} %get-tuple-element.49), channel_id=1, source_target_pairs={{0,3},{1,0},{2,1},{3,2},{4,7},{5,4},{6,5},{7,6},{8,11},{9,8},{10,9... | collective-permute-start | bytes 786440 | tf_op jit(solution)/shard_map/ppermute | solution.py:28
  13.0 22.9 %collective-permute-start.2 = (bf16[1024,128]{1,0:T(8,128)(2,1)}, bf16[1024,128]{1,0:T(8,128)(2,1)}, u32[]{:S(2)}, u32[]{:S(2)}) collective-permute-start(bf16[1024,128]{1,0:T(8,128)(2,1)} %get-tuple-element.49), channel_id=1, source_target_pairs={{0,1},{1,2},{2,3},{3,0},{4,5},{5,6},{6,7},{7,4},{8,9},{9,10},{10,1... | collective-permute-start | bytes 786440 | tf_op jit(solution)/shard_map/ppermute | solution.py:28
  15.6 15.3 %all-to-all-start = ((bf16[16,64,128]{2,1,0:T(8,128)(2,1)}), bf16[16,64,128]{2,1,0:T(8,128)(2,1)S(1)}, u32[]{:S(2)}, u32[]{:S(2)}) async-start(bf16[16,64,128]{2,1,0:T(8,128)(2,1)} %broadcast_in_dim.7), calls=%async_computation | async-start | bytes 524288 | tf_op jit(solution)/shard_map/all_to_all | solution.py:32
  23.2 13.9 %collective-permute-start = (bf16[32,512]{1,0:T(8,128)(2,1)}, bf16[32,512]{1,0:T(8,128)(2,1)S(1)}, u32[]{:S(2)}, u32[]{:S(2)}) collective-permute-start(bf16[32,512]{1,0:T(8,128)(2,1)} %get-tuple-element.47), channel_id=1, source_target_pairs={{0,1},{1,2},{2,3},{3,4},{4,5},{5,6},{6,7},{7,8},{8,9},{9,10},{10,1... | collective-permute-start | bytes 98312 | tf_op jit(solution)/shard_map/ppermute | solution.py:24
  23.3 14.4 %collective-permute-start.1 = (bf16[32,512]{1,0:T(8,128)(2,1)}, bf16[32,512]{1,0:T(8,128)(2,1)S(1)}, u32[]{:S(2)}, u32[]{:S(2)}) collective-permute-start(bf16[32,512]{1,0:T(8,128)(2,1)} %get-tuple-element.48), channel_id=1, source_target_pairs={{0,127},{1,0},{2,1},{3,2},{4,3},{5,4},{6,5},{7,6},{8,7},{9,8},{10,... | collective-permute-start | bytes 98312 | tf_op jit(solution)/shard_map/ppermute | solution.py:24
  30.9 20.3 %collective-permute-start.13 = (bf16[16,64,128]{2,1,0:T(8,128)(2,1)S(1)}, bf16[16,64,128]{2,1,0:T(8,128)(2,1)}, u32[]{:S(2)}, u32[]{:S(2)}) collective-permute-start(bf16[16,64,128]{2,1,0:T(8,128)(2,1)S(1)} %all-to-all-done.refs_4_), channel_id=1, source_target_pairs={{0,4},{4,0},{1,5},{5,1},{2,6},{6,2},{3,7},{7,3},{8,12},{12,8},{9,1... | collective-permute-start | bytes 786440 | tf_op jit(solution)/shard_map/ppermute | solution.py:20
  34.6 5.3 %collective-permute-start.4 = (bf16[512,128]{1,0:T(8,128)(2,1)S(1)}, bf16[512,128]{1,0:T(8,128)(2,1)}, u32[]{:S(2)}, u32[]{:S(2)}) collective-permute-start(bf16[512,128]{1,0:T(8,128)(2,1)S(1)} %slice.22), channel_id=1, source_target_pairs={{0,3},{1,0},{2,1},{3,2},{4,7},{5,4},{6,5},{7,6},{8,11},{9,8},{10,9... | collective-permute-start | bytes 393224 | tf_op jit(solution)/shard_map/ppermute | solution.py:28
  36.8 6.2 %collective-permute-start.5 = (bf16[512,128]{1,0:T(8,128)(2,1)S(1)}, bf16[512,128]{1,0:T(8,128)(2,1)}, u32[]{:S(2)}, u32[]{:S(2)}) collective-permute-start(bf16[512,128]{1,0:T(8,128)(2,1)S(1)} %slice.23), channel_id=1, source_target_pairs={{0,1},{1,2},{2,3},{3,0},{4,5},{5,6},{6,7},{7,4},{8,9},{9,10},{10,1... | collective-permute-start | bytes 393224 | tf_op jit(solution)/shard_map/ppermute | solution.py:28
  37.1 14.1 %collective-permute-start.10 = (bf16[1024,128]{1,0:T(8,128)(2,1)S(1)}, bf16[1024,128]{1,0:T(8,128)(2,1)}, u32[]{:S(2)}, u32[]{:S(2)}) collective-permute-start(bf16[1024,128]{1,0:T(8,128)(2,1)S(1)} %collective-permute-done.3.refs_1_), channel_id=1, source_target_pairs={{0,4},{4,0},{1,5},{5,1},{2,6},{6,2},{3,7},{7,3},{8,12},{12,8},{9,1... | collective-permute-start | bytes 786440 | tf_op jit(solution)/shard_map/ppermute | solution.py:20
  37.7 13.5 %collective-permute-start.9 = (bf16[1024,128]{1,0:T(8,128)(2,1)}, bf16[1024,128]{1,0:T(8,128)(2,1)}, u32[]{:S(2)}, u32[]{:S(2)}) collective-permute-start(bf16[1024,128]{1,0:T(8,128)(2,1)} %collective-permute-done.2.refs_0_), channel_id=1, source_target_pairs={{0,4},{4,0},{1,5},{5,1},{2,6},{6,2},{3,7},{7,3},{8,12},{12,8},{9,1... | collective-permute-start | bytes 786440 | tf_op jit(solution)/shard_map/ppermute | solution.py:20
  39.9 11.3 %collective-permute-start.11 = (bf16[512,128]{1,0:T(8,128)(2,1)}, bf16[512,128]{1,0:T(8,128)(2,1)}, u32[]{:S(2)}, u32[]{:S(2)}) collective-permute-start(bf16[512,128]{1,0:T(8,128)(2,1)} %collective-permute-done.4.refs_2_), channel_id=1, source_target_pairs={{0,4},{4,0},{1,5},{5,1},{2,6},{6,2},{3,7},{7,3},{8,12},{12,8},{9,1... | collective-permute-start | bytes 393224 | tf_op jit(solution)/shard_map/ppermute | solution.py:20
  43.0 8.2 %collective-permute-start.12 = (bf16[512,128]{1,0:T(8,128)(2,1)}, bf16[512,128]{1,0:T(8,128)(2,1)}, u32[]{:S(2)}, u32[]{:S(2)}) collective-permute-start(bf16[512,128]{1,0:T(8,128)(2,1)} %collective-permute-done.5.refs_3_), channel_id=1, source_target_pairs={{0,4},{4,0},{1,5},{5,1},{2,6},{6,2},{3,7},{7,3},{8,12},{12,8},{9,1... | collective-permute-start | bytes 393224 | tf_op jit(solution)/shard_map/ppermute | solution.py:20
  44.7 8.1 %copy-start.8 = (s32[4,512]{1,0:T(4,128)S(1)}, s32[4,512]{1,0:T(4,128)}, u32[]{:S(2)}) copy-start(s32[4,512]{1,0:T(4,128)} %reshape.49.refs_12_.dst_wide) | copy-start | bytes 24580
  45.3 5.9 %copy-start.17 = (bf16[768,128]{1,0:T(8,128)(2,1)S(1)}, bf16[768,128]{1,0:T(8,128)(2,1)}, u32[]{:S(2)}) copy-start(bf16[768,128]{1,0:T(8,128)(2,1)} %get-tuple-element.58) | copy-start | bytes 589828
  51.3 14.4 %collective-permute-start.16 = (bf16[768,128]{1,0:T(8,128)(2,1)S(1)}, bf16[768,128]{1,0:T(8,128)(2,1)S(1)}, u32[]{:S(2)}, u32[]{:S(2)}) collective-permute-start(bf16[768,128]{1,0:T(8,128)(2,1)S(1)} %copy-done.17), channel_id=1, source_target_pairs={{0,3},{1,0},{2,1},{3,2},{4,7},{5,4},{6,5},{7,6},{8,11},{9,8},{10,9... | collective-permute-start | bytes 589832 | tf_op jit(solution)/shard_map/ppermute | solution.py:28
  51.3 14.4 %collective-permute-start.15 = (bf16[768,128]{1,0:T(8,128)(2,1)S(1)}, bf16[768,128]{1,0:T(8,128)(2,1)S(1)}, u32[]{:S(2)}, u32[]{:S(2)}) collective-permute-start(bf16[768,128]{1,0:T(8,128)(2,1)S(1)} %copy-done.17), channel_id=1, source_target_pairs={{0,2},{1,3},{2,0},{3,1},{4,6},{5,7},{6,4},{7,5},{8,10},{9,11},{10,... | collective-permute-start | bytes 589832 | tf_op jit(solution)/shard_map/ppermute | solution.py:28
  52.2 13.5 %collective-permute-start.14 = (bf16[768,128]{1,0:T(8,128)(2,1)S(1)}, bf16[768,128]{1,0:T(8,128)(2,1)S(1)}, u32[]{:S(2)}, u32[]{:S(2)}) collective-permute-start(bf16[768,128]{1,0:T(8,128)(2,1)S(1)} %copy-done.17), channel_id=1, source_target_pairs={{0,1},{1,2},{2,3},{3,0},{4,5},{5,6},{6,7},{7,4},{8,9},{9,10},{10,1... | collective-permute-start | bytes 589832 | tf_op jit(solution)/shard_map/ppermute | solution.py:28
  52.8 15.3 %copy-start.3 = (bf16[2,512,128]{2,1,0:T(8,128)(2,1)S(1)}, bf16[2,512,128]{2,1,0:T(8,128)(2,1)}, u32[]{:S(2)}) copy-start(bf16[2,512,128]{2,1,0:T(8,128)(2,1)} %own_first.3) | copy-start | bytes 786436
  52.9 15.2 %copy-start.5 = (bf16[128,512]{1,0:T(8,128)(2,1)S(1)}, bf16[128,512]{1,0:T(8,128)(2,1)}, u32[]{:S(2)}) copy-start(bf16[128,512]{1,0:T(8,128)(2,1)} %own_second.3) | copy-start | bytes 393220
  52.9 15.2 %copy-start.12 = (bf16[1152,2048]{1,0:T(8,128)(2,1)S(1)}, bf16[1152,2048]{1,0:T(8,128)(2,1)}, u32[]{:S(2)}) copy-start(bf16[1152,2048]{1,0:T(8,128)(2,1)} %get-tuple-element.70.refs_16_) | copy-start | bytes 14155780
  52.9 15.2 %copy-start.13 = (bf16[2048,512]{1,0:T(8,128)(2,1)S(1)}, bf16[2048,512]{1,0:T(8,128)(2,1)}, u32[]{:S(2)}) copy-start(bf16[2048,512]{1,0:T(8,128)(2,1)} %refs_14_.1) | copy-start | bytes 6291460
  52.9 15.2 %copy-start.14 = (bf16[512,2048]{1,0:T(8,128)(2,1)S(1)}, bf16[512,2048]{1,0:T(8,128)(2,1)}, u32[]{:S(2)}) copy-start(bf16[512,2048]{1,0:T(8,128)(2,1)} %get-tuple-element.65.refs_9_) | copy-start | bytes 6291460
  52.9 15.2 %copy-start.15 = (bf16[2048,256]{1,0:T(8,128)(2,1)S(1)}, bf16[2048,256]{1,0:T(8,128)(2,1)}, u32[]{:S(2)}) copy-start(bf16[2048,256]{1,0:T(8,128)(2,1)} %get-tuple-element.57.refs_15_) | copy-start | bytes 3145732
  52.9 15.2 %copy-start.16 = (bf16[256,512]{1,0:T(8,128)(2,1)S(1)}, bf16[256,512]{1,0:T(8,128)(2,1)}, u32[]{:S(2)}) copy-start(bf16[256,512]{1,0:T(8,128)(2,1)} %grad_node.1) | copy-start | bytes 786436
  65.7 1.7 %collective-permute-start.17 = (bf16[768,128]{1,0:T(8,128)(2,1)S(1)}, bf16[768,128]{1,0:T(8,128)(2,1)S(1)}, u32[]{:S(2)}, u32[]{:S(2)}) collective-permute-start(bf16[768,128]{1,0:T(8,128)(2,1)S(1)} %collective-permute-done.14.refs_0_), channel_id=1, source_target_pairs={{0,4},{4,0},{1,5},{5,1},{2,6},{6,2},{3,7},{7,3},{8,12},{12,8},{9,1... | collective-permute-start | bytes 589832 | tf_op jit(solution)/shard_map/ppermute | solution.py:20
  66.4 1.4 collective-permute-start.18
  66.5 1.6 %collective-permute-start.19 = (bf16[768,128]{1,0:T(8,128)(2,1)S(1)}, bf16[768,128]{1,0:T(8,128)(2,1)S(1)}, u32[]{:S(2)}, u32[]{:S(2)}) collective-permute-start(bf16[768,128]{1,0:T(8,128)(2,1)S(1)} %collective-permute-done.16.refs_2_), channel_id=1, source_target_pairs={{0,4},{4,0},{1,5},{5,1},{2,6},{6,2},{3,7},{7,3},{8,12},{12,8},{9,1... | collective-permute-start | bytes 589832 | tf_op jit(solution)/shard_map/ppermute | solution.py:20
  84.5 4.2 %collective-permute-start.20 = (bf16[8,2,4,128,128]{4,3,2,1,0:T(8,128)(2,1)S(1)}, bf16[8,2,4,128,128]{4,3,2,1,0:T(8,128)(2,1)S(1)}, u32[]{:S(2)}, u32[]{:S(2)}) collective-permute-start(bf16[8,2,4,128,128]{4,3,2,1,0:T(8,128)(2,1)S(1)} %get-tuple-element.73), channel_id=1, source_target_pairs={{0,4},{4,0},{1,5},{5,1},{2,6},{6,2},{3,7},{7,3},{8,12},{12,8},{9,1... | collective-permute-start | bytes 6291464 | tf_op jit(solution)/shard_map/ppermute | solution.py:20
  91.1 35.6 %all-to-all-start.1 = ((bf16[64,128,128]{2,1,0:T(8,128)(2,1)}), bf16[64,128,128]{2,1,0:T(8,128)(2,1)}, u32[]{:S(2)}, u32[]{:S(2)}) async-start(bf16[64,128,128]{2,1,0:T(8,128)(2,1)} %bitcast.9), calls=%async_computation.1 | async-start | bytes 4194304 | tf_op jit(solution)/shard_map/all_to_all | solution.py:32
  98.7 48.1 %copy-start.11 = (s32[1,128]{1,0:T(1,128)S(1)}, s32[1,128]{1,0:T(1,128)}, u32[]{:S(2)}) copy-start(s32[1,128]{1,0:T(1,128)} %add_bitcast_fusion.targets) | copy-start | bytes 1540
  98.7 29.9 %collective-permute-start.21 = (bf16[32,512]{1,0:T(8,128)(2,1)S(1)}, bf16[32,512]{1,0:T(8,128)(2,1)S(1)}, u32[]{:S(2)}, u32[]{:S(2)}) collective-permute-start(bf16[32,512]{1,0:T(8,128)(2,1)S(1)} %get-tuple-element.75), channel_id=1, source_target_pairs={{0,127},{1,0},{2,1},{3,2},{4,3},{5,4},{6,5},{7,6},{8,7},{9,8},{10,... | collective-permute-start | bytes 98312 | tf_op jit(solution)/shard_map/ppermute | solution.py:24
  101.6 27.0 %collective-permute-start.22 = (bf16[32,512]{1,0:T(8,128)(2,1)S(1)}, bf16[32,512]{1,0:T(8,128)(2,1)S(1)}, u32[]{:S(2)}, u32[]{:S(2)}) collective-permute-start(bf16[32,512]{1,0:T(8,128)(2,1)S(1)} %get-tuple-element.77), channel_id=1, source_target_pairs={{0,1},{1,2},{2,3},{3,4},{4,5},{5,6},{6,7},{7,8},{8,9},{9,10},{10,1... | collective-permute-start | bytes 98312 | tf_op jit(solution)/shard_map/ppermute | solution.py:24
  142.5 4.3 %collective-permute-start.23 = (bf16[16,112,128]{2,1,0:T(8,128)(2,1)S(1)}, bf16[16,112,128]{2,1,0:T(8,128)(2,1)S(1)}, u32[]{:S(2)}, u32[]{:S(2)}) collective-permute-start(bf16[16,112,128]{2,1,0:T(8,128)(2,1)S(1)} %all_to_all.15.tiles), channel_id=1, source_target_pairs={{0,4},{4,0},{1,5},{5,1},{2,6},{6,2},{3,7},{7,3},{8,12},{12,8},{9,1... | collective-permute-start | bytes 1376264 | tf_op jit(solution)/shard_map/ppermute | solution.py:20

commit v9 on v7

--- a/solution.py
+++ b/solution.py
@@ -16,6 +16,12 @@
 MIB = 1024 * 1024
 
 
+def places(count):
+    core = lax.axis_index("core")
+    patch = (lax.axis_index("z") * 4 + lax.axis_index("x")) * 2 + core
+    return patch, patch, core, lax.axis_index("feat"), count[0]
+
+
 def other_core(value):
     return lax.ppermute(value, "core", [(0, 1), (1, 0)])
 
@@ -85,7 +91,8 @@
     return jnp.where(lanes + step * CHUNK < count, row, -1)
 
 
-def hot_kernel(co, dst, src_wide, dst_wide, edge, hot, turned, edge_turned):
+def hot_kernel(count, dst, src_wide, dst_wide, edge, hot, turned, edge_turned):
+    co = places(count)
     step = pl.program_id(0)
     edge_turned[...] = jnp.transpose(edge[...])
     lanes = lax.broadcasted_iota(jnp.int32, (1, 128), 1)
@@ -101,16 +108,31 @@
         turned[j * 128 : (j + 1) * 128, :] = block
 
 
-def pack_kernel(co, node, targets, edge_first, edge_second, first, second, *outs):
+def halo_match(lists):
+    place = lax.broadcasted_iota(jnp.int32, (256, 32), 0)
+    return [jnp.where(place == lists[k : k + 1, :], 1.0, 0.0).astype(BF16) for k in range(2)]
+
+
+def coarse_match(owned):
+    place = lax.broadcasted_iota(jnp.int32, (256, 16), 0)
+    slot = lax.broadcasted_iota(jnp.int32, (256, 16), 1) % 4
+    hot = jnp.zeros((256, 16), F32)
+    for j in range(4):
+        hot = jnp.where((place == owned[0, j]) & (slot == j), 1.0, hot)
+    return hot.astype(BF16)
+
+
+def pack_kernel(count, owned, node, lists, edge_first, edge_second, first, second, *outs):
     tiles, to_next, to_prev, packed = outs
-    match = lax.broadcasted_iota(jnp.int32, (256, 128), 0) == targets[...]
-    rows = dot_tn(jnp.where(match, 1.0, 0.0).astype(BF16), node[...])
-    to_next[...] = rows[0:32].astype(BF16)
-    to_prev[...] = rows[32:64].astype(BF16)
+    co = places(count)
+    halo_hot, coarse_hot = halo_match(lists), coarse_match(owned)
+    to_prev[...] = dot_tn(halo_hot[0], node[...]).astype(BF16)
+    to_next[...] = dot_tn(halo_hot[1], node[...]).astype(BF16)
+    rows = dot_tn(coarse_hot, node[...])
     group = lax.broadcasted_iota(jnp.int32, (16, 128), 0) // 4
     coarse = jnp.zeros((16, 128), F32)
     for b in range(4):
-        coarse = jnp.where(group == b, rows[64:80, b * 128 : (b + 1) * 128], coarse)
+        coarse = jnp.where(group == b, rows[:, b * 128 : (b + 1) * 128], coarse)
     patch = co[0]
     at = pl.ds(pl.multiple_of(patch * 16, 16), 16)
     parts = [edge_first[m, at, :] for m in range(3)]
@@ -133,7 +155,7 @@
     return jnp.where(place < count, 1.0, 0.0)
 
 
-HALVES = (slice(0, CHUNK // 2), slice(CHUNK // 2, CHUNK))
+HALVES = (slice(0, CHUNK),)
 
 
 def place_weights(co, own_first, own_second, near, far, first, second):
@@ -182,9 +204,10 @@
         lookup[320:832, half * 256 + 128 : half * 256 + 256] = other_block.astype(BF16)
 
 
-def forward_kernel(co, node, prev, following, near, far, src, dst, dst_wide, edge, *refs):
+def forward_kernel(count, node, prev, following, near, far, src, dst, dst_wide, edge, *refs):
     edge_out, incoming, act_out, normed_out, slope_out, factor_out, lookup, first, second = refs[:9]
     table, total, coarse = refs[9:]
+    co = places(count)
     step = pl.program_id(0)
 
     @pl.when(step == 0)
@@ -220,7 +243,7 @@
         factor = lax.rsqrt(mean(centre * centre) + EPSILON) * live[h]
         normed = centre * factor
         normed_out[h, :] = normed.astype(BF16)
-        factor_out[h, :] = jnp.broadcast_to(factor, (CHUNK // 2, 128))
+        factor_out[h, :] = jnp.broadcast_to(factor, (CHUNK, 128))
         edge_out[h, :] = (edge[h, :].astype(F32) + normed).astype(BF16)
     total[...] += dot(turned, edge_out[...])
 
@@ -264,8 +287,9 @@
         target[:, :, :, 112:128, :] = value
 
 
-def backward_kernel(co, node, incoming, grad_node, own_first, own_second, *refs):
+def backward_kernel(count, node, incoming, grad_node, own_first, own_second, *refs):
     near, far, refs = refs[:3], refs[3:6], refs[6:]
+    co = places(count)
     edge_first, edge_second, lookup = refs[:3]
     edge_turned, act, normed, slope, factor, grad_edge, hot, turned = refs[3:11]
     node_out, node_total, edge_grad, to_prev, to_next, keep, give = refs[11:18]
@@ -322,8 +346,9 @@
         put_owned(co, back[320:832], owned, keep, give)
 
 
-def final_kernel(co, tiles, far, own, ahead, behind, targets, node_total, *refs):
-    edge_first, edge_second, node_first, node_second, node_grad, rows = refs
+def final_kernel(count, owned, tiles, far, own, ahead, behind, lists, node_total, *refs):
+    edge_first, edge_second, node_first, node_second, node_grad = refs
+    co = places(count)
     for part, core in ((tiles, co[2]), (far, 1 - co[2])):
         for m in range(3):
             value = part[:, m * 16 : (m + 1) * 16, :].astype(F32)
@@ -336,16 +361,16 @@
             b = pl.ds(pl.multiple_of((k % 2 * 2 + core) * 128, 128), 128)
             edge_second[r : r + 16, b] = part[k, 80:96, :].astype(F32)
             node_second[r : r + 16, b] = part[k, 96:112, :].astype(F32)
-    rows[0:32, :] = ahead[...]
-    rows[32:64, :] = behind[...]
+    halo_hot, coarse_hot = halo_match(lists), coarse_match(owned)
     group = lax.broadcasted_iota(jnp.int32, (16, 128), 0) // 4
-    for b in range(4):
-        value = jnp.where(group == b, own[112:128, :].astype(F32), 0.0)
-        rows[64:80, b * 128 : (b + 1) * 128] = value.astype(BF16)
-    rows[80:128, :] = jnp.zeros((48, 512), BF16)
-    match = lax.broadcasted_iota(jnp.int32, (256, 128), 0) == targets[...]
-    hot = jnp.where(match, 1.0, 0.0).astype(BF16)
-    node_grad[...] = node_total[...] + dot(hot, rows[...])
+    rows = own[112:128, :].astype(F32)
+    blocks = [jnp.where(group == b, rows, 0.0).astype(BF16) for b in range(4)]
+    node_grad[...] = (
+        node_total[...]
+        + dot(halo_hot[1], ahead[...])
+        + dot(halo_hot[0], behind[...])
+        + dot(coarse_hot, jnp.concatenate(blocks, axis=1))
+    )
 
 
 SMEM = pl.BlockSpec(memory_space=pltpu.SMEM)
@@ -405,17 +430,11 @@
     grad_node,
     grad_edge,
 ):
-    core = lax.axis_index("core")
-    patch = (lax.axis_index("z") * 4 + lax.axis_index("x")) * 2 + core
-    co = jnp.stack([patch, patch, core, lax.axis_index("feat"), edge_count[0]]).astype(jnp.int32)
-    lists, owned = halo_send[0], coarse_of[0]
-    unused = jnp.full((48,), -1, jnp.int32)
-    targets = jnp.concatenate([lists[1], lists[0], jnp.tile(owned, 4), unused]).reshape(1, 128)
-
+    lists = halo_send.reshape(2, 32)
     packed, to_next, to_prev, node_half = plain_call(
         pack_kernel,
-        [co],
-        [node_lat, targets, edge_w1, edge_w2, node_w1, node_w2],
+        [edge_count, coarse_of],
+        [node_lat, lists, edge_w1, edge_w2, node_w1, node_w2],
         [shape(64, 80, 128), shape(32, 512), shape(32, 512), shape(768, 128)],
         mib=60,
     )
@@ -438,10 +457,10 @@
         cost_estimate=pl.CostEstimate(
             flops=20_000_000, bytes_accessed=14_000_000, transcendentals=0
         ),
-    )(co, *indices, edge_lat)
+    )(edge_count, *indices, edge_lat)
     near = after(near, from_prev, from_next, hot)
     far = other_core(near)
-    node_half = after(node_half, near, far)
+    node_half = after(node_half, near)
     node_near = [
         lax.ppermute(node_half, "feat", [(k, (k + s) % 4) for k in range(4)]) for s in (1, 2, 3)
     ]
@@ -476,7 +495,7 @@
         cost_estimate=pl.CostEstimate(
             flops=7_000_000_000, bytes_accessed=18_000_000, transcendentals=1_000_000
         ),
-    )(co, *fixed, edge_lat)
+    )(edge_count, *fixed, edge_lat)
 
     node_near = [after(part, incoming) for part in node_near]
     node_far = [other_core(part) for part in node_near]
@@ -517,7 +536,7 @@
         cost_estimate=pl.CostEstimate(
             flops=9_000_000_000, bytes_accessed=24_000_000, transcendentals=100_000
         ),
-    )(co, *fixed, *moving)
+    )(edge_count, *fixed, *moving)
 
     pair = (keep.astype(F32) + other_core(give).astype(F32)).astype(BF16).reshape(64, 128, 128)
     ahead = shifted(after(to_prev, pair), -1)
@@ -528,8 +547,8 @@
     far_tiles = other_core(tiles)
     edge_first, edge_second, node_first, node_second, node_grad = plain_call(
         final_kernel,
-        [co],
-        [tiles, far_tiles, own, ahead, behind, targets, node_total],
+        [edge_count, coarse_of],
+        [tiles, far_tiles, own, ahead, behind, lists, node_total],
         [
             shape(3, 16, 2, 16, 128, dtype=F32),
             shape(128, 512, dtype=F32),
@@ -537,7 +556,6 @@
             shape(128, 512, dtype=F32),
             shape(256, 512, dtype=F32),
         ],
-        [pltpu.VMEM((128, 512), BF16)],
     )
     return (
         edge_out,

time: 141 us -> 135 us (0.957)
  waiting for transfers between devices: 43.5 us -> 41 us
  local copies, waits for them, and re-layouts: 4.4 us -> 2.3 us
    ppermute x6, waiting for transfers between devices: 9.19 us -> 6.59 us  [other_core(): return lax.ppermute(value, 'core', [(0, 1), (1, 0)])]
  transfers between devices with their start and end apart: 15 -> 15, of which waited for: 9 -> 8; matrix products, arithmetic and copies ran while one was open for 1% -> 1% of each run, Pallas kernels for 12% -> 13%
where the time goes in v9:
time: 135 us
  waiting for transfers between devices  41 us (30%)
  Pallas kernels  39 us (29%)
  starting transfers between devices  34.5 us (26%)
  blocking collectives  13.8 us (10%)
  other arithmetic  2.76 us (2%)
  local copies, waits for them, and re-layouts  2.3 us (2%)
  between operations  1.51 us (1%)
    all_to_all x2, waiting for transfers between devices, exchange(): return lax.all_to_all(value, axes, 0, 0, tiled=True)  34.3 us
    all_to_all x2, starting transfers between devices, exchange(): return lax.all_to_all(value, axes, 0, 0, tiled=True)  18.7 us
    pallas_call x1, Pallas kernels, shards(): pl.pallas_call(backward_kernel, grid=(STEPS,), in_specs=[SMEM] + [like(v)...  16.4 us
    all_to_all x1, blocking collectives, exchange(): return lax.all_to_all(value, axes, 0, 0, tiled=True)  13.8 us
    pallas_call x1, Pallas kernels, shards(): pl.pallas_call(forward_kernel, grid=(STEPS,), in_specs=[SMEM] + [like(v)...  11.8 us
    ppermute x6, starting transfers between devices, other_core(): return lax.ppermute(value, 'core', [(0, 1), (1, 0)])  6.65 us
    ppermute x6, waiting for transfers between devices, other_core(): return lax.ppermute(value, 'core', [(0, 1), (1, 0)])  6.59 us
    ppermute x4, starting transfers between devices, shifted(): lax.ppermute(value, BOTH, [(k, (k + steps) % 128) for k in range(128)])  6.5 us
  transfers between devices with their start and end apart: 15, of which 8 were waited for; matrix products, arithmetic and copies ran while one was open for 1% of the time, Pallas kernels for 13%

profile of v9, /device:TPU:1, one launch (start us, length us, event | category | flops | bytes accessed | tf_op | source)
XLA Modules:
  0.0 134.9 jit_solution(2552114258743198723)
XLA Ops:
  0.6 0.0 copy-start.5
  1.3 2.7 %shard_map.188 = (bf16[64,80,128]{2,1,0:T(8,128)(2,1)}, bf16[32,512]{1,0:T(8,128)(2,1)}, bf16[32,512]{1,0:T(8,128)(2,1)}, bf16[768,128]{1,0:T(8,128)(2,1)}) custom-call(s32[1]{0:T(128)S(6)} %copy.21.count, s32[1,4]{1,0:T(1,128)} %owned.3, bf16[256,512]{1,0:T(8,128)(2,1)} %node.5, s32[2,32]{1,0:T(2,128)} %bitcast.12, bf16[3,512,128]{2,1,0:T(8,128)(2,1)} %edge_first.1, ...), custom_call_target="tpu_custom_call" | custom-call | tf_op jit(solution)/shard_map/pallas_call | solution.py:385
  4.0 0.0 copy-start.6
  4.0 12.1 %all-to-all-start = ((bf16[64,80,128]{2,1,0:T(8,128)(2,1)}), bf16[64,80,128]{2,1,0:T(8,128)(2,1)S(1)}, u32[]{:S(2)}, u32[]{:S(2)}) async-start(bf16[64,80,128]{2,1,0:T(8,128)(2,1)} %get-tuple-element.49), calls=%async_computation | async-start | bytes 2621440 | tf_op jit(solution)/shard_map/all_to_all | solution.py:34
  16.1 1.1 collective-permute-start
  17.2 2.4 %collective-permute-start.1 = (bf16[32,512]{1,0:T(8,128)(2,1)S(1)}, bf16[32,512]{1,0:T(8,128)(2,1)S(1)}, u32[]{:S(2)}, u32[]{:S(2)}) collective-permute-start(bf16[32,512]{1,0:T(8,128)(2,1)S(1)} %copy-done.16), channel_id=1, source_target_pairs={{0,127},{1,0},{2,1},{3,2},{4,3},{5,4},{6,5},{7,6},{8,7},{9,8},{10,... | collective-permute-start | bytes 98312 | tf_op jit(solution)/shard_map/ppermute | solution.py:30
  19.7 0.6 reshape.48.dst_wide
  20.3 0.6 reshape.47.src_wide
  20.9 5.8 %shard_map.189 = (bf16[2048,256]{1,0:T(8,128)(2,1)}, bf16[1152,2048]{1,0:T(8,128)(2,1)}, bf16[512,2048]{1,0:T(8,128)(2,1)}) custom-call(s32[1]{0:T(128)S(6)} %copy.21.count, s32[16,128]{1,0:T(8,128)} %bitcast.9, s32[4,512]{1,0:T(4,128)} %reshape.47.src_wide, s32[4,512]{1,0:T(4,128)} %reshape.48.dst_wide, bf16[2048,512]{1,0:T(8,128)(2,1)} %edge.3), custom_call_target="tpu_custom_call" | custom-call | flops 20000000 | bytes 14000000 | tf_op jit(solution)/shard_map/pallas_call | solution.py:450
  26.7 0.2 collective-permute-done.prev
  26.9 0.0 collective-permute-done.1.following
  26.9 9.1 %all-to-all-done = bf16[64,80,128]{2,1,0:T(8,128)(2,1)S(1)} async-done(((bf16[64,80,128]{2,1,0:T(8,128)(2,1)}), bf16[64,80,128]{2,1,0:T(8,128)(2,1)S(1)}, u32[]{:S(2)}, u32[]{:S(2)}) %all-to-all-start) | async-done | bytes 1310752 | tf_op jit(solution)/shard_map/all_to_all | solution.py:34
  35.9 2.6 %collective-permute-start.2 = (bf16[16,4,80,128]{3,2,1,0:T(8,128)(2,1)S(1)}, bf16[16,4,80,128]{3,2,1,0:T(8,128)(2,1)S(1)}, u32[]{:S(2)}, u32[]{:S(2)}) collective-permute-start(bf16[16,4,80,128]{3,2,1,0:T(8,128)(2,1)S(1)} %bitcast.7), channel_id=1, source_target_pairs={{0,4},{4,0},{1,5},{5,1},{2,6},{6,2},{3,7},{7,3},{8,12},{12,8},{9,1... | collective-permute-start | bytes 3932168 | tf_op jit(solution)/shard_map/ppermute | solution.py:26
  38.5 0.4 collective-permute-start.5
  38.9 2.3 %collective-permute-start.4 = (bf16[768,128]{1,0:T(8,128)(2,1)}, bf16[768,128]{1,0:T(8,128)(2,1)S(1)}, u32[]{:S(2)}, u32[]{:S(2)}) collective-permute-start(bf16[768,128]{1,0:T(8,128)(2,1)} %get-tuple-element.58), channel_id=1, source_target_pairs={{0,2},{1,3},{2,0},{3,1},{4,6},{5,7},{6,4},{7,5},{8,10},{9,11},{10,... | collective-permute-start | bytes 589832 | tf_op jit(solution)/shard_map/ppermute | solution.py:465
  41.2 0.0 collective-permute-start.3
  41.2 0.0 collective-permute-done.2.far
  41.2 0.0 copy-start.1
  41.2 0.9 copy-done.1
  42.2 0.0 copy-start.12
  42.2 0.0 copy-start.13
  42.2 0.0 copy-start.15
  42.2 11.8 %shard_map.190 = (bf16[2048,512]{1,0:T(8,128)(2,1)}, bf16[256,512]{1,0:T(8,128)(2,1)S(1)}, bf16[2048,512]{1,0:T(8,128)(2,1)S(1)}, bf16[2048,512]{1,0:T(8,128)(2,...) custom-call(s32[1]{0:T(128)S(6)} %copy.21.count, ...), custom_call_target="tpu_custom_call" | custom-call | flops 7000000000 | bytes 18000000 | tf_op jit(solution)/shard_map/pallas_call | solution.py:470
  54.0 0.0 collective-permute-done.5.refs_2_
  54.0 0.0 collective-permute-done.4.refs_1_
  54.1 0.6 collective-permute-start.6
  54.7 0.1 collective-permute-start.7
  54.8 0.4 collective-permute-start.8
  55.2 0.6 collective-permute-done.6.refs_3_
  55.8 0.4 collective-permute-done.7.refs_4_
  56.1 0.3 collective-permute-done.8.refs_5_
  56.5 16.4 %shard_map.191 = (bf16[256,512]{1,0:T(8,128)(2,1)}, f32[256,512]{1,0:T(8,128)S(1)}, bf16[2048,512]{1,0:T(8,128)(2,1)}, bf16[32,512]{1,0:T(8,128)(2,1)S(1)}, bf16...) custom-call(s32[1]{0:T(128)S(6)} %copy.21.count, ...), custom_call_target="tpu_custom_call" | custom-call | flops 8999999488 | bytes 24000000 | tf_op jit(solution)/shard_map/pallas_call | solution.py:506
  72.9 0.2 collective-permute-start.9
  73.1 3.9 %collective-permute-done.9 = bf16[8,2,4,128,128]{4,3,2,1,0:T(8,128)(2,1)S(1)} collective-permute-done((bf16[8,2,4,128,128]{4,3,2,1,0:T(8,128)(2,1)S(1)}, bf16[8,2,4,128,128]{4,3,2,1,0:T(8,128)(2,1)S(1)}, u32[]{:S(2)}, u32[]{:S(2)}) %collective-permute-start.9) | collective-permute-done | bytes 2097184 | tf_op jit(solution)/shard_map/ppermute | solution.py:26
  77.1 2.4 %add_convert_fusion = bf16[8,2,4,128,128]{4,3,2,1,0:T(8,128)(2,1)} fusion(bf16[8,2,4,128,128]{4,3,2,1,0:T(8,128)(2,1)S(1)} %collective-permute-done.9, bf16[8,2,4,128,128]{4,3,2,1,0:T(8,128)(2,1)S(1)} %get-tuple-element.72), kind=kLoop, calls=%fused_computation | loop fusion | flops 4194304 | bytes 6291456 | tf_op jit(solution)/shard_map/convert_element_type | solution.py:541
  79.5 6.6 %all-to-all-start.1 = ((bf16[64,128,128]{2,1,0:T(8,128)(2,1)}), bf16[64,128,128]{2,1,0:T(8,128)(2,1)S(1)}, u32[]{:S(2)}, u32[]{:S(2)}) async-start(bf16[64,128,128]{2,1,0:T(8,128)(2,1)} %bitcast.4), calls=%async_computation.1 | async-start | bytes 4194304 | tf_op jit(solution)/shard_map/all_to_all | solution.py:34
  86.1 0.0 copy-start.9
  86.1 0.0 copy-start.10
  86.1 3.0 %collective-permute-start.10 = (bf16[32,512]{1,0:T(8,128)(2,1)S(1)}, bf16[32,512]{1,0:T(8,128)(2,1)S(1)}, u32[]{:S(2)}, u32[]{:S(2)}) collective-permute-start(bf16[32,512]{1,0:T(8,128)(2,1)S(1)} %get-tuple-element.75), channel_id=1, source_target_pairs={{0,127},{1,0},{2,1},{3,2},{4,3},{5,4},{6,5},{7,6},{8,7},{9,8},{10,... | collective-permute-start | bytes 98312 | tf_op jit(solution)/shard_map/ppermute | solution.py:30
  89.1 0.0 collective-permute-start.11
  89.1 25.2 %all-to-all-done.1 = bf16[64,128,128]{2,1,0:T(8,128)(2,1)S(1)} async-done(((bf16[64,128,128]{2,1,0:T(8,128)(2,1)}), bf16[64,128,128]{2,1,0:T(8,128)(2,1)S(1)}, u32[]{:S(2)}, u32[]{:S(2)}) %all-to-all-start.1) | async-done | bytes 2097184 | tf_op jit(solution)/shard_map/all_to_all | solution.py:34
  114.3 0.3 reduce_sum.12.own
  114.7 0.0 collective-permute-done.11.behind
  114.7 0.1 broadcast_in_dim.2
  114.8 13.8 %all_to_all.15.tiles = bf16[16,112,128]{2,1,0:T(8,128)(2,1)S(1)} all-to-all(bf16[16,112,128]{2,1,0:T(8,128)(2,1)S(1)} %broadcast_in_dim.2), channel_id=1, replica_groups=mesh['z'=4,'x'=4,'core'=2,'feat'=4] {'z','x'}, dimensions={0} | all-to-all | bytes 917504 | tf_op jit(solution)/shard_map/all_to_all | solution.py:34
  128.6 2.7 %collective-permute-start.12 = (bf16[16,112,128]{2,1,0:T(8,128)(2,1)S(1)}, bf16[16,112,128]{2,1,0:T(8,128)(2,1)S(1)}, u32[]{:S(2)}, u32[]{:S(2)}) collective-permute-start(bf16[16,112,128]{2,1,0:T(8,128)(2,1)S(1)} %all_to_all.15.tiles), channel_id=1, source_target_pairs={{0,4},{4,0},{1,5},{5,1},{2,6},{6,2},{3,7},{7,3},{8,12},{12,8},{9,1... | collective-permute-start | bytes 1376264 | tf_op jit(solution)/shard_map/ppermute | solution.py:26
  131.3 1.4 %collective-permute-done.12.far = bf16[16,112,128]{2,1,0:T(8,128)(2,1)S(1)} collective-permute-done((bf16[16,112,128]{2,1,0:T(8,128)(2,1)S(1)}, bf16[16,112,128]{2,1,0:T(8,128)(2,1)S(1)}, u32[]{:S(2)}, u32[]{:S(2)}) %collective-permute-start.12) | collective-permute-done | bytes 458784 | tf_op jit(solution)/shard_map/ppermute | solution.py:26
  132.7 2.2 %shard_map.192 = (f32[3,16,2,16,128]{4,3,2,1,0:T(8,128)}, f32[128,512]{1,0:T(8,128)}, f32[2,16,2,16,128]{4,3,2,1,0:T(8,128)}, f32[128,512]{1,0:T(8,128)}, f32[256,512]{1,0:T(8,128)}) custom-call(s32[1]{0:T(128)S(6)} %copy.21.count, s32[1,4]{1,0:T(1,128)S(1)} %copy-done.10, bf16[16,112,128]{2,1,0:T(8,128)(2,1)S(1)} %all_to_all.15.tiles, ...), custom_call_target="tpu_custom_call" | custom-call | tf_op jit(solution)/shard_map/pallas_call | solution.py:385
  (28 shorter events, 0.1 us)
Async XLA Ops:
  0.6 19.0 %copy-start.5 = (s32[2048]{0:T(1024)S(1)}, s32[2048]{0:T(1024)}, u32[]{:S(2)}) copy-start(s32[2048]{0:T(1024)} %param.16) | copy-start | bytes 24580
  0.6 19.6 %copy-start.8 = (s32[2048]{0:T(1024)S(1)}, s32[2048]{0:T(1024)}, u32[]{:S(2)}) copy-start(s32[2048]{0:T(1024)} %param.15) | copy-start | bytes 24580
  4.0 13.2 %copy-start.16 = (bf16[32,512]{1,0:T(8,128)(2,1)S(1)}, bf16[32,512]{1,0:T(8,128)(2,1)}, u32[]{:S(2)}) copy-start(bf16[32,512]{1,0:T(8,128)(2,1)} %get-tuple-element.48) | copy-start | bytes 98308
  4.0 37.2 %copy-start = (bf16[2048,512]{1,0:T(8,128)(2,1)S(1)}, bf16[2048,512]{1,0:T(8,128)(2,1)}, u32[]{:S(2)}) copy-start(bf16[2048,512]{1,0:T(8,128)(2,1)} %edge.3) | copy-start | bytes 6291460
  4.0 37.2 %copy-start.6 = (s32[2048]{0:T(1024)S(1)}, s32[2048]{0:T(1024)}, u32[]{:S(2)}) copy-start(s32[2048]{0:T(1024)} %param.16) | copy-start | bytes 24580
  4.0 31.9 %all-to-all-start = ((bf16[64,80,128]{2,1,0:T(8,128)(2,1)}), bf16[64,80,128]{2,1,0:T(8,128)(2,1)S(1)}, u32[]{:S(2)}, u32[]{:S(2)}) async-start(bf16[64,80,128]{2,1,0:T(8,128)(2,1)} %get-tuple-element.49), calls=%async_computation | async-start | bytes 2621440 | tf_op jit(solution)/shard_map/all_to_all | solution.py:34
  16.1 10.7 %collective-permute-start = (bf16[32,512]{1,0:T(8,128)(2,1)}, bf16[32,512]{1,0:T(8,128)(2,1)S(1)}, u32[]{:S(2)}, u32[]{:S(2)}) collective-permute-start(bf16[32,512]{1,0:T(8,128)(2,1)} %get-tuple-element.47), channel_id=1, source_target_pairs={{0,1},{1,2},{2,3},{3,4},{4,5},{5,6},{6,7},{7,8},{8,9},{9,10},{10,1... | collective-permute-start | bytes 98312 | tf_op jit(solution)/shard_map/ppermute | solution.py:30
  17.2 9.6 %collective-permute-start.1 = (bf16[32,512]{1,0:T(8,128)(2,1)S(1)}, bf16[32,512]{1,0:T(8,128)(2,1)S(1)}, u32[]{:S(2)}, u32[]{:S(2)}) collective-permute-start(bf16[32,512]{1,0:T(8,128)(2,1)S(1)} %copy-done.16), channel_id=1, source_target_pairs={{0,127},{1,0},{2,1},{3,2},{4,3},{5,4},{6,5},{7,6},{8,7},{9,8},{10,... | collective-permute-start | bytes 98312 | tf_op jit(solution)/shard_map/ppermute | solution.py:30
  20.3 20.9 %copy-start.7 = (s32[4,512]{1,0:T(4,128)S(1)}, s32[4,512]{1,0:T(4,128)}, u32[]{:S(2)}) copy-start(s32[4,512]{1,0:T(4,128)} %reshape.48.dst_wide) | copy-start | bytes 24580
  35.9 5.3 %collective-permute-start.2 = (bf16[16,4,80,128]{3,2,1,0:T(8,128)(2,1)S(1)}, bf16[16,4,80,128]{3,2,1,0:T(8,128)(2,1)S(1)}, u32[]{:S(2)}, u32[]{:S(2)}) collective-permute-start(bf16[16,4,80,128]{3,2,1,0:T(8,128)(2,1)S(1)} %bitcast.7), channel_id=1, source_target_pairs={{0,4},{4,0},{1,5},{5,1},{2,6},{6,2},{3,7},{7,3},{8,12},{12,8},{9,1... | collective-permute-start | bytes 3932168 | tf_op jit(solution)/shard_map/ppermute | solution.py:26
  38.5 15.5 %collective-permute-start.5 = (bf16[768,128]{1,0:T(8,128)(2,1)}, bf16[768,128]{1,0:T(8,128)(2,1)S(1)}, u32[]{:S(2)}, u32[]{:S(2)}) collective-permute-start(bf16[768,128]{1,0:T(8,128)(2,1)} %get-tuple-element.58), channel_id=1, source_target_pairs={{0,3},{1,0},{2,1},{3,2},{4,7},{5,4},{6,5},{7,6},{8,11},{9,8},{10,9... | collective-permute-start | bytes 589832 | tf_op jit(solution)/shard_map/ppermute | solution.py:465
  38.9 15.1 %collective-permute-start.4 = (bf16[768,128]{1,0:T(8,128)(2,1)}, bf16[768,128]{1,0:T(8,128)(2,1)S(1)}, u32[]{:S(2)}, u32[]{:S(2)}) collective-permute-start(bf16[768,128]{1,0:T(8,128)(2,1)} %get-tuple-element.58), channel_id=1, source_target_pairs={{0,2},{1,3},{2,0},{3,1},{4,6},{5,7},{6,4},{7,5},{8,10},{9,11},{10,... | collective-permute-start | bytes 589832 | tf_op jit(solution)/shard_map/ppermute | solution.py:465
  41.2 12.9 %collective-permute-start.3 = (bf16[768,128]{1,0:T(8,128)(2,1)}, bf16[768,128]{1,0:T(8,128)(2,1)S(1)}, u32[]{:S(2)}, u32[]{:S(2)}) collective-permute-start(bf16[768,128]{1,0:T(8,128)(2,1)} %get-tuple-element.58), channel_id=1, source_target_pairs={{0,1},{1,2},{2,3},{3,0},{4,5},{5,6},{6,7},{7,4},{8,9},{9,10},{10,1... | collective-permute-start | bytes 589832 | tf_op jit(solution)/shard_map/ppermute | solution.py:465
  41.2 1.0 copy-start.1
  42.2 14.2 %copy-start.2 = (bf16[256,512]{1,0:T(8,128)(2,1)S(1)}, bf16[256,512]{1,0:T(8,128)(2,1)}, u32[]{:S(2)}) copy-start(bf16[256,512]{1,0:T(8,128)(2,1)} %node.5) | copy-start | bytes 786436
  42.2 14.2 %copy-start.3 = (bf16[2,512,128]{2,1,0:T(8,128)(2,1)S(1)}, bf16[2,512,128]{2,1,0:T(8,128)(2,1)}, u32[]{:S(2)}) copy-start(bf16[2,512,128]{2,1,0:T(8,128)(2,1)} %own_first.1) | copy-start | bytes 786436
  42.2 14.2 %copy-start.4 = (bf16[128,512]{1,0:T(8,128)(2,1)S(1)}, bf16[128,512]{1,0:T(8,128)(2,1)}, u32[]{:S(2)}) copy-start(bf16[128,512]{1,0:T(8,128)(2,1)} %own_second.1) | copy-start | bytes 393220
  42.2 14.2 %copy-start.11 = (bf16[1152,2048]{1,0:T(8,128)(2,1)S(1)}, bf16[1152,2048]{1,0:T(8,128)(2,1)}, u32[]{:S(2)}) copy-start(bf16[1152,2048]{1,0:T(8,128)(2,1)} %get-tuple-element.70.refs_16_) | copy-start | bytes 14155780
  42.2 14.2 %copy-start.12 = (bf16[2048,512]{1,0:T(8,128)(2,1)S(1)}, bf16[2048,512]{1,0:T(8,128)(2,1)}, u32[]{:S(2)}) copy-start(bf16[2048,512]{1,0:T(8,128)(2,1)} %refs_14_.1) | copy-start | bytes 6291460
  42.2 14.2 %copy-start.13 = (bf16[512,2048]{1,0:T(8,128)(2,1)S(1)}, bf16[512,2048]{1,0:T(8,128)(2,1)}, u32[]{:S(2)}) copy-start(bf16[512,2048]{1,0:T(8,128)(2,1)} %get-tuple-element.65.refs_9_) | copy-start | bytes 6291460
  42.2 14.2 %copy-start.14 = (bf16[2048,256]{1,0:T(8,128)(2,1)S(1)}, bf16[2048,256]{1,0:T(8,128)(2,1)}, u32[]{:S(2)}) copy-start(bf16[2048,256]{1,0:T(8,128)(2,1)} %get-tuple-element.53.refs_15_) | copy-start | bytes 3145732
  42.2 14.2 %copy-start.15 = (bf16[256,512]{1,0:T(8,128)(2,1)S(1)}, bf16[256,512]{1,0:T(8,128)(2,1)}, u32[]{:S(2)}) copy-start(bf16[256,512]{1,0:T(8,128)(2,1)} %grad_node.1) | copy-start | bytes 786436
  54.1 1.7 %collective-permute-start.6 = (bf16[768,128]{1,0:T(8,128)(2,1)S(1)}, bf16[768,128]{1,0:T(8,128)(2,1)S(1)}, u32[]{:S(2)}, u32[]{:S(2)}) collective-permute-start(bf16[768,128]{1,0:T(8,128)(2,1)S(1)} %collective-permute-done.3.refs_0_), channel_id=1, source_target_pairs={{0,4},{4,0},{1,5},{5,1},{2,6},{6,2},{3,7},{7,3},{8,12},{12,8},{9,1... | collective-permute-start | bytes 589832 | tf_op jit(solution)/shard_map/ppermute | solution.py:26
  54.7 1.4 %collective-permute-start.7 = (bf16[768,128]{1,0:T(8,128)(2,1)S(1)}, bf16[768,128]{1,0:T(8,128)(2,1)S(1)}, u32[]{:S(2)}, u32[]{:S(2)}) collective-permute-start(bf16[768,128]{1,0:T(8,128)(2,1)S(1)} %collective-permute-done.4.refs_1_), channel_id=1, source_target_pairs={{0,4},{4,0},{1,5},{5,1},{2,6},{6,2},{3,7},{7,3},{8,12},{12,8},{9,1... | collective-permute-start | bytes 589832 | tf_op jit(solution)/shard_map/ppermute | solution.py:26
  54.8 1.6 %collective-permute-start.8 = (bf16[768,128]{1,0:T(8,128)(2,1)S(1)}, bf16[768,128]{1,0:T(8,128)(2,1)S(1)}, u32[]{:S(2)}, u32[]{:S(2)}) collective-permute-start(bf16[768,128]{1,0:T(8,128)(2,1)S(1)} %collective-permute-done.5.refs_2_), channel_id=1, source_target_pairs={{0,4},{4,0},{1,5},{5,1},{2,6},{6,2},{3,7},{7,3},{8,12},{12,8},{9,1... | collective-permute-start | bytes 589832 | tf_op jit(solution)/shard_map/ppermute | solution.py:26
  72.9 4.2 %collective-permute-start.9 = (bf16[8,2,4,128,128]{4,3,2,1,0:T(8,128)(2,1)S(1)}, bf16[8,2,4,128,128]{4,3,2,1,0:T(8,128)(2,1)S(1)}, u32[]{:S(2)}, u32[]{:S(2)}) collective-permute-start(bf16[8,2,4,128,128]{4,3,2,1,0:T(8,128)(2,1)S(1)} %get-tuple-element.73), channel_id=1, source_target_pairs={{0,4},{4,0},{1,5},{5,1},{2,6},{6,2},{3,7},{7,3},{8,12},{12,8},{9,1... | collective-permute-start | bytes 6291464 | tf_op jit(solution)/shard_map/ppermute | solution.py:26
  79.5 34.8 %all-to-all-start.1 = ((bf16[64,128,128]{2,1,0:T(8,128)(2,1)}), bf16[64,128,128]{2,1,0:T(8,128)(2,1)S(1)}, u32[]{:S(2)}, u32[]{:S(2)}) async-start(bf16[64,128,128]{2,1,0:T(8,128)(2,1)} %bitcast.4), calls=%async_computation.1 | async-start | bytes 4194304 | tf_op jit(solution)/shard_map/all_to_all | solution.py:34
  86.1 46.6 %copy-start.9 = (s32[1,2,32]{2,1,0:T(2,128)S(1)}, s32[1,2,32]{2,1,0:T(2,128)}, u32[]{:S(2)}) copy-start(s32[1,2,32]{2,1,0:T(2,128)} %param.18) | copy-start | bytes 772
  86.1 46.6 %copy-start.10 = (s32[1,4]{1,0:T(1,128)S(1)}, s32[1,4]{1,0:T(1,128)}, u32[]{:S(2)}) copy-start(s32[1,4]{1,0:T(1,128)} %owned.3) | copy-start | bytes 52
  86.1 28.5 %collective-permute-start.10 = (bf16[32,512]{1,0:T(8,128)(2,1)S(1)}, bf16[32,512]{1,0:T(8,128)(2,1)S(1)}, u32[]{:S(2)}, u32[]{:S(2)}) collective-permute-start(bf16[32,512]{1,0:T(8,128)(2,1)S(1)} %get-tuple-element.75), channel_id=1, source_target_pairs={{0,127},{1,0},{2,1},{3,2},{4,3},{5,4},{6,5},{7,6},{8,7},{9,8},{10,... | collective-permute-start | bytes 98312 | tf_op jit(solution)/shard_map/ppermute | solution.py:30
  89.1 25.5 %collective-permute-start.11 = (bf16[32,512]{1,0:T(8,128)(2,1)S(1)}, bf16[32,512]{1,0:T(8,128)(2,1)S(1)}, u32[]{:S(2)}, u32[]{:S(2)}) collective-permute-start(bf16[32,512]{1,0:T(8,128)(2,1)S(1)} %get-tuple-element.77), channel_id=1, source_target_pairs={{0,1},{1,2},{2,3},{3,4},{4,5},{5,6},{6,7},{7,8},{8,9},{9,10},{10,1... | collective-permute-start | bytes 98312 | tf_op jit(solution)/shard_map/ppermute | solution.py:30
  128.6 4.1 %collective-permute-start.12 = (bf16[16,112,128]{2,1,0:T(8,128)(2,1)S(1)}, bf16[16,112,128]{2,1,0:T(8,128)(2,1)S(1)}, u32[]{:S(2)}, u32[]{:S(2)}) collective-permute-start(bf16[16,112,128]{2,1,0:T(8,128)(2,1)S(1)} %all_to_all.15.tiles), channel_id=1, source_target_pairs={{0,4},{4,0},{1,5},{5,1},{2,6},{6,2},{3,7},{7,3},{8,12},{12,8},{9,1... | collective-permute-start | bytes 1376264 | tf_op jit(solution)/shard_map/ppermute | solution.py:26

commit v10 on v9

--- a/solution.py
+++ b/solution.py
@@ -150,12 +150,13 @@
         packed[512 + b * 64 : 576 + b * 64, :] = second[row, b * 128 : (b + 1) * 128]
 
 
-def live_rows(step, count):
-    place = lax.broadcasted_iota(jnp.int32, (CHUNK, 1), 0) + step * CHUNK
+def live_rows(step, start, count):
+    place = lax.broadcasted_iota(jnp.int32, (STRIP, 1), 0) + (step * CHUNK + start)
     return jnp.where(place < count, 1.0, 0.0)
 
 
-HALVES = (slice(0, CHUNK),)
+STRIP = 64
+STRIPS = [slice(r, r + STRIP) for r in range(0, CHUNK, STRIP)]
 
 
 def place_weights(co, own_first, own_second, near, far, first, second):
@@ -206,7 +207,7 @@
 
 def forward_kernel(count, node, prev, following, near, far, src, dst, dst_wide, edge, *refs):
     edge_out, incoming, act_out, normed_out, slope_out, factor_out, lookup, first, second = refs[:9]
-    table, total, coarse = refs[9:]
+    table, total, coarse, hot, turned, held = refs[9:]
     co = places(count)
     step = pl.program_id(0)
 
@@ -221,31 +222,30 @@
         table[256:, :] = dot(lookup[...], whole(first, 1)).astype(BF16)
         total[...] = jnp.zeros_like(total)
 
-    hots = []
     for r in range(CHUNK // 128):
         row = pl.ds(step * (CHUNK // 128) + r, 1)
         tiles = hot_tiles(dst[row, :], 2) + hot_tiles(src[row, :], 7)
-        hots.append(jnp.concatenate(tiles, axis=1))
-    hot = jnp.concatenate(hots, axis=0)
-    turned = turned_rows(live_targets(step, dst_wide[pl.ds(step, 1), :], co[4]), 2)
-    turned = jnp.concatenate(turned, axis=0)
-    live = live_rows(step, co[4])
-    pres = [dot(edge[h, :], whole(first, 0)) + dot(hot[h, :], table[...]) for h in HALVES]
-    acts = []
-    for h, pre in zip(HALVES, pres):
-        act, slope = swish(pre)
-        acts.append(act.astype(BF16))
-        act_out[h, :] = acts[-1]
+        for j, tile in enumerate(tiles):
+            hot[r * 128 : (r + 1) * 128, j * 128 : (j + 1) * 128] = tile
+    blocks = turned_rows(live_targets(step, dst_wide[pl.ds(step, 1), :], co[4]), 2)
+    for j, block in enumerate(blocks):
+        turned[j * 128 : (j + 1) * 128, :] = block
+    held[...] = dot(edge[...], whole(first, 0)) + dot(hot[...], table[...])
+    for h in STRIPS:
+        act, slope = swish(held[h, :])
+        act_out[h, :] = act.astype(BF16)
         slope_out[h, :] = slope.astype(BF16)
-    values = [dot(act, second[...]) for act in acts]
-    for h, value in zip(HALVES, values):
+    held[...] = dot(act_out[...], second[...])
+    for h in STRIPS:
+        value = held[h, :]
         centre = value - mean(value)
-        factor = lax.rsqrt(mean(centre * centre) + EPSILON) * live[h]
+        live = live_rows(step, h.start, co[4])
+        factor = lax.rsqrt(mean(centre * centre) + EPSILON) * live
         normed = centre * factor
         normed_out[h, :] = normed.astype(BF16)
-        factor_out[h, :] = jnp.broadcast_to(factor, (CHUNK, 128))
+        factor_out[h, :] = jnp.broadcast_to(factor, (STRIP, 128))
         edge_out[h, :] = (edge[h, :].astype(F32) + normed).astype(BF16)
-    total[...] += dot(turned, edge_out[...])
+    total[...] += dot(turned[...], edge_out[...])
 
     @pl.when(step == STEPS - 1)
     def _():
@@ -293,7 +293,8 @@
     edge_first, edge_second, lookup = refs[:3]
     edge_turned, act, normed, slope, factor, grad_edge, hot, turned = refs[3:11]
     node_out, node_total, edge_grad, to_prev, to_next, keep, give = refs[11:18]
-    first, second, spread, sum_second, sum_first, sums, columns, rows, owned = refs[18:]
+    first, second, spread, sum_second, sum_first, sums, columns, rows, owned = refs[18:27]
+    held, back, deltas, pre_grads = refs[27:]
     step = pl.program_id(0)
 
     @pl.when(step == 0)
@@ -317,19 +318,21 @@
         sum_first[...] = jnp.zeros_like(sum_first)
         sums[...] = jnp.zeros_like(sums)
 
-    totals = [grad_edge[h, :].astype(F32) + dot(hot[h, :], spread[...]) for h in HALVES]
-    deltas = []
-    for h, total in zip(HALVES, totals):
+    held[...] = dot(hot[...], spread[...])
+    for h in STRIPS:
+        total = grad_edge[h, :].astype(F32) + held[h, :]
+        held[h, :] = total
         delta = normalize_back(total, normed[h, :].astype(F32), factor[h, 0:1])
-        deltas.append(delta.astype(BF16))
-    grads = [dot_nt(delta, edge_second[...]) for delta in deltas]
-    pre_grads = [(g * slope[h, :].astype(F32)).astype(BF16) for h, g in zip(HALVES, grads)]
-    for h, total, pre_grad in zip(HALVES, totals, pre_grads):
-        edge_grad[h, :] = (total + dot_nt(pre_grad, whole(edge_first, 0))).astype(BF16)
-    pre_grad = jnp.concatenate(pre_grads, axis=0)
-    sum_second[...] += dot_tn(act[...], jnp.concatenate(deltas, axis=0))
-    sum_first[...] += dot(edge_turned[...], pre_grad)
-    sums[...] += dot(turned[...], pre_grad)
+        deltas[h, :] = delta.astype(BF16)
+    back[...] = dot_nt(deltas[...], edge_second[...])
+    for h in STRIPS:
+        pre_grads[h, :] = (back[h, :] * slope[h, :].astype(F32)).astype(BF16)
+    back[...] = dot_nt(pre_grads[...], whole(edge_first, 0))
+    for h in STRIPS:
+        edge_grad[h, :] = (held[h, :] + back[h, :]).astype(BF16)
+    sum_second[...] += dot_tn(act[...], deltas[...])
+    sum_first[...] += dot(edge_turned[...], pre_grads[...])
+    sums[...] += dot(turned[...], pre_grads[...])
 
     @pl.when(step == STEPS - 1)
     def _():
@@ -339,11 +342,11 @@
         sent = sums[256:, :].astype(BF16)
         put_columns(co, dot_tn(lookup[...], sent), 1, columns, keep, give)
         put_columns(co, dot_tn(node[...], received), 2, columns, keep, give)
-        back = dot_nt(sent, whole(edge_first, 1))
-        node_total[...] += back[0:256] + dot_nt(received, whole(edge_first, 2))
-        to_prev[...] = back[256:288].astype(BF16)
-        to_next[...] = back[288:320].astype(BF16)
-        put_owned(co, back[320:832], owned, keep, give)
+        remote = dot_nt(sent, whole(edge_first, 1))
+        node_total[...] += remote[0:256] + dot_nt(received, whole(edge_first, 2))
+        to_prev[...] = remote[256:288].astype(BF16)
+        to_next[...] = remote[288:320].astype(BF16)
+        put_owned(co, remote[320:832], owned, keep, give)
 
 
 def final_kernel(count, owned, tiles, far, own, ahead, behind, lists, node_total, *refs):
@@ -490,6 +493,9 @@
             pltpu.VMEM((TABLE + 256, 512), BF16),
             pltpu.VMEM((256, 512), F32),
             pltpu.VMEM((16, 2, 4, 16, 128), BF16),
+            pltpu.VMEM((CHUNK, high), BF16),
+            pltpu.VMEM((256, CHUNK), BF16),
+            pltpu.VMEM((CHUNK, 512), F32),
         ],
         compiler_params=limit(16),
         cost_estimate=pl.CostEstimate(
@@ -531,6 +537,10 @@
             pltpu.VMEM((16, 2, 16, 512), BF16),
             pltpu.VMEM((4, 512, 128), BF16),
             pltpu.VMEM((16, 2, 4, 16, 128), BF16),
+            pltpu.VMEM((CHUNK, 512), F32),
+            pltpu.VMEM((CHUNK, 512), F32),
+            pltpu.VMEM((CHUNK, 512), BF16),
+            pltpu.VMEM((CHUNK, 512), BF16),
         ],
         compiler_params=limit(24),
         cost_estimate=pl.CostEstimate(

time: 135 us -> 135 us (level)
  no operation moved by 1% of the time
where the time goes in v10:
time: 135 us
  waiting for transfers between devices  41.4 us (31%)
  Pallas kernels  38.8 us (29%)
  starting transfers between devices  34.5 us (26%)
  blocking collectives  13.5 us (10%)
  other arithmetic  2.76 us (2%)
  local copies, waits for them, and re-layouts  2.3 us (2%)
  between operations  1.51 us (1%)
    all_to_all x2, waiting for transfers between devices, exchange(): return lax.all_to_all(value, axes, 0, 0, tiled=True)  34.6 us
    all_to_all x2, starting transfers between devices, exchange(): return lax.all_to_all(value, axes, 0, 0, tiled=True)  18.8 us
    pallas_call x1, Pallas kernels, shards(): pl.pallas_call(backward_kernel, grid=(STEPS,), in_specs=[SMEM] + [like(v)...  16.4 us
    all_to_all x1, blocking collectives, exchange(): return lax.all_to_all(value, axes, 0, 0, tiled=True)  13.5 us
    pallas_call x1, Pallas kernels, shards(): pl.pallas_call(forward_kernel, grid=(STEPS,), in_specs=[SMEM] + [like(v)...  11.7 us
    ppermute x6, waiting for transfers between devices, other_core(): return lax.ppermute(value, 'core', [(0, 1), (1, 0)])  6.6 us
    ppermute x6, starting transfers between devices, other_core(): return lax.ppermute(value, 'core', [(0, 1), (1, 0)])  6.6 us
    ppermute x4, starting transfers between devices, shifted(): lax.ppermute(value, BOTH, [(k, (k + steps) % 128) for k in range(128)])  6.46 us
  transfers between devices with their start and end apart: 15, of which 8 were waited for; matrix products, arithmetic and copies ran while one was open for 1% of the time, Pallas kernels for 13%

profile of v10, /device:TPU:1, one launch (start us, length us, event | category | flops | bytes accessed | tf_op | source)
XLA Modules:
  0.0 134.8 jit_solution(13605489727900735190)
XLA Ops:
  0.6 0.0 copy-start.5
  1.3 2.7 %shard_map.188 = (bf16[64,80,128]{2,1,0:T(8,128)(2,1)}, bf16[32,512]{1,0:T(8,128)(2,1)}, bf16[32,512]{1,0:T(8,128)(2,1)}, bf16[768,128]{1,0:T(8,128)(2,1)}) custom-call(s32[1]{0:T(128)S(6)} %copy.21.count, s32[1,4]{1,0:T(1,128)} %owned.3, bf16[256,512]{1,0:T(8,128)(2,1)} %node.5, s32[2,32]{1,0:T(2,128)} %bitcast.12, bf16[3,512,128]{2,1,0:T(8,128)(2,1)} %edge_first.1, ...), custom_call_target="tpu_custom_call" | custom-call | tf_op jit(solution)/shard_map/pallas_call | solution.py:388
  4.0 0.0 copy-start.6
  4.0 12.1 %all-to-all-start = ((bf16[64,80,128]{2,1,0:T(8,128)(2,1)}), bf16[64,80,128]{2,1,0:T(8,128)(2,1)S(1)}, u32[]{:S(2)}, u32[]{:S(2)}) async-start(bf16[64,80,128]{2,1,0:T(8,128)(2,1)} %get-tuple-element.49), calls=%async_computation | async-start | bytes 2621440 | tf_op jit(solution)/shard_map/all_to_all | solution.py:34
  16.1 1.1 collective-permute-start
  17.2 2.4 %collective-permute-start.1 = (bf16[32,512]{1,0:T(8,128)(2,1)S(1)}, bf16[32,512]{1,0:T(8,128)(2,1)S(1)}, u32[]{:S(2)}, u32[]{:S(2)}) collective-permute-start(bf16[32,512]{1,0:T(8,128)(2,1)S(1)} %copy-done.16), channel_id=1, source_target_pairs={{0,127},{1,0},{2,1},{3,2},{4,3},{5,4},{6,5},{7,6},{8,7},{9,8},{10,... | collective-permute-start | bytes 98312 | tf_op jit(solution)/shard_map/ppermute | solution.py:30
  19.7 0.6 reshape.48.dst_wide
  20.3 0.6 reshape.47.src_wide
  20.9 5.8 %shard_map.189 = (bf16[2048,256]{1,0:T(8,128)(2,1)}, bf16[1152,2048]{1,0:T(8,128)(2,1)}, bf16[512,2048]{1,0:T(8,128)(2,1)}) custom-call(s32[1]{0:T(128)S(6)} %copy.21.count, s32[16,128]{1,0:T(8,128)} %bitcast.9, s32[4,512]{1,0:T(4,128)} %reshape.47.src_wide, s32[4,512]{1,0:T(4,128)} %reshape.48.dst_wide, bf16[2048,512]{1,0:T(8,128)(2,1)} %edge.3), custom_call_target="tpu_custom_call" | custom-call | flops 20000000 | bytes 14000000 | tf_op jit(solution)/shard_map/pallas_call | solution.py:453
  26.7 0.2 collective-permute-done.prev
  26.9 0.0 collective-permute-done.1.following
  26.9 9.1 %all-to-all-done = bf16[64,80,128]{2,1,0:T(8,128)(2,1)S(1)} async-done(((bf16[64,80,128]{2,1,0:T(8,128)(2,1)}), bf16[64,80,128]{2,1,0:T(8,128)(2,1)S(1)}, u32[]{:S(2)}, u32[]{:S(2)}) %all-to-all-start) | async-done | bytes 1310752 | tf_op jit(solution)/shard_map/all_to_all | solution.py:34
  35.9 2.6 %collective-permute-start.2 = (bf16[16,4,80,128]{3,2,1,0:T(8,128)(2,1)S(1)}, bf16[16,4,80,128]{3,2,1,0:T(8,128)(2,1)S(1)}, u32[]{:S(2)}, u32[]{:S(2)}) collective-permute-start(bf16[16,4,80,128]{3,2,1,0:T(8,128)(2,1)S(1)} %bitcast.7), channel_id=1, source_target_pairs={{0,4},{4,0},{1,5},{5,1},{2,6},{6,2},{3,7},{7,3},{8,12},{12,8},{9,1... | collective-permute-start | bytes 3932168 | tf_op jit(solution)/shard_map/ppermute | solution.py:26
  38.5 0.4 collective-permute-start.5
  38.9 2.3 %collective-permute-start.4 = (bf16[768,128]{1,0:T(8,128)(2,1)}, bf16[768,128]{1,0:T(8,128)(2,1)S(1)}, u32[]{:S(2)}, u32[]{:S(2)}) collective-permute-start(bf16[768,128]{1,0:T(8,128)(2,1)} %get-tuple-element.58), channel_id=1, source_target_pairs={{0,2},{1,3},{2,0},{3,1},{4,6},{5,7},{6,4},{7,5},{8,10},{9,11},{10,... | collective-permute-start | bytes 589832 | tf_op jit(solution)/shard_map/ppermute | solution.py:468
  41.2 0.0 collective-permute-start.3
  41.2 0.0 collective-permute-done.2.far
  41.2 0.0 copy-start.1
  41.2 0.9 copy-done.1
  42.2 0.0 copy-start.12
  42.2 0.0 copy-start.13
  42.2 0.0 copy-start.15
  42.2 11.7 %shard_map.190 = (bf16[2048,512]{1,0:T(8,128)(2,1)}, bf16[256,512]{1,0:T(8,128)(2,1)S(1)}, bf16[2048,512]{1,0:T(8,128)(2,1)S(1)}, bf16[2048,512]{1,0:T(8,128)(2,...) custom-call(s32[1]{0:T(128)S(6)} %copy.21.count, ...), custom_call_target="tpu_custom_call" | custom-call | flops 7000000000 | bytes 18000000 | tf_op jit(solution)/shard_map/pallas_call | solution.py:473
  53.9 0.0 collective-permute-done.5.refs_2_
  53.9 0.0 collective-permute-done.4.refs_1_
  53.9 0.0 collective-permute-done.3.refs_0_
  53.9 0.6 collective-permute-start.6
  54.5 0.1 collective-permute-start.7
  54.6 0.4 collective-permute-start.8
  55.0 0.6 collective-permute-done.6.refs_3_
  55.6 0.4 collective-permute-done.7.refs_4_
  55.9 0.3 collective-permute-done.8.refs_5_
  56.3 16.4 %shard_map.191 = (bf16[256,512]{1,0:T(8,128)(2,1)}, f32[256,512]{1,0:T(8,128)S(1)}, bf16[2048,512]{1,0:T(8,128)(2,1)}, bf16[32,512]{1,0:T(8,128)(2,1)S(1)}, bf16...) custom-call(s32[1]{0:T(128)S(6)} %copy.21.count, ...), custom_call_target="tpu_custom_call" | custom-call | flops 8999999488 | bytes 24000000 | tf_op jit(solution)/shard_map/pallas_call | solution.py:512
  72.7 0.2 collective-permute-start.9
  72.9 3.9 %collective-permute-done.9 = bf16[8,2,4,128,128]{4,3,2,1,0:T(8,128)(2,1)S(1)} collective-permute-done((bf16[8,2,4,128,128]{4,3,2,1,0:T(8,128)(2,1)S(1)}, bf16[8,2,4,128,128]{4,3,2,1,0:T(8,128)(2,1)S(1)}, u32[]{:S(2)}, u32[]{:S(2)}) %collective-permute-start.9) | collective-permute-done | bytes 2097184 | tf_op jit(solution)/shard_map/ppermute | solution.py:26
  76.9 2.4 %add_convert_fusion = bf16[8,2,4,128,128]{4,3,2,1,0:T(8,128)(2,1)} fusion(bf16[8,2,4,128,128]{4,3,2,1,0:T(8,128)(2,1)S(1)} %collective-permute-done.9, bf16[8,2,4,128,128]{4,3,2,1,0:T(8,128)(2,1)S(1)} %get-tuple-element.72), kind=kLoop, calls=%fused_computation | loop fusion | flops 4194304 | bytes 6291456 | tf_op jit(solution)/shard_map/convert_element_type | solution.py:551
  79.3 6.7 %all-to-all-start.1 = ((bf16[64,128,128]{2,1,0:T(8,128)(2,1)}), bf16[64,128,128]{2,1,0:T(8,128)(2,1)S(1)}, u32[]{:S(2)}, u32[]{:S(2)}) async-start(bf16[64,128,128]{2,1,0:T(8,128)(2,1)} %bitcast.4), calls=%async_computation.1 | async-start | bytes 4194304 | tf_op jit(solution)/shard_map/all_to_all | solution.py:34
  86.0 0.0 copy-start.9
  86.0 0.0 copy-start.10
  86.0 3.0 %collective-permute-start.10 = (bf16[32,512]{1,0:T(8,128)(2,1)S(1)}, bf16[32,512]{1,0:T(8,128)(2,1)S(1)}, u32[]{:S(2)}, u32[]{:S(2)}) collective-permute-start(bf16[32,512]{1,0:T(8,128)(2,1)S(1)} %get-tuple-element.75), channel_id=1, source_target_pairs={{0,127},{1,0},{2,1},{3,2},{4,3},{5,4},{6,5},{7,6},{8,7},{9,8},{10,... | collective-permute-start | bytes 98312 | tf_op jit(solution)/shard_map/ppermute | solution.py:30
  89.0 0.0 collective-permute-start.11
  89.0 25.5 %all-to-all-done.1 = bf16[64,128,128]{2,1,0:T(8,128)(2,1)S(1)} async-done(((bf16[64,128,128]{2,1,0:T(8,128)(2,1)}), bf16[64,128,128]{2,1,0:T(8,128)(2,1)S(1)}, u32[]{:S(2)}, u32[]{:S(2)}) %all-to-all-start.1) | async-done | bytes 2097184 | tf_op jit(solution)/shard_map/all_to_all | solution.py:34
  114.5 0.3 reduce_sum.12.own
  114.8 0.1 broadcast_in_dim.2
  114.9 13.5 %all_to_all.15.tiles = bf16[16,112,128]{2,1,0:T(8,128)(2,1)S(1)} all-to-all(bf16[16,112,128]{2,1,0:T(8,128)(2,1)S(1)} %broadcast_in_dim.2), channel_id=1, replica_groups=mesh['z'=4,'x'=4,'core'=2,'feat'=4] {'z','x'}, dimensions={0} | all-to-all | bytes 917504 | tf_op jit(solution)/shard_map/all_to_all | solution.py:34
  128.4 2.7 %collective-permute-start.12 = (bf16[16,112,128]{2,1,0:T(8,128)(2,1)S(1)}, bf16[16,112,128]{2,1,0:T(8,128)(2,1)S(1)}, u32[]{:S(2)}, u32[]{:S(2)}) collective-permute-start(bf16[16,112,128]{2,1,0:T(8,128)(2,1)S(1)} %all_to_all.15.tiles), channel_id=1, source_target_pairs={{0,4},{4,0},{1,5},{5,1},{2,6},{6,2},{3,7},{7,3},{8,12},{12,8},{9,1... | collective-permute-start | bytes 1376264 | tf_op jit(solution)/shard_map/ppermute | solution.py:26
  131.1 1.4 %collective-permute-done.12.far = bf16[16,112,128]{2,1,0:T(8,128)(2,1)S(1)} collective-permute-done((bf16[16,112,128]{2,1,0:T(8,128)(2,1)S(1)}, bf16[16,112,128]{2,1,0:T(8,128)(2,1)S(1)}, u32[]{:S(2)}, u32[]{:S(2)}) %collective-permute-start.12) | collective-permute-done | bytes 458784 | tf_op jit(solution)/shard_map/ppermute | solution.py:26
  132.6 2.2 %shard_map.192 = (f32[3,16,2,16,128]{4,3,2,1,0:T(8,128)}, f32[128,512]{1,0:T(8,128)}, f32[2,16,2,16,128]{4,3,2,1,0:T(8,128)}, f32[128,512]{1,0:T(8,128)}, f32[256,512]{1,0:T(8,128)}) custom-call(s32[1]{0:T(128)S(6)} %copy.21.count, s32[1,4]{1,0:T(1,128)S(1)} %copy-done.10, bf16[16,112,128]{2,1,0:T(8,128)(2,1)S(1)} %all_to_all.15.tiles, ...), custom_call_target="tpu_custom_call" | custom-call | tf_op jit(solution)/shard_map/pallas_call | solution.py:388
  (28 shorter events, 0.1 us)
Async XLA Ops:
  0.6 19.0 %copy-start.5 = (s32[2048]{0:T(1024)S(1)}, s32[2048]{0:T(1024)}, u32[]{:S(2)}) copy-start(s32[2048]{0:T(1024)} %param.16) | copy-start | bytes 24580
  0.6 19.6 %copy-start.8 = (s32[2048]{0:T(1024)S(1)}, s32[2048]{0:T(1024)}, u32[]{:S(2)}) copy-start(s32[2048]{0:T(1024)} %param.15) | copy-start | bytes 24580
  4.0 13.2 %copy-start.16 = (bf16[32,512]{1,0:T(8,128)(2,1)S(1)}, bf16[32,512]{1,0:T(8,128)(2,1)}, u32[]{:S(2)}) copy-start(bf16[32,512]{1,0:T(8,128)(2,1)} %get-tuple-element.48) | copy-start | bytes 98308
  4.0 37.2 %copy-start = (bf16[2048,512]{1,0:T(8,128)(2,1)S(1)}, bf16[2048,512]{1,0:T(8,128)(2,1)}, u32[]{:S(2)}) copy-start(bf16[2048,512]{1,0:T(8,128)(2,1)} %edge.3) | copy-start | bytes 6291460
  4.0 37.2 %copy-start.6 = (s32[2048]{0:T(1024)S(1)}, s32[2048]{0:T(1024)}, u32[]{:S(2)}) copy-start(s32[2048]{0:T(1024)} %param.16) | copy-start | bytes 24580
  4.0 31.9 %all-to-all-start = ((bf16[64,80,128]{2,1,0:T(8,128)(2,1)}), bf16[64,80,128]{2,1,0:T(8,128)(2,1)S(1)}, u32[]{:S(2)}, u32[]{:S(2)}) async-start(bf16[64,80,128]{2,1,0:T(8,128)(2,1)} %get-tuple-element.49), calls=%async_computation | async-start | bytes 2621440 | tf_op jit(solution)/shard_map/all_to_all | solution.py:34
  16.1 10.7 %collective-permute-start = (bf16[32,512]{1,0:T(8,128)(2,1)}, bf16[32,512]{1,0:T(8,128)(2,1)S(1)}, u32[]{:S(2)}, u32[]{:S(2)}) collective-permute-start(bf16[32,512]{1,0:T(8,128)(2,1)} %get-tuple-element.47), channel_id=1, source_target_pairs={{0,1},{1,2},{2,3},{3,4},{4,5},{5,6},{6,7},{7,8},{8,9},{9,10},{10,1... | collective-permute-start | bytes 98312 | tf_op jit(solution)/shard_map/ppermute | solution.py:30
  17.2 9.6 %collective-permute-start.1 = (bf16[32,512]{1,0:T(8,128)(2,1)S(1)}, bf16[32,512]{1,0:T(8,128)(2,1)S(1)}, u32[]{:S(2)}, u32[]{:S(2)}) collective-permute-start(bf16[32,512]{1,0:T(8,128)(2,1)S(1)} %copy-done.16), channel_id=1, source_target_pairs={{0,127},{1,0},{2,1},{3,2},{4,3},{5,4},{6,5},{7,6},{8,7},{9,8},{10,... | collective-permute-start | bytes 98312 | tf_op jit(solution)/shard_map/ppermute | solution.py:30
  20.3 20.9 %copy-start.7 = (s32[4,512]{1,0:T(4,128)S(1)}, s32[4,512]{1,0:T(4,128)}, u32[]{:S(2)}) copy-start(s32[4,512]{1,0:T(4,128)} %reshape.48.dst_wide) | copy-start | bytes 24580
  35.9 5.3 %collective-permute-start.2 = (bf16[16,4,80,128]{3,2,1,0:T(8,128)(2,1)S(1)}, bf16[16,4,80,128]{3,2,1,0:T(8,128)(2,1)S(1)}, u32[]{:S(2)}, u32[]{:S(2)}) collective-permute-start(bf16[16,4,80,128]{3,2,1,0:T(8,128)(2,1)S(1)} %bitcast.7), channel_id=1, source_target_pairs={{0,4},{4,0},{1,5},{5,1},{2,6},{6,2},{3,7},{7,3},{8,12},{12,8},{9,1... | collective-permute-start | bytes 3932168 | tf_op jit(solution)/shard_map/ppermute | solution.py:26
  38.5 15.4 %collective-permute-start.5 = (bf16[768,128]{1,0:T(8,128)(2,1)}, bf16[768,128]{1,0:T(8,128)(2,1)S(1)}, u32[]{:S(2)}, u32[]{:S(2)}) collective-permute-start(bf16[768,128]{1,0:T(8,128)(2,1)} %get-tuple-element.58), channel_id=1, source_target_pairs={{0,3},{1,0},{2,1},{3,2},{4,7},{5,4},{6,5},{7,6},{8,11},{9,8},{10,9... | collective-permute-start | bytes 589832 | tf_op jit(solution)/shard_map/ppermute | solution.py:468
  38.9 15.0 %collective-permute-start.4 = (bf16[768,128]{1,0:T(8,128)(2,1)}, bf16[768,128]{1,0:T(8,128)(2,1)S(1)}, u32[]{:S(2)}, u32[]{:S(2)}) collective-permute-start(bf16[768,128]{1,0:T(8,128)(2,1)} %get-tuple-element.58), channel_id=1, source_target_pairs={{0,2},{1,3},{2,0},{3,1},{4,6},{5,7},{6,4},{7,5},{8,10},{9,11},{10,... | collective-permute-start | bytes 589832 | tf_op jit(solution)/shard_map/ppermute | solution.py:468
  41.2 12.7 %collective-permute-start.3 = (bf16[768,128]{1,0:T(8,128)(2,1)}, bf16[768,128]{1,0:T(8,128)(2,1)S(1)}, u32[]{:S(2)}, u32[]{:S(2)}) collective-permute-start(bf16[768,128]{1,0:T(8,128)(2,1)} %get-tuple-element.58), channel_id=1, source_target_pairs={{0,1},{1,2},{2,3},{3,0},{4,5},{5,6},{6,7},{7,4},{8,9},{9,10},{10,1... | collective-permute-start | bytes 589832 | tf_op jit(solution)/shard_map/ppermute | solution.py:468
  41.2 1.0 copy-start.1
  42.2 14.1 %copy-start.2 = (bf16[256,512]{1,0:T(8,128)(2,1)S(1)}, bf16[256,512]{1,0:T(8,128)(2,1)}, u32[]{:S(2)}) copy-start(bf16[256,512]{1,0:T(8,128)(2,1)} %node.5) | copy-start | bytes 786436
  42.2 14.1 %copy-start.3 = (bf16[2,512,128]{2,1,0:T(8,128)(2,1)S(1)}, bf16[2,512,128]{2,1,0:T(8,128)(2,1)}, u32[]{:S(2)}) copy-start(bf16[2,512,128]{2,1,0:T(8,128)(2,1)} %own_first.1) | copy-start | bytes 786436
  42.2 14.1 %copy-start.4 = (bf16[128,512]{1,0:T(8,128)(2,1)S(1)}, bf16[128,512]{1,0:T(8,128)(2,1)}, u32[]{:S(2)}) copy-start(bf16[128,512]{1,0:T(8,128)(2,1)} %own_second.1) | copy-start | bytes 393220
  42.2 14.1 %copy-start.11 = (bf16[1152,2048]{1,0:T(8,128)(2,1)S(1)}, bf16[1152,2048]{1,0:T(8,128)(2,1)}, u32[]{:S(2)}) copy-start(bf16[1152,2048]{1,0:T(8,128)(2,1)} %get-tuple-element.70.refs_16_) | copy-start | bytes 14155780
  42.2 14.1 %copy-start.12 = (bf16[2048,512]{1,0:T(8,128)(2,1)S(1)}, bf16[2048,512]{1,0:T(8,128)(2,1)}, u32[]{:S(2)}) copy-start(bf16[2048,512]{1,0:T(8,128)(2,1)} %refs_14_.1) | copy-start | bytes 6291460
  42.2 14.1 %copy-start.13 = (bf16[512,2048]{1,0:T(8,128)(2,1)S(1)}, bf16[512,2048]{1,0:T(8,128)(2,1)}, u32[]{:S(2)}) copy-start(bf16[512,2048]{1,0:T(8,128)(2,1)} %get-tuple-element.65.refs_9_) | copy-start | bytes 6291460
  42.2 14.1 %copy-start.14 = (bf16[2048,256]{1,0:T(8,128)(2,1)S(1)}, bf16[2048,256]{1,0:T(8,128)(2,1)}, u32[]{:S(2)}) copy-start(bf16[2048,256]{1,0:T(8,128)(2,1)} %get-tuple-element.53.refs_15_) | copy-start | bytes 3145732
  42.2 14.1 %copy-start.15 = (bf16[256,512]{1,0:T(8,128)(2,1)S(1)}, bf16[256,512]{1,0:T(8,128)(2,1)}, u32[]{:S(2)}) copy-start(bf16[256,512]{1,0:T(8,128)(2,1)} %grad_node.1) | copy-start | bytes 786436
  53.9 1.7 %collective-permute-start.6 = (bf16[768,128]{1,0:T(8,128)(2,1)S(1)}, bf16[768,128]{1,0:T(8,128)(2,1)S(1)}, u32[]{:S(2)}, u32[]{:S(2)}) collective-permute-start(bf16[768,128]{1,0:T(8,128)(2,1)S(1)} %collective-permute-done.3.refs_0_), channel_id=1, source_target_pairs={{0,4},{4,0},{1,5},{5,1},{2,6},{6,2},{3,7},{7,3},{8,12},{12,8},{9,1... | collective-permute-start | bytes 589832 | tf_op jit(solution)/shard_map/ppermute | solution.py:26
  54.5 1.4 %collective-permute-start.7 = (bf16[768,128]{1,0:T(8,128)(2,1)S(1)}, bf16[768,128]{1,0:T(8,128)(2,1)S(1)}, u32[]{:S(2)}, u32[]{:S(2)}) collective-permute-start(bf16[768,128]{1,0:T(8,128)(2,1)S(1)} %collective-permute-done.4.refs_1_), channel_id=1, source_target_pairs={{0,4},{4,0},{1,5},{5,1},{2,6},{6,2},{3,7},{7,3},{8,12},{12,8},{9,1... | collective-permute-start | bytes 589832 | tf_op jit(solution)/shard_map/ppermute | solution.py:26
  54.6 1.6 %collective-permute-start.8 = (bf16[768,128]{1,0:T(8,128)(2,1)S(1)}, bf16[768,128]{1,0:T(8,128)(2,1)S(1)}, u32[]{:S(2)}, u32[]{:S(2)}) collective-permute-start(bf16[768,128]{1,0:T(8,128)(2,1)S(1)} %collective-permute-done.5.refs_2_), channel_id=1, source_target_pairs={{0,4},{4,0},{1,5},{5,1},{2,6},{6,2},{3,7},{7,3},{8,12},{12,8},{9,1... | collective-permute-start | bytes 589832 | tf_op jit(solution)/shard_map/ppermute | solution.py:26
  72.7 4.2 %collective-permute-start.9 = (bf16[8,2,4,128,128]{4,3,2,1,0:T(8,128)(2,1)S(1)}, bf16[8,2,4,128,128]{4,3,2,1,0:T(8,128)(2,1)S(1)}, u32[]{:S(2)}, u32[]{:S(2)}) collective-permute-start(bf16[8,2,4,128,128]{4,3,2,1,0:T(8,128)(2,1)S(1)} %get-tuple-element.73), channel_id=1, source_target_pairs={{0,4},{4,0},{1,5},{5,1},{2,6},{6,2},{3,7},{7,3},{8,12},{12,8},{9,1... | collective-permute-start | bytes 6291464 | tf_op jit(solution)/shard_map/ppermute | solution.py:26
  79.3 35.2 %all-to-all-start.1 = ((bf16[64,128,128]{2,1,0:T(8,128)(2,1)}), bf16[64,128,128]{2,1,0:T(8,128)(2,1)S(1)}, u32[]{:S(2)}, u32[]{:S(2)}) async-start(bf16[64,128,128]{2,1,0:T(8,128)(2,1)} %bitcast.4), calls=%async_computation.1 | async-start | bytes 4194304 | tf_op jit(solution)/shard_map/all_to_all | solution.py:34
  86.0 46.6 %copy-start.9 = (s32[1,2,32]{2,1,0:T(2,128)S(1)}, s32[1,2,32]{2,1,0:T(2,128)}, u32[]{:S(2)}) copy-start(s32[1,2,32]{2,1,0:T(2,128)} %param.18) | copy-start | bytes 772
  86.0 46.6 %copy-start.10 = (s32[1,4]{1,0:T(1,128)S(1)}, s32[1,4]{1,0:T(1,128)}, u32[]{:S(2)}) copy-start(s32[1,4]{1,0:T(1,128)} %owned.3) | copy-start | bytes 52
  86.0 28.8 %collective-permute-start.10 = (bf16[32,512]{1,0:T(8,128)(2,1)S(1)}, bf16[32,512]{1,0:T(8,128)(2,1)S(1)}, u32[]{:S(2)}, u32[]{:S(2)}) collective-permute-start(bf16[32,512]{1,0:T(8,128)(2,1)S(1)} %get-tuple-element.75), channel_id=1, source_target_pairs={{0,127},{1,0},{2,1},{3,2},{4,3},{5,4},{6,5},{7,6},{8,7},{9,8},{10,... | collective-permute-start | bytes 98312 | tf_op jit(solution)/shard_map/ppermute | solution.py:30
  89.0 25.9 %collective-permute-start.11 = (bf16[32,512]{1,0:T(8,128)(2,1)S(1)}, bf16[32,512]{1,0:T(8,128)(2,1)S(1)}, u32[]{:S(2)}, u32[]{:S(2)}) collective-permute-start(bf16[32,512]{1,0:T(8,128)(2,1)S(1)} %get-tuple-element.77), channel_id=1, source_target_pairs={{0,1},{1,2},{2,3},{3,4},{4,5},{5,6},{6,7},{7,8},{8,9},{9,10},{10,1... | collective-permute-start | bytes 98312 | tf_op jit(solution)/shard_map/ppermute | solution.py:30
  128.4 4.1 %collective-permute-start.12 = (bf16[16,112,128]{2,1,0:T(8,128)(2,1)S(1)}, bf16[16,112,128]{2,1,0:T(8,128)(2,1)S(1)}, u32[]{:S(2)}, u32[]{:S(2)}) collective-permute-start(bf16[16,112,128]{2,1,0:T(8,128)(2,1)S(1)} %all_to_all.15.tiles), channel_id=1, source_target_pairs={{0,4},{4,0},{1,5},{5,1},{2,6},{6,2},{3,7},{7,3},{8,12},{12,8},{9,1... | collective-permute-start | bytes 1376264 | tf_op jit(solution)/shard_map/ppermute | solution.py:26

commit v11 on v10

--- a/solution.py
+++ b/solution.py
@@ -292,9 +292,9 @@
     co = places(count)
     edge_first, edge_second, lookup = refs[:3]
     edge_turned, act, normed, slope, factor, grad_edge, hot, turned = refs[3:11]
-    node_out, node_total, edge_grad, to_prev, to_next, keep, give = refs[11:18]
-    first, second, spread, sum_second, sum_first, sums, columns, rows, owned = refs[18:27]
-    held, back, deltas, pre_grads = refs[27:]
+    node_out, node_total, pre_grads, to_prev, to_next, keep, give, spread = refs[11:19]
+    first, second, sum_second, sum_first, sums, columns, rows, owned = refs[19:27]
+    held, back, deltas = refs[27:]
     step = pl.program_id(0)
 
     @pl.when(step == 0)
@@ -321,15 +321,11 @@
     held[...] = dot(hot[...], spread[...])
     for h in STRIPS:
         total = grad_edge[h, :].astype(F32) + held[h, :]
-        held[h, :] = total
         delta = normalize_back(total, normed[h, :].astype(F32), factor[h, 0:1])
         deltas[h, :] = delta.astype(BF16)
     back[...] = dot_nt(deltas[...], edge_second[...])
     for h in STRIPS:
         pre_grads[h, :] = (back[h, :] * slope[h, :].astype(F32)).astype(BF16)
-    back[...] = dot_nt(pre_grads[...], whole(edge_first, 0))
-    for h in STRIPS:
-        edge_grad[h, :] = (held[h, :] + back[h, :]).astype(BF16)
     sum_second[...] += dot_tn(act[...], deltas[...])
     sum_first[...] += dot(edge_turned[...], pre_grads[...])
     sums[...] += dot(turned[...], pre_grads[...])
@@ -347,6 +343,11 @@
         to_prev[...] = remote[256:288].astype(BF16)
         to_next[...] = remote[288:320].astype(BF16)
         put_owned(co, remote[320:832], owned, keep, give)
+
+
+def edge_kernel(spread, first, grad_edge, hot, pre_grads, edge_grad):
+    total = grad_edge[...].astype(F32) + dot(hot[...], spread[...])
+    edge_grad[...] = (total + dot_nt(pre_grads[...], whole(first, 0))).astype(BF16)
 
 
 def final_kernel(count, owned, tiles, far, own, ahead, behind, lists, node_total, *refs):
@@ -509,7 +510,7 @@
     fixed += [first, second, lookup]
     moving = [edge_turned, act, normed, slope, factor, grad_edge, hot, turned]
     tiles = (8, 2, 4, 128, 128)
-    node_out, node_total, edge_grad, to_prev, to_next, keep, give = pl.pallas_call(
+    node_out, node_total, pre_grads, to_prev, to_next, keep, give, spread = pl.pallas_call(
         backward_kernel,
         grid=(STEPS,),
         in_specs=[SMEM]
@@ -517,7 +518,7 @@
         + [column(512, CHUNK), wide, wide, wide, chunk(CHUNK, 128), wide, chunk(CHUNK, 256)]
         + [column(high, CHUNK)],
         out_specs=[same(256, 512), same(256, 512), wide, same(32, 512), same(32, 512)]
-        + [same(*tiles), same(*tiles)],
+        + [same(*tiles), same(*tiles), same(256, 512)],
         out_shape=[
             shape(256, 512),
             shape(256, 512, dtype=F32),
@@ -526,11 +527,11 @@
             shape(32, 512),
             shape(*tiles),
             shape(*tiles),
+            shape(256, 512),
         ],
         scratch_shapes=[
             pltpu.VMEM((2, 512, 512), BF16),
             pltpu.VMEM((512, 512), BF16),
-            pltpu.VMEM((256, 512), BF16),
             pltpu.VMEM((512, 512), F32),
             pltpu.VMEM((512, 512), F32),
             pltpu.VMEM((TABLE + 256, 512), F32),
@@ -540,7 +541,6 @@
             pltpu.VMEM((CHUNK, 512), F32),
             pltpu.VMEM((CHUNK, 512), F32),
             pltpu.VMEM((CHUNK, 512), BF16),
-            pltpu.VMEM((CHUNK, 512), BF16),
         ],
         compiler_params=limit(24),
         cost_estimate=pl.CostEstimate(
@@ -549,10 +549,23 @@
     )(edge_count, *fixed, *moving)
 
     pair = (keep.astype(F32) + other_core(give).astype(F32)).astype(BF16).reshape(64, 128, 128)
+    edge_first = after(first, pair)
+    edge_grad = pl.pallas_call(
+        edge_kernel,
+        grid=(STEPS,),
+        in_specs=[same(256, 512), same(3, 16, 2, 16, 512), wide, chunk(CHUNK, 256), wide],
+        out_specs=wide,
+        out_shape=shape(2048, 512),
+        input_output_aliases={4: 0},
+        compiler_params=limit(60),
+        cost_estimate=pl.CostEstimate(
+            flops=1_600_000_000, bytes_accessed=9_000_000, transcendentals=0
+        ),
+    )(spread, edge_first, grad_edge, hot, pre_grads)
     ahead = shifted(after(to_prev, pair), -1)
     behind = shifted(after(to_next, pair), 1)
     own = jnp.sum(exchange(pair, ("z", "x", "feat")).astype(F32), axis=0).astype(BF16)
-    own = after(own, ahead, behind)
+    own = after(own, ahead, behind, edge_grad)
     tiles = exchange(repeated(own[:112], 16), ("z", "x"))
     far_tiles = other_core(tiles)
     edge_first, edge_second, node_first, node_second, node_grad = plain_call(

time: 135 us -> 134 us (level)
  waiting for transfers between devices: 41.4 us -> 35 us
  Pallas kernels: 38.8 us -> 43.7 us
    all_to_all x2, waiting for transfers between devices: 34.6 us -> 28.2 us  [exchange(): return lax.all_to_all(value, axes, 0, 0, tiled=True)]
    pallas_call x0 -> x1, Pallas kernels: none -> 6.09 us  [shards(): pl.pallas_call(edge_kernel, grid=(STEPS,), in_specs=[same(256, 512), same...]
  transfers between devices with their start and end apart: 15 -> 15, of which waited for: 8 -> 8; matrix products, arithmetic and copies ran while one was open for 1% -> 1% of each run, Pallas kernels for 13% -> 18%
where the time goes in v11:
time: 134 us
  Pallas kernels  43.7 us (33%)
  waiting for transfers between devices  35 us (26%)
  starting transfers between devices  34.5 us (26%)
  blocking collectives  13.8 us (10%)
  other arithmetic  2.79 us (2%)
  local copies, waits for them, and re-layouts  2.3 us (2%)
  between operations  1.51 us (1%)
    all_to_all x2, waiting for transfers between devices, exchange(): return lax.all_to_all(value, axes, 0, 0, tiled=True)  28.2 us
    all_to_all x2, starting transfers between devices, exchange(): return lax.all_to_all(value, axes, 0, 0, tiled=True)  18.8 us
    pallas_call x1, Pallas kernels, shards(): pl.pallas_call(backward_kernel, grid=(STEPS,), in_specs=[SMEM] + [like(v)...  15.3 us
    all_to_all x1, blocking collectives, exchange(): return lax.all_to_all(value, axes, 0, 0, tiled=True)  13.8 us
    pallas_call x1, Pallas kernels, shards(): pl.pallas_call(forward_kernel, grid=(STEPS,), in_specs=[SMEM] + [like(v)...  11.7 us
    ppermute x6, starting transfers between devices, other_core(): return lax.ppermute(value, 'core', [(0, 1), (1, 0)])  6.63 us
    ppermute x6, waiting for transfers between devices, other_core(): return lax.ppermute(value, 'core', [(0, 1), (1, 0)])  6.59 us
    ppermute x4, starting transfers between devices, shifted(): lax.ppermute(value, BOTH, [(k, (k + steps) % 128) for k in range(128)])  6.49 us
  transfers between devices with their start and end apart: 15, of which 8 were waited for; matrix products, arithmetic and copies ran while one was open for 1% of the time, Pallas kernels for 18%

profile of v11, /device:TPU:1, one launch (start us, length us, event | category | flops | bytes accessed | tf_op | source)
XLA Modules:
  0.0 133.7 jit_solution(12872794024381019942)
XLA Ops:
  0.6 0.0 copy-start.9
  1.3 2.7 %shard_map.188 = (bf16[64,80,128]{2,1,0:T(8,128)(2,1)}, bf16[32,512]{1,0:T(8,128)(2,1)}, bf16[32,512]{1,0:T(8,128)(2,1)}, bf16[768,128]{1,0:T(8,128)(2,1)}) custom-call(s32[1]{0:T(128)S(6)} %copy.23.count, s32[1,4]{1,0:T(1,128)} %owned.3, bf16[256,512]{1,0:T(8,128)(2,1)} %node.5, s32[2,32]{1,0:T(2,128)} %bitcast.12, bf16[3,512,128]{2,1,0:T(8,128)(2,1)} %edge_first.1, ...), custom_call_target="tpu_custom_call" | custom-call | tf_op jit(solution)/shard_map/pallas_call | solution.py:389
  4.0 0.0 copy-start.10
  4.0 12.1 %all-to-all-start = ((bf16[64,80,128]{2,1,0:T(8,128)(2,1)}), bf16[64,80,128]{2,1,0:T(8,128)(2,1)S(1)}, u32[]{:S(2)}, u32[]{:S(2)}) async-start(bf16[64,80,128]{2,1,0:T(8,128)(2,1)} %get-tuple-element.51), calls=%async_computation | async-start | bytes 2621440 | tf_op jit(solution)/shard_map/all_to_all | solution.py:34
  16.1 1.1 collective-permute-start
  17.2 2.4 %collective-permute-start.1 = (bf16[32,512]{1,0:T(8,128)(2,1)S(1)}, bf16[32,512]{1,0:T(8,128)(2,1)S(1)}, u32[]{:S(2)}, u32[]{:S(2)}) collective-permute-start(bf16[32,512]{1,0:T(8,128)(2,1)S(1)} %copy-done.18), channel_id=1, source_target_pairs={{0,127},{1,0},{2,1},{3,2},{4,3},{5,4},{6,5},{7,6},{8,7},{9,8},{10,... | collective-permute-start | bytes 98312 | tf_op jit(solution)/shard_map/ppermute | solution.py:30
  19.7 0.6 reshape.48.dst_wide
  20.3 0.6 reshape.47.src_wide
  20.9 5.8 %shard_map.189 = (bf16[2048,256]{1,0:T(8,128)(2,1)}, bf16[1152,2048]{1,0:T(8,128)(2,1)}, bf16[512,2048]{1,0:T(8,128)(2,1)}) custom-call(s32[1]{0:T(128)S(6)} %copy.23.count, s32[16,128]{1,0:T(8,128)} %bitcast.9, s32[4,512]{1,0:T(4,128)} %reshape.47.src_wide, s32[4,512]{1,0:T(4,128)} %reshape.48.dst_wide, bf16[2048,512]{1,0:T(8,128)(2,1)} %edge.3), custom_call_target="tpu_custom_call" | custom-call | flops 20000000 | bytes 14000000 | tf_op jit(solution)/shard_map/pallas_call | solution.py:454
  26.7 0.2 collective-permute-done.prev
  26.9 0.0 collective-permute-done.1.following
  26.9 9.1 %all-to-all-done = bf16[64,80,128]{2,1,0:T(8,128)(2,1)S(1)} async-done(((bf16[64,80,128]{2,1,0:T(8,128)(2,1)}), bf16[64,80,128]{2,1,0:T(8,128)(2,1)S(1)}, u32[]{:S(2)}, u32[]{:S(2)}) %all-to-all-start) | async-done | bytes 1310752 | tf_op jit(solution)/shard_map/all_to_all | solution.py:34
  35.9 2.6 %collective-permute-start.2 = (bf16[16,4,80,128]{3,2,1,0:T(8,128)(2,1)S(1)}, bf16[16,4,80,128]{3,2,1,0:T(8,128)(2,1)S(1)}, u32[]{:S(2)}, u32[]{:S(2)}) collective-permute-start(bf16[16,4,80,128]{3,2,1,0:T(8,128)(2,1)S(1)} %bitcast.7), channel_id=1, source_target_pairs={{0,4},{4,0},{1,5},{5,1},{2,6},{6,2},{3,7},{7,3},{8,12},{12,8},{9,1... | collective-permute-start | bytes 3932168 | tf_op jit(solution)/shard_map/ppermute | solution.py:26
  38.5 0.4 collective-permute-start.5
  38.9 2.3 %collective-permute-start.4 = (bf16[768,128]{1,0:T(8,128)(2,1)}, bf16[768,128]{1,0:T(8,128)(2,1)S(1)}, u32[]{:S(2)}, u32[]{:S(2)}) collective-permute-start(bf16[768,128]{1,0:T(8,128)(2,1)} %get-tuple-element.60), channel_id=1, source_target_pairs={{0,2},{1,3},{2,0},{3,1},{4,6},{5,7},{6,4},{7,5},{8,10},{9,11},{10,... | collective-permute-start | bytes 589832 | tf_op jit(solution)/shard_map/ppermute | solution.py:469
  41.2 0.0 collective-permute-start.3
  41.2 0.0 collective-permute-done.2.far
  41.2 0.0 copy-start.5
  41.2 0.9 copy-done.5
  42.2 0.0 copy-start.8
  42.2 0.0 copy-start.16
  42.2 0.0 copy-start.17
  42.2 11.7 %shard_map.190 = (bf16[2048,512]{1,0:T(8,128)(2,1)}, bf16[256,512]{1,0:T(8,128)(2,1)S(1)}, bf16[2048,512]{1,0:T(8,128)(2,1)S(1)}, bf16[2048,512]{1,0:T(8,128)(2,...) custom-call(s32[1]{0:T(128)S(6)} %copy.23.count, ...), custom_call_target="tpu_custom_call" | custom-call | flops 7000000000 | bytes 18000000 | tf_op jit(solution)/shard_map/pallas_call | solution.py:474
  53.9 0.0 collective-permute-done.5.refs_2_
  53.9 0.0 collective-permute-done.4.refs_1_
  53.9 0.0 collective-permute-done.3.refs_0_
  53.9 0.6 collective-permute-start.6
  54.5 0.1 collective-permute-start.7
  54.6 0.4 collective-permute-start.8
  55.0 0.6 collective-permute-done.6.refs_3_
  55.6 0.4 collective-permute-done.7.refs_4_
  56.0 0.3 collective-permute-done.8.refs_5_
  56.3 15.3 %shard_map.191 = (bf16[256,512]{1,0:T(8,128)(2,1)}, f32[256,512]{1,0:T(8,128)S(1)}, bf16[2048,512]{1,0:T(8,128)(2,1)}, bf16[32,512]{1,0:T(8,128)(2,1)S(1)}, bf16...) custom-call(s32[1]{0:T(128)S(6)} %copy.23.count, ...), custom_call_target="tpu_custom_call" | custom-call | flops 8999999488 | bytes 24000000 | tf_op jit(solution)/shard_map/pallas_call | solution.py:513
  71.6 0.2 collective-permute-start.9
  71.8 3.9 %collective-permute-done.9 = bf16[8,2,4,128,128]{4,3,2,1,0:T(8,128)(2,1)S(1)} collective-permute-done((bf16[8,2,4,128,128]{4,3,2,1,0:T(8,128)(2,1)S(1)}, bf16[8,2,4,128,128]{4,3,2,1,0:T(8,128)(2,1)S(1)}, u32[]{:S(2)}, u32[]{:S(2)}) %collective-permute-start.9) | collective-permute-done | bytes 2097184 | tf_op jit(solution)/shard_map/ppermute | solution.py:26
  75.7 2.5 %add_convert_fusion = bf16[8,2,4,128,128]{4,3,2,1,0:T(8,128)(2,1)} fusion(bf16[8,2,4,128,128]{4,3,2,1,0:T(8,128)(2,1)S(1)} %collective-permute-done.9, bf16[8,2,4,128,128]{4,3,2,1,0:T(8,128)(2,1)S(1)} %get-tuple-element.74), kind=kLoop, calls=%fused_computation | loop fusion | flops 4194304 | bytes 6291456 | tf_op jit(solution)/shard_map/convert_element_type | solution.py:551
  78.2 6.7 %all-to-all-start.1 = ((bf16[64,128,128]{2,1,0:T(8,128)(2,1)}), bf16[64,128,128]{2,1,0:T(8,128)(2,1)S(1)}, u32[]{:S(2)}, u32[]{:S(2)}) async-start(bf16[64,128,128]{2,1,0:T(8,128)(2,1)} %bitcast.4), calls=%async_computation.1 | async-start | bytes 4194304 | tf_op jit(solution)/shard_map/all_to_all | solution.py:34
  84.9 3.0 %collective-permute-start.10 = (bf16[32,512]{1,0:T(8,128)(2,1)S(1)}, bf16[32,512]{1,0:T(8,128)(2,1)S(1)}, u32[]{:S(2)}, u32[]{:S(2)}) collective-permute-start(bf16[32,512]{1,0:T(8,128)(2,1)S(1)} %get-tuple-element.77), channel_id=1, source_target_pairs={{0,127},{1,0},{2,1},{3,2},{4,3},{5,4},{6,5},{7,6},{8,7},{9,8},{10,... | collective-permute-start | bytes 98312 | tf_op jit(solution)/shard_map/ppermute | solution.py:30
  87.9 0.0 collective-permute-start.11
  87.9 6.1 %shard_map.192 = bf16[2048,512]{1,0:T(8,128)(2,1)} custom-call(bf16[256,512]{1,0:T(8,128)(2,1)} %copy-done.4, bf16[3,16,2,16,512]{4,3,2,1,0:T(8,128)(2,1)} %copy-done.2, bf16[2048,512]{1,0:T(8,128)(2,1)} %grad_edge.1, bf16[2048,256]{1,0:T(8,128)(2,1)} %get-tuple-element.55.refs_15_.hot, ...), custom_call_target="tpu_custom_call", output_to_operand_aliasing={{}: (4, {})} | custom-call | flops 1600000000 | bytes 9000000 | tf_op jit(solution)/shard_map/pallas_call | solution.py:553
  94.0 19.2 %all-to-all-done.1 = bf16[64,128,128]{2,1,0:T(8,128)(2,1)S(1)} async-done(((bf16[64,128,128]{2,1,0:T(8,128)(2,1)}), bf16[64,128,128]{2,1,0:T(8,128)(2,1)S(1)}, u32[]{:S(2)}, u32[]{:S(2)}) %all-to-all-start.1) | async-done | bytes 2097184 | tf_op jit(solution)/shard_map/all_to_all | solution.py:34
  113.1 0.3 reduce_sum.12.own
  113.4 0.0 collective-permute-done.10.ahead
  113.5 0.1 broadcast_in_dim.2
  113.5 13.8 %all_to_all.15.tiles = bf16[16,112,128]{2,1,0:T(8,128)(2,1)S(1)} all-to-all(bf16[16,112,128]{2,1,0:T(8,128)(2,1)S(1)} %broadcast_in_dim.2), channel_id=1, replica_groups=mesh['z'=4,'x'=4,'core'=2,'feat'=4] {'z','x'}, dimensions={0} | all-to-all | bytes 917504 | tf_op jit(solution)/shard_map/all_to_all | solution.py:34
  127.3 2.7 %collective-permute-start.12 = (bf16[16,112,128]{2,1,0:T(8,128)(2,1)S(1)}, bf16[16,112,128]{2,1,0:T(8,128)(2,1)S(1)}, u32[]{:S(2)}, u32[]{:S(2)}) collective-permute-start(bf16[16,112,128]{2,1,0:T(8,128)(2,1)S(1)} %all_to_all.15.tiles), channel_id=1, source_target_pairs={{0,4},{4,0},{1,5},{5,1},{2,6},{6,2},{3,7},{7,3},{8,12},{12,8},{9,1... | collective-permute-start | bytes 1376264 | tf_op jit(solution)/shard_map/ppermute | solution.py:26
  130.0 1.4 %collective-permute-done.12.far = bf16[16,112,128]{2,1,0:T(8,128)(2,1)S(1)} collective-permute-done((bf16[16,112,128]{2,1,0:T(8,128)(2,1)S(1)}, bf16[16,112,128]{2,1,0:T(8,128)(2,1)S(1)}, u32[]{:S(2)}, u32[]{:S(2)}) %collective-permute-start.12) | collective-permute-done | bytes 458784 | tf_op jit(solution)/shard_map/ppermute | solution.py:26
  131.5 2.2 %shard_map.193 = (f32[3,16,2,16,128]{4,3,2,1,0:T(8,128)}, f32[128,512]{1,0:T(8,128)}, f32[2,16,2,16,128]{4,3,2,1,0:T(8,128)}, f32[128,512]{1,0:T(8,128)}, f32[256,512]{1,0:T(8,128)}) custom-call(s32[1]{0:T(128)S(6)} %copy.23.count, s32[1,4]{1,0:T(1,128)S(1)} %copy-done.14, bf16[16,112,128]{2,1,0:T(8,128)(2,1)S(1)} %all_to_all.15.tiles, ...), custom_call_target="tpu_custom_call" | custom-call | tf_op jit(solution)/shard_map/pallas_call | solution.py:389
  (33 shorter events, 0.1 us)
Async XLA Ops:
  0.6 19.0 %copy-start.9 = (s32[2048]{0:T(1024)S(1)}, s32[2048]{0:T(1024)}, u32[]{:S(2)}) copy-start(s32[2048]{0:T(1024)} %param.16) | copy-start | bytes 24580
  0.6 19.6 %copy-start.12 = (s32[2048]{0:T(1024)S(1)}, s32[2048]{0:T(1024)}, u32[]{:S(2)}) copy-start(s32[2048]{0:T(1024)} %param.15) | copy-start | bytes 24580
  4.0 13.2 %copy-start.18 = (bf16[32,512]{1,0:T(8,128)(2,1)S(1)}, bf16[32,512]{1,0:T(8,128)(2,1)}, u32[]{:S(2)}) copy-start(bf16[32,512]{1,0:T(8,128)(2,1)} %get-tuple-element.50) | copy-start | bytes 98308
  4.0 37.2 %copy-start = (bf16[2048,512]{1,0:T(8,128)(2,1)S(1)}, bf16[2048,512]{1,0:T(8,128)(2,1)}, u32[]{:S(2)}) copy-start(bf16[2048,512]{1,0:T(8,128)(2,1)} %edge.3) | copy-start | bytes 6291460
  4.0 37.2 %copy-start.10 = (s32[2048]{0:T(1024)S(1)}, s32[2048]{0:T(1024)}, u32[]{:S(2)}) copy-start(s32[2048]{0:T(1024)} %param.16) | copy-start | bytes 24580
  4.0 31.9 %all-to-all-start = ((bf16[64,80,128]{2,1,0:T(8,128)(2,1)}), bf16[64,80,128]{2,1,0:T(8,128)(2,1)S(1)}, u32[]{:S(2)}, u32[]{:S(2)}) async-start(bf16[64,80,128]{2,1,0:T(8,128)(2,1)} %get-tuple-element.51), calls=%async_computation | async-start | bytes 2621440 | tf_op jit(solution)/shard_map/all_to_all | solution.py:34
  16.1 10.7 %collective-permute-start = (bf16[32,512]{1,0:T(8,128)(2,1)}, bf16[32,512]{1,0:T(8,128)(2,1)S(1)}, u32[]{:S(2)}, u32[]{:S(2)}) collective-permute-start(bf16[32,512]{1,0:T(8,128)(2,1)} %get-tuple-element.49), channel_id=1, source_target_pairs={{0,1},{1,2},{2,3},{3,4},{4,5},{5,6},{6,7},{7,8},{8,9},{9,10},{10,1... | collective-permute-start | bytes 98312 | tf_op jit(solution)/shard_map/ppermute | solution.py:30
  17.2 9.6 %collective-permute-start.1 = (bf16[32,512]{1,0:T(8,128)(2,1)S(1)}, bf16[32,512]{1,0:T(8,128)(2,1)S(1)}, u32[]{:S(2)}, u32[]{:S(2)}) collective-permute-start(bf16[32,512]{1,0:T(8,128)(2,1)S(1)} %copy-done.18), channel_id=1, source_target_pairs={{0,127},{1,0},{2,1},{3,2},{4,3},{5,4},{6,5},{7,6},{8,7},{9,8},{10,... | collective-permute-start | bytes 98312 | tf_op jit(solution)/shard_map/ppermute | solution.py:30
  20.3 20.9 %copy-start.11 = (s32[4,512]{1,0:T(4,128)S(1)}, s32[4,512]{1,0:T(4,128)}, u32[]{:S(2)}) copy-start(s32[4,512]{1,0:T(4,128)} %reshape.48.dst_wide) | copy-start | bytes 24580
  35.9 5.3 %collective-permute-start.2 = (bf16[16,4,80,128]{3,2,1,0:T(8,128)(2,1)S(1)}, bf16[16,4,80,128]{3,2,1,0:T(8,128)(2,1)S(1)}, u32[]{:S(2)}, u32[]{:S(2)}) collective-permute-start(bf16[16,4,80,128]{3,2,1,0:T(8,128)(2,1)S(1)} %bitcast.7), channel_id=1, source_target_pairs={{0,4},{4,0},{1,5},{5,1},{2,6},{6,2},{3,7},{7,3},{8,12},{12,8},{9,1... | collective-permute-start | bytes 3932168 | tf_op jit(solution)/shard_map/ppermute | solution.py:26
  38.5 15.4 %collective-permute-start.5 = (bf16[768,128]{1,0:T(8,128)(2,1)}, bf16[768,128]{1,0:T(8,128)(2,1)S(1)}, u32[]{:S(2)}, u32[]{:S(2)}) collective-permute-start(bf16[768,128]{1,0:T(8,128)(2,1)} %get-tuple-element.60), channel_id=1, source_target_pairs={{0,3},{1,0},{2,1},{3,2},{4,7},{5,4},{6,5},{7,6},{8,11},{9,8},{10,9... | collective-permute-start | bytes 589832 | tf_op jit(solution)/shard_map/ppermute | solution.py:469
  38.9 15.0 %collective-permute-start.4 = (bf16[768,128]{1,0:T(8,128)(2,1)}, bf16[768,128]{1,0:T(8,128)(2,1)S(1)}, u32[]{:S(2)}, u32[]{:S(2)}) collective-permute-start(bf16[768,128]{1,0:T(8,128)(2,1)} %get-tuple-element.60), channel_id=1, source_target_pairs={{0,2},{1,3},{2,0},{3,1},{4,6},{5,7},{6,4},{7,5},{8,10},{9,11},{10,... | collective-permute-start | bytes 589832 | tf_op jit(solution)/shard_map/ppermute | solution.py:469
  41.2 12.7 %collective-permute-start.3 = (bf16[768,128]{1,0:T(8,128)(2,1)}, bf16[768,128]{1,0:T(8,128)(2,1)S(1)}, u32[]{:S(2)}, u32[]{:S(2)}) collective-permute-start(bf16[768,128]{1,0:T(8,128)(2,1)} %get-tuple-element.60), channel_id=1, source_target_pairs={{0,1},{1,2},{2,3},{3,0},{4,5},{5,6},{6,7},{7,4},{8,9},{9,10},{10,1... | collective-permute-start | bytes 589832 | tf_op jit(solution)/shard_map/ppermute | solution.py:469
  41.2 1.0 copy-start.5
  42.2 14.1 %copy-start.1 = (bf16[2048,512]{1,0:T(8,128)(2,1)S(1)}, bf16[2048,512]{1,0:T(8,128)(2,1)}, u32[]{:S(2)}) copy-start(bf16[2048,512]{1,0:T(8,128)(2,1)} %grad_edge.1) | copy-start | bytes 6291460
  42.2 14.1 %copy-start.3 = (bf16[2048,256]{1,0:T(8,128)(2,1)S(1)}, bf16[2048,256]{1,0:T(8,128)(2,1)}, u32[]{:S(2)}) copy-start(bf16[2048,256]{1,0:T(8,128)(2,1)} %get-tuple-element.55.refs_15_.hot) | copy-start | bytes 3145732
  42.2 14.1 %copy-start.6 = (bf16[256,512]{1,0:T(8,128)(2,1)S(1)}, bf16[256,512]{1,0:T(8,128)(2,1)}, u32[]{:S(2)}) copy-start(bf16[256,512]{1,0:T(8,128)(2,1)} %node.5) | copy-start | bytes 786436
  42.2 14.1 %copy-start.7 = (bf16[2,512,128]{2,1,0:T(8,128)(2,1)S(1)}, bf16[2,512,128]{2,1,0:T(8,128)(2,1)}, u32[]{:S(2)}) copy-start(bf16[2,512,128]{2,1,0:T(8,128)(2,1)} %own_first.1) | copy-start | bytes 786436
  42.2 14.1 %copy-start.8 = (bf16[128,512]{1,0:T(8,128)(2,1)S(1)}, bf16[128,512]{1,0:T(8,128)(2,1)}, u32[]{:S(2)}) copy-start(bf16[128,512]{1,0:T(8,128)(2,1)} %own_second.1) | copy-start | bytes 393220
  42.2 14.1 %copy-start.15 = (bf16[1152,2048]{1,0:T(8,128)(2,1)S(1)}, bf16[1152,2048]{1,0:T(8,128)(2,1)}, u32[]{:S(2)}) copy-start(bf16[1152,2048]{1,0:T(8,128)(2,1)} %get-tuple-element.72.refs_16_) | copy-start | bytes 14155780
  42.2 14.1 %copy-start.16 = (bf16[512,2048]{1,0:T(8,128)(2,1)S(1)}, bf16[512,2048]{1,0:T(8,128)(2,1)}, u32[]{:S(2)}) copy-start(bf16[512,2048]{1,0:T(8,128)(2,1)} %get-tuple-element.67.refs_9_) | copy-start | bytes 6291460
  42.2 14.1 %copy-start.17 = (bf16[256,512]{1,0:T(8,128)(2,1)S(1)}, bf16[256,512]{1,0:T(8,128)(2,1)}, u32[]{:S(2)}) copy-start(bf16[256,512]{1,0:T(8,128)(2,1)} %grad_node.1) | copy-start | bytes 786436
  53.9 17.7 %copy-start.2 = (bf16[3,16,2,16,512]{4,3,2,1,0:T(8,128)(2,1)}, bf16[3,16,2,16,512]{4,3,2,1,0:T(8,128)(2,1)S(1)}, u32[]{:S(2)}) copy-start(bf16[3,16,2,16,512]{4,3,2,1,0:T(8,128)(2,1)S(1)} %get-tuple-element.81.refs_6_.first) | copy-start | bytes 4718596
  53.9 1.7 %collective-permute-start.6 = (bf16[768,128]{1,0:T(8,128)(2,1)S(1)}, bf16[768,128]{1,0:T(8,128)(2,1)S(1)}, u32[]{:S(2)}, u32[]{:S(2)}) collective-permute-start(bf16[768,128]{1,0:T(8,128)(2,1)S(1)} %collective-permute-done.3.refs_0_), channel_id=1, source_target_pairs={{0,4},{4,0},{1,5},{5,1},{2,6},{6,2},{3,7},{7,3},{8,12},{12,8},{9,1... | collective-permute-start | bytes 589832 | tf_op jit(solution)/shard_map/ppermute | solution.py:26
  54.5 1.4 %collective-permute-start.7 = (bf16[768,128]{1,0:T(8,128)(2,1)S(1)}, bf16[768,128]{1,0:T(8,128)(2,1)S(1)}, u32[]{:S(2)}, u32[]{:S(2)}) collective-permute-start(bf16[768,128]{1,0:T(8,128)(2,1)S(1)} %collective-permute-done.4.refs_1_), channel_id=1, source_target_pairs={{0,4},{4,0},{1,5},{5,1},{2,6},{6,2},{3,7},{7,3},{8,12},{12,8},{9,1... | collective-permute-start | bytes 589832 | tf_op jit(solution)/shard_map/ppermute | solution.py:26
  54.6 1.6 %collective-permute-start.8 = (bf16[768,128]{1,0:T(8,128)(2,1)S(1)}, bf16[768,128]{1,0:T(8,128)(2,1)S(1)}, u32[]{:S(2)}, u32[]{:S(2)}) collective-permute-start(bf16[768,128]{1,0:T(8,128)(2,1)S(1)} %collective-permute-done.5.refs_2_), channel_id=1, source_target_pairs={{0,4},{4,0},{1,5},{5,1},{2,6},{6,2},{3,7},{7,3},{8,12},{12,8},{9,1... | collective-permute-start | bytes 589832 | tf_op jit(solution)/shard_map/ppermute | solution.py:26
  71.6 6.6 %copy-start.4 = (bf16[256,512]{1,0:T(8,128)(2,1)}, bf16[256,512]{1,0:T(8,128)(2,1)S(1)}, u32[]{:S(2)}) copy-start(bf16[256,512]{1,0:T(8,128)(2,1)S(1)} %get-tuple-element.80.spread) | copy-start | bytes 786436
  71.6 4.2 %collective-permute-start.9 = (bf16[8,2,4,128,128]{4,3,2,1,0:T(8,128)(2,1)S(1)}, bf16[8,2,4,128,128]{4,3,2,1,0:T(8,128)(2,1)S(1)}, u32[]{:S(2)}, u32[]{:S(2)}) collective-permute-start(bf16[8,2,4,128,128]{4,3,2,1,0:T(8,128)(2,1)S(1)} %get-tuple-element.75), channel_id=1, source_target_pairs={{0,4},{4,0},{1,5},{5,1},{2,6},{6,2},{3,7},{7,3},{8,12},{12,8},{9,1... | collective-permute-start | bytes 6291464 | tf_op jit(solution)/shard_map/ppermute | solution.py:26
  78.2 34.9 %all-to-all-start.1 = ((bf16[64,128,128]{2,1,0:T(8,128)(2,1)}), bf16[64,128,128]{2,1,0:T(8,128)(2,1)S(1)}, u32[]{:S(2)}, u32[]{:S(2)}) async-start(bf16[64,128,128]{2,1,0:T(8,128)(2,1)} %bitcast.4), calls=%async_computation.1 | async-start | bytes 4194304 | tf_op jit(solution)/shard_map/all_to_all | solution.py:34
  84.9 28.6 %collective-permute-start.10 = (bf16[32,512]{1,0:T(8,128)(2,1)S(1)}, bf16[32,512]{1,0:T(8,128)(2,1)S(1)}, u32[]{:S(2)}, u32[]{:S(2)}) collective-permute-start(bf16[32,512]{1,0:T(8,128)(2,1)S(1)} %get-tuple-element.77), channel_id=1, source_target_pairs={{0,127},{1,0},{2,1},{3,2},{4,3},{5,4},{6,5},{7,6},{8,7},{9,8},{10,... | collective-permute-start | bytes 98312 | tf_op jit(solution)/shard_map/ppermute | solution.py:30
  87.9 25.6 %collective-permute-start.11 = (bf16[32,512]{1,0:T(8,128)(2,1)S(1)}, bf16[32,512]{1,0:T(8,128)(2,1)S(1)}, u32[]{:S(2)}, u32[]{:S(2)}) collective-permute-start(bf16[32,512]{1,0:T(8,128)(2,1)S(1)} %get-tuple-element.79), channel_id=1, source_target_pairs={{0,1},{1,2},{2,3},{3,4},{4,5},{5,6},{6,7},{7,8},{8,9},{9,10},{10,1... | collective-permute-start | bytes 98312 | tf_op jit(solution)/shard_map/ppermute | solution.py:30
  93.9 37.5 %copy-start.13 = (s32[1,2,32]{2,1,0:T(2,128)S(1)}, s32[1,2,32]{2,1,0:T(2,128)}, u32[]{:S(2)}) copy-start(s32[1,2,32]{2,1,0:T(2,128)} %param.18) | copy-start | bytes 772
  93.9 37.5 %copy-start.14 = (s32[1,4]{1,0:T(1,128)S(1)}, s32[1,4]{1,0:T(1,128)}, u32[]{:S(2)}) copy-start(s32[1,4]{1,0:T(1,128)} %owned.3) | copy-start | bytes 52
  127.3 4.1 %collective-permute-start.12 = (bf16[16,112,128]{2,1,0:T(8,128)(2,1)S(1)}, bf16[16,112,128]{2,1,0:T(8,128)(2,1)S(1)}, u32[]{:S(2)}, u32[]{:S(2)}) collective-permute-start(bf16[16,112,128]{2,1,0:T(8,128)(2,1)S(1)} %all_to_all.15.tiles), channel_id=1, source_target_pairs={{0,4},{4,0},{1,5},{5,1},{2,6},{6,2},{3,7},{7,3},{8,12},{12,8},{9,1... | collective-permute-start | bytes 1376264 | tf_op jit(solution)/shard_map/ppermute | solution.py:26

commit v12 on v11

--- a/solution.py
+++ b/solution.py
@@ -295,54 +295,54 @@
     node_out, node_total, pre_grads, to_prev, to_next, keep, give, spread = refs[11:19]
     first, second, sum_second, sum_first, sums, columns, rows, owned = refs[19:27]
     held, back, deltas = refs[27:]
-    step = pl.program_id(0)
-
-    @pl.when(step == 0)
-    def _():
-        place_weights(co, own_first, own_second, near, far, first, second)
-        lat, summed = node[...], incoming[...]
-        pre = dot(lat, first[0]) + dot(summed, first[1])
-        node_act, node_slope = swish(pre)
-        node_act = node_act.astype(BF16)
-        node_normed, node_factor = normalize(dot(node_act, second[...]))
-        node_out[...] = (lat.astype(F32) + node_normed).astype(BF16)
-        upstream = grad_node[...].astype(F32)
-        delta = normalize_back(upstream, node_normed, node_factor).astype(BF16)
-        put_rows(co, dot_tn(node_act, delta), 6, rows, keep, give)
-        pre_grad = (dot_nt(delta, second[...]) * node_slope).astype(BF16)
-        put_columns(co, dot_tn(lat, pre_grad), 3, columns, keep, give)
-        put_columns(co, dot_tn(summed, pre_grad), 4, columns, keep, give)
-        node_total[...] = upstream + dot_nt(pre_grad, first[0])
-        spread[...] = dot_nt(pre_grad, first[1]).astype(BF16)
-        sum_second[...] = jnp.zeros_like(sum_second)
-        sum_first[...] = jnp.zeros_like(sum_first)
-        sums[...] = jnp.zeros_like(sums)
-
-    held[...] = dot(hot[...], spread[...])
-    for h in STRIPS:
-        total = grad_edge[h, :].astype(F32) + held[h, :]
-        delta = normalize_back(total, normed[h, :].astype(F32), factor[h, 0:1])
-        deltas[h, :] = delta.astype(BF16)
-    back[...] = dot_nt(deltas[...], edge_second[...])
-    for h in STRIPS:
-        pre_grads[h, :] = (back[h, :] * slope[h, :].astype(F32)).astype(BF16)
-    sum_second[...] += dot_tn(act[...], deltas[...])
-    sum_first[...] += dot(edge_turned[...], pre_grads[...])
-    sums[...] += dot(turned[...], pre_grads[...])
-
-    @pl.when(step == STEPS - 1)
-    def _():
-        put_rows(co, sum_second[...], 5, rows, keep, give)
-        put_columns(co, sum_first[...], 0, columns, keep, give)
-        received = sums[0:256, :].astype(BF16)
-        sent = sums[256:, :].astype(BF16)
-        put_columns(co, dot_tn(lookup[...], sent), 1, columns, keep, give)
-        put_columns(co, dot_tn(node[...], received), 2, columns, keep, give)
-        remote = dot_nt(sent, whole(edge_first, 1))
-        node_total[...] += remote[0:256] + dot_nt(received, whole(edge_first, 2))
-        to_prev[...] = remote[256:288].astype(BF16)
-        to_next[...] = remote[288:320].astype(BF16)
-        put_owned(co, remote[320:832], owned, keep, give)
+    place_weights(co, own_first, own_second, near, far, first, second)
+    lat, summed = node[...], incoming[...]
+    pre = dot(lat, first[0]) + dot(summed, first[1])
+    node_act, node_slope = swish(pre)
+    node_act = node_act.astype(BF16)
+    node_normed, node_factor = normalize(dot(node_act, second[...]))
+    node_out[...] = (lat.astype(F32) + node_normed).astype(BF16)
+    upstream = grad_node[...].astype(F32)
+    delta = normalize_back(upstream, node_normed, node_factor).astype(BF16)
+    put_rows(co, dot_tn(node_act, delta), 6, rows, keep, give)
+    pre_grad = (dot_nt(delta, second[...]) * node_slope).astype(BF16)
+    put_columns(co, dot_tn(lat, pre_grad), 3, columns, keep, give)
+    put_columns(co, dot_tn(summed, pre_grad), 4, columns, keep, give)
+    node_total[...] = upstream + dot_nt(pre_grad, first[0])
+    spread[...] = dot_nt(pre_grad, first[1]).astype(BF16)
+    sum_second[...] = jnp.zeros_like(sum_second)
+    sum_first[...] = jnp.zeros_like(sum_first)
+    sums[...] = jnp.zeros_like(sums)
+
+    def block(step, carry):
+        at = pl.ds(pl.multiple_of(step * CHUNK, CHUNK), CHUNK)
+        normed_at, slope_at, factor_at = normed.at[at], slope.at[at], factor.at[at]
+        grad_at, pre_at, columns_at = grad_edge.at[at], pre_grads.at[at], edge_turned.at[:, at]
+        held[...] = dot(hot[at, :], spread[...])
+        for h in STRIPS:
+            total = grad_at[h, :].astype(F32) + held[h, :]
+            delta = normalize_back(total, normed_at[h, :].astype(F32), factor_at[h, 0:1])
+            deltas[h, :] = delta.astype(BF16)
+        back[...] = dot_nt(deltas[...], edge_second[...])
+        for h in STRIPS:
+            pre_at[h, :] = (back[h, :] * slope_at[h, :].astype(F32)).astype(BF16)
+        sum_second[...] += dot_tn(act[at, :], deltas[...])
+        sum_first[...] += dot(columns_at[...], pre_at[...])
+        sums[...] += dot(turned[:, at], pre_at[...])
+        return carry
+
+    lax.fori_loop(0, STEPS, block, 0)
+    put_rows(co, sum_second[...], 5, rows, keep, give)
+    put_columns(co, sum_first[...], 0, columns, keep, give)
+    received = sums[0:256, :].astype(BF16)
+    sent = sums[256:, :].astype(BF16)
+    put_columns(co, dot_tn(lookup[...], sent), 1, columns, keep, give)
+    put_columns(co, dot_tn(node[...], received), 2, columns, keep, give)
+    remote = dot_nt(sent, whole(edge_first, 1))
+    node_total[...] += remote[0:256] + dot_nt(received, whole(edge_first, 2))
+    to_prev[...] = remote[256:288].astype(BF16)
+    to_next[...] = remote[288:320].astype(BF16)
+    put_owned(co, remote[320:832], owned, keep, give)
 
 
 def edge_kernel(spread, first, grad_edge, hot, pre_grads, edge_grad):
@@ -510,16 +510,11 @@
     fixed += [first, second, lookup]
     moving = [edge_turned, act, normed, slope, factor, grad_edge, hot, turned]
     tiles = (8, 2, 4, 128, 128)
-    node_out, node_total, pre_grads, to_prev, to_next, keep, give, spread = pl.pallas_call(
+    node_out, node_total, pre_grads, to_prev, to_next, keep, give, spread = plain_call(
         backward_kernel,
-        grid=(STEPS,),
-        in_specs=[SMEM]
-        + [like(v) for v in fixed]
-        + [column(512, CHUNK), wide, wide, wide, chunk(CHUNK, 128), wide, chunk(CHUNK, 256)]
-        + [column(high, CHUNK)],
-        out_specs=[same(256, 512), same(256, 512), wide, same(32, 512), same(32, 512)]
-        + [same(*tiles), same(*tiles), same(256, 512)],
-        out_shape=[
+        [edge_count],
+        fixed + moving,
+        [
             shape(256, 512),
             shape(256, 512, dtype=F32),
             shape(2048, 512),
@@ -529,7 +524,7 @@
             shape(*tiles),
             shape(256, 512),
         ],
-        scratch_shapes=[
+        [
             pltpu.VMEM((2, 512, 512), BF16),
             pltpu.VMEM((512, 512), BF16),
             pltpu.VMEM((512, 512), F32),
@@ -542,11 +537,8 @@
             pltpu.VMEM((CHUNK, 512), F32),
             pltpu.VMEM((CHUNK, 512), BF16),
         ],
-        compiler_params=limit(24),
-        cost_estimate=pl.CostEstimate(
-            flops=9_000_000_000, bytes_accessed=24_000_000, transcendentals=100_000
-        ),
-    )(edge_count, *fixed, *moving)
+        mib=34,
+    )
 
     pair = (keep.astype(F32) + other_core(give).astype(F32)).astype(BF16).reshape(64, 128, 128)
     edge_first = after(first, pair)

time: 134 us -> 140 us (1.045)
  local copies, waits for them, and re-layouts: 2.3 us -> 5.31 us
  Pallas kernels: 43.7 us -> 46.4 us
    pallas_call x2 -> x3, Pallas kernels: 4.92 us -> 22.8 us  [plain_call(): pl.pallas_call(kernel, in_specs=[SMEM] * len(scalars) + [WHOLE] * len(ope...]
    pallas_call x1 -> x0, Pallas kernels: 15.3 us -> none  [shards(): pl.pallas_call(backward_kernel, grid=(STEPS,), in_specs=[SMEM] + [like(v)...]
    unnamed x38 -> x40, local copies, waits for them, and re-layouts: 1.03 us -> 4.03 us
  transfers between devices with their start and end apart: 15 -> 15, of which waited for: 8 -> 8; matrix products, arithmetic and copies ran while one was open for 1% -> 1% of each run, Pallas kernels for 18% -> 17%
where the time goes in v12:
time: 140 us; the launch traced here: 139 us
  Pallas kernels  46.4 us (33%)
  waiting for transfers between devices  35.4 us (25%)
  starting transfers between devices  34.3 us (24%)
  blocking collectives  13.8 us (10%)
  local copies, waits for them, and re-layouts  5.31 us (4%)
  other arithmetic  2.77 us (2%)
  between operations  1.49 us (1%)
    all_to_all x2, waiting for transfers between devices, exchange(): return lax.all_to_all(value, axes, 0, 0, tiled=True)  28.6 us
    pallas_call x3, Pallas kernels, plain_call(): pl.pallas_call(kernel, in_specs=[SMEM] * len(scalars) + [WHOLE] * len(ope...  22.8 us
    all_to_all x2, starting transfers between devices, exchange(): return lax.all_to_all(value, axes, 0, 0, tiled=True)  18.7 us
    all_to_all x1, blocking collectives, exchange(): return lax.all_to_all(value, axes, 0, 0, tiled=True)  13.8 us
    pallas_call x1, Pallas kernels, shards(): pl.pallas_call(forward_kernel, grid=(STEPS,), in_specs=[SMEM] + [like(v)...  11.7 us
    ppermute x6, waiting for transfers between devices, other_core(): return lax.ppermute(value, 'core', [(0, 1), (1, 0)])  6.63 us
    ppermute x6, starting transfers between devices, other_core(): return lax.ppermute(value, 'core', [(0, 1), (1, 0)])  6.46 us
    ppermute x4, starting transfers between devices, shifted(): lax.ppermute(value, BOTH, [(k, (k + steps) % 128) for k in range(128)])  6.44 us
  transfers between devices with their start and end apart: 15, of which 8 were waited for; matrix products, arithmetic and copies ran while one was open for 1% of the time, Pallas kernels for 17%

profile of v12, /device:TPU:1, one launch (start us, length us, event | category | flops | bytes accessed | tf_op | source)
XLA Modules:
  0.0 139.4 jit_solution(12309175883044870129)
XLA Ops:
  0.6 0.0 copy-start.11
  1.3 2.7 %shard_map.188 = (bf16[64,80,128]{2,1,0:T(8,128)(2,1)}, bf16[32,512]{1,0:T(8,128)(2,1)}, bf16[32,512]{1,0:T(8,128)(2,1)}, bf16[768,128]{1,0:T(8,128)(2,1)}) custom-call(s32[1]{0:T(128)S(6)} %copy.23.count, s32[1,4]{1,0:T(1,128)} %owned.3, bf16[256,512]{1,0:T(8,128)(2,1)} %node.5, s32[2,32]{1,0:T(2,128)} %bitcast.12, bf16[3,512,128]{2,1,0:T(8,128)(2,1)} %edge_first.1, ...), custom_call_target="tpu_custom_call" | custom-call | tf_op jit(solution)/shard_map/pallas_call | solution.py:389
  4.0 0.0 copy-start.17
  4.0 0.0 copy-start.6
  4.0 0.0 copy-start.12
  4.1 12.1 %all-to-all-start = ((bf16[64,80,128]{2,1,0:T(8,128)(2,1)}), bf16[64,80,128]{2,1,0:T(8,128)(2,1)S(1)}, u32[]{:S(2)}, u32[]{:S(2)}) async-start(bf16[64,80,128]{2,1,0:T(8,128)(2,1)} %get-tuple-element.51), calls=%async_computation | async-start | bytes 2621440 | tf_op jit(solution)/shard_map/all_to_all | solution.py:34
  16.2 1.1 collective-permute-start
  17.3 2.4 %collective-permute-start.1 = (bf16[32,512]{1,0:T(8,128)(2,1)S(1)}, bf16[32,512]{1,0:T(8,128)(2,1)S(1)}, u32[]{:S(2)}, u32[]{:S(2)}) collective-permute-start(bf16[32,512]{1,0:T(8,128)(2,1)S(1)} %copy-done.18), channel_id=1, source_target_pairs={{0,127},{1,0},{2,1},{3,2},{4,3},{5,4},{6,5},{7,6},{8,7},{9,8},{10,... | collective-permute-start | bytes 98312 | tf_op jit(solution)/shard_map/ppermute | solution.py:30
  19.7 0.6 reshape.48.dst_wide
  20.3 0.6 reshape.47.src_wide
  20.9 5.8 %shard_map.189 = (bf16[2048,256]{1,0:T(8,128)(2,1)}, bf16[1152,2048]{1,0:T(8,128)(2,1)}, bf16[512,2048]{1,0:T(8,128)(2,1)}) custom-call(s32[1]{0:T(128)S(6)} %copy.23.count, s32[16,128]{1,0:T(8,128)} %bitcast.9, s32[4,512]{1,0:T(4,128)} %reshape.47.src_wide, s32[4,512]{1,0:T(4,128)} %reshape.48.dst_wide, bf16[2048,512]{1,0:T(8,128)(2,1)} %edge.3), custom_call_target="tpu_custom_call" | custom-call | flops 20000000 | bytes 14000000 | tf_op jit(solution)/shard_map/pallas_call | solution.py:454
  26.7 0.2 collective-permute-done.prev
  26.9 9.1 %all-to-all-done = bf16[64,80,128]{2,1,0:T(8,128)(2,1)S(1)} async-done(((bf16[64,80,128]{2,1,0:T(8,128)(2,1)}), bf16[64,80,128]{2,1,0:T(8,128)(2,1)S(1)}, u32[]{:S(2)}, u32[]{:S(2)}) %all-to-all-start) | async-done | bytes 1310752 | tf_op jit(solution)/shard_map/all_to_all | solution.py:34
  36.0 2.6 %collective-permute-start.2 = (bf16[16,4,80,128]{3,2,1,0:T(8,128)(2,1)S(1)}, bf16[16,4,80,128]{3,2,1,0:T(8,128)(2,1)S(1)}, u32[]{:S(2)}, u32[]{:S(2)}) collective-permute-start(bf16[16,4,80,128]{3,2,1,0:T(8,128)(2,1)S(1)} %bitcast.7), channel_id=1, source_target_pairs={{0,4},{4,0},{1,5},{5,1},{2,6},{6,2},{3,7},{7,3},{8,12},{12,8},{9,1... | collective-permute-start | bytes 3932168 | tf_op jit(solution)/shard_map/ppermute | solution.py:26
  38.6 1.1 copy-done.4
  39.6 0.4 collective-permute-start.5
  40.0 2.3 %collective-permute-start.4 = (bf16[768,128]{1,0:T(8,128)(2,1)S(1)}, bf16[768,128]{1,0:T(8,128)(2,1)S(1)}, u32[]{:S(2)}, u32[]{:S(2)}) collective-permute-start(bf16[768,128]{1,0:T(8,128)(2,1)S(1)} %copy-done.17), channel_id=1, source_target_pairs={{0,2},{1,3},{2,0},{3,1},{4,6},{5,7},{6,4},{7,5},{8,10},{9,11},{10,... | collective-permute-start | bytes 589832 | tf_op jit(solution)/shard_map/ppermute | solution.py:469
  42.3 0.0 collective-permute-start.3
  42.3 0.0 collective-permute-done.2.far
  42.3 0.0 copy-start.3
  42.3 1.6 %copy-done.3 = bf16[2048,512]{1,0:T(8,128)(2,1)S(1)} copy-done((bf16[2048,512]{1,0:T(8,128)(2,1)S(1)}, bf16[2048,512]{1,0:T(8,128)(2,1)}, u32[]{:S(2)}) %copy-start.3) | copy-done | bytes 2097176
  43.9 1.3 copy-done.5
  45.2 0.0 copy-start.9
  45.2 11.7 %shard_map.190 = (bf16[2048,512]{1,0:T(8,128)(2,1)}, bf16[256,512]{1,0:T(8,128)(2,1)S(1)}, bf16[2048,512]{1,0:T(8,128)(2,1)S(1)}, bf16[2048,512]{1,0:T(8,128)(2,...) custom-call(s32[1]{0:T(128)S(6)} %copy.23.count, ...), custom_call_target="tpu_custom_call" | custom-call | flops 7000000000 | bytes 18000000 | tf_op jit(solution)/shard_map/pallas_call | solution.py:474
  57.0 0.0 collective-permute-done.5.refs_2_
  57.0 0.0 collective-permute-done.3.refs_0_
  57.0 0.6 collective-permute-start.6
  57.6 0.1 collective-permute-start.7
  57.6 0.4 collective-permute-start.8
  58.1 0.6 collective-permute-done.6.refs_3_
  58.6 0.4 collective-permute-done.7.refs_4_
  59.0 0.3 collective-permute-done.8.refs_5_
  59.3 17.9 %shard_map.191 = (bf16[256,512]{1,0:T(8,128)(2,1)}, f32[256,512]{1,0:T(8,128)S(1)}, bf16[2048,512]{1,0:T(8,128)(2,1)}, bf16[32,512]{1,0:T(8,128)(2,1)S(1)}, bf16...) custom-call(s32[1]{0:T(128)S(6)} %copy.23.count, ...), custom_call_target="tpu_custom_call" | custom-call | tf_op jit(solution)/shard_map/pallas_call | solution.py:389
  77.2 0.2 collective-permute-start.9
  77.4 4.0 %collective-permute-done.9 = bf16[8,2,4,128,128]{4,3,2,1,0:T(8,128)(2,1)S(1)} collective-permute-done((bf16[8,2,4,128,128]{4,3,2,1,0:T(8,128)(2,1)S(1)}, bf16[8,2,4,128,128]{4,3,2,1,0:T(8,128)(2,1)S(1)}, u32[]{:S(2)}, u32[]{:S(2)}) %collective-permute-start.9) | collective-permute-done | bytes 2097184 | tf_op jit(solution)/shard_map/ppermute | solution.py:26
  81.3 2.5 %add_convert_fusion = bf16[8,2,4,128,128]{4,3,2,1,0:T(8,128)(2,1)} fusion(bf16[8,2,4,128,128]{4,3,2,1,0:T(8,128)(2,1)S(1)} %collective-permute-done.9, bf16[8,2,4,128,128]{4,3,2,1,0:T(8,128)(2,1)S(1)} %get-tuple-element.74), kind=kLoop, calls=%fused_computation | loop fusion | flops 4194304 | bytes 6291456 | tf_op jit(solution)/shard_map/convert_element_type | solution.py:543
  83.8 6.6 %all-to-all-start.1 = ((bf16[64,128,128]{2,1,0:T(8,128)(2,1)}), bf16[64,128,128]{2,1,0:T(8,128)(2,1)S(1)}, u32[]{:S(2)}, u32[]{:S(2)}) async-start(bf16[64,128,128]{2,1,0:T(8,128)(2,1)} %bitcast.4), calls=%async_computation.1 | async-start | bytes 4194304 | tf_op jit(solution)/shard_map/all_to_all | solution.py:34
  90.4 2.9 %collective-permute-start.10 = (bf16[32,512]{1,0:T(8,128)(2,1)S(1)}, bf16[32,512]{1,0:T(8,128)(2,1)S(1)}, u32[]{:S(2)}, u32[]{:S(2)}) collective-permute-start(bf16[32,512]{1,0:T(8,128)(2,1)S(1)} %get-tuple-element.77), channel_id=1, source_target_pairs={{0,127},{1,0},{2,1},{3,2},{4,3},{5,4},{6,5},{7,6},{8,7},{9,8},{10,... | collective-permute-start | bytes 98312 | tf_op jit(solution)/shard_map/ppermute | solution.py:30
  93.4 0.0 collective-permute-start.11
  93.4 6.1 %shard_map.192 = bf16[2048,512]{1,0:T(8,128)(2,1)} custom-call(bf16[256,512]{1,0:T(8,128)(2,1)} %copy-done.10, bf16[3,16,2,16,512]{4,3,2,1,0:T(8,128)(2,1)} %copy-done, bf16[2048,512]{1,0:T(8,128)(2,1)} %grad_edge.1, bf16[2048,256]{1,0:T(8,128)(2,1)} %get-tuple-element.55.refs_15_.hot, ...), custom_call_target="tpu_custom_call", output_to_operand_aliasing={{}: (4, {})} | custom-call | flops 1600000000 | bytes 9000000 | tf_op jit(solution)/shard_map/pallas_call | solution.py:545
  99.5 19.5 %all-to-all-done.1 = bf16[64,128,128]{2,1,0:T(8,128)(2,1)S(1)} async-done(((bf16[64,128,128]{2,1,0:T(8,128)(2,1)}), bf16[64,128,128]{2,1,0:T(8,128)(2,1)S(1)}, u32[]{:S(2)}, u32[]{:S(2)}) %all-to-all-start.1) | async-done | bytes 2097184 | tf_op jit(solution)/shard_map/all_to_all | solution.py:34
  119.0 0.3 reduce_sum.12.own
  119.3 0.0 collective-permute-done.11.behind
  119.3 0.1 broadcast_in_dim.2
  119.4 13.8 %all_to_all.15.tiles = bf16[16,112,128]{2,1,0:T(8,128)(2,1)S(1)} all-to-all(bf16[16,112,128]{2,1,0:T(8,128)(2,1)S(1)} %broadcast_in_dim.2), channel_id=1, replica_groups=mesh['z'=4,'x'=4,'core'=2,'feat'=4] {'z','x'}, dimensions={0} | all-to-all | bytes 917504 | tf_op jit(solution)/shard_map/all_to_all | solution.py:34
  133.2 2.6 %collective-permute-start.12 = (bf16[16,112,128]{2,1,0:T(8,128)(2,1)S(1)}, bf16[16,112,128]{2,1,0:T(8,128)(2,1)S(1)}, u32[]{:S(2)}, u32[]{:S(2)}) collective-permute-start(bf16[16,112,128]{2,1,0:T(8,128)(2,1)S(1)} %all_to_all.15.tiles), channel_id=1, source_target_pairs={{0,4},{4,0},{1,5},{5,1},{2,6},{6,2},{3,7},{7,3},{8,12},{12,8},{9,1... | collective-permute-start | bytes 1376264 | tf_op jit(solution)/shard_map/ppermute | solution.py:26
  135.8 1.4 %collective-permute-done.12.far = bf16[16,112,128]{2,1,0:T(8,128)(2,1)S(1)} collective-permute-done((bf16[16,112,128]{2,1,0:T(8,128)(2,1)S(1)}, bf16[16,112,128]{2,1,0:T(8,128)(2,1)S(1)}, u32[]{:S(2)}, u32[]{:S(2)}) %collective-permute-start.12) | collective-permute-done | bytes 458784 | tf_op jit(solution)/shard_map/ppermute | solution.py:26
  137.2 2.2 %shard_map.193 = (f32[3,16,2,16,128]{4,3,2,1,0:T(8,128)}, f32[128,512]{1,0:T(8,128)}, f32[2,16,2,16,128]{4,3,2,1,0:T(8,128)}, f32[128,512]{1,0:T(8,128)}, f32[256,512]{1,0:T(8,128)}) custom-call(s32[1]{0:T(128)S(6)} %copy.23.count, s32[1,4]{1,0:T(1,128)S(1)} %copy-done.16, bf16[16,112,128]{2,1,0:T(8,128)(2,1)S(1)} %all_to_all.15.tiles, ...), custom_call_target="tpu_custom_call" | custom-call | tf_op jit(solution)/shard_map/pallas_call | solution.py:389
  (35 shorter events, 0.1 us)
Async XLA Ops:
  0.6 19.1 %copy-start.11 = (s32[2048]{0:T(1024)S(1)}, s32[2048]{0:T(1024)}, u32[]{:S(2)}) copy-start(s32[2048]{0:T(1024)} %param.16) | copy-start | bytes 24580
  0.6 19.7 %copy-start.14 = (s32[2048]{0:T(1024)S(1)}, s32[2048]{0:T(1024)}, u32[]{:S(2)}) copy-start(s32[2048]{0:T(1024)} %param.15) | copy-start | bytes 24580
  4.0 12.2 %copy-start.19 = (bf16[32,512]{1,0:T(8,128)(2,1)S(1)}, bf16[32,512]{1,0:T(8,128)(2,1)}, u32[]{:S(2)}) copy-start(bf16[32,512]{1,0:T(8,128)(2,1)} %get-tuple-element.49) | copy-start | bytes 98308
  4.0 13.3 %copy-start.18 = (bf16[32,512]{1,0:T(8,128)(2,1)S(1)}, bf16[32,512]{1,0:T(8,128)(2,1)}, u32[]{:S(2)}) copy-start(bf16[32,512]{1,0:T(8,128)(2,1)} %get-tuple-element.50) | copy-start | bytes 98308
  4.0 35.6 %copy-start.17 = (bf16[768,128]{1,0:T(8,128)(2,1)S(1)}, bf16[768,128]{1,0:T(8,128)(2,1)}, u32[]{:S(2)}) copy-start(bf16[768,128]{1,0:T(8,128)(2,1)} %get-tuple-element.60) | copy-start | bytes 589828
  4.0 38.2 %copy-start.6 = (bf16[256,512]{1,0:T(8,128)(2,1)S(1)}, bf16[256,512]{1,0:T(8,128)(2,1)}, u32[]{:S(2)}) copy-start(bf16[256,512]{1,0:T(8,128)(2,1)} %node.5) | copy-start | bytes 786436
  4.0 38.2 %copy-start.12 = (s32[2048]{0:T(1024)S(1)}, s32[2048]{0:T(1024)}, u32[]{:S(2)}) copy-start(s32[2048]{0:T(1024)} %param.16) | copy-start | bytes 24580
  4.1 31.9 %all-to-all-start = ((bf16[64,80,128]{2,1,0:T(8,128)(2,1)}), bf16[64,80,128]{2,1,0:T(8,128)(2,1)S(1)}, u32[]{:S(2)}, u32[]{:S(2)}) async-start(bf16[64,80,128]{2,1,0:T(8,128)(2,1)} %get-tuple-element.51), calls=%async_computation | async-start | bytes 2621440 | tf_op jit(solution)/shard_map/all_to_all | solution.py:34
  16.2 10.7 %collective-permute-start = (bf16[32,512]{1,0:T(8,128)(2,1)S(1)}, bf16[32,512]{1,0:T(8,128)(2,1)S(1)}, u32[]{:S(2)}, u32[]{:S(2)}) collective-permute-start(bf16[32,512]{1,0:T(8,128)(2,1)S(1)} %copy-done.19), channel_id=1, source_target_pairs={{0,1},{1,2},{2,3},{3,4},{4,5},{5,6},{6,7},{7,8},{8,9},{9,10},{10,1... | collective-permute-start | bytes 98312 | tf_op jit(solution)/shard_map/ppermute | solution.py:30
  17.3 9.6 %collective-permute-start.1 = (bf16[32,512]{1,0:T(8,128)(2,1)S(1)}, bf16[32,512]{1,0:T(8,128)(2,1)S(1)}, u32[]{:S(2)}, u32[]{:S(2)}) collective-permute-start(bf16[32,512]{1,0:T(8,128)(2,1)S(1)} %copy-done.18), channel_id=1, source_target_pairs={{0,127},{1,0},{2,1},{3,2},{4,3},{5,4},{6,5},{7,6},{8,7},{9,8},{10,... | collective-permute-start | bytes 98312 | tf_op jit(solution)/shard_map/ppermute | solution.py:30
  20.3 22.0 %copy-start.13 = (s32[4,512]{1,0:T(4,128)S(1)}, s32[4,512]{1,0:T(4,128)}, u32[]{:S(2)}) copy-start(s32[4,512]{1,0:T(4,128)} %reshape.48.dst_wide) | copy-start | bytes 24580
  36.0 6.3 %collective-permute-start.2 = (bf16[16,4,80,128]{3,2,1,0:T(8,128)(2,1)S(1)}, bf16[16,4,80,128]{3,2,1,0:T(8,128)(2,1)S(1)}, u32[]{:S(2)}, u32[]{:S(2)}) collective-permute-start(bf16[16,4,80,128]{3,2,1,0:T(8,128)(2,1)S(1)} %bitcast.7), channel_id=1, source_target_pairs={{0,4},{4,0},{1,5},{5,1},{2,6},{6,2},{3,7},{7,3},{8,12},{12,8},{9,1... | collective-permute-start | bytes 3932168 | tf_op jit(solution)/shard_map/ppermute | solution.py:26
  38.6 1.1 copy-start.4
  39.6 17.3 %collective-permute-start.5 = (bf16[768,128]{1,0:T(8,128)(2,1)S(1)}, bf16[768,128]{1,0:T(8,128)(2,1)S(1)}, u32[]{:S(2)}, u32[]{:S(2)}) collective-permute-start(bf16[768,128]{1,0:T(8,128)(2,1)S(1)} %copy-done.17), channel_id=1, source_target_pairs={{0,3},{1,0},{2,1},{3,2},{4,7},{5,4},{6,5},{7,6},{8,11},{9,8},{10,9... | collective-permute-start | bytes 589832 | tf_op jit(solution)/shard_map/ppermute | solution.py:469
  40.0 16.9 %collective-permute-start.4 = (bf16[768,128]{1,0:T(8,128)(2,1)S(1)}, bf16[768,128]{1,0:T(8,128)(2,1)S(1)}, u32[]{:S(2)}, u32[]{:S(2)}) collective-permute-start(bf16[768,128]{1,0:T(8,128)(2,1)S(1)} %copy-done.17), channel_id=1, source_target_pairs={{0,2},{1,3},{2,0},{3,1},{4,6},{5,7},{6,4},{7,5},{8,10},{9,11},{10,... | collective-permute-start | bytes 589832 | tf_op jit(solution)/shard_map/ppermute | solution.py:469
  42.3 14.7 %collective-permute-start.3 = (bf16[768,128]{1,0:T(8,128)(2,1)S(1)}, bf16[768,128]{1,0:T(8,128)(2,1)S(1)}, u32[]{:S(2)}, u32[]{:S(2)}) collective-permute-start(bf16[768,128]{1,0:T(8,128)(2,1)S(1)} %copy-done.17), channel_id=1, source_target_pairs={{0,1},{1,2},{2,3},{3,0},{4,5},{5,6},{6,7},{7,4},{8,9},{9,10},{10,1... | collective-permute-start | bytes 589832 | tf_op jit(solution)/shard_map/ppermute | solution.py:469
  42.3 1.6 %copy-start.3 = (bf16[2048,512]{1,0:T(8,128)(2,1)S(1)}, bf16[2048,512]{1,0:T(8,128)(2,1)}, u32[]{:S(2)}) copy-start(bf16[2048,512]{1,0:T(8,128)(2,1)} %edge.3) | copy-start | bytes 6291460
  43.9 1.3 copy-start.5
  45.2 14.1 %copy-start.1 = (bf16[2048,256]{1,0:T(8,128)(2,1)S(1)}, bf16[2048,256]{1,0:T(8,128)(2,1)}, u32[]{:S(2)}) copy-start(bf16[2048,256]{1,0:T(8,128)(2,1)} %get-tuple-element.55.refs_15_.hot) | copy-start | bytes 3145732
  45.2 14.1 %copy-start.2 = (bf16[512,2048]{1,0:T(8,128)(2,1)S(1)}, bf16[512,2048]{1,0:T(8,128)(2,1)}, u32[]{:S(2)}) copy-start(bf16[512,2048]{1,0:T(8,128)(2,1)} %get-tuple-element.67.refs_9_) | copy-start | bytes 6291460
  45.2 14.1 %copy-start.7 = (bf16[2,512,128]{2,1,0:T(8,128)(2,1)S(1)}, bf16[2,512,128]{2,1,0:T(8,128)(2,1)}, u32[]{:S(2)}) copy-start(bf16[2,512,128]{2,1,0:T(8,128)(2,1)} %own_first.1) | copy-start | bytes 786436
  45.2 14.1 %copy-start.8 = (bf16[128,512]{1,0:T(8,128)(2,1)S(1)}, bf16[128,512]{1,0:T(8,128)(2,1)}, u32[]{:S(2)}) copy-start(bf16[128,512]{1,0:T(8,128)(2,1)} %own_second.1) | copy-start | bytes 393220
  45.2 14.1 %copy-start.9 = (bf16[256,512]{1,0:T(8,128)(2,1)S(1)}, bf16[256,512]{1,0:T(8,128)(2,1)}, u32[]{:S(2)}) copy-start(bf16[256,512]{1,0:T(8,128)(2,1)} %grad_node.1) | copy-start | bytes 786436
  56.9 20.2 %copy-start = (bf16[3,16,2,16,512]{4,3,2,1,0:T(8,128)(2,1)}, bf16[3,16,2,16,512]{4,3,2,1,0:T(8,128)(2,1)S(1)}, u32[]{:S(2)}) copy-start(bf16[3,16,2,16,512]{4,3,2,1,0:T(8,128)(2,1)S(1)} %get-tuple-element.81.refs_6_.first) | copy-start | bytes 4718596
  57.0 1.7 %collective-permute-start.6 = (bf16[768,128]{1,0:T(8,128)(2,1)S(1)}, bf16[768,128]{1,0:T(8,128)(2,1)S(1)}, u32[]{:S(2)}, u32[]{:S(2)}) collective-permute-start(bf16[768,128]{1,0:T(8,128)(2,1)S(1)} %collective-permute-done.3.refs_0_), channel_id=1, source_target_pairs={{0,4},{4,0},{1,5},{5,1},{2,6},{6,2},{3,7},{7,3},{8,12},{12,8},{9,1... | collective-permute-start | bytes 589832 | tf_op jit(solution)/shard_map/ppermute | solution.py:26
  57.6 1.4 %collective-permute-start.7 = (bf16[768,128]{1,0:T(8,128)(2,1)S(1)}, bf16[768,128]{1,0:T(8,128)(2,1)S(1)}, u32[]{:S(2)}, u32[]{:S(2)}) collective-permute-start(bf16[768,128]{1,0:T(8,128)(2,1)S(1)} %collective-permute-done.4.refs_1_), channel_id=1, source_target_pairs={{0,4},{4,0},{1,5},{5,1},{2,6},{6,2},{3,7},{7,3},{8,12},{12,8},{9,1... | collective-permute-start | bytes 589832 | tf_op jit(solution)/shard_map/ppermute | solution.py:26
  57.6 1.6 %collective-permute-start.8 = (bf16[768,128]{1,0:T(8,128)(2,1)S(1)}, bf16[768,128]{1,0:T(8,128)(2,1)S(1)}, u32[]{:S(2)}, u32[]{:S(2)}) collective-permute-start(bf16[768,128]{1,0:T(8,128)(2,1)S(1)} %collective-permute-done.5.refs_2_), channel_id=1, source_target_pairs={{0,4},{4,0},{1,5},{5,1},{2,6},{6,2},{3,7},{7,3},{8,12},{12,8},{9,1... | collective-permute-start | bytes 589832 | tf_op jit(solution)/shard_map/ppermute | solution.py:26
  77.2 6.6 %copy-start.10 = (bf16[256,512]{1,0:T(8,128)(2,1)}, bf16[256,512]{1,0:T(8,128)(2,1)S(1)}, u32[]{:S(2)}) copy-start(bf16[256,512]{1,0:T(8,128)(2,1)S(1)} %get-tuple-element.80.spread) | copy-start | bytes 786436
  77.2 4.2 %collective-permute-start.9 = (bf16[8,2,4,128,128]{4,3,2,1,0:T(8,128)(2,1)S(1)}, bf16[8,2,4,128,128]{4,3,2,1,0:T(8,128)(2,1)S(1)}, u32[]{:S(2)}, u32[]{:S(2)}) collective-permute-start(bf16[8,2,4,128,128]{4,3,2,1,0:T(8,128)(2,1)S(1)} %get-tuple-element.75), channel_id=1, source_target_pairs={{0,4},{4,0},{1,5},{5,1},{2,6},{6,2},{3,7},{7,3},{8,12},{12,8},{9,1... | collective-permute-start | bytes 6291464 | tf_op jit(solution)/shard_map/ppermute | solution.py:26
  83.8 35.2 %all-to-all-start.1 = ((bf16[64,128,128]{2,1,0:T(8,128)(2,1)}), bf16[64,128,128]{2,1,0:T(8,128)(2,1)S(1)}, u32[]{:S(2)}, u32[]{:S(2)}) async-start(bf16[64,128,128]{2,1,0:T(8,128)(2,1)} %bitcast.4), calls=%async_computation.1 | async-start | bytes 4194304 | tf_op jit(solution)/shard_map/all_to_all | solution.py:34
  90.4 28.9 %collective-permute-start.10 = (bf16[32,512]{1,0:T(8,128)(2,1)S(1)}, bf16[32,512]{1,0:T(8,128)(2,1)S(1)}, u32[]{:S(2)}, u32[]{:S(2)}) collective-permute-start(bf16[32,512]{1,0:T(8,128)(2,1)S(1)} %get-tuple-element.77), channel_id=1, source_target_pairs={{0,127},{1,0},{2,1},{3,2},{4,3},{5,4},{6,5},{7,6},{8,7},{9,8},{10,... | collective-permute-start | bytes 98312 | tf_op jit(solution)/shard_map/ppermute | solution.py:30
  93.4 25.9 %collective-permute-start.11 = (bf16[32,512]{1,0:T(8,128)(2,1)S(1)}, bf16[32,512]{1,0:T(8,128)(2,1)S(1)}, u32[]{:S(2)}, u32[]{:S(2)}) collective-permute-start(bf16[32,512]{1,0:T(8,128)(2,1)S(1)} %get-tuple-element.79), channel_id=1, source_target_pairs={{0,1},{1,2},{2,3},{3,4},{4,5},{5,6},{6,7},{7,8},{8,9},{9,10},{10,1... | collective-permute-start | bytes 98312 | tf_op jit(solution)/shard_map/ppermute | solution.py:30
  99.5 37.7 %copy-start.15 = (s32[1,2,32]{2,1,0:T(2,128)S(1)}, s32[1,2,32]{2,1,0:T(2,128)}, u32[]{:S(2)}) copy-start(s32[1,2,32]{2,1,0:T(2,128)} %param.18) | copy-start | bytes 772
  99.5 37.7 %copy-start.16 = (s32[1,4]{1,0:T(1,128)S(1)}, s32[1,4]{1,0:T(1,128)}, u32[]{:S(2)}) copy-start(s32[1,4]{1,0:T(1,128)} %owned.3) | copy-start | bytes 52
  133.2 4.0 %collective-permute-start.12 = (bf16[16,112,128]{2,1,0:T(8,128)(2,1)S(1)}, bf16[16,112,128]{2,1,0:T(8,128)(2,1)S(1)}, u32[]{:S(2)}, u32[]{:S(2)}) collective-permute-start(bf16[16,112,128]{2,1,0:T(8,128)(2,1)S(1)} %all_to_all.15.tiles), channel_id=1, source_target_pairs={{0,4},{4,0},{1,5},{5,1},{2,6},{6,2},{3,7},{7,3},{8,12},{12,8},{9,1... | collective-permute-start | bytes 1376264 | tf_op jit(solution)/shard_map/ppermute | solution.py:26

commit v13 on v11

--- a/solution.py
+++ b/solution.py
@@ -343,6 +343,12 @@
         to_prev[...] = remote[256:288].astype(BF16)
         to_next[...] = remote[288:320].astype(BF16)
         put_owned(co, remote[320:832], owned, keep, give)
+
+
+def pair_kernel(keep, got, pair):
+    for a in range(8):
+        for b in range(2):
+            pair[a, b] = (keep[a, b].astype(F32) + got[a, b].astype(F32)).astype(BF16)
 
 
 def edge_kernel(spread, first, grad_edge, hot, pre_grads, edge_grad):
@@ -548,7 +554,8 @@
         ),
     )(edge_count, *fixed, *moving)
 
-    pair = (keep.astype(F32) + other_core(give).astype(F32)).astype(BF16).reshape(64, 128, 128)
+    (pair,) = plain_call(pair_kernel, [], [keep, other_core(give)], [shape(*tiles)])
+    pair = pair.reshape(64, 128, 128)
     edge_first = after(first, pair)
     edge_grad = pl.pallas_call(
         edge_kernel,

time: 134 us -> 134 us (level)
  other arithmetic: 2.79 us -> 0.32 us
  Pallas kernels: 43.7 us -> 45.6 us
    convert_element_type x1 -> x0, other arithmetic: 2.47 us -> none  [shards(): (keep.astype(F32) + other_core(give).astype(F32)).astype(BF16)]
    pallas_call x2 -> x3, Pallas kernels: 4.92 us -> 6.76 us  [plain_call(): pl.pallas_call(kernel, in_specs=[SMEM] * len(scalars) + [WHOLE] * len(ope...]
where the time goes in v13:
time: 134 us; the launch traced here: 133 us
  Pallas kernels  45.6 us (34%)
  waiting for transfers between devices  35 us (26%)
  starting transfers between devices  34.5 us (26%)
  blocking collectives  13.8 us (10%)
  local copies, waits for them, and re-layouts  2.3 us (2%)
  between operations  1.51 us (1%)
    all_to_all x2, waiting for transfers between devices, exchange(): return lax.all_to_all(value, axes, 0, 0, tiled=True)  28.2 us
    all_to_all x2, starting transfers between devices, exchange(): return lax.all_to_all(value, axes, 0, 0, tiled=True)  18.8 us
    pallas_call x1, Pallas kernels, shards(): pl.pallas_call(backward_kernel, grid=(STEPS,), in_specs=[SMEM] + [like(v)...  15.3 us
    all_to_all x1, blocking collectives, exchange(): return lax.all_to_all(value, axes, 0, 0, tiled=True)  13.8 us
    pallas_call x1, Pallas kernels, shards(): pl.pallas_call(forward_kernel, grid=(STEPS,), in_specs=[SMEM] + [like(v)...  11.7 us
    pallas_call x3, Pallas kernels, plain_call(): pl.pallas_call(kernel, in_specs=[SMEM] * len(scalars) + [WHOLE] * len(ope...  6.76 us
    ppermute x6, starting transfers between devices, other_core(): return lax.ppermute(value, 'core', [(0, 1), (1, 0)])  6.63 us
    ppermute x6, waiting for transfers between devices, other_core(): return lax.ppermute(value, 'core', [(0, 1), (1, 0)])  6.59 us
  transfers between devices with their start and end apart: 15, of which 8 were waited for; matrix products, arithmetic and copies ran while one was open for 1% of the time, Pallas kernels for 18%

profile of v13, /device:TPU:1, one launch (start us, length us, event | category | flops | bytes accessed | tf_op | source)
XLA Modules:
  0.0 133.1 jit_solution(6435789605311303832)
XLA Ops:
  0.6 0.0 copy-start.9
  1.3 2.7 %shard_map.188 = (bf16[64,80,128]{2,1,0:T(8,128)(2,1)}, bf16[32,512]{1,0:T(8,128)(2,1)}, bf16[32,512]{1,0:T(8,128)(2,1)}, bf16[768,128]{1,0:T(8,128)(2,1)}) custom-call(s32[1]{0:T(128)S(6)} %copy.23.count, s32[1,4]{1,0:T(1,128)} %owned.3, bf16[256,512]{1,0:T(8,128)(2,1)} %node.5, s32[2,32]{1,0:T(2,128)} %bitcast.12, bf16[3,512,128]{2,1,0:T(8,128)(2,1)} %edge_first.1, ...), custom_call_target="tpu_custom_call" | custom-call | tf_op jit(solution)/shard_map/pallas_call | solution.py:395
  4.0 0.0 copy-start.10
  4.0 12.1 %all-to-all-start = ((bf16[64,80,128]{2,1,0:T(8,128)(2,1)}), bf16[64,80,128]{2,1,0:T(8,128)(2,1)S(1)}, u32[]{:S(2)}, u32[]{:S(2)}) async-start(bf16[64,80,128]{2,1,0:T(8,128)(2,1)} %get-tuple-element.51), calls=%async_computation | async-start | bytes 2621440 | tf_op jit(solution)/shard_map/all_to_all | solution.py:34
  16.1 1.1 collective-permute-start
  17.2 2.4 %collective-permute-start.1 = (bf16[32,512]{1,0:T(8,128)(2,1)S(1)}, bf16[32,512]{1,0:T(8,128)(2,1)S(1)}, u32[]{:S(2)}, u32[]{:S(2)}) collective-permute-start(bf16[32,512]{1,0:T(8,128)(2,1)S(1)} %copy-done.18), channel_id=1, source_target_pairs={{0,127},{1,0},{2,1},{3,2},{4,3},{5,4},{6,5},{7,6},{8,7},{9,8},{10,... | collective-permute-start | bytes 98312 | tf_op jit(solution)/shard_map/ppermute | solution.py:30
  19.7 0.6 reshape.48.dst_wide
  20.3 0.6 reshape.47.src_wide
  20.9 5.8 %shard_map.189 = (bf16[2048,256]{1,0:T(8,128)(2,1)}, bf16[1152,2048]{1,0:T(8,128)(2,1)}, bf16[512,2048]{1,0:T(8,128)(2,1)}) custom-call(s32[1]{0:T(128)S(6)} %copy.23.count, s32[16,128]{1,0:T(8,128)} %bitcast.9, s32[4,512]{1,0:T(4,128)} %reshape.47.src_wide, s32[4,512]{1,0:T(4,128)} %reshape.48.dst_wide, bf16[2048,512]{1,0:T(8,128)(2,1)} %edge.3), custom_call_target="tpu_custom_call" | custom-call | flops 20000000 | bytes 14000000 | tf_op jit(solution)/shard_map/pallas_call | solution.py:460
  26.7 0.2 collective-permute-done.prev
  26.9 0.0 collective-permute-done.1.following
  26.9 9.1 %all-to-all-done = bf16[64,80,128]{2,1,0:T(8,128)(2,1)S(1)} async-done(((bf16[64,80,128]{2,1,0:T(8,128)(2,1)}), bf16[64,80,128]{2,1,0:T(8,128)(2,1)S(1)}, u32[]{:S(2)}, u32[]{:S(2)}) %all-to-all-start) | async-done | bytes 1310752 | tf_op jit(solution)/shard_map/all_to_all | solution.py:34
  35.9 2.6 %collective-permute-start.2 = (bf16[16,4,80,128]{3,2,1,0:T(8,128)(2,1)S(1)}, bf16[16,4,80,128]{3,2,1,0:T(8,128)(2,1)S(1)}, u32[]{:S(2)}, u32[]{:S(2)}) collective-permute-start(bf16[16,4,80,128]{3,2,1,0:T(8,128)(2,1)S(1)} %bitcast.7), channel_id=1, source_target_pairs={{0,4},{4,0},{1,5},{5,1},{2,6},{6,2},{3,7},{7,3},{8,12},{12,8},{9,1... | collective-permute-start | bytes 3932168 | tf_op jit(solution)/shard_map/ppermute | solution.py:26
  38.5 0.4 collective-permute-start.5
  38.9 2.3 %collective-permute-start.4 = (bf16[768,128]{1,0:T(8,128)(2,1)}, bf16[768,128]{1,0:T(8,128)(2,1)S(1)}, u32[]{:S(2)}, u32[]{:S(2)}) collective-permute-start(bf16[768,128]{1,0:T(8,128)(2,1)} %get-tuple-element.60), channel_id=1, source_target_pairs={{0,2},{1,3},{2,0},{3,1},{4,6},{5,7},{6,4},{7,5},{8,10},{9,11},{10,... | collective-permute-start | bytes 589832 | tf_op jit(solution)/shard_map/ppermute | solution.py:475
  41.2 0.0 collective-permute-start.3
  41.2 0.0 collective-permute-done.2.far
  41.2 0.0 copy-start.5
  41.2 0.9 copy-done.5
  42.2 0.0 copy-start.8
  42.2 0.0 copy-start.16
  42.2 0.0 copy-start.17
  42.2 11.7 %shard_map.190 = (bf16[2048,512]{1,0:T(8,128)(2,1)}, bf16[256,512]{1,0:T(8,128)(2,1)S(1)}, bf16[2048,512]{1,0:T(8,128)(2,1)S(1)}, bf16[2048,512]{1,0:T(8,128)(2,...) custom-call(s32[1]{0:T(128)S(6)} %copy.23.count, ...), custom_call_target="tpu_custom_call" | custom-call | flops 7000000000 | bytes 18000000 | tf_op jit(solution)/shard_map/pallas_call | solution.py:480
  53.9 0.0 collective-permute-done.5.refs_2_
  53.9 0.0 collective-permute-done.4.refs_1_
  53.9 0.0 collective-permute-done.3.refs_0_
  53.9 0.6 collective-permute-start.6
  54.5 0.1 collective-permute-start.7
  54.6 0.4 collective-permute-start.8
  55.0 0.6 collective-permute-done.6.refs_3_
  55.6 0.4 collective-permute-done.7.refs_4_
  56.0 0.3 collective-permute-done.8.refs_5_
  56.3 15.3 %shard_map.191 = (bf16[256,512]{1,0:T(8,128)(2,1)}, f32[256,512]{1,0:T(8,128)S(1)}, bf16[2048,512]{1,0:T(8,128)(2,1)}, bf16[32,512]{1,0:T(8,128)(2,1)S(1)}, bf16...) custom-call(s32[1]{0:T(128)S(6)} %copy.23.count, ...), custom_call_target="tpu_custom_call" | custom-call | flops 8999999488 | bytes 24000000 | tf_op jit(solution)/shard_map/pallas_call | solution.py:519
  71.6 0.2 collective-permute-start.9
  71.8 3.9 %collective-permute-done.9.got = bf16[8,2,4,128,128]{4,3,2,1,0:T(8,128)(2,1)S(1)} collective-permute-done((bf16[8,2,4,128,128]{4,3,2,1,0:T(8,128)(2,1)S(1)}, bf16[8,2,4,128,128]{4,3,2,1,0:T(8,128)(2,1)S(1)}, u32[]{:S(2)}, u32[]{:S(2)}) %collective-permute-start.9) | collective-permute-done | bytes 2097184 | tf_op jit(solution)/shard_map/ppermute | solution.py:26
  75.7 1.8 %shard_map.192 = bf16[8,2,4,128,128]{4,3,2,1,0:T(8,128)(2,1)} custom-call(bf16[8,2,4,128,128]{4,3,2,1,0:T(8,128)(2,1)S(1)} %get-tuple-element.74.keep, bf16[8,2,4,128,128]{4,3,2,1,0:T(8,128)(2,1)S(1)} %collective-permute-done.9.got), custom_call_target="tpu_custom_call" | custom-call | tf_op jit(solution)/shard_map/pallas_call | solution.py:395
  77.6 6.7 %all-to-all-start.1 = ((bf16[64,128,128]{2,1,0:T(8,128)(2,1)}), bf16[64,128,128]{2,1,0:T(8,128)(2,1)S(1)}, u32[]{:S(2)}, u32[]{:S(2)}) async-start(bf16[64,128,128]{2,1,0:T(8,128)(2,1)} %bitcast.4), calls=%async_computation.1 | async-start | bytes 4194304 | tf_op jit(solution)/shard_map/all_to_all | solution.py:34
  84.2 3.0 %collective-permute-start.10 = (bf16[32,512]{1,0:T(8,128)(2,1)S(1)}, bf16[32,512]{1,0:T(8,128)(2,1)S(1)}, u32[]{:S(2)}, u32[]{:S(2)}) collective-permute-start(bf16[32,512]{1,0:T(8,128)(2,1)S(1)} %get-tuple-element.77), channel_id=1, source_target_pairs={{0,127},{1,0},{2,1},{3,2},{4,3},{5,4},{6,5},{7,6},{8,7},{9,8},{10,... | collective-permute-start | bytes 98312 | tf_op jit(solution)/shard_map/ppermute | solution.py:30
  87.2 0.0 collective-permute-start.11
  87.2 6.1 %shard_map.193 = bf16[2048,512]{1,0:T(8,128)(2,1)} custom-call(bf16[256,512]{1,0:T(8,128)(2,1)} %copy-done.4, bf16[3,16,2,16,512]{4,3,2,1,0:T(8,128)(2,1)} %copy-done.2, bf16[2048,512]{1,0:T(8,128)(2,1)} %grad_edge.1, bf16[2048,256]{1,0:T(8,128)(2,1)} %get-tuple-element.55.refs_15_.hot, ...), custom_call_target="tpu_custom_call", output_to_operand_aliasing={{}: (4, {})} | custom-call | flops 1600000000 | bytes 9000000 | tf_op jit(solution)/shard_map/pallas_call | solution.py:560
  93.3 19.2 %all-to-all-done.1 = bf16[64,128,128]{2,1,0:T(8,128)(2,1)S(1)} async-done(((bf16[64,128,128]{2,1,0:T(8,128)(2,1)}), bf16[64,128,128]{2,1,0:T(8,128)(2,1)S(1)}, u32[]{:S(2)}, u32[]{:S(2)}) %all-to-all-start.1) | async-done | bytes 2097184 | tf_op jit(solution)/shard_map/all_to_all | solution.py:34
  112.5 0.3 reduce_sum.12.own
  112.8 0.0 collective-permute-done.11.behind
  112.8 0.1 broadcast_in_dim.2
  112.9 13.8 %all_to_all.15.tiles = bf16[16,112,128]{2,1,0:T(8,128)(2,1)S(1)} all-to-all(bf16[16,112,128]{2,1,0:T(8,128)(2,1)S(1)} %broadcast_in_dim.2), channel_id=1, replica_groups=mesh['z'=4,'x'=4,'core'=2,'feat'=4] {'z','x'}, dimensions={0} | all-to-all | bytes 917504 | tf_op jit(solution)/shard_map/all_to_all | solution.py:34
  126.7 2.7 %collective-permute-start.12 = (bf16[16,112,128]{2,1,0:T(8,128)(2,1)S(1)}, bf16[16,112,128]{2,1,0:T(8,128)(2,1)S(1)}, u32[]{:S(2)}, u32[]{:S(2)}) collective-permute-start(bf16[16,112,128]{2,1,0:T(8,128)(2,1)S(1)} %all_to_all.15.tiles), channel_id=1, source_target_pairs={{0,4},{4,0},{1,5},{5,1},{2,6},{6,2},{3,7},{7,3},{8,12},{12,8},{9,1... | collective-permute-start | bytes 1376264 | tf_op jit(solution)/shard_map/ppermute | solution.py:26
  129.4 1.4 %collective-permute-done.12.far = bf16[16,112,128]{2,1,0:T(8,128)(2,1)S(1)} collective-permute-done((bf16[16,112,128]{2,1,0:T(8,128)(2,1)S(1)}, bf16[16,112,128]{2,1,0:T(8,128)(2,1)S(1)}, u32[]{:S(2)}, u32[]{:S(2)}) %collective-permute-start.12) | collective-permute-done | bytes 458784 | tf_op jit(solution)/shard_map/ppermute | solution.py:26
  130.8 2.2 %shard_map.194 = (f32[3,16,2,16,128]{4,3,2,1,0:T(8,128)}, f32[128,512]{1,0:T(8,128)}, f32[2,16,2,16,128]{4,3,2,1,0:T(8,128)}, f32[128,512]{1,0:T(8,128)}, f32[256,512]{1,0:T(8,128)}) custom-call(s32[1]{0:T(128)S(6)} %copy.23.count, s32[1,4]{1,0:T(1,128)S(1)} %copy-done.14, bf16[16,112,128]{2,1,0:T(8,128)(2,1)S(1)} %all_to_all.15.tiles, ...), custom_call_target="tpu_custom_call" | custom-call | tf_op jit(solution)/shard_map/pallas_call | solution.py:395
  (33 shorter events, 0.1 us)
Async XLA Ops:
  0.6 19.0 %copy-start.9 = (s32[2048]{0:T(1024)S(1)}, s32[2048]{0:T(1024)}, u32[]{:S(2)}) copy-start(s32[2048]{0:T(1024)} %param.16) | copy-start | bytes 24580
  0.6 19.6 %copy-start.12 = (s32[2048]{0:T(1024)S(1)}, s32[2048]{0:T(1024)}, u32[]{:S(2)}) copy-start(s32[2048]{0:T(1024)} %param.15) | copy-start | bytes 24580
  4.0 13.2 %copy-start.18 = (bf16[32,512]{1,0:T(8,128)(2,1)S(1)}, bf16[32,512]{1,0:T(8,128)(2,1)}, u32[]{:S(2)}) copy-start(bf16[32,512]{1,0:T(8,128)(2,1)} %get-tuple-element.50) | copy-start | bytes 98308
  4.0 37.2 %copy-start = (bf16[2048,512]{1,0:T(8,128)(2,1)S(1)}, bf16[2048,512]{1,0:T(8,128)(2,1)}, u32[]{:S(2)}) copy-start(bf16[2048,512]{1,0:T(8,128)(2,1)} %edge.3) | copy-start | bytes 6291460
  4.0 37.2 %copy-start.10 = (s32[2048]{0:T(1024)S(1)}, s32[2048]{0:T(1024)}, u32[]{:S(2)}) copy-start(s32[2048]{0:T(1024)} %param.16) | copy-start | bytes 24580
  4.0 31.9 %all-to-all-start = ((bf16[64,80,128]{2,1,0:T(8,128)(2,1)}), bf16[64,80,128]{2,1,0:T(8,128)(2,1)S(1)}, u32[]{:S(2)}, u32[]{:S(2)}) async-start(bf16[64,80,128]{2,1,0:T(8,128)(2,1)} %get-tuple-element.51), calls=%async_computation | async-start | bytes 2621440 | tf_op jit(solution)/shard_map/all_to_all | solution.py:34
  16.1 10.7 %collective-permute-start = (bf16[32,512]{1,0:T(8,128)(2,1)}, bf16[32,512]{1,0:T(8,128)(2,1)S(1)}, u32[]{:S(2)}, u32[]{:S(2)}) collective-permute-start(bf16[32,512]{1,0:T(8,128)(2,1)} %get-tuple-element.49), channel_id=1, source_target_pairs={{0,1},{1,2},{2,3},{3,4},{4,5},{5,6},{6,7},{7,8},{8,9},{9,10},{10,1... | collective-permute-start | bytes 98312 | tf_op jit(solution)/shard_map/ppermute | solution.py:30
  17.2 9.6 %collective-permute-start.1 = (bf16[32,512]{1,0:T(8,128)(2,1)S(1)}, bf16[32,512]{1,0:T(8,128)(2,1)S(1)}, u32[]{:S(2)}, u32[]{:S(2)}) collective-permute-start(bf16[32,512]{1,0:T(8,128)(2,1)S(1)} %copy-done.18), channel_id=1, source_target_pairs={{0,127},{1,0},{2,1},{3,2},{4,3},{5,4},{6,5},{7,6},{8,7},{9,8},{10,... | collective-permute-start | bytes 98312 | tf_op jit(solution)/shard_map/ppermute | solution.py:30
  20.3 20.9 %copy-start.11 = (s32[4,512]{1,0:T(4,128)S(1)}, s32[4,512]{1,0:T(4,128)}, u32[]{:S(2)}) copy-start(s32[4,512]{1,0:T(4,128)} %reshape.48.dst_wide) | copy-start | bytes 24580
  35.9 5.3 %collective-permute-start.2 = (bf16[16,4,80,128]{3,2,1,0:T(8,128)(2,1)S(1)}, bf16[16,4,80,128]{3,2,1,0:T(8,128)(2,1)S(1)}, u32[]{:S(2)}, u32[]{:S(2)}) collective-permute-start(bf16[16,4,80,128]{3,2,1,0:T(8,128)(2,1)S(1)} %bitcast.7), channel_id=1, source_target_pairs={{0,4},{4,0},{1,5},{5,1},{2,6},{6,2},{3,7},{7,3},{8,12},{12,8},{9,1... | collective-permute-start | bytes 3932168 | tf_op jit(solution)/shard_map/ppermute | solution.py:26
  38.5 15.4 %collective-permute-start.5 = (bf16[768,128]{1,0:T(8,128)(2,1)}, bf16[768,128]{1,0:T(8,128)(2,1)S(1)}, u32[]{:S(2)}, u32[]{:S(2)}) collective-permute-start(bf16[768,128]{1,0:T(8,128)(2,1)} %get-tuple-element.60), channel_id=1, source_target_pairs={{0,3},{1,0},{2,1},{3,2},{4,7},{5,4},{6,5},{7,6},{8,11},{9,8},{10,9... | collective-permute-start | bytes 589832 | tf_op jit(solution)/shard_map/ppermute | solution.py:475
  38.9 15.0 %collective-permute-start.4 = (bf16[768,128]{1,0:T(8,128)(2,1)}, bf16[768,128]{1,0:T(8,128)(2,1)S(1)}, u32[]{:S(2)}, u32[]{:S(2)}) collective-permute-start(bf16[768,128]{1,0:T(8,128)(2,1)} %get-tuple-element.60), channel_id=1, source_target_pairs={{0,2},{1,3},{2,0},{3,1},{4,6},{5,7},{6,4},{7,5},{8,10},{9,11},{10,... | collective-permute-start | bytes 589832 | tf_op jit(solution)/shard_map/ppermute | solution.py:475
  41.2 12.7 %collective-permute-start.3 = (bf16[768,128]{1,0:T(8,128)(2,1)}, bf16[768,128]{1,0:T(8,128)(2,1)S(1)}, u32[]{:S(2)}, u32[]{:S(2)}) collective-permute-start(bf16[768,128]{1,0:T(8,128)(2,1)} %get-tuple-element.60), channel_id=1, source_target_pairs={{0,1},{1,2},{2,3},{3,0},{4,5},{5,6},{6,7},{7,4},{8,9},{9,10},{10,1... | collective-permute-start | bytes 589832 | tf_op jit(solution)/shard_map/ppermute | solution.py:475
  41.2 1.0 copy-start.5
  42.2 14.1 %copy-start.1 = (bf16[2048,512]{1,0:T(8,128)(2,1)S(1)}, bf16[2048,512]{1,0:T(8,128)(2,1)}, u32[]{:S(2)}) copy-start(bf16[2048,512]{1,0:T(8,128)(2,1)} %grad_edge.1) | copy-start | bytes 6291460
  42.2 14.1 %copy-start.3 = (bf16[2048,256]{1,0:T(8,128)(2,1)S(1)}, bf16[2048,256]{1,0:T(8,128)(2,1)}, u32[]{:S(2)}) copy-start(bf16[2048,256]{1,0:T(8,128)(2,1)} %get-tuple-element.55.refs_15_.hot) | copy-start | bytes 3145732
  42.2 14.1 %copy-start.6 = (bf16[256,512]{1,0:T(8,128)(2,1)S(1)}, bf16[256,512]{1,0:T(8,128)(2,1)}, u32[]{:S(2)}) copy-start(bf16[256,512]{1,0:T(8,128)(2,1)} %node.5) | copy-start | bytes 786436
  42.2 14.1 %copy-start.7 = (bf16[2,512,128]{2,1,0:T(8,128)(2,1)S(1)}, bf16[2,512,128]{2,1,0:T(8,128)(2,1)}, u32[]{:S(2)}) copy-start(bf16[2,512,128]{2,1,0:T(8,128)(2,1)} %own_first.1) | copy-start | bytes 786436
  42.2 14.1 %copy-start.8 = (bf16[128,512]{1,0:T(8,128)(2,1)S(1)}, bf16[128,512]{1,0:T(8,128)(2,1)}, u32[]{:S(2)}) copy-start(bf16[128,512]{1,0:T(8,128)(2,1)} %own_second.1) | copy-start | bytes 393220
  42.2 14.1 %copy-start.15 = (bf16[1152,2048]{1,0:T(8,128)(2,1)S(1)}, bf16[1152,2048]{1,0:T(8,128)(2,1)}, u32[]{:S(2)}) copy-start(bf16[1152,2048]{1,0:T(8,128)(2,1)} %get-tuple-element.72.refs_16_) | copy-start | bytes 14155780
  42.2 14.1 %copy-start.16 = (bf16[512,2048]{1,0:T(8,128)(2,1)S(1)}, bf16[512,2048]{1,0:T(8,128)(2,1)}, u32[]{:S(2)}) copy-start(bf16[512,2048]{1,0:T(8,128)(2,1)} %get-tuple-element.67.refs_9_) | copy-start | bytes 6291460
  42.2 14.1 %copy-start.17 = (bf16[256,512]{1,0:T(8,128)(2,1)S(1)}, bf16[256,512]{1,0:T(8,128)(2,1)}, u32[]{:S(2)}) copy-start(bf16[256,512]{1,0:T(8,128)(2,1)} %grad_node.1) | copy-start | bytes 786436
  53.9 17.7 %copy-start.2 = (bf16[3,16,2,16,512]{4,3,2,1,0:T(8,128)(2,1)}, bf16[3,16,2,16,512]{4,3,2,1,0:T(8,128)(2,1)S(1)}, u32[]{:S(2)}) copy-start(bf16[3,16,2,16,512]{4,3,2,1,0:T(8,128)(2,1)S(1)} %get-tuple-element.81.refs_6_.first) | copy-start | bytes 4718596
  53.9 1.7 %collective-permute-start.6 = (bf16[768,128]{1,0:T(8,128)(2,1)S(1)}, bf16[768,128]{1,0:T(8,128)(2,1)S(1)}, u32[]{:S(2)}, u32[]{:S(2)}) collective-permute-start(bf16[768,128]{1,0:T(8,128)(2,1)S(1)} %collective-permute-done.3.refs_0_), channel_id=1, source_target_pairs={{0,4},{4,0},{1,5},{5,1},{2,6},{6,2},{3,7},{7,3},{8,12},{12,8},{9,1... | collective-permute-start | bytes 589832 | tf_op jit(solution)/shard_map/ppermute | solution.py:26
  54.5 1.4 %collective-permute-start.7 = (bf16[768,128]{1,0:T(8,128)(2,1)S(1)}, bf16[768,128]{1,0:T(8,128)(2,1)S(1)}, u32[]{:S(2)}, u32[]{:S(2)}) collective-permute-start(bf16[768,128]{1,0:T(8,128)(2,1)S(1)} %collective-permute-done.4.refs_1_), channel_id=1, source_target_pairs={{0,4},{4,0},{1,5},{5,1},{2,6},{6,2},{3,7},{7,3},{8,12},{12,8},{9,1... | collective-permute-start | bytes 589832 | tf_op jit(solution)/shard_map/ppermute | solution.py:26
  54.6 1.6 %collective-permute-start.8 = (bf16[768,128]{1,0:T(8,128)(2,1)S(1)}, bf16[768,128]{1,0:T(8,128)(2,1)S(1)}, u32[]{:S(2)}, u32[]{:S(2)}) collective-permute-start(bf16[768,128]{1,0:T(8,128)(2,1)S(1)} %collective-permute-done.5.refs_2_), channel_id=1, source_target_pairs={{0,4},{4,0},{1,5},{5,1},{2,6},{6,2},{3,7},{7,3},{8,12},{12,8},{9,1... | collective-permute-start | bytes 589832 | tf_op jit(solution)/shard_map/ppermute | solution.py:26
  71.6 6.0 %copy-start.4 = (bf16[256,512]{1,0:T(8,128)(2,1)}, bf16[256,512]{1,0:T(8,128)(2,1)S(1)}, u32[]{:S(2)}) copy-start(bf16[256,512]{1,0:T(8,128)(2,1)S(1)} %get-tuple-element.80.spread) | copy-start | bytes 786436
  71.6 4.2 %collective-permute-start.9 = (bf16[8,2,4,128,128]{4,3,2,1,0:T(8,128)(2,1)S(1)}, bf16[8,2,4,128,128]{4,3,2,1,0:T(8,128)(2,1)S(1)}, u32[]{:S(2)}, u32[]{:S(2)}) collective-permute-start(bf16[8,2,4,128,128]{4,3,2,1,0:T(8,128)(2,1)S(1)} %get-tuple-element.75), channel_id=1, source_target_pairs={{0,4},{4,0},{1,5},{5,1},{2,6},{6,2},{3,7},{7,3},{8,12},{12,8},{9,1... | collective-permute-start | bytes 6291464 | tf_op jit(solution)/shard_map/ppermute | solution.py:26
  77.6 34.9 %all-to-all-start.1 = ((bf16[64,128,128]{2,1,0:T(8,128)(2,1)}), bf16[64,128,128]{2,1,0:T(8,128)(2,1)S(1)}, u32[]{:S(2)}, u32[]{:S(2)}) async-start(bf16[64,128,128]{2,1,0:T(8,128)(2,1)} %bitcast.4), calls=%async_computation.1 | async-start | bytes 4194304 | tf_op jit(solution)/shard_map/all_to_all | solution.py:34
  84.2 28.6 %collective-permute-start.10 = (bf16[32,512]{1,0:T(8,128)(2,1)S(1)}, bf16[32,512]{1,0:T(8,128)(2,1)S(1)}, u32[]{:S(2)}, u32[]{:S(2)}) collective-permute-start(bf16[32,512]{1,0:T(8,128)(2,1)S(1)} %get-tuple-element.77), channel_id=1, source_target_pairs={{0,127},{1,0},{2,1},{3,2},{4,3},{5,4},{6,5},{7,6},{8,7},{9,8},{10,... | collective-permute-start | bytes 98312 | tf_op jit(solution)/shard_map/ppermute | solution.py:30
  87.2 25.6 %collective-permute-start.11 = (bf16[32,512]{1,0:T(8,128)(2,1)S(1)}, bf16[32,512]{1,0:T(8,128)(2,1)S(1)}, u32[]{:S(2)}, u32[]{:S(2)}) collective-permute-start(bf16[32,512]{1,0:T(8,128)(2,1)S(1)} %get-tuple-element.79), channel_id=1, source_target_pairs={{0,1},{1,2},{2,3},{3,4},{4,5},{5,6},{6,7},{7,8},{8,9},{9,10},{10,1... | collective-permute-start | bytes 98312 | tf_op jit(solution)/shard_map/ppermute | solution.py:30
  93.3 37.5 %copy-start.13 = (s32[1,2,32]{2,1,0:T(2,128)S(1)}, s32[1,2,32]{2,1,0:T(2,128)}, u32[]{:S(2)}) copy-start(s32[1,2,32]{2,1,0:T(2,128)} %param.18) | copy-start | bytes 772
  93.3 37.5 %copy-start.14 = (s32[1,4]{1,0:T(1,128)S(1)}, s32[1,4]{1,0:T(1,128)}, u32[]{:S(2)}) copy-start(s32[1,4]{1,0:T(1,128)} %owned.3) | copy-start | bytes 52
  126.7 4.1 %collective-permute-start.12 = (bf16[16,112,128]{2,1,0:T(8,128)(2,1)S(1)}, bf16[16,112,128]{2,1,0:T(8,128)(2,1)S(1)}, u32[]{:S(2)}, u32[]{:S(2)}) collective-permute-start(bf16[16,112,128]{2,1,0:T(8,128)(2,1)S(1)} %all_to_all.15.tiles), channel_id=1, source_target_pairs={{0,4},{4,0},{1,5},{5,1},{2,6},{6,2},{3,7},{7,3},{8,12},{12,8},{9,1... | collective-permute-start | bytes 1376264 | tf_op jit(solution)/shard_map/ppermute | solution.py:26
